TPU v7x, 32 devices: a whole 2x2x4 slice. The times are simulated.
32 devices in a mesh: seq: 8 (over z, y), sub: 4 (over x, core).
Axes of the slice: x: 2, y: 2, z: 4, core: 2. Of those that a mesh axis runs over, the one named last changes fastest.
Arguments:
- normed: bfloat16 [4096, 2048], P(('seq', 'sub')), as said below
- w_query: bfloat16 [2048, 2048], P(None, 'sub'), as said below
- w_key: bfloat16 [2048, 2048], P(None, 'sub'), as said below
- w_value: bfloat16 [2048, 2048], P(None, 'sub'), may hold values from -0.125 to 0.125
- w_out: bfloat16 [2048, 2048], P('sub'), may hold values from -0.25 to 0.25
- pattern: int32 [16, 128], P('sub'), may hold values from 0 to 127, each once within a row
- slide_lengths: int32 [8], replicated, may hold values from 1 to 20, 32 in all
Outputs:
- mixed: bfloat16 [4096, 2048], P(('seq', 'sub'))
Inputs may be any that keep to these rules, and one draw needn't show every extreme that they name: `pattern`: each row is an ordering of the 128 positions of a block. `slide_lengths`: the slides lie end to end and fill all 32 blocks. `normed`: entries of order one. `w_query`: entries of order 2048 ** -0.5. `w_key`: entries of order 2048 ** -0.5.
All inputs are finite; a program needn't handle non-finite values.
Results may differ from a plain program's by a relative error of at most 0.012.
Values may be sent and summed in bfloat16 or wider, within the bound.
No kernel may reach another device: no remote copies, remote signals or barrier semaphores. Data moves between devices by JAX's collectives and lax.ppermute only.
A program may use at most 128 MiB of HBM per device.

v0:
```python
import math

import jax
import jax.numpy as jnp
from jax import lax
from jax.sharding import PartitionSpec as P

HEAD_SIZE = 128
BLOCK = 128
DILATED_KEPT = 16


def slide_count(block_index, slide_ends):
    return jnp.sum((block_index[:, None] >= slide_ends[None, :]).astype(jnp.int32), axis=1)


def shards(normed, w_query, w_key, w_value, w_out, pattern, slide_lengths):
    head_cols = w_query.shape[1]
    nearby_heads = head_cols // HEAD_SIZE
    piece = lax.all_gather(normed, "sub", axis=0, tiled=True)
    outputs = [
        jnp.dot(piece, weight, preferred_element_type=jnp.float32).astype(jnp.bfloat16)
        for weight in (w_query, w_key, w_value)
    ]
    projected = jnp.concatenate(outputs, axis=1)
    queries = projected[:, :head_cols]
    keys_all = projected[:, head_cols : 2 * head_cols]
    values_all = projected[:, 2 * head_cols :]
    span_len = projected.shape[0]
    span_of_blocks = span_len // BLOCK
    my_span = lax.axis_index("seq")
    slide_ends = jnp.cumsum(slide_lengths)
    kept_positions = pattern[:, :DILATED_KEPT]

    def dilate(source):
        blocked = source.reshape(span_of_blocks, BLOCK, nearby_heads, HEAD_SIZE)
        selected_keys = [
            blocked[:, kept_positions[head_index], head_index, :]
            for head_index in range(nearby_heads)
        ]
        return jnp.stack(selected_keys).reshape(
            nearby_heads, span_of_blocks * DILATED_KEPT, HEAD_SIZE
        )

    far_keys, far_values = (
        lax.all_gather(dilate(keys_all), "seq", axis=1, tiled=True),
        lax.all_gather(dilate(values_all), "seq", axis=1, tiled=True),
    )
    distant_count = far_keys.shape[1]
    distant_block = jnp.arange(distant_count, dtype=jnp.int32) // DILATED_KEPT
    distant_slide = slide_count(distant_block, slide_ends)
    far_span = distant_block // span_of_blocks
    row_block = my_span * span_of_blocks + jnp.arange(span_len, dtype=jnp.int32) // BLOCK
    row_slide = slide_count(row_block, slide_ends)
    near_mask = row_slide[:, None] == row_slide[None, :]
    far_mask = (row_slide[:, None] == distant_slide[None, :]) & (far_span != my_span)[None, :]
    scale = 1.0 / math.sqrt(HEAD_SIZE)
    outputs = []
    for head_index in range(nearby_heads):
        columns = slice(head_index * HEAD_SIZE, (head_index + 1) * HEAD_SIZE)
        query_head = queries[:, columns]
        near = (
            jnp.einsum(
                "qd,kd->qk", query_head, keys_all[:, columns], preferred_element_type=jnp.float32
            )
            * scale
        )
        far = (
            jnp.einsum(
                "qd,kd->qk", query_head, far_keys[head_index], preferred_element_type=jnp.float32
            )
            * scale
        )
        near = jnp.where(near_mask, near, -1e30)
        far = jnp.where(far_mask, far, -1e30)
        peak = jnp.maximum(
            jnp.max(near, axis=1, keepdims=True), jnp.max(far, axis=1, keepdims=True)
        )
        near_exp = jnp.exp(near - peak)
        far_exp = jnp.exp(far - peak)
        total = jnp.sum(near_exp, axis=1, keepdims=True) + jnp.sum(far_exp, axis=1, keepdims=True)
        near_weight = (near_exp / total).astype(jnp.bfloat16)
        far_weight = (far_exp / total).astype(jnp.bfloat16)
        context_head = jnp.dot(
            near_weight, values_all[:, columns], preferred_element_type=jnp.float32
        )
        context_head = context_head + jnp.dot(
            far_weight, far_values[head_index], preferred_element_type=jnp.float32
        )
        outputs.append(context_head.astype(jnp.bfloat16))
    context = jnp.concatenate(outputs, axis=1)
    return lax.psum_scatter(
        jnp.dot(context, w_out, preferred_element_type=jnp.float32),
        "sub",
        scatter_dimension=0,
        tiled=True,
    ).astype(jnp.bfloat16)


def solution(mesh):
    placed = (
        P(("seq", "sub"), None),
        P(None, "sub"),
        P(None, "sub"),
        P(None, "sub"),
        P("sub", None),
        P("sub", None),
        P(),
    )
    return jax.shard_map(
        shards, mesh=mesh, in_specs=placed, out_specs=P(("seq", "sub"), None), check_vma=False
    )
```

profile of v0, /device:TPU:0, one launch (start us, length us, event | category | flops | bytes accessed | tf_op | source)
XLA Modules:
  0.0 186.3 jit_solution(6494151695068165737)
XLA Ops:
  6.5 0.7 all-gather.2.cloned.1.call-update
  7.3 0.8 reduce-window.8
  8.3 0.8 fusion.55
  9.1 25.1 %all-gather.2.cloned.1.call-done = bf16[512,2048]{1,0:T(8,128)(2,1)} async-done(((bf16[128,2048]{1,0:T(8,128)(2,1)}), bf16[512,2048]{1,0:T(8,128)(2,1)}) %all-gather.2.cloned.1.call-update) | async-done | bytes 2097168 | tf_op jit(solution)/shard_map/all_gather | solution.py:20
  34.2 3.5 %convolution_convert_fusion.1 = bf16[512,512]{1,0:T(8,128)(2,1)S(1)} fusion(bf16[512,2048]{1,0:T(8,128)(2,1)} %all-gather.2.cloned.1.call-done, bf16[2048,512]{1,0:T(8,128)(2,1)} %param.9), kind=kOutput, calls=%fused_computation.25 | convolution fusion | flops 1074003968 | bytes 4718592 | tf_op jit(solution)/shard_map/dot_general | solution.py:22
  37.7 0.8 copy-done.2
  38.6 0.7 copy.32
  39.3 0.6 gather_fusion
  39.9 0.6 gather_fusion.1
  40.6 4.3 %convolution_convert_fusion = bf16[512,512]{1,0:T(8,128)(2,1)} fusion(bf16[512,2048]{1,0:T(8,128)(2,1)} %all-gather.2.cloned.1.call-done, bf16[2048,512]{1,0:T(8,128)(2,1)} %param.10), kind=kOutput, calls=%fused_computation.24 | convolution fusion | flops 1074003968 | bytes 4718592 | tf_op jit(solution)/shard_map/dot_general | solution.py:22
  44.8 1.2 reshape.271
  46.0 1.5 copy.40
  47.5 1.7 gather_fusion.4
  49.1 1.7 gather_fusion.5
  50.8 0.6 gather_fusion.2
  51.4 1.7 gather_fusion.6
  53.1 0.6 gather_fusion.3
  53.7 1.7 gather_fusion.7
  55.4 31.5 %all_gather.10 = bf16[4,512,128]{2,1,0:T(8,128)(2,1)S(1)} all-gather(bf16[4,64,128]{2,1,0:T(8,128)(2,1)S(1)} %pad_maximum_fusion), channel_id=1, replica_groups=mesh['seq'=8,'sub'=4] {'seq'}, dimensions={1}, use_global_device_ids=true | all-gather | bytes 589824 | tf_op jit(solution)/shard_map/all_gather | solution.py:46
  86.9 3.5 %convolution_convert_fusion.2 = bf16[512,512]{1,0:T(8,128)(2,1)S(1)} fusion(bf16[512,2048]{1,0:T(8,128)(2,1)} %all-gather.2.cloned.1.call-done, bf16[2048,512]{1,0:T(8,128)(2,1)} %param.8), kind=kOutput, calls=%fused_computation.26 | convolution fusion | flops 1074003968 | bytes 4718592 | tf_op jit(solution)/shard_map/dot_general | solution.py:22
  90.7 0.4 fusion.76
  91.1 0.4 fusion.74
  91.9 0.4 fusion.72
  92.6 0.4 fusion.70
  93.7 0.4 copy-done.1
  94.5 31.4 %all_gather.11 = bf16[4,512,128]{2,1,0:T(8,128)(2,1)S(1)} all-gather(bf16[4,64,128]{2,1,0:T(8,128)(2,1)S(1)} %pad_maximum_fusion.1), channel_id=1, replica_groups=mesh['seq'=8,'sub'=4] {'seq'}, dimensions={1}, use_global_device_ids=true | all-gather | bytes 589824 | tf_op jit(solution)/shard_map/all_gather | solution.py:47
  126.9 0.3 fusion.5
  127.5 0.3 fusion.26
  127.9 0.3 fusion.6
  129.3 3.2 %fusion.16 = f32[512,2048]{1,0:T(8,128)} fusion(bf16[512,2048]{1,0:T(8,128)(2,1)S(1)} %copy-done, bf16[512,128]{0,1:T(8,128)(2,1)S(1)} %fusion.7, bf16[512,128]{0,1:T(8,128)(2,1)S(1)} %fusion.6, bf16[512,128]{0,1:T(8,128)(2,1)S(1)} %fusion.5, bf16[512,128]{0,1:T(8,128)(2,1)S(1)} %fusion.4), kind=kOutput, calls=%fused_computation.60 | convolution fusion | flops 1075838976 | bytes 6815744 | tf_op jit(solution)/shard_map/dot_general | solution.py:93
  132.5 44.9 %reduce-scatter.2.cloned.1.call-done = f32[128,2048]{1,0:T(8,128)} async-done(((f32[512,2048]{1,0:T(8,128)}), f32[128,2048]{1,0:T(8,128)}) %reduce-scatter.2.cloned.1.call-update) | async-done | bytes 1048592 | tf_op jit(solution)/shard_map/reduce_scatter | solution.py:92
  177.4 2.1 %convert_element_type.71 = bf16[128,2048]{1,0:T(8,128)(2,1)} convert(f32[128,2048]{1,0:T(8,128)} %reduce-scatter.2.cloned.1.call-done) | non-fusion elementwise | flops 262144 | bytes 1572864 | tf_op jit(solution)/shard_map/convert_element_type | solution.py:97
  (44 shorter events, 4.6 us)
Async XLA Ops:
  6.5 122.7 %copy-start = (bf16[512,2048]{1,0:T(8,128)(2,1)S(1)}, bf16[512,2048]{1,0:T(8,128)(2,1)}, u32[]{:S(2)}) copy-start(bf16[512,2048]{1,0:T(8,128)(2,1)} %param.11) | copy-start | bytes 6291460
  6.5 27.7 %all-gather.2.cloned.1.call-start = ((), (), s32[]{:S(2)}) async-start(), calls=%async_computation.1 | async-start | bytes 2621440 | tf_op jit(solution)/shard_map/all_gather | solution.py:20
  7.3 170.1 %reduce-scatter.2.cloned.1.call-start = ((), (), s32[]{:S(2)}) async-start(), calls=%async_computation.2 | async-start | bytes 5242880 | tf_op jit(solution)/shard_map/reduce_scatter | solution.py:92
  37.7 0.8 copy-start.2
  86.9 3.5 %copy-start.3 = (bf16[512,512]{1,0:T(8,128)(2,1)S(1)}, bf16[512,512]{1,0:T(8,128)(2,1)}, u32[]{:S(2)}) copy-start(bf16[512,512]{1,0:T(8,128)(2,1)} %copy-done.2) | copy-start | bytes 1572868
  93.0 1.0 copy-start.1
Sparse Core Ops, SparseCore 0:
  8.9 25.2 all-gather.1
  132.6 44.7 reduce-scatter.1
where the time goes:
time: 187 us; the launch traced here: 186 us
  waiting for transfers between devices  70.7 us (38%)
  blocking collectives  62.8 us (34%)
  matrix products  20.1 us (11%)
  local copies, waits for them, and re-layouts  13.8 us (7%)
  between operations  13.7 us (7%)
  other arithmetic  5.13 us (3%)
    reduce_scatter x1, waiting for transfers between devices, shards(): lax.psum_scatter(jnp.dot(context, w_out, preferred_element_type=jnp.float...  44.9 us
    all_gather x1, blocking collectives, shards(): lax.all_gather(dilate(keys_all), 'seq', axis=1, tiled=True)  31.5 us
    all_gather x1, blocking collectives, shards(): lax.all_gather(dilate(values_all), 'seq', axis=1, tiled=True)  31.4 us
    all_gather x1, waiting for transfers between devices, shards(): piece = lax.all_gather(normed, 'sub', axis=0, tiled=True)  25.1 us
    dot_general x3, matrix products, shards(): jnp.dot(piece, weight, preferred_element_type=jnp.float32)  11.3 us
    gather x16, local copies, waits for them, and re-layouts, dilate(): blocked[:, kept_positions[head_index], head_index, :]  9.13 us
  transfers between devices with their start and end apart: 2, of which 2 were waited for; matrix products, arithmetic and copies ran while one was open for 1% of the time, Pallas kernels for 0%

commit v1 on v0

v1 whole, which is shorter than its diff:
```python
import functools
import math

import jax
import jax.numpy as jnp
from jax import lax
from jax.experimental import pallas as pl
from jax.experimental.pallas import tpu as pltpu
from jax.sharding import PartitionSpec as P

HEAD_SIZE = 128
BLOCK = 128
DILATED_KEPT = 16
BLOCKS_HALF = 2
FAR_ROWS = BLOCKS_HALF * DILATED_KEPT
HIDDEN = -1e30
SCALE = math.log2(math.e) / math.sqrt(HEAD_SIZE)
BF16 = jnp.bfloat16
F32 = jnp.float32


def dot(a, b):
    return jnp.dot(a, b, preferred_element_type=F32)


def dot_t(a, b):
    return lax.dot_general(a, b, (((1,), (1,)), ((), ())), preferred_element_type=F32)


def params(vmem_mib=40):
    return pltpu.CompilerParams(vmem_limit_bytes=vmem_mib * 2**20)


def project_kernel(weight_count, dilated, *refs):
    first, second = refs[0], refs[1]
    weights = refs[2 : 2 + weight_count]
    rest = refs[2 + weight_count :]
    rows = jnp.concatenate([first[...], second[...]], axis=0)
    outs = rest[1:] if dilated else rest
    results = []
    for index in range(weight_count):
        result = dot(rows, weights[index][...]).astype(BF16)
        outs[index][...] = result
        results.append(result)
    if not dilated:
        return
    pattern, kept = rest[0], outs[weight_count]
    keys, values = results[0], results[1]
    heads = keys.shape[1] // HEAD_SIZE
    base = pl.program_id(0) * heads
    positions = lax.broadcasted_iota(jnp.int32, (BLOCK, BLOCK), 0)
    for head in range(heads):
        row = pattern[pl.ds(base + head, 1), :]
        chosen = (positions == row).astype(F32).T[:DILATED_KEPT].astype(BF16)
        columns = slice(head * HEAD_SIZE, (head + 1) * HEAD_SIZE)
        for block in range(BLOCKS_HALF):
            where = slice(block * BLOCK, (block + 1) * BLOCK)
            pair = jnp.concatenate([keys[where, columns], values[where, columns]], axis=1)
            picked = dot(chosen, pair).astype(BF16)
            spot = slice(block * DILATED_KEPT, (block + 1) * DILATED_KEPT)
            kept[0, head, spot, :] = picked[:, :HEAD_SIZE]
            kept[1, head, spot, :] = picked[:, HEAD_SIZE:]


def project(first, second, weights, pattern=None):
    depth, width = weights[0].shape
    tile = min(256, width)
    heads = tile // HEAD_SIZE
    rows = first.shape[0] + second.shape[0]
    whole = pl.BlockSpec((first.shape[0], depth), lambda i: (0, 0))
    in_specs = [whole, whole]
    in_specs += [pl.BlockSpec((depth, tile), lambda i: (0, i)) for _ in weights]
    operands = [first, second, *weights]
    out_shape = [jax.ShapeDtypeStruct((rows, width), BF16) for _ in weights]
    out_specs = [pl.BlockSpec((rows, tile), lambda i: (0, i)) for _ in weights]
    if pattern is not None:
        in_specs.append(pl.BlockSpec(pattern.shape, lambda i: (0, 0)))
        operands.append(pattern)
        out_shape.append(
            jax.ShapeDtypeStruct((2, width // HEAD_SIZE, FAR_ROWS, HEAD_SIZE), BF16)
        )
        out_specs.append(pl.BlockSpec((2, heads, FAR_ROWS, HEAD_SIZE), lambda i: (0, i, 0, 0)))
    count = len(weights)
    return pl.pallas_call(
        functools.partial(project_kernel, count, pattern is not None),
        grid=(width // tile,),
        in_specs=in_specs,
        out_specs=out_specs,
        out_shape=out_shape,
        compiler_params=params(),
        cost_estimate=pl.CostEstimate(
            flops=2 * rows * depth * width * count,
            bytes_accessed=2 * count * depth * width,
            transcendentals=0,
        ),
    )(*operands)


def slide_of(place, slides, block):
    end, total = jnp.int32(0), jnp.zeros_like(block)
    for index in range(slides):
        end = end + place[index]
        total = total + (block >= end).astype(jnp.int32)
    return total


def hidden_if(condition):
    return jnp.where(condition, jnp.float32(0), jnp.float32(HIDDEN))


def my_block(place, slides, subs, relative):
    return place[slides] * subs + (place[slides + 1] ^ relative)


def far_bias(place, slides, subs, sources, blocks, row_slides):
    column = lax.broadcasted_iota(jnp.int32, (1, len(sources) * FAR_ROWS), 1)
    span = jnp.zeros_like(column)
    for index, source in enumerate(sources):
        span = jnp.where(column // FAR_ROWS == index, source, span)
    upper = (column // DILATED_KEPT) % BLOCKS_HALF
    me = place[slides + 1]
    block = span * subs + jnp.where(upper == 0, me ^ blocks[0], me ^ blocks[1])
    slide = slide_of(place, slides, block)
    elsewhere = span != place[slides]
    return [hidden_if((slide == mine) & elsewhere) for mine in row_slides]


def far_update(query, pieces, bias, state):
    keys = jnp.concatenate([piece[0] for piece in pieces], axis=0)
    values = jnp.concatenate([piece[1] for piece in pieces], axis=0)
    scores = dot_t(query, keys)
    scores = jnp.concatenate(
        [scores[i * BLOCK : (i + 1) * BLOCK] + bias[i] for i in range(len(bias))], axis=0
    )
    peak, total, gathered = state
    higher = jnp.maximum(peak, jnp.max(scores, axis=1, keepdims=True))
    shrink = jnp.exp2((peak - higher) * SCALE)
    weight = jnp.exp2((scores - higher) * SCALE)
    total = total * shrink + jnp.sum(weight, axis=1, keepdims=True)
    gathered = gathered * shrink + dot(weight.astype(BF16), values)
    return higher, total, gathered


def near_kernel(slides, subs, sources_of, far_count, place, *refs):
    query_parts, key_parts, value_parts = refs[0:2], refs[2:4], refs[4:6]
    far = refs[6 : 6 + far_count]
    gathered_out, stats_out = refs[6 + far_count :]
    query = jnp.concatenate([part[...] for part in query_parts], axis=0)
    keys = jnp.concatenate([part[...] for part in key_parts], axis=0)
    values = jnp.concatenate([part[...] for part in value_parts], axis=0)
    mine = [slide_of(place, slides, my_block(place, slides, subs, r)) for r in range(subs)]
    scores = dot_t(query, keys)
    rows = []
    for r in range(subs):
        bias = jnp.concatenate(
            [jnp.full((1, BLOCK), hidden_if(mine[r] == mine[c]), F32) for c in range(subs)], axis=1
        )
        rows.append(scores[r * BLOCK : (r + 1) * BLOCK] + bias)
    scores = jnp.concatenate(rows, axis=0)
    peak = jnp.max(scores, axis=1, keepdims=True)
    weight = jnp.exp2((scores - peak) * SCALE)
    total = jnp.sum(weight, axis=1, keepdims=True)
    state = peak, total, dot(weight.astype(BF16), values)
    if far_count:
        bias = far_bias(place, slides, subs, sources_of(place[slides]), (0, 1), mine)
        state = far_update(query, [piece[:, 0] for piece in far], bias, state)
    peak, total, gathered = state
    gathered_out[...] = gathered
    lane = lax.broadcasted_iota(jnp.int32, gathered.shape, 1)
    stats_out[0] = jnp.where(lane == 0, peak, total)


def far_kernel(slides, subs, sources_of, halves, relative, place, *refs):
    query = refs[0][...]
    gathered, stats = refs[1][...], refs[2][0]
    keep, send = refs[-2:]
    state = stats[:, 0:1], stats[:, 1:2], gathered
    mine = [slide_of(place, slides, my_block(place, slides, subs, r)) for r in relative]
    sources = sources_of(place[slides])
    start = 3
    for blocks in halves:
        if sources is None:
            pieces = refs[start]
            start += 1
            group = 8
            spans = pieces.shape[0]

            def step(index, state, pieces=pieces, blocks=blocks):
                base = index * group
                bias = far_bias(
                    place, slides, subs, [base + i for i in range(group)], blocks, mine
                )
                return far_update(query, [pieces[base + i][:, 0] for i in range(group)], bias, state)

            state = lax.fori_loop(0, spans // group, step, state)
        else:
            pieces = refs[start : start + len(sources)]
            start += len(sources)
            bias = far_bias(place, slides, subs, sources, blocks, mine)
            state = far_update(query, [piece[:, 0] for piece in pieces], bias, state)
    _, total, gathered = state
    context = (gathered / total).astype(BF16)
    keep[...] = context[:BLOCK]
    send[...] = context[BLOCK:]


def far_spec(piece):
    if piece.ndim == 4:
        return pl.BlockSpec((2, 1, FAR_ROWS, HEAD_SIZE), lambda h, place: (0, h, 0, 0))
    return pl.BlockSpec(
        (piece.shape[0], 2, 1, FAR_ROWS, HEAD_SIZE), lambda h, place: (0, 0, h, 0, 0)
    )


def near_attention(place, slides, subs, sources_of, queries, keys, values, far):
    half, width = queries[0].shape
    span = 2 * half
    heads = width // HEAD_SIZE
    part = pl.BlockSpec((half, HEAD_SIZE), lambda h, place: (0, h))
    columns = span + FAR_ROWS * len(far)
    return pl.pallas_call(
        functools.partial(near_kernel, slides, subs, sources_of, len(far)),
        grid_spec=pltpu.PrefetchScalarGridSpec(
            num_scalar_prefetch=1,
            grid=(heads,),
            in_specs=[part] * 6 + [far_spec(piece) for piece in far],
            out_specs=[
                pl.BlockSpec((span, HEAD_SIZE), lambda h, place: (0, h)),
                pl.BlockSpec((1, span, HEAD_SIZE), lambda h, place: (h, 0, 0)),
            ],
        ),
        out_shape=[
            jax.ShapeDtypeStruct((span, width), F32),
            jax.ShapeDtypeStruct((heads, span, HEAD_SIZE), F32),
        ],
        compiler_params=params(),
        cost_estimate=pl.CostEstimate(
            flops=4 * span * columns * width,
            bytes_accessed=6 * half * width * 2,
            transcendentals=heads * span * columns,
        ),
    )(place, *queries, *keys, *values, *far)


def far_attention(place, slides, subs, sources_of, relative, query, gathered, stats, halves):
    half, width = query.shape
    heads = width // HEAD_SIZE
    row = relative[0] // BLOCKS_HALF
    far = [piece for _, pieces in halves for piece in pieces]
    count = sum(1 if piece.ndim == 4 else piece.shape[0] for piece in far)
    result = pl.BlockSpec((BLOCK, HEAD_SIZE), lambda h, place: (0, h))
    return pl.pallas_call(
        functools.partial(
            far_kernel, slides, subs, sources_of, [blocks for blocks, _ in halves], relative
        ),
        grid_spec=pltpu.PrefetchScalarGridSpec(
            num_scalar_prefetch=1,
            grid=(heads,),
            in_specs=[
                pl.BlockSpec((half, HEAD_SIZE), lambda h, place: (0, h)),
                pl.BlockSpec((half, HEAD_SIZE), lambda h, place: (row, h)),
                pl.BlockSpec((1, half, HEAD_SIZE), lambda h, place: (h, row, 0)),
            ]
            + [far_spec(piece) for piece in far],
            out_specs=[result, result],
        ),
        out_shape=[jax.ShapeDtypeStruct((BLOCK, width), BF16)] * 2,
        compiler_params=params(),
        cost_estimate=pl.CostEstimate(
            flops=4 * half * FAR_ROWS * count * width,
            bytes_accessed=8 * half * width,
            transcendentals=heads * half * FAR_ROWS * count,
        ),
    )(place, query, gathered, stats, *far)


def mix_kernel(first, second, weight_first, weight_second, out):
    total = dot(first[...], weight_first[...]) + dot(second[...], weight_second[...])
    out[...] = total.astype(out.dtype)


def mix(first, second, weight_first, weight_second, dtype):
    rows, depth = first.shape
    width = weight_first.shape[1]
    tile = min(512, width)
    left = pl.BlockSpec((rows, depth), lambda i: (0, 0))
    right = pl.BlockSpec((depth, tile), lambda i: (0, i))
    return pl.pallas_call(
        mix_kernel,
        grid=(width // tile,),
        in_specs=[left, left, right, right],
        out_specs=pl.BlockSpec((rows, tile), lambda i: (0, i)),
        out_shape=jax.ShapeDtypeStruct((rows, width), dtype),
        compiler_params=params(),
        cost_estimate=pl.CostEstimate(
            flops=4 * rows * depth * width, bytes_accessed=4 * depth * width, transcendentals=0
        ),
    )(first, second, weight_first, weight_second)


def shards(seqs, subs, normed, w_query, w_key, w_value, w_out, pattern, slide_lengths):
    slides = slide_lengths.shape[0]
    place = jnp.concatenate(
        [
            slide_lengths,
            lax.axis_index("seq").astype(jnp.int32)[None],
            lax.axis_index("sub").astype(jnp.int32)[None],
        ]
    )

    def swap(array, bit):
        return lax.ppermute(array, "sub", [(i, i ^ bit) for i in range(subs)])

    across = swap(normed, 2)
    beside = swap(normed, 1)
    few = seqs == 8
    if few:
        moves = [(z, y) for z in range(4) for y in range(2) if (z, y) != (0, 0)]

        def sources_of(me):
            return [((me // 2 - z) % 4) * 2 + (me % 2 ^ y) for z, y in moves]

        def spread(kept):
            return [
                lax.ppermute(
                    kept,
                    "seq",
                    [(i, ((i // 2 + z) % 4) * 2 + (i % 2 ^ y)) for i in range(seqs)],
                )
                for z, y in moves
            ]

    else:

        def sources_of(me):
            return None

        def spread(kept):
            return [lax.all_gather(kept, "seq", axis=0)]

    keys_a, values_a, query_a, kept_a = project(
        normed, beside, [w_key, w_value, w_query], pattern
    )
    far_a = spread(kept_a)
    across_beside = swap(across, 1)
    w_out_beside = swap(lax.optimization_barrier((w_out, beside))[0], 1)
    keys_b, values_b, kept_b = project(across, across_beside, [w_key, w_value], pattern)
    far_b = spread(kept_b)
    (query_b,) = project(across, across_beside, [w_query])
    attend = (place, slides, subs, sources_of)
    gathered, stats = near_attention(
        *attend,
        (query_a, query_b),
        (keys_a, keys_b),
        (values_a, values_b),
        far_a if few else [],
    )
    halves = [((2, 3), far_b)] if few else [((0, 1), far_a), ((2, 3), far_b)]
    keep_b, send_b = far_attention(*attend, (2, 3), query_b, gathered, stats, halves)
    other_b = swap(send_b, 1)
    leaving = mix(keep_b, other_b, w_out, w_out_beside, BF16)
    arriving = swap(leaving, 2)
    keep_a, send_a = far_attention(*attend, (0, 1), query_a, gathered, stats, halves)
    other_a = swap(send_a, 1)
    own = mix(keep_a, other_a, w_out, w_out_beside, F32)
    return (own + arriving.astype(F32)).astype(BF16)


def solution(mesh):
    placed = (
        P(("seq", "sub"), None),
        P(None, "sub"),
        P(None, "sub"),
        P(None, "sub"),
        P("sub", None),
        P("sub", None),
        P(),
    )
    return jax.shard_map(
        functools.partial(shards, mesh.shape["seq"], mesh.shape["sub"]),
        mesh=mesh,
        in_specs=placed,
        out_specs=P(("seq", "sub"), None),
        check_vma=False,
    )
```

time: 187 us -> 88 us (0.47)
  blocking collectives: 62.8 us -> 0 us
  waiting for transfers between devices: 70.7 us -> 26.2 us
  starting transfers between devices: 0.04 us -> 26.9 us
  Pallas kernels: 0 us -> 23.7 us
  matrix products: 20.1 us -> 0 us
  between operations: 13.7 us -> 0.2 us
  local copies, waits for them, and re-layouts: 13.8 us -> 9.52 us
  other arithmetic: 5.13 us -> 1 us
    all_gather x2 -> x0, blocking collectives: 62.8 us -> none  [the longest x1 31.5 us: shards(): lax.all_gather(dilate(keys_all), 'seq', axis=1, tiled=True)]
    reduce_scatter x1 -> x0, waiting for transfers between devices: 44.9 us -> none  [shards(): lax.psum_scatter(jnp.dot(context, w_out, preferred_element_type=jnp.float...]
    ppermute x0 -> x21, starting transfers between devices: none -> 26.9 us  [the longest x14 21.7 us: spread(): lax.ppermute(kept, 'seq', [(i, (i // 2 + z) % 4 * 2 + (i % 2 ^ y)) for i...]
    ppermute x0 -> x21, waiting for transfers between devices: none -> 26.2 us  [the longest x7 21.5 us: swap(): return lax.ppermute(array, 'sub', [(i, i ^ bit) for i in range(subs)])]
    all_gather x1 -> x0, waiting for transfers between devices: 25.1 us -> none  [shards(): piece = lax.all_gather(normed, 'sub', axis=0, tiled=True)]
    pallas_call x0 -> x8, Pallas kernels: none -> 23.7 us  [the longest x2 6.81 us: far_attention(): pl.pallas_call(functools.partial(far_kernel, slides, subs, sources_of, [b...]
    dot_general x20 -> x0, matrix products: 20.1 us -> none  [the longest x3 11.3 us: shards(): jnp.dot(piece, weight, preferred_element_type=jnp.float32)]
    gather x16 -> x0, local copies, waits for them, and re-layouts: 9.13 us -> none  [dilate(): blocked[:, kept_positions[head_index], head_index, :]]
  transfers between devices with their start and end apart: 2 -> 21, of which waited for: 2 -> 8; matrix products, arithmetic and copies ran while one was open for 1% -> 0% of each run, Pallas kernels for 0% -> 23%
where the time goes in v1:
time: 88 us; the launch traced here: 87.6 us
  starting transfers between devices  26.9 us (31%)
  waiting for transfers between devices  26.2 us (30%)
  Pallas kernels  23.7 us (27%)
  local copies, waits for them, and re-layouts  9.52 us (11%)
  other arithmetic  1 us (1%)
    ppermute x14, starting transfers between devices, spread(): lax.ppermute(kept, 'seq', [(i, (i // 2 + z) % 4 * 2 + (i % 2 ^ y)) for i...  21.7 us
    ppermute x7, waiting for transfers between devices, swap(): return lax.ppermute(array, 'sub', [(i, i ^ bit) for i in range(subs)])  21.5 us
    unnamed x30, local copies, waits for them, and re-layouts  9.52 us
    pallas_call x2, Pallas kernels, far_attention(): pl.pallas_call(functools.partial(far_kernel, slides, subs, sources_of, [b...  6.81 us
    pallas_call x2, Pallas kernels, mix(): pl.pallas_call(mix_kernel, grid=(width // tile,), in_specs=[left, left, r...  6.48 us
    pallas_call x3, Pallas kernels, project(): pl.pallas_call(functools.partial(project_kernel, count, pattern is not No...  6.37 us
    ppermute x7, starting transfers between devices, swap(): return lax.ppermute(array, 'sub', [(i, i ^ bit) for i in range(subs)])  5.17 us
    ppermute x14, waiting for transfers between devices, spread(): lax.ppermute(kept, 'seq', [(i, (i // 2 + z) % 4 * 2 + (i % 2 ^ y)) for i...  4.76 us
  transfers between devices with their start and end apart: 21, of which 8 were waited for; matrix products, arithmetic and copies ran while one was open for 0% of the time, Pallas kernels for 23%

profile of v1, /device:TPU:0, one launch (start us, length us, event | category | flops | bytes accessed | tf_op | source)
XLA Modules:
  0.0 87.6 jit_solution(17383396025693258412)
XLA Ops:
  0.5 1.7 %collective-permute-done.refs_1_ = bf16[128,2048]{1,0:T(8,128)(2,1)S(1)} collective-permute-done((bf16[128,2048]{1,0:T(8,128)(2,1)}, bf16[128,2048]{1,0:T(8,128)(2,1)S(1)}, u32[]{:S(2)}, u32[]{:S(2)}) %collective-permute-start) | collective-permute-done | bytes 524320 | tf_op jit(solution)/shard_map/ppermute | solution.py:312
  2.6 2.6 %collective-permute-start.1 = (bf16[128,2048]{1,0:T(8,128)(2,1)}, bf16[128,2048]{1,0:T(8,128)(2,1)S(1)}, u32[]{:S(2)}, u32[]{:S(2)}) collective-permute-start(bf16[128,2048]{1,0:T(8,128)(2,1)} %refs_0_.1), channel_id=1, source_target_pairs={{0,2},{1,3},{2,0},{3,1},{4,6},{5,7},{6,4},{7,5},{8,10},{9,11},{10,... | collective-permute-start | bytes 1572872 | tf_op jit(solution)/shard_map/ppermute | solution.py:312
  5.2 12.7 %collective-permute-done.1.refs_0_ = bf16[128,2048]{1,0:T(8,128)(2,1)S(1)} collective-permute-done((bf16[128,2048]{1,0:T(8,128)(2,1)}, bf16[128,2048]{1,0:T(8,128)(2,1)S(1)}, u32[]{:S(2)}, u32[]{:S(2)}) %collective-permute-start.1) | collective-permute-done | bytes 524320 | tf_op jit(solution)/shard_map/ppermute | solution.py:312
  17.9 1.6 %copy-done = bf16[2048,512]{1,0:T(8,128)(2,1)S(1)} copy-done((bf16[2048,512]{1,0:T(8,128)(2,1)S(1)}, bf16[2048,512]{1,0:T(8,128)(2,1)}, u32[]{:S(2)}) %copy-start) | copy-done | bytes 2097176
  19.5 1.6 %copy-done.2 = bf16[2048,512]{1,0:T(8,128)(2,1)S(1)} copy-done((bf16[2048,512]{1,0:T(8,128)(2,1)S(1)}, bf16[2048,512]{1,0:T(8,128)(2,1)}, u32[]{:S(2)}) %copy-start.2) | copy-done | bytes 2097176
  21.1 1.6 %copy-done.5 = bf16[2048,512]{1,0:T(8,128)(2,1)S(1)} copy-done((bf16[2048,512]{1,0:T(8,128)(2,1)S(1)}, bf16[2048,512]{1,0:T(8,128)(2,1)}, u32[]{:S(2)}) %copy-start.5) | copy-done | bytes 2097176
  22.6 1.0 %copy-done.7 = bf16[128,2048]{1,0:T(8,128)(2,1)S(1)} copy-done((bf16[128,2048]{1,0:T(8,128)(2,1)S(1)}, bf16[128,2048]{1,0:T(8,128)(2,1)}, u32[]{:S(2)}) %copy-start.7) | copy-done | bytes 524312
  24.4 3.2 %shard_map.73 = (bf16[256,512]{1,0:T(8,128)(2,1)S(1)}, bf16[256,512]{1,0:T(8,128)(2,1)S(1)}, bf16[256,512]{1,0:T(8,128)(2,1)S(1)}, bf16[2,4,32,128]{3,2,1,0:T(8,128)(2,1)}) custom-call(bf16[128,2048]{1,0:T(8,128)(2,1)S(1)} %copy-done.7, bf16[128,2048]{1,0:T(8,128)(2,1)S(1)} %collective-permute-done.refs_1_, bf16[2048,512]{1,0:T(8,128)(2,1)S(1)} %copy-done, ...), custom_call_target="tpu_custom_call" | custom-call | flops 1610612736 | bytes 6291456 | tf_op jit(solution)/shard_map/pallas_call | solution.py:84
  27.6 0.7 copy-done.10
  28.3 0.7 copy-done.12
  29.0 4.8 %collective-permute-start.9 = (bf16[2,4,32,128]{3,2,1,0:T(8,128)(2,1)}, bf16[2,4,32,128]{3,2,1,0:T(8,128)(2,1)S(1)}, u32[]{:S(2)}, u32[]{:S(2)}) collective-permute-start(bf16[2,4,32,128]{3,2,1,0:T(8,128)(2,1)} %get-tuple-element.24), channel_id=1, source_target_pairs={{0,28},{4,24},{8,4},{12,0},{16,12},{20,8},{24,20},{28,16},{1,29},{... | collective-permute-start | bytes 196616 | tf_op jit(solution)/shard_map/ppermute | solution.py:325
  34.3 2.3 %collective-permute-done.9.refs_12_ = bf16[2,4,32,128]{3,2,1,0:T(8,128)(2,1)S(1)} collective-permute-done((bf16[2,4,32,128]{3,2,1,0:T(8,128)(2,1)}, bf16[2,4,32,128]{3,2,1,0:T(8,128)(2,1)S(1)}, u32[]{:S(2)}, u32[]{:S(2)}) %collective-permute-start.9) | collective-permute-done | bytes 65568 | tf_op jit(solution)/shard_map/ppermute | solution.py:325
  36.6 1.3 %collective-permute-start.6 = (bf16[2,4,32,128]{3,2,1,0:T(8,128)(2,1)}, bf16[2,4,32,128]{3,2,1,0:T(8,128)(2,1)S(1)}, u32[]{:S(2)}, u32[]{:S(2)}) collective-permute-start(bf16[2,4,32,128]{3,2,1,0:T(8,128)(2,1)} %get-tuple-element.24), channel_id=1, source_target_pairs={{0,16},{4,20},{8,24},{12,28},{16,0},{20,4},{24,8},{28,12},{1,17},{... | collective-permute-start | bytes 196616 | tf_op jit(solution)/shard_map/ppermute | solution.py:325
  37.9 1.2 %collective-permute-done.8.refs_11_ = bf16[2,4,32,128]{3,2,1,0:T(8,128)(2,1)S(1)} collective-permute-done((bf16[2,4,32,128]{3,2,1,0:T(8,128)(2,1)}, bf16[2,4,32,128]{3,2,1,0:T(8,128)(2,1)S(1)}, u32[]{:S(2)}, u32[]{:S(2)}) %collective-permute-start.8) | collective-permute-done | bytes 65568 | tf_op jit(solution)/shard_map/ppermute | solution.py:325
  39.0 3.3 %collective-permute-start.5 = (bf16[2,4,32,128]{3,2,1,0:T(8,128)(2,1)}, bf16[2,4,32,128]{3,2,1,0:T(8,128)(2,1)S(1)}, u32[]{:S(2)}, u32[]{:S(2)}) collective-permute-start(bf16[2,4,32,128]{3,2,1,0:T(8,128)(2,1)} %get-tuple-element.24), channel_id=1, source_target_pairs={{0,12},{4,8},{8,20},{12,16},{16,28},{20,24},{24,4},{28,0},{1,13},{... | collective-permute-start | bytes 196616 | tf_op jit(solution)/shard_map/ppermute | solution.py:325
  42.3 1.6 %copy-done.3 = bf16[2048,512]{1,0:T(8,128)(2,1)S(1)} copy-done((bf16[2048,512]{1,0:T(8,128)(2,1)S(1)}, bf16[2048,512]{1,0:T(8,128)(2,1)}, u32[]{:S(2)}) %copy-start.3) | copy-done | bytes 2097176
  43.9 2.0 %shard_map.75 = (bf16[256,512]{1,0:T(8,128)(2,1)S(1)}, bf16[256,512]{1,0:T(8,128)(2,1)S(1)}, bf16[2,4,32,128]{3,2,1,0:T(8,128)(2,1)S(1)}) custom-call(bf16[128,2048]{1,0:T(8,128)(2,1)S(1)} %collective-permute-done.1.refs_0_, bf16[128,2048]{1,0:T(8,128)(2,1)S(1)} %collective-permute-done.2.refs_1_, bf16[2048,512]{1,0:T(8,128)(2,1)S(1)} %copy-done.1, ...), custom_call_target="tpu_custom_call" | custom-call | flops 1073741824 | bytes 4194304 | tf_op jit(solution)/shard_map/pallas_call | solution.py:84
  46.7 4.7 %collective-permute-start.16 = (bf16[2,4,32,128]{3,2,1,0:T(8,128)(2,1)S(1)}, bf16[2,4,32,128]{3,2,1,0:T(8,128)(2,1)S(1)}, u32[]{:S(2)}, u32[]{:S(2)}) collective-permute-start(bf16[2,4,32,128]{3,2,1,0:T(8,128)(2,1)S(1)} %get-tuple-element.27), channel_id=1, source_target_pairs={{0,28},{4,24},{8,4},{12,0},{16,12},{20,8},{24,20},{28,16},{1,29},{... | collective-permute-start | bytes 196616 | tf_op jit(solution)/shard_map/ppermute | solution.py:325
  51.5 1.1 %shard_map.74.refs_1_.refs_0_ = bf16[256,512]{1,0:T(8,128)(2,1)S(1)} custom-call(bf16[128,2048]{1,0:T(8,128)(2,1)S(1)} %collective-permute-done.1.refs_0_, bf16[128,2048]{1,0:T(8,128)(2,1)S(1)} %collective-permute-done.2.refs_1_, bf16[2048,512]{1,0:T(8,128)(2,1)S(1)} %copy-done.6), custom_call_target="tpu_custom_call" | custom-call | flops 536870912 | bytes 2097152 | tf_op jit(solution)/shard_map/pallas_call | solution.py:84
  52.6 3.0 %collective-permute-start.13 = (bf16[2,4,32,128]{3,2,1,0:T(8,128)(2,1)S(1)}, bf16[2,4,32,128]{3,2,1,0:T(8,128)(2,1)S(1)}, u32[]{:S(2)}, u32[]{:S(2)}) collective-permute-start(bf16[2,4,32,128]{3,2,1,0:T(8,128)(2,1)S(1)} %get-tuple-element.27), channel_id=1, source_target_pairs={{0,16},{4,20},{8,24},{12,28},{16,0},{20,4},{24,8},{28,12},{1,17},{... | collective-permute-start | bytes 196616 | tf_op jit(solution)/shard_map/ppermute | solution.py:325
  55.6 2.9 %collective-permute-start.12 = (bf16[2,4,32,128]{3,2,1,0:T(8,128)(2,1)S(1)}, bf16[2,4,32,128]{3,2,1,0:T(8,128)(2,1)S(1)}, u32[]{:S(2)}, u32[]{:S(2)}) collective-permute-start(bf16[2,4,32,128]{3,2,1,0:T(8,128)(2,1)S(1)} %get-tuple-element.27), channel_id=1, source_target_pairs={{0,12},{4,8},{8,20},{12,16},{16,28},{20,24},{24,4},{28,0},{1,13},{... | collective-permute-start | bytes 196616 | tf_op jit(solution)/shard_map/ppermute | solution.py:325
  59.1 4.1 %shard_map.76 = (f32[512,512]{1,0:T(8,128)S(1)}, f32[4,512,128]{2,1,0:T(8,128)S(1)}) custom-call(s32[10]{0:T(128)S(1)} %pad_add_fusion.place, bf16[256,512]{1,0:T(8,128)(2,1)S(1)} %get-tuple-element.19.refs_0_, bf16[256,512]{1,0:T(8,128)(2,1)S(1)} %shard_map.74.refs_1_.refs_0_, bf16[256,512]{1,0:T(8,128)(2,1)S(1)} %copy-done.11, ...), custom_call_target="tpu_custom_call" | custom-call | flops 771751936 | bytes 1572864 | tf_op jit(solution)/shard_map/pallas_call | solution.py:221
  63.2 1.3 %collective-permute-done.11.refs_4_ = bf16[2,4,32,128]{3,2,1,0:T(8,128)(2,1)S(1)} collective-permute-done((bf16[2,4,32,128]{3,2,1,0:T(8,128)(2,1)S(1)}, bf16[2,4,32,128]{3,2,1,0:T(8,128)(2,1)S(1)}, u32[]{:S(2)}, u32[]{:S(2)}) %collective-permute-start.11) | collective-permute-done | bytes 65568 | tf_op jit(solution)/shard_map/ppermute | solution.py:325
  64.5 3.4 %shard_map.79 = (bf16[128,512]{1,0:T(8,128)(2,1)S(1)}, bf16[128,512]{1,0:T(8,128)(2,1)S(1)}) custom-call(s32[10]{0:T(128)S(1)} %pad_add_fusion.place, bf16[256,512]{1,0:T(8,128)(2,1)S(1)} %shard_map.74.refs_1_.refs_0_, f32[512,512]{1,0:T(8,128)S(1)} %get-tuple-element.25.refs_1_, f32[4,512,128]{2,1,0:T(8,128)S(1)} %get-tuple-element.26.refs_2_, ...), custom_call_target="tpu_custom_call" | custom-call | flops 117440512 | bytes 1048576 | tf_op jit(solution)/shard_map/pallas_call | solution.py:252
  68.0 1.3 %collective-permute-done.19.second = bf16[128,512]{1,0:T(8,128)(2,1)S(1)} collective-permute-done((bf16[128,512]{1,0:T(8,128)(2,1)S(1)}, bf16[128,512]{1,0:T(8,128)(2,1)S(1)}, u32[]{:S(2)}, u32[]{:S(2)}) %collective-permute-start.19) | collective-permute-done | bytes 131104 | tf_op jit(solution)/shard_map/ppermute | solution.py:312
  69.4 3.2 %shard_map.80 = bf16[128,2048]{1,0:T(8,128)(2,1)S(1)} custom-call(bf16[128,512]{1,0:T(8,128)(2,1)S(1)} %get-tuple-element.31.first, bf16[128,512]{1,0:T(8,128)(2,1)S(1)} %collective-permute-done.19.second, bf16[512,2048]{1,0:T(8,128)(2,1)S(1)} %copy-done.4, bf16[512,2048]{1,0:T(8,128)(2,1)} %collective-permute-done.18.weight_second), custom_call_target="tpu_custom_call" | custom-call | flops 536870912 | bytes 4194304 | tf_op jit(solution)/shard_map/pallas_call | solution.py:288
  72.6 1.6 %collective-permute-start.20 = (bf16[128,2048]{1,0:T(8,128)(2,1)S(1)}, bf16[128,2048]{1,0:T(8,128)(2,1)S(1)}, u32[]{:S(2)}, u32[]{:S(2)}) collective-permute-start(bf16[128,2048]{1,0:T(8,128)(2,1)S(1)} %shard_map.80), channel_id=1, source_target_pairs={{0,2},{1,3},{2,0},{3,1},{4,6},{5,7},{6,4},{7,5},{8,10},{9,11},{10,... | collective-permute-start | bytes 1572872 | tf_op jit(solution)/shard_map/ppermute | solution.py:312
  74.2 3.4 %shard_map.77 = (bf16[128,512]{1,0:T(8,128)(2,1)S(1)}, bf16[128,512]{1,0:T(8,128)(2,1)S(1)}) custom-call(s32[10]{0:T(128)S(1)} %pad_add_fusion.place, bf16[256,512]{1,0:T(8,128)(2,1)S(1)} %get-tuple-element.19.refs_0_, f32[512,512]{1,0:T(8,128)S(1)} %get-tuple-element.25.refs_1_, f32[4,512,128]{2,1,0:T(8,128)S(1)} %get-tuple-element.26.refs_2_, ...), custom_call_target="tpu_custom_call" | custom-call | flops 117440512 | bytes 1048576 | tf_op jit(solution)/shard_map/pallas_call | solution.py:252
  77.6 1.3 %collective-permute-done.17.second = bf16[128,512]{1,0:T(8,128)(2,1)S(1)} collective-permute-done((bf16[128,512]{1,0:T(8,128)(2,1)S(1)}, bf16[128,512]{1,0:T(8,128)(2,1)S(1)}, u32[]{:S(2)}, u32[]{:S(2)}) %collective-permute-start.17) | collective-permute-done | bytes 131104 | tf_op jit(solution)/shard_map/ppermute | solution.py:312
  79.0 3.2 %shard_map.78 = f32[128,2048]{1,0:T(8,128)S(1)} custom-call(bf16[128,512]{1,0:T(8,128)(2,1)S(1)} %get-tuple-element.28.first, bf16[128,512]{1,0:T(8,128)(2,1)S(1)} %collective-permute-done.17.second, bf16[512,2048]{1,0:T(8,128)(2,1)S(1)} %copy-done.4, bf16[512,2048]{1,0:T(8,128)(2,1)} %collective-permute-done.18.weight_second), custom_call_target="tpu_custom_call" | custom-call | flops 536870912 | bytes 4194304 | tf_op jit(solution)/shard_map/pallas_call | solution.py:288
  82.2 4.4 %collective-permute-done.20 = bf16[128,2048]{1,0:T(8,128)(2,1)S(1)} collective-permute-done((bf16[128,2048]{1,0:T(8,128)(2,1)S(1)}, bf16[128,2048]{1,0:T(8,128)(2,1)S(1)}, u32[]{:S(2)}, u32[]{:S(2)}) %collective-permute-start.20) | collective-permute-done | bytes 524320 | tf_op jit(solution)/shard_map/ppermute | solution.py:312
  86.6 0.9 %add_convert_fusion = bf16[128,2048]{1,0:T(8,128)(2,1)} fusion(f32[128,2048]{1,0:T(8,128)S(1)} %shard_map.78, bf16[128,2048]{1,0:T(8,128)(2,1)S(1)} %collective-permute-done.20), kind=kLoop, calls=%fused_computation | loop fusion | flops 786432 | bytes 2097152 | tf_op jit(solution)/shard_map/convert_element_type | solution.py:366
  (50 shorter events, 3.6 us)
Async XLA Ops:
  0.0 2.2 %collective-permute-start = (bf16[128,2048]{1,0:T(8,128)(2,1)}, bf16[128,2048]{1,0:T(8,128)(2,1)S(1)}, u32[]{:S(2)}, u32[]{:S(2)}) collective-permute-start(bf16[128,2048]{1,0:T(8,128)(2,1)} %refs_0_.1), channel_id=1, source_target_pairs={{0,1},{1,0},{2,3},{3,2},{4,5},{5,4},{6,7},{7,6},{8,9},{9,8},{10,11... | collective-permute-start | bytes 1572872 | tf_op jit(solution)/shard_map/ppermute | solution.py:312
  2.2 67.2 %collective-permute-start.18 = (bf16[512,2048]{1,0:T(8,128)(2,1)}, bf16[512,2048]{1,0:T(8,128)(2,1)}, u32[]{:S(2)}, u32[]{:S(2)}) collective-permute-start(bf16[512,2048]{1,0:T(8,128)(2,1)} %weight_first.3), channel_id=1, source_target_pairs={{0,1},{1,0},{2,3},{3,2},{4,5},{5,4},{6,7},{7,6},{8,9},{9,8},{10,11... | collective-permute-start | bytes 6291464 | tf_op jit(solution)/shard_map/ppermute | solution.py:312
  2.6 15.3 %collective-permute-start.1 = (bf16[128,2048]{1,0:T(8,128)(2,1)}, bf16[128,2048]{1,0:T(8,128)(2,1)S(1)}, u32[]{:S(2)}, u32[]{:S(2)}) collective-permute-start(bf16[128,2048]{1,0:T(8,128)(2,1)} %refs_0_.1), channel_id=1, source_target_pairs={{0,2},{1,3},{2,0},{3,1},{4,6},{5,7},{6,4},{7,5},{8,10},{9,11},{10,... | collective-permute-start | bytes 1572872 | tf_op jit(solution)/shard_map/ppermute | solution.py:312
  17.9 24.4 %collective-permute-start.2 = (bf16[128,2048]{1,0:T(8,128)(2,1)S(1)}, bf16[128,2048]{1,0:T(8,128)(2,1)S(1)}, u32[]{:S(2)}, u32[]{:S(2)}) collective-permute-start(bf16[128,2048]{1,0:T(8,128)(2,1)S(1)} %collective-permute-done.1.refs_0_), channel_id=1, source_target_pairs={{0,1},{1,0},{2,3},{3,2},{4,5},{5,4},{6,7},{7,6},{8,9},{9,8},{10,11... | collective-permute-start | bytes 1572872 | tf_op jit(solution)/shard_map/ppermute | solution.py:312
  17.9 1.6 %copy-start = (bf16[2048,512]{1,0:T(8,128)(2,1)S(1)}, bf16[2048,512]{1,0:T(8,128)(2,1)}, u32[]{:S(2)}) copy-start(bf16[2048,512]{1,0:T(8,128)(2,1)} %refs_2_.5) | copy-start | bytes 6291460
  19.5 1.6 %copy-start.2 = (bf16[2048,512]{1,0:T(8,128)(2,1)S(1)}, bf16[2048,512]{1,0:T(8,128)(2,1)}, u32[]{:S(2)}) copy-start(bf16[2048,512]{1,0:T(8,128)(2,1)} %refs_3_.3) | copy-start | bytes 6291460
  21.1 1.6 %copy-start.5 = (bf16[2048,512]{1,0:T(8,128)(2,1)S(1)}, bf16[2048,512]{1,0:T(8,128)(2,1)}, u32[]{:S(2)}) copy-start(bf16[2048,512]{1,0:T(8,128)(2,1)} %refs_2_.4) | copy-start | bytes 6291460
  24.4 17.9 %copy-start.1 = (bf16[2048,512]{1,0:T(8,128)(2,1)S(1)}, bf16[2048,512]{1,0:T(8,128)(2,1)}, u32[]{:S(2)}) copy-start(bf16[2048,512]{1,0:T(8,128)(2,1)} %refs_2_.5) | copy-start | bytes 6291460
  24.4 17.9 %copy-start.9 = (s32[4,128]{1,0:T(4,128)S(1)}, s32[4,128]{1,0:T(4,128)}, u32[]{:S(2)}) copy-start(s32[4,128]{1,0:T(4,128)} %refs_4_.3) | copy-start | bytes 6148
  29.0 7.5 %collective-permute-start.9 = (bf16[2,4,32,128]{3,2,1,0:T(8,128)(2,1)}, bf16[2,4,32,128]{3,2,1,0:T(8,128)(2,1)S(1)}, u32[]{:S(2)}, u32[]{:S(2)}) collective-permute-start(bf16[2,4,32,128]{3,2,1,0:T(8,128)(2,1)} %get-tuple-element.24), channel_id=1, source_target_pairs={{0,28},{4,24},{8,4},{12,0},{16,12},{20,8},{24,20},{28,16},{1,29},{... | collective-permute-start | bytes 196616 | tf_op jit(solution)/shard_map/ppermute | solution.py:325
  33.8 5.2 %collective-permute-start.8 = (bf16[2,4,32,128]{3,2,1,0:T(8,128)(2,1)}, bf16[2,4,32,128]{3,2,1,0:T(8,128)(2,1)S(1)}, u32[]{:S(2)}, u32[]{:S(2)}) collective-permute-start(bf16[2,4,32,128]{3,2,1,0:T(8,128)(2,1)} %get-tuple-element.24), channel_id=1, source_target_pairs={{0,24},{4,28},{8,0},{12,4},{16,8},{20,12},{24,16},{28,20},{1,25},{... | collective-permute-start | bytes 196616 | tf_op jit(solution)/shard_map/ppermute | solution.py:325
  34.3 17.1 %copy-start.14 = (s32[8]{0:T(128)S(1)}, s32[8]{0:T(128)}, u32[]{:S(2)}) copy-start(s32[8]{0:T(128)} %param.13) | copy-start | bytes 100
  34.3 11.7 %collective-permute-start.7 = (bf16[2,4,32,128]{3,2,1,0:T(8,128)(2,1)}, bf16[2,4,32,128]{3,2,1,0:T(8,128)(2,1)S(1)}, u32[]{:S(2)}, u32[]{:S(2)}) collective-permute-start(bf16[2,4,32,128]{3,2,1,0:T(8,128)(2,1)} %get-tuple-element.24), channel_id=1, source_target_pairs={{0,20},{4,16},{8,28},{12,24},{16,4},{20,0},{24,12},{28,8},{1,21},{... | collective-permute-start | bytes 196616 | tf_op jit(solution)/shard_map/ppermute | solution.py:325
  36.6 10.1 %collective-permute-start.6 = (bf16[2,4,32,128]{3,2,1,0:T(8,128)(2,1)}, bf16[2,4,32,128]{3,2,1,0:T(8,128)(2,1)S(1)}, u32[]{:S(2)}, u32[]{:S(2)}) collective-permute-start(bf16[2,4,32,128]{3,2,1,0:T(8,128)(2,1)} %get-tuple-element.24), channel_id=1, source_target_pairs={{0,16},{4,20},{8,24},{12,28},{16,0},{20,4},{24,8},{28,12},{1,17},{... | collective-permute-start | bytes 196616 | tf_op jit(solution)/shard_map/ppermute | solution.py:325
  39.0 12.3 %collective-permute-start.5 = (bf16[2,4,32,128]{3,2,1,0:T(8,128)(2,1)}, bf16[2,4,32,128]{3,2,1,0:T(8,128)(2,1)S(1)}, u32[]{:S(2)}, u32[]{:S(2)}) collective-permute-start(bf16[2,4,32,128]{3,2,1,0:T(8,128)(2,1)} %get-tuple-element.24), channel_id=1, source_target_pairs={{0,12},{4,8},{8,20},{12,16},{16,28},{20,24},{24,4},{28,0},{1,13},{... | collective-permute-start | bytes 196616 | tf_op jit(solution)/shard_map/ppermute | solution.py:325
  42.3 9.0 %collective-permute-start.4 = (bf16[2,4,32,128]{3,2,1,0:T(8,128)(2,1)}, bf16[2,4,32,128]{3,2,1,0:T(8,128)(2,1)S(1)}, u32[]{:S(2)}, u32[]{:S(2)}) collective-permute-start(bf16[2,4,32,128]{3,2,1,0:T(8,128)(2,1)} %get-tuple-element.24), channel_id=1, source_target_pairs={{0,8},{4,12},{8,16},{12,20},{16,24},{20,28},{24,0},{28,4},{1,9},{5... | collective-permute-start | bytes 196616 | tf_op jit(solution)/shard_map/ppermute | solution.py:325
  42.3 1.6 %copy-start.3 = (bf16[2048,512]{1,0:T(8,128)(2,1)S(1)}, bf16[2048,512]{1,0:T(8,128)(2,1)}, u32[]{:S(2)}) copy-start(bf16[2048,512]{1,0:T(8,128)(2,1)} %refs_3_.3) | copy-start | bytes 6291460
  43.9 7.6 %copy-start.6 = (bf16[2048,512]{1,0:T(8,128)(2,1)S(1)}, bf16[2048,512]{1,0:T(8,128)(2,1)}, u32[]{:S(2)}) copy-start(bf16[2048,512]{1,0:T(8,128)(2,1)} %refs_2_.4) | copy-start | bytes 6291460
  46.0 13.1 %copy-start.11 = (bf16[256,512]{1,0:T(8,128)(2,1)S(1)}, bf16[256,512]{1,0:T(8,128)(2,1)}, u32[]{:S(2)}) copy-start(bf16[256,512]{1,0:T(8,128)(2,1)} %copy-done.10) | copy-start | bytes 786436
  46.0 13.1 %copy-start.13 = (bf16[256,512]{1,0:T(8,128)(2,1)S(1)}, bf16[256,512]{1,0:T(8,128)(2,1)}, u32[]{:S(2)}) copy-start(bf16[256,512]{1,0:T(8,128)(2,1)} %copy-done.12) | copy-start | bytes 786436
  46.0 6.6 %collective-permute-start.3 = (bf16[2,4,32,128]{3,2,1,0:T(8,128)(2,1)}, bf16[2,4,32,128]{3,2,1,0:T(8,128)(2,1)S(1)}, u32[]{:S(2)}, u32[]{:S(2)}) collective-permute-start(bf16[2,4,32,128]{3,2,1,0:T(8,128)(2,1)} %get-tuple-element.24), channel_id=1, source_target_pairs={{0,4},{4,0},{8,12},{12,8},{16,20},{20,16},{24,28},{28,24},{1,5},{5... | collective-permute-start | bytes 196616 | tf_op jit(solution)/shard_map/ppermute | solution.py:325
  46.7 8.9 %collective-permute-start.16 = (bf16[2,4,32,128]{3,2,1,0:T(8,128)(2,1)S(1)}, bf16[2,4,32,128]{3,2,1,0:T(8,128)(2,1)S(1)}, u32[]{:S(2)}, u32[]{:S(2)}) collective-permute-start(bf16[2,4,32,128]{3,2,1,0:T(8,128)(2,1)S(1)} %get-tuple-element.27), channel_id=1, source_target_pairs={{0,28},{4,24},{8,4},{12,0},{16,12},{20,8},{24,20},{28,16},{1,29},{... | collective-permute-start | bytes 196616 | tf_op jit(solution)/shard_map/ppermute | solution.py:325
  51.3 7.1 %collective-permute-start.15 = (bf16[2,4,32,128]{3,2,1,0:T(8,128)(2,1)S(1)}, bf16[2,4,32,128]{3,2,1,0:T(8,128)(2,1)S(1)}, u32[]{:S(2)}, u32[]{:S(2)}) collective-permute-start(bf16[2,4,32,128]{3,2,1,0:T(8,128)(2,1)S(1)} %get-tuple-element.27), channel_id=1, source_target_pairs={{0,24},{4,28},{8,0},{12,4},{16,8},{20,12},{24,16},{28,20},{1,25},{... | collective-permute-start | bytes 196616 | tf_op jit(solution)/shard_map/ppermute | solution.py:325
  51.3 7.1 %collective-permute-start.14 = (bf16[2,4,32,128]{3,2,1,0:T(8,128)(2,1)S(1)}, bf16[2,4,32,128]{3,2,1,0:T(8,128)(2,1)S(1)}, u32[]{:S(2)}, u32[]{:S(2)}) collective-permute-start(bf16[2,4,32,128]{3,2,1,0:T(8,128)(2,1)S(1)} %get-tuple-element.27), channel_id=1, source_target_pairs={{0,20},{4,16},{8,28},{12,24},{16,4},{20,0},{24,12},{28,8},{1,21},{... | collective-permute-start | bytes 196616 | tf_op jit(solution)/shard_map/ppermute | solution.py:325
  52.6 10.6 %collective-permute-start.13 = (bf16[2,4,32,128]{3,2,1,0:T(8,128)(2,1)S(1)}, bf16[2,4,32,128]{3,2,1,0:T(8,128)(2,1)S(1)}, u32[]{:S(2)}, u32[]{:S(2)}) collective-permute-start(bf16[2,4,32,128]{3,2,1,0:T(8,128)(2,1)S(1)} %get-tuple-element.27), channel_id=1, source_target_pairs={{0,16},{4,20},{8,24},{12,28},{16,0},{20,4},{24,8},{28,12},{1,17},{... | collective-permute-start | bytes 196616 | tf_op jit(solution)/shard_map/ppermute | solution.py:325
  55.6 7.6 %collective-permute-start.12 = (bf16[2,4,32,128]{3,2,1,0:T(8,128)(2,1)S(1)}, bf16[2,4,32,128]{3,2,1,0:T(8,128)(2,1)S(1)}, u32[]{:S(2)}, u32[]{:S(2)}) collective-permute-start(bf16[2,4,32,128]{3,2,1,0:T(8,128)(2,1)S(1)} %get-tuple-element.27), channel_id=1, source_target_pairs={{0,12},{4,8},{8,20},{12,16},{16,28},{20,24},{24,4},{28,0},{1,13},{... | collective-permute-start | bytes 196616 | tf_op jit(solution)/shard_map/ppermute | solution.py:325
  58.5 6.1 %collective-permute-start.11 = (bf16[2,4,32,128]{3,2,1,0:T(8,128)(2,1)S(1)}, bf16[2,4,32,128]{3,2,1,0:T(8,128)(2,1)S(1)}, u32[]{:S(2)}, u32[]{:S(2)}) collective-permute-start(bf16[2,4,32,128]{3,2,1,0:T(8,128)(2,1)S(1)} %get-tuple-element.27), channel_id=1, source_target_pairs={{0,8},{4,12},{8,16},{12,20},{16,24},{20,28},{24,0},{28,4},{1,9},{5... | collective-permute-start | bytes 196616 | tf_op jit(solution)/shard_map/ppermute | solution.py:325
  58.5 6.1 %collective-permute-start.10 = (bf16[2,4,32,128]{3,2,1,0:T(8,128)(2,1)S(1)}, bf16[2,4,32,128]{3,2,1,0:T(8,128)(2,1)S(1)}, u32[]{:S(2)}, u32[]{:S(2)}) collective-permute-start(bf16[2,4,32,128]{3,2,1,0:T(8,128)(2,1)S(1)} %get-tuple-element.27), channel_id=1, source_target_pairs={{0,4},{4,0},{8,12},{12,8},{16,20},{20,16},{24,28},{28,24},{1,5},{5... | collective-permute-start | bytes 196616 | tf_op jit(solution)/shard_map/ppermute | solution.py:325
  63.2 6.2 %copy-start.4 = (bf16[512,2048]{1,0:T(8,128)(2,1)S(1)}, bf16[512,2048]{1,0:T(8,128)(2,1)}, u32[]{:S(2)}) copy-start(bf16[512,2048]{1,0:T(8,128)(2,1)} %weight_first.3) | copy-start | bytes 6291460
  67.9 1.4 %collective-permute-start.19 = (bf16[128,512]{1,0:T(8,128)(2,1)S(1)}, bf16[128,512]{1,0:T(8,128)(2,1)S(1)}, u32[]{:S(2)}, u32[]{:S(2)}) collective-permute-start(bf16[128,512]{1,0:T(8,128)(2,1)S(1)} %get-tuple-element.32), channel_id=1, source_target_pairs={{0,1},{1,0},{2,3},{3,2},{4,5},{5,4},{6,7},{7,6},{8,9},{9,8},{10,11... | collective-permute-start | bytes 393224 | tf_op jit(solution)/shard_map/ppermute | solution.py:312
  72.6 14.0 %collective-permute-start.20 = (bf16[128,2048]{1,0:T(8,128)(2,1)S(1)}, bf16[128,2048]{1,0:T(8,128)(2,1)S(1)}, u32[]{:S(2)}, u32[]{:S(2)}) collective-permute-start(bf16[128,2048]{1,0:T(8,128)(2,1)S(1)} %shard_map.80), channel_id=1, source_target_pairs={{0,2},{1,3},{2,0},{3,1},{4,6},{5,7},{6,4},{7,5},{8,10},{9,11},{10,... | collective-permute-start | bytes 1572872 | tf_op jit(solution)/shard_map/ppermute | solution.py:312
  77.6 1.4 %collective-permute-start.17 = (bf16[128,512]{1,0:T(8,128)(2,1)S(1)}, bf16[128,512]{1,0:T(8,128)(2,1)S(1)}, u32[]{:S(2)}, u32[]{:S(2)}) collective-permute-start(bf16[128,512]{1,0:T(8,128)(2,1)S(1)} %get-tuple-element.29), channel_id=1, source_target_pairs={{0,1},{1,0},{2,3},{3,2},{4,5},{5,4},{6,7},{7,6},{8,9},{9,8},{10,11... | collective-permute-start | bytes 393224 | tf_op jit(solution)/shard_map/ppermute | solution.py:312
  (4 other events, 3.1 us)

commit v2 on v0

v2 whole, which is shorter than its diff:
```python
import functools
import math

import jax
import jax.numpy as jnp
from jax import lax
from jax.experimental import pallas as pl
from jax.experimental.pallas import tpu as pltpu
from jax.sharding import PartitionSpec as P

HEAD_SIZE = 128
BLOCK = 128
DILATED_KEPT = 16
BLOCKS_HALF = 2
FAR_ROWS = BLOCKS_HALF * DILATED_KEPT
GROUP = 8
HIDDEN = -1e30
SCALE = math.log2(math.e) / math.sqrt(HEAD_SIZE)
BF16 = jnp.bfloat16
F32 = jnp.float32
IN_VMEM = pl.BlockSpec(memory_space=pltpu.VMEM)
IN_HBM = pl.BlockSpec(memory_space=pltpu.HBM)
IN_SMEM = pl.BlockSpec(memory_space=pltpu.SMEM)
KEY_BITS = (1, 4, 2)
VALUE_BITS = (4, 2, 1)


def dot(a, b):
    return jnp.dot(a, b, preferred_element_type=F32)


def dot_t(a, b):
    return lax.dot_general(a, b, (((1,), (1,)), ((), ())), preferred_element_type=F32)


def params():
    return pltpu.CompilerParams(vmem_limit_bytes=40 * 2**20)


def cost(flops, bytes_accessed, transcendentals=0):
    return pl.CostEstimate(
        flops=flops, bytes_accessed=bytes_accessed, transcendentals=transcendentals
    )


def shape(dims, dtype=BF16):
    return jax.ShapeDtypeStruct(tuple(dims), dtype)


def keep_in_hbm(array):
    return pltpu.with_memory_space_constraint(array, pltpu.HBM)


def halves_of(width):
    tile = min(256, width)
    return [slice(i * tile, (i + 1) * tile) for i in range(width // tile)]


def pick_dilated(pattern, blocks, kept_keys, kept_values):
    positions = lax.broadcasted_iota(jnp.int32, (BLOCK, BLOCK), 0)
    for head in range(kept_keys.shape[0]):
        row = pattern[head : head + 1, :]
        chosen = (positions == row).astype(F32).T[:DILATED_KEPT].astype(BF16)
        for index, block in enumerate(blocks):
            picked = dot(chosen, jnp.concatenate(block(head), axis=1)).astype(BF16)
            spot = slice(index * DILATED_KEPT, (index + 1) * DILATED_KEPT)
            kept_keys[head, spot, :] = picked[:, :HEAD_SIZE]
            kept_values[head, spot, :] = picked[:, HEAD_SIZE:]


def head_of(ref, head, rows=slice(None)):
    return ref[rows, head * HEAD_SIZE : (head + 1) * HEAD_SIZE]


def first_kernel(rows_hbm, wk_hbm, wv_hbm, rows, wk, wv, keys, values, sems):
    parts = halves_of(wk.shape[1])
    whole = pltpu.make_async_copy(rows_hbm, rows, sems.at[0])
    whole.start()
    copies = []
    for index, part in enumerate(parts):
        for side, (source, target) in enumerate(((wk_hbm, wk), (wv_hbm, wv))):
            copy = pltpu.make_async_copy(
                source.at[:, part], target.at[:, part], sems.at[1 + 2 * index + side]
            )
            copy.start()
            copies.append((copy, target, part, (keys, values)[side]))
    whole.wait()
    for copy, weight, part, out in copies:
        copy.wait()
        out[:, part] = dot(rows[...], weight[:, part]).astype(BF16)


def first(rows, w_key, w_value):
    count, depth = rows.shape
    width = w_key.shape[1]
    return pl.pallas_call(
        first_kernel,
        in_specs=[IN_HBM] * 3,
        out_specs=[IN_VMEM] * 5,
        out_shape=[
            pltpu.VMEM(rows.shape, BF16),
            pltpu.VMEM(w_key.shape, BF16),
            pltpu.VMEM(w_value.shape, BF16),
            shape((count, width)),
            shape((count, width)),
        ],
        scratch_shapes=[pltpu.SemaphoreType.DMA((1 + 2 * len(halves_of(width)),))],
        compiler_params=params(),
        cost_estimate=cost(4 * count * depth * width, 4 * depth * width),
    )(keep_in_hbm(rows), keep_in_hbm(w_key), keep_in_hbm(w_value))


def second_kernel(
    rows, wk, wv, keys_0, values_0, pattern, wq_hbm, wq, keys, values, kept_k, kept_v, sem
):
    copy = pltpu.make_async_copy(wq_hbm, wq, sem)
    copy.start()
    for part in halves_of(wk.shape[1]):
        keys[:, part] = dot(rows[...], wk[:, part]).astype(BF16)
        values[:, part] = dot(rows[...], wv[:, part]).astype(BF16)
    blocks = [
        lambda head: (head_of(keys_0, head), head_of(values_0, head)),
        lambda head: (head_of(keys, head), head_of(values, head)),
    ]
    pick_dilated(pattern, blocks, kept_k, kept_v)
    copy.wait()


def second(rows, wk, wv, keys_0, values_0, pattern, w_query):
    count, depth = rows.shape
    width = wk.shape[1]
    kept = (width // HEAD_SIZE, FAR_ROWS, HEAD_SIZE)
    return pl.pallas_call(
        second_kernel,
        in_specs=[IN_VMEM] * 6 + [IN_HBM],
        out_specs=[IN_VMEM] * 5,
        out_shape=[
            pltpu.VMEM(w_query.shape, BF16),
            shape((count, width)),
            shape((count, width)),
            shape(kept),
            shape(kept),
        ],
        scratch_shapes=[pltpu.SemaphoreType.DMA],
        compiler_params=params(),
        cost_estimate=cost(4 * count * depth * width, 2 * depth * width),
    )(rows, wk, wv, keys_0, values_0, pattern, keep_in_hbm(w_query))


def query_kernel(carry, *refs):
    rows_0, rows_1, wq = refs[:3]
    if carry:
        w_hbm, queries, w, sem = refs[3:]
        copy = pltpu.make_async_copy(w_hbm, w, sem)
        copy.start()
    else:
        queries = refs[3]
    rows = jnp.concatenate([rows_0[...], rows_1[...]], axis=0)
    for part in halves_of(wq.shape[1]):
        queries[:, part] = dot(rows, wq[:, part]).astype(BF16)
    if carry:
        copy.wait()


def query(rows_0, rows_1, wq, carried=None):
    count, depth = rows_0.shape
    width = wq.shape[1]
    carry = carried is not None
    return pl.pallas_call(
        functools.partial(query_kernel, carry),
        in_specs=[IN_VMEM] * 3 + [IN_HBM] * carry,
        out_specs=[IN_VMEM] * (1 + carry),
        out_shape=[shape((2 * count, width))]
        + ([pltpu.VMEM(carried.shape, BF16)] if carry else []),
        scratch_shapes=[pltpu.SemaphoreType.DMA] * carry,
        compiler_params=params(),
        cost_estimate=cost(4 * count * depth * width, 2 * depth * width * carry),
    )(rows_0, rows_1, wq, *([keep_in_hbm(carried)] if carry else []))


def third_kernel(rows_0, rows_1, wk, wv, pattern, keys, values, kept_k, kept_v):
    rows = jnp.concatenate([rows_0[...], rows_1[...]], axis=0)
    for part in halves_of(wk.shape[1]):
        keys[:, part] = dot(rows, wk[:, part]).astype(BF16)
        values[:, part] = dot(rows, wv[:, part]).astype(BF16)

    def block(where):
        return lambda head: (head_of(keys, head, where), head_of(values, head, where))

    blocks = [block(slice(i * BLOCK, (i + 1) * BLOCK)) for i in range(BLOCKS_HALF)]
    pick_dilated(pattern, blocks, kept_k, kept_v)


def third(rows_0, rows_1, wk, wv, pattern):
    count, depth = rows_0.shape
    width = wk.shape[1]
    kept = (width // HEAD_SIZE, FAR_ROWS, HEAD_SIZE)
    return pl.pallas_call(
        third_kernel,
        in_specs=[IN_VMEM] * 5,
        out_specs=[IN_VMEM] * 4,
        out_shape=[shape((2 * count, width))] * 2 + [shape(kept)] * 2,
        compiler_params=params(),
        cost_estimate=cost(8 * count * depth * width, 4 * count * depth),
    )(rows_0, rows_1, wk, wv, pattern)


def slide_of(place, slides, block):
    end, total = jnp.int32(0), jnp.zeros_like(block)
    for index in range(slides):
        end = end + place[index]
        total = total + (block >= end).astype(jnp.int32)
    return total


def hidden_if_not(condition):
    return jnp.where(condition, jnp.float32(0), jnp.float32(HIDDEN))


def far_bias(place, slides, subs, span_of, blocks, row_slides):
    column = lax.broadcasted_iota(jnp.int32, (1, GROUP * FAR_ROWS), 1)
    span = span_of(column // FAR_ROWS)
    upper = (column // DILATED_KEPT) % BLOCKS_HALF
    me = place[slides + 1]
    block = span * subs + jnp.where(upper == 0, me ^ blocks[0], me ^ blocks[1])
    slide = slide_of(place, slides, block)
    elsewhere = span != place[slides]
    return [hidden_if_not((slide == mine) & elsewhere) for mine in row_slides]


def add_rows(scores, bias):
    return jnp.concatenate(
        [scores[i * BLOCK : (i + 1) * BLOCK] + row for i, row in enumerate(bias)], axis=0
    )


def far_update(queries, keys, values, bias, state):
    scores = add_rows(dot_t(queries, keys), bias)
    peak, total, gathered = state
    higher = jnp.maximum(peak, jnp.max(scores, axis=1, keepdims=True))
    shrink = jnp.exp2((peak - higher) * SCALE)
    weight = jnp.exp2((scores - higher) * SCALE)
    total = total * shrink + jnp.sum(weight, axis=1, keepdims=True)
    return higher, total, gathered * shrink + dot(weight.astype(BF16), values)


def far_group(keys, values, head):
    found = []
    for refs, bits in ((keys, KEY_BITS), (values, VALUE_BITS)):
        order = [0]
        for bit in bits:
            order += [place ^ bit for place in order]
        half = len(order) // 2
        found.append(
            jnp.concatenate(
                [
                    refs[order.index(i) // half][order.index(i) % half, head]
                    for i in range(len(order))
                ],
                axis=0,
            )
        )
    return found


def attend_kernel(slides, subs, relative, near, halves, few, finish, place, *refs):
    refs = list(refs)
    queries = refs.pop(0)
    if near:
        keys, values = refs[0:3], refs[3:6]
        del refs[:6]
    else:
        gathered_in, stats_in = refs[0:2]
        del refs[:2]
    far = []
    for blocks in halves:
        size = 2 if few else 1
        far.append((blocks, refs[:size], refs[size : 2 * size]))
        del refs[: 2 * size]
    sub = place[slides + 1]
    slide = [
        slide_of(place, slides, place[slides] * subs + (sub ^ r)) for r in range(subs)
    ]
    mine = [slide[r] for r in relative]
    if near:
        near_bias = [
            jnp.concatenate(
                [
                    jnp.full((1, BLOCK), hidden_if_not(slide[r] == slide[c]), F32)
                    for c in range(subs)
                ],
                axis=1,
            )
            for r in relative
        ]
    if few:
        biases = [
            far_bias(place, slides, subs, lambda i: place[slides] ^ i, blocks, mine)
            for blocks, _, _ in far
        ]
    for head in range(queries.shape[1] // HEAD_SIZE):
        asked = head_of(queries, head)
        if near:
            near_keys = jnp.concatenate([head_of(ref, head) for ref in keys], axis=0)
            near_values = jnp.concatenate([head_of(ref, head) for ref in values], axis=0)
            scores = add_rows(dot_t(asked, near_keys), near_bias)
            peak = jnp.max(scores, axis=1, keepdims=True)
            weight = jnp.exp2((scores - peak) * SCALE)
            total = jnp.sum(weight, axis=1, keepdims=True)
            state = peak, total, dot(weight.astype(BF16), near_values)
        else:
            state = stats_in[head, :, 0:1], stats_in[head, :, 1:2], head_of(gathered_in, head)
        for index, (blocks, far_keys, far_values) in enumerate(far):
            if few:
                group = far_group(far_keys, far_values, head)
                state = far_update(asked, *group, biases[index], state)
                continue

            def step(number, state, blocks=blocks, k=far_keys[0], v=far_values[0]):
                base = number * GROUP
                bias = far_bias(place, slides, subs, lambda i: base + i, blocks, mine)
                group = [
                    jnp.concatenate([ref[base + i, head] for i in range(GROUP)], axis=0)
                    for ref in (k, v)
                ]
                return far_update(asked, *group, bias, state)

            state = lax.fori_loop(0, far_keys[0].shape[0] // GROUP, step, state)
        peak, total, gathered = state
        columns = slice(head * HEAD_SIZE, (head + 1) * HEAD_SIZE)
        if finish:
            keep, send = refs
            context = (gathered / total).astype(BF16)
            keep[:, columns] = context[:BLOCK]
            send[:, columns] = context[BLOCK:]
        else:
            gathered_out, stats_out = refs
            gathered_out[:, columns] = gathered
            lane = lax.broadcasted_iota(jnp.int32, gathered.shape, 1)
            stats_out[head] = jnp.where(lane == 0, peak, total)


def attend(place, slides, subs, few, relative, queries, halves, near=None, begun=None, finish=True):
    rows, width = queries.shape
    heads = width // HEAD_SIZE
    operands = [queries]
    operands += [*near[0], *near[1]] if near else list(begun)
    columns = subs * BLOCK if near else 0
    for _, keys, values in halves:
        operands += [*keys, *values]
        columns += sum(part.shape[0] for part in keys) * FAR_ROWS
    if finish:
        out_shape = [shape((BLOCK, width))] * 2
    else:
        out_shape = [shape((rows, width), F32), shape((heads, rows, HEAD_SIZE), F32)]
    return pl.pallas_call(
        functools.partial(
            attend_kernel,
            slides,
            subs,
            relative,
            near is not None,
            [half[0] for half in halves],
            few,
            finish,
        ),
        in_specs=[IN_SMEM] + [IN_VMEM] * len(operands),
        out_specs=[IN_VMEM] * 2,
        out_shape=out_shape,
        compiler_params=params(),
        cost_estimate=cost(
            4 * rows * columns * width, 4 * rows * width, heads * rows * columns
        ),
    )(place, *operands)


def mix_kernel(rows_0, rows_1, weight_0, weight_1, out):
    tile = min(512, out.shape[1])
    for index in range(out.shape[1] // tile):
        part = slice(index * tile, (index + 1) * tile)
        total = dot(rows_0[...], weight_0[:, part]) + dot(rows_1[...], weight_1[:, part])
        out[:, part] = total.astype(out.dtype)


def mix(rows_0, rows_1, weight_0, weight_1, dtype):
    rows, depth = rows_0.shape
    width = weight_0.shape[1]
    return pl.pallas_call(
        mix_kernel,
        in_specs=[IN_VMEM] * 4,
        out_specs=IN_VMEM,
        out_shape=shape((rows, width), dtype),
        compiler_params=params(),
        cost_estimate=cost(4 * rows * depth * width, 4 * rows * width),
    )(rows_0, rows_1, weight_0, weight_1)


def shards(seqs, subs, normed, w_query, w_key, w_value, w_out, pattern, slide_lengths):
    slides = slide_lengths.shape[0]
    place = jnp.concatenate(
        [
            slide_lengths,
            lax.axis_index("seq").astype(jnp.int32)[None],
            lax.axis_index("sub").astype(jnp.int32)[None],
        ]
    )
    few = seqs == GROUP

    def swap(array, bit, axis="sub"):
        count = subs if axis == "sub" else seqs
        return lax.ppermute(array, axis, [(i, i ^ bit) for i in range(count)])

    def after(array, *others):
        return lax.optimization_barrier((array, *others))[0]

    def double(parts, bit):
        return jnp.concatenate([parts, swap(parts, bit, "seq")], axis=0)

    def spread(kept, start, middle):
        if not few:
            return [[lax.all_gather(part, "seq", axis=0)] for part in kept]
        (key_1, key_2, key_3), (value_1, value_2, value_3) = KEY_BITS, VALUE_BITS
        k, v = start(double(kept[0][None], key_1), double(kept[1][None], value_1))
        k, v = middle(double(k, key_2), double(v, value_2))
        return [k, swap(k, key_3, "seq")], [v, swap(v, value_3, "seq")]

    across = swap(normed, 2)
    beside = swap(normed, 1)
    mine, wk, wv, keys_0, values_0 = first(normed, w_key, w_value)
    wq, keys_1, values_1, *kept = second(beside, wk, wv, keys_0, values_0, pattern, w_query)
    query_a, wo = query(mine, beside, wq, w_out)
    held = [across]

    def before_across(k, v):
        *held[:], k, v, _ = lax.optimization_barrier((*held, k, v, query_a))
        return k, v

    half_a = (0, 1), *spread(kept, lambda k, v: (k, v), before_across)
    across = held[0]
    across_beside = swap(across, 1)
    wo_beside = swap(after(w_out, across_beside), 1)
    keys_2, values_2, *kept = third(across, across_beside, wk, wv, pattern)
    near = [keys_0, keys_1, keys_2], [values_0, values_1, values_2]
    call = functools.partial(attend, place, slides, subs, few)
    (query_b,) = query(across, across_beside, wq)
    begun = call((2, 3), query_b, [half_a], near=near, finish=False)
    half_b = (2, 3), *spread(
        kept,
        lambda k, v: lax.optimization_barrier((k, v, query_b))[:2],
        lambda k, v: lax.optimization_barrier((k, v, *begun))[:2],
    )
    keep_b, send_b = call((2, 3), query_b, [half_b], begun=begun)
    other_b = swap(send_b, 1)
    leaving = mix(keep_b, other_b, wo, wo_beside, BF16)
    arriving = swap(leaving, 2)
    query_a = after(query_a, leaving)
    keep_a, send_a = call((0, 1), query_a, [half_a, half_b], near=near)
    other_a = swap(send_a, 1)
    own = mix(keep_a, other_a, wo, wo_beside, F32)
    return (own + arriving.astype(F32)).astype(BF16)


def solution(mesh):
    placed = (
        P(("seq", "sub"), None),
        P(None, "sub"),
        P(None, "sub"),
        P(None, "sub"),
        P("sub", None),
        P("sub", None),
        P(),
    )
    return jax.shard_map(
        functools.partial(shards, mesh.shape["seq"], mesh.shape["sub"]),
        mesh=mesh,
        in_specs=placed,
        out_specs=P(("seq", "sub"), None),
        check_vma=False,
    )
```

time: 187 us -> 73.6 us (0.39)
  blocking collectives: 62.8 us -> 0 us
  waiting for transfers between devices: 70.7 us -> 24.6 us
  Pallas kernels: 0 us -> 24 us
  matrix products: 20.1 us -> 0 us
  starting transfers between devices: 0.04 us -> 20.1 us
  between operations: 13.7 us -> 0.33 us
  local copies, waits for them, and re-layouts: 13.8 us -> 3.24 us
  other arithmetic: 5.13 us -> 1.06 us
    all_gather x2 -> x0, blocking collectives: 62.8 us -> none  [the longest x1 31.5 us: shards(): lax.all_gather(dilate(keys_all), 'seq', axis=1, tiled=True)]
    reduce_scatter x1 -> x0, waiting for transfers between devices: 44.9 us -> none  [shards(): lax.psum_scatter(jnp.dot(context, w_out, preferred_element_type=jnp.float...]
    all_gather x1 -> x0, waiting for transfers between devices: 25.1 us -> none  [shards(): piece = lax.all_gather(normed, 'sub', axis=0, tiled=True)]
    ppermute x0 -> x19, waiting for transfers between devices: none -> 24.6 us  [swap(): return lax.ppermute(array, axis, [(i, i ^ bit) for i in range(count)])]
    pallas_call x0 -> x10, Pallas kernels: none -> 24 us  [the longest x3 9.4 us: attend(): pl.pallas_call(functools.partial(attend_kernel, slides, subs, relative, n...]
    ppermute x0 -> x19, starting transfers between devices: none -> 20.1 us  [swap(): return lax.ppermute(array, axis, [(i, i ^ bit) for i in range(count)])]
    dot_general x20 -> x0, matrix products: 20.1 us -> none  [the longest x3 11.3 us: shards(): jnp.dot(piece, weight, preferred_element_type=jnp.float32)]
    gather x16 -> x0, local copies, waits for them, and re-layouts: 9.13 us -> none  [dilate(): blocked[:, kept_positions[head_index], head_index, :]]
  transfers between devices with their start and end apart: 2 -> 19, of which waited for: 2 -> 11; matrix products, arithmetic and copies ran while one was open for 1% -> 0% of each run, Pallas kernels for 0% -> 29%
where the time goes in v2:
time: 73.6 us; the launch traced here: 73.3 us
  waiting for transfers between devices  24.6 us (33%)
  Pallas kernels  24 us (33%)
  starting transfers between devices  20.1 us (27%)
  local copies, waits for them, and re-layouts  3.24 us (4%)
  other arithmetic  1.06 us (1%)
    ppermute x19, waiting for transfers between devices, swap(): return lax.ppermute(array, axis, [(i, i ^ bit) for i in range(count)])  24.6 us
    ppermute x19, starting transfers between devices, swap(): return lax.ppermute(array, axis, [(i, i ^ bit) for i in range(count)])  20.1 us
    pallas_call x3, Pallas kernels, attend(): pl.pallas_call(functools.partial(attend_kernel, slides, subs, relative, n...  9.4 us
    pallas_call x2, Pallas kernels, mix(): pl.pallas_call(mix_kernel, in_specs=[IN_VMEM] * 4, out_specs=IN_VMEM, out...  4.68 us
    unnamed x32, local copies, waits for them, and re-layouts  3.24 us
    pallas_call x1, Pallas kernels, first(): pl.pallas_call(first_kernel, in_specs=[IN_HBM] * 3, out_specs=[IN_VMEM] *...  3.12 us
    pallas_call x1, Pallas kernels, second(): pl.pallas_call(second_kernel, in_specs=[IN_VMEM] * 6 + [IN_HBM], out_spec...  3.06 us
    pallas_call x2, Pallas kernels, query(): pl.pallas_call(functools.partial(query_kernel, carry), in_specs=[IN_VMEM]...  2.33 us
  transfers between devices with their start and end apart: 19, of which 11 were waited for; matrix products, arithmetic and copies ran while one was open for 0% of the time, Pallas kernels for 29%

profile of v2, /device:TPU:0, one launch (start us, length us, event | category | flops | bytes accessed | tf_op | source)
XLA Modules:
  0.0 73.3 jit_solution(7317050437474642821)
XLA Ops:
  0.5 2.5 %collective-permute-start.1 = (bf16[128,2048]{1,0:T(8,128)(2,1)}, bf16[128,2048]{1,0:T(8,128)(2,1)S(1)}, u32[]{:S(2)}, u32[]{:S(2)}) collective-permute-start(bf16[128,2048]{1,0:T(8,128)(2,1)} %rows_hbm.1), channel_id=1, source_target_pairs={{0,2},{1,3},{2,0},{3,1},{4,6},{5,7},{6,4},{7,5},{8,10},{9,11},{10,... | collective-permute-start | bytes 1572872 | tf_op jit(solution)/shard_map/ppermute | solution.py:411
  3.0 3.1 %shard_map.73 = (bf16[128,2048]{1,0:T(8,128)(2,1)S(1)}, bf16[2048,512]{1,0:T(8,128)(2,1)S(1)}, bf16[2048,512]{1,0:T(8,128)(2,1)S(1)}, bf16[128,512]{1,0:T(8,128)(2,1)S(1)}, bf16[128,512]{1,0:T(8,128)(2,1)S(1)}) custom-call(bf16[128,2048]{1,0:T(8,128)(2,1)} %rows_hbm.1, bf16[2048,512]{1,0:T(8,128)(2,1)} %wk_hbm.1, bf16[2048,512]{1,0:T(8,128)(2,1)} %wv_hbm.1), custom_call_target="tpu_custom_call" | custom-call | flops 536870912 | bytes 4194304 | tf_op jit(solution)/shard_map/pallas_call | solution.py:96
  6.2 3.1 %shard_map.74 = (bf16[2048,512]{1,0:T(8,128)(2,1)S(1)}, bf16[128,512]{1,0:T(8,128)(2,1)S(1)}, bf16[128,512]{1,0:T(8,128)(2,1)S(1)}, bf16[4,32,128]{2,1,0:T(8,128)(2,1)S(1)}, bf16[4,32,128]{2,1,0:T(8,128)(2,1)S(1)}) custom-call(bf16[128,2048]{1,0:T(8,128)(2,1)S(1)} %collective-permute-done.rows.refs_1_, bf16[2048,512]{1,0:T(8,128)(2,1)S(1)} %get-tuple-element.37.wk, ...), custom_call_target="tpu_custom_call" | custom-call | flops 536870912 | bytes 2097152 | tf_op jit(solution)/shard_map/pallas_call | solution.py:133
  9.3 1.6 %collective-permute-start.2 = (bf16[1,4,32,128]{3,2,1,0:T(8,128)(2,1)S(1)}, bf16[1,4,32,128]{3,2,1,0:T(8,128)(2,1)S(1)}, u32[]{:S(2)}, u32[]{:S(2)}) collective-permute-start(bf16[1,4,32,128]{3,2,1,0:T(8,128)(2,1)S(1)} %bitcast.9), channel_id=1, source_target_pairs={{0,4},{4,0},{8,12},{12,8},{16,20},{20,16},{24,28},{28,24},{1,5},{5... | collective-permute-start | bytes 98312 | tf_op jit(solution)/shard_map/ppermute | solution.py:411
  10.9 2.6 %collective-permute-start.4 = (bf16[1,4,32,128]{3,2,1,0:T(8,128)(2,1)S(1)}, bf16[1,4,32,128]{3,2,1,0:T(8,128)(2,1)S(1)}, u32[]{:S(2)}, u32[]{:S(2)}) collective-permute-start(bf16[1,4,32,128]{3,2,1,0:T(8,128)(2,1)S(1)} %bitcast.6), channel_id=1, source_target_pairs={{0,16},{4,20},{8,24},{12,28},{16,0},{20,4},{24,8},{28,12},{1,17},{... | collective-permute-start | bytes 98312 | tf_op jit(solution)/shard_map/ppermute | solution.py:411
  13.5 1.6 %shard_map.75 = (bf16[256,512]{1,0:T(8,128)(2,1)S(1)}, bf16[512,2048]{1,0:T(8,128)(2,1)S(1)}) custom-call(bf16[128,2048]{1,0:T(8,128)(2,1)S(1)} %get-tuple-element.36.refs_0_, bf16[128,2048]{1,0:T(8,128)(2,1)S(1)} %collective-permute-done.rows.refs_1_, bf16[2048,512]{1,0:T(8,128)(2,1)S(1)} %get-tuple-element.41.refs_2_, bf16[512,2048]{1,0:T(8,128)(2,1)} %refs_3_.1), custom_call_target="tpu_custom_call" | custom-call | flops 536870912 | bytes 2097152 | tf_op jit(solution)/shard_map/pallas_call | solution.py:169
  15.2 0.8 %collective-permute-start.3 = (bf16[2,4,32,128]{3,2,1,0:T(8,128)(2,1)S(1)}, bf16[2,4,32,128]{3,2,1,0:T(8,128)(2,1)S(1)}, u32[]{:S(2)}, u32[]{:S(2)}) collective-permute-start(bf16[2,4,32,128]{3,2,1,0:T(8,128)(2,1)S(1)} %pad_maximum_fusion.4), channel_id=1, source_target_pairs={{0,16},{4,20},{8,24},{12,28},{16,0},{20,4},{24,8},{28,12},{1,17},{... | collective-permute-start | bytes 196616 | tf_op jit(solution)/shard_map/ppermute | solution.py:411
  16.0 1.6 %collective-permute-start.5 = (bf16[2,4,32,128]{3,2,1,0:T(8,128)(2,1)S(1)}, bf16[2,4,32,128]{3,2,1,0:T(8,128)(2,1)S(1)}, u32[]{:S(2)}, u32[]{:S(2)}) collective-permute-start(bf16[2,4,32,128]{3,2,1,0:T(8,128)(2,1)S(1)} %pad_maximum_fusion.5), channel_id=1, source_target_pairs={{0,8},{4,12},{8,0},{12,4},{16,24},{20,28},{24,16},{28,20},{1,9},{5... | collective-permute-start | bytes 196616 | tf_op jit(solution)/shard_map/ppermute | solution.py:411
  17.6 3.3 %collective-permute-done.3 = bf16[2,4,32,128]{3,2,1,0:T(8,128)(2,1)S(1)} collective-permute-done((bf16[2,4,32,128]{3,2,1,0:T(8,128)(2,1)S(1)}, bf16[2,4,32,128]{3,2,1,0:T(8,128)(2,1)S(1)}, u32[]{:S(2)}, u32[]{:S(2)}) %collective-permute-start.3) | collective-permute-done | bytes 65568 | tf_op jit(solution)/shard_map/ppermute | solution.py:411
  21.2 1.9 %collective-permute-done.6.refs_1_.rows_1 = bf16[128,2048]{1,0:T(8,128)(2,1)S(1)} collective-permute-done((bf16[128,2048]{1,0:T(8,128)(2,1)S(1)}, bf16[128,2048]{1,0:T(8,128)(2,1)S(1)}, u32[]{:S(2)}, u32[]{:S(2)}) %collective-permute-start.6) | collective-permute-done | bytes 524320 | tf_op jit(solution)/shard_map/ppermute | solution.py:411
  23.2 1.0 %collective-permute-start.7 = (bf16[4,4,32,128]{3,2,1,0:T(8,128)(2,1)S(1)}, bf16[4,4,32,128]{3,2,1,0:T(8,128)(2,1)S(1)}, u32[]{:S(2)}, u32[]{:S(2)}) collective-permute-start(bf16[4,4,32,128]{3,2,1,0:T(8,128)(2,1)S(1)} %pad_maximum_fusion.refs_7_), channel_id=1, source_target_pairs={{0,8},{4,12},{8,0},{12,4},{16,24},{20,28},{24,16},{28,20},{1,9},{5... | collective-permute-start | bytes 393224 | tf_op jit(solution)/shard_map/ppermute | solution.py:411
  24.2 1.3 %collective-permute-start.8 = (bf16[4,4,32,128]{3,2,1,0:T(8,128)(2,1)S(1)}, bf16[4,4,32,128]{3,2,1,0:T(8,128)(2,1)S(1)}, u32[]{:S(2)}, u32[]{:S(2)}) collective-permute-start(bf16[4,4,32,128]{3,2,1,0:T(8,128)(2,1)S(1)} %pad_maximum_fusion.1.refs_9_), channel_id=1, source_target_pairs={{0,4},{4,0},{8,12},{12,8},{16,20},{20,16},{24,28},{28,24},{1,5},{5... | collective-permute-start | bytes 393224 | tf_op jit(solution)/shard_map/ppermute | solution.py:411
  25.6 1.6 %copy-done.3 = bf16[2048,512]{1,0:T(8,128)(2,1)S(1)} copy-done((bf16[2048,512]{1,0:T(8,128)(2,1)S(1)}, bf16[2048,512]{1,0:T(8,128)(2,1)}, u32[]{:S(2)}) %copy-start.3) | copy-done | bytes 2097176
  27.2 1.6 %copy-done.5 = bf16[2048,512]{1,0:T(8,128)(2,1)S(1)} copy-done((bf16[2048,512]{1,0:T(8,128)(2,1)S(1)}, bf16[2048,512]{1,0:T(8,128)(2,1)}, u32[]{:S(2)}) %copy-start.5) | copy-done | bytes 2097176
  28.8 1.4 %shard_map.77 = (bf16[256,512]{1,0:T(8,128)(2,1)S(1)}, bf16[256,512]{1,0:T(8,128)(2,1)S(1)}, bf16[4,32,128]{2,1,0:T(8,128)(2,1)S(1)}, bf16[4,32,128]{2,1,0:T(8,128)(2,1)S(1)}) custom-call(bf16[128,2048]{1,0:T(8,128)(2,1)S(1)} %collective-permute-done.1.refs_0_.rows_0, bf16[128,2048]{1,0:T(8,128)(2,1)S(1)} %collective-permute-done.6.refs_1_.rows_1, ...), custom_call_target="tpu_custom_call" | custom-call | flops 1073741824 | bytes 1048576 | tf_op jit(solution)/shard_map/pallas_call | solution.py:198
  30.2 0.8 %collective-permute-start.9 = (bf16[1,4,32,128]{3,2,1,0:T(8,128)(2,1)S(1)}, bf16[1,4,32,128]{3,2,1,0:T(8,128)(2,1)S(1)}, u32[]{:S(2)}, u32[]{:S(2)}) collective-permute-start(bf16[1,4,32,128]{3,2,1,0:T(8,128)(2,1)S(1)} %bitcast.14), channel_id=1, source_target_pairs={{0,4},{4,0},{8,12},{12,8},{16,20},{20,16},{24,28},{28,24},{1,5},{5... | collective-permute-start | bytes 98312 | tf_op jit(solution)/shard_map/ppermute | solution.py:411
  30.9 2.4 %collective-permute-start.10 = (bf16[1,4,32,128]{3,2,1,0:T(8,128)(2,1)S(1)}, bf16[1,4,32,128]{3,2,1,0:T(8,128)(2,1)S(1)}, u32[]{:S(2)}, u32[]{:S(2)}) collective-permute-start(bf16[1,4,32,128]{3,2,1,0:T(8,128)(2,1)S(1)} %bitcast.12), channel_id=1, source_target_pairs={{0,16},{4,20},{8,24},{12,28},{16,0},{20,4},{24,8},{28,12},{1,17},{... | collective-permute-start | bytes 98312 | tf_op jit(solution)/shard_map/ppermute | solution.py:411
  33.3 0.7 shard_map.76.refs_0_
  34.2 1.6 %collective-permute-done.10 = bf16[1,4,32,128]{3,2,1,0:T(8,128)(2,1)S(1)} collective-permute-done((bf16[1,4,32,128]{3,2,1,0:T(8,128)(2,1)S(1)}, bf16[1,4,32,128]{3,2,1,0:T(8,128)(2,1)S(1)}, u32[]{:S(2)}, u32[]{:S(2)}) %collective-permute-start.10) | collective-permute-done | bytes 32800 | tf_op jit(solution)/shard_map/ppermute | solution.py:411
  35.8 2.5 %collective-permute-start.11 = (bf16[2,4,32,128]{3,2,1,0:T(8,128)(2,1)S(1)}, bf16[2,4,32,128]{3,2,1,0:T(8,128)(2,1)S(1)}, u32[]{:S(2)}, u32[]{:S(2)}) collective-permute-start(bf16[2,4,32,128]{3,2,1,0:T(8,128)(2,1)S(1)} %pad_maximum_fusion.6), channel_id=1, source_target_pairs={{0,16},{4,20},{8,24},{12,28},{16,0},{20,4},{24,8},{28,12},{1,17},{... | collective-permute-start | bytes 196616 | tf_op jit(solution)/shard_map/ppermute | solution.py:411
  38.3 3.0 %shard_map.78 = (f32[256,512]{1,0:T(8,128)S(1)}, f32[4,256,128]{2,1,0:T(8,128)S(1)}) custom-call(s32[10]{0:T(128)S(1)} %pad_add_fusion.place, bf16[256,512]{1,0:T(8,128)(2,1)S(1)} %shard_map.76.refs_0_, bf16[128,512]{1,0:T(8,128)(2,1)S(1)} %get-tuple-element.39.keys_0.refs_1_, bf16[128,512]{1,0:T(8,128)(2,1)S(1)} %copy-done.9, ...), custom_call_target="tpu_custom_call" | custom-call | flops 402653184 | bytes 524288 | tf_op jit(solution)/shard_map/pallas_call | solution.py:356
  41.8 4.3 %collective-permute-done.12 = bf16[2,4,32,128]{3,2,1,0:T(8,128)(2,1)S(1)} collective-permute-done((bf16[2,4,32,128]{3,2,1,0:T(8,128)(2,1)S(1)}, bf16[2,4,32,128]{3,2,1,0:T(8,128)(2,1)S(1)}, u32[]{:S(2)}, u32[]{:S(2)}) %collective-permute-start.12) | collective-permute-done | bytes 65568 | tf_op jit(solution)/shard_map/ppermute | solution.py:411
  46.5 0.8 %collective-permute-start.14 = (bf16[4,4,32,128]{3,2,1,0:T(8,128)(2,1)S(1)}, bf16[4,4,32,128]{3,2,1,0:T(8,128)(2,1)S(1)}, u32[]{:S(2)}, u32[]{:S(2)}) collective-permute-start(bf16[4,4,32,128]{3,2,1,0:T(8,128)(2,1)S(1)} %pad_maximum_fusion.3.refs_5_.refs_13_), channel_id=1, source_target_pairs={{0,4},{4,0},{8,12},{12,8},{16,20},{20,16},{24,28},{28,24},{1,5},{5... | collective-permute-start | bytes 393224 | tf_op jit(solution)/shard_map/ppermute | solution.py:411
  47.3 3.8 %collective-permute-done.13.refs_4_.refs_12_ = bf16[4,4,32,128]{3,2,1,0:T(8,128)(2,1)S(1)} collective-permute-done((bf16[4,4,32,128]{3,2,1,0:T(8,128)(2,1)S(1)}, bf16[4,4,32,128]{3,2,1,0:T(8,128)(2,1)S(1)}, u32[]{:S(2)}, u32[]{:S(2)}) %collective-permute-start.13) | collective-permute-done | bytes 131104 | tf_op jit(solution)/shard_map/ppermute | solution.py:411
  51.5 3.1 %shard_map.79 = (bf16[128,512]{1,0:T(8,128)(2,1)S(1)}, bf16[128,512]{1,0:T(8,128)(2,1)S(1)}) custom-call(s32[10]{0:T(128)S(1)} %pad_add_fusion.place, bf16[256,512]{1,0:T(8,128)(2,1)S(1)} %shard_map.76.refs_0_, f32[256,512]{1,0:T(8,128)S(1)} %get-tuple-element.52.refs_1_, f32[4,256,128]{2,1,0:T(8,128)S(1)} %get-tuple-element.53.refs_2_, ...), custom_call_target="tpu_custom_call" | custom-call | flops 134217728 | bytes 524288 | tf_op jit(solution)/shard_map/pallas_call | solution.py:356
  54.7 1.3 %collective-permute-done.15.rows_1 = bf16[128,512]{1,0:T(8,128)(2,1)S(1)} collective-permute-done((bf16[128,512]{1,0:T(8,128)(2,1)S(1)}, bf16[128,512]{1,0:T(8,128)(2,1)S(1)}, u32[]{:S(2)}, u32[]{:S(2)}) %collective-permute-start.15) | collective-permute-done | bytes 131104 | tf_op jit(solution)/shard_map/ppermute | solution.py:411
  56.0 2.4 %shard_map.80 = bf16[128,2048]{1,0:T(8,128)(2,1)S(1)} custom-call(bf16[128,512]{1,0:T(8,128)(2,1)S(1)} %get-tuple-element.60.rows_0, bf16[128,512]{1,0:T(8,128)(2,1)S(1)} %collective-permute-done.15.rows_1, bf16[512,2048]{1,0:T(8,128)(2,1)S(1)} %get-tuple-element.62.weight_0, bf16[512,2048]{1,0:T(8,128)(2,1)} %collective-permute-done.16.weight_1), custom_call_target="tpu_custom_call" | custom-call | flops 536870912 | bytes 1048576 | tf_op jit(solution)/shard_map/pallas_call | solution.py:388
  59.0 3.3 %shard_map.81 = (bf16[128,512]{1,0:T(8,128)(2,1)S(1)}, bf16[128,512]{1,0:T(8,128)(2,1)S(1)}) custom-call(s32[10]{0:T(128)S(1)} %pad_add_fusion.place, bf16[256,512]{1,0:T(8,128)(2,1)S(1)} %copy-done.13, bf16[128,512]{1,0:T(8,128)(2,1)S(1)} %get-tuple-element.39.keys_0.refs_1_, bf16[128,512]{1,0:T(8,128)(2,1)S(1)} %copy-done.9, ...), custom_call_target="tpu_custom_call" | custom-call | flops 536870912 | bytes 524288 | tf_op jit(solution)/shard_map/pallas_call | solution.py:356
  62.4 1.3 %collective-permute-done.17.rows_1 = bf16[128,512]{1,0:T(8,128)(2,1)S(1)} collective-permute-done((bf16[128,512]{1,0:T(8,128)(2,1)S(1)}, bf16[128,512]{1,0:T(8,128)(2,1)S(1)}, u32[]{:S(2)}, u32[]{:S(2)}) %collective-permute-start.17) | collective-permute-done | bytes 131104 | tf_op jit(solution)/shard_map/ppermute | solution.py:411
  63.7 2.3 %shard_map.82 = f32[128,2048]{1,0:T(8,128)S(1)} custom-call(bf16[128,512]{1,0:T(8,128)(2,1)S(1)} %get-tuple-element.65.rows_0, bf16[128,512]{1,0:T(8,128)(2,1)S(1)} %collective-permute-done.17.rows_1, bf16[512,2048]{1,0:T(8,128)(2,1)S(1)} %get-tuple-element.62.weight_0, bf16[512,2048]{1,0:T(8,128)(2,1)} %collective-permute-done.16.weight_1), custom_call_target="tpu_custom_call" | custom-call | flops 536870912 | bytes 1048576 | tf_op jit(solution)/shard_map/pallas_call | solution.py:388
  66.0 6.4 %collective-permute-done.18 = bf16[128,2048]{1,0:T(8,128)(2,1)S(1)} collective-permute-done((bf16[128,2048]{1,0:T(8,128)(2,1)S(1)}, bf16[128,2048]{1,0:T(8,128)(2,1)S(1)}, u32[]{:S(2)}, u32[]{:S(2)}) %collective-permute-start.18) | collective-permute-done | bytes 524320 | tf_op jit(solution)/shard_map/ppermute | solution.py:411
  72.4 0.9 %add_convert_fusion = bf16[128,2048]{1,0:T(8,128)(2,1)} fusion(f32[128,2048]{1,0:T(8,128)S(1)} %shard_map.82, bf16[128,2048]{1,0:T(8,128)(2,1)S(1)} %collective-permute-done.18), kind=kLoop, calls=%fused_computation | loop fusion | flops 786432 | bytes 2097152 | tf_op jit(solution)/shard_map/convert_element_type | solution.py:460
  (58 shorter events, 3.2 us)
Async XLA Ops:
  0.0 6.2 %copy-start.14 = (s32[4,128]{1,0:T(4,128)S(1)}, s32[4,128]{1,0:T(4,128)}, u32[]{:S(2)}) copy-start(s32[4,128]{1,0:T(4,128)} %pattern.3) | copy-start | bytes 6148
  0.0 6.2 %collective-permute-start = (bf16[128,2048]{1,0:T(8,128)(2,1)}, bf16[128,2048]{1,0:T(8,128)(2,1)S(1)}, u32[]{:S(2)}, u32[]{:S(2)}) collective-permute-start(bf16[128,2048]{1,0:T(8,128)(2,1)} %rows_hbm.1), channel_id=1, source_target_pairs={{0,1},{1,0},{2,3},{3,2},{4,5},{5,4},{6,7},{7,6},{8,9},{9,8},{10,11... | collective-permute-start | bytes 1572872 | tf_op jit(solution)/shard_map/ppermute | solution.py:411
  0.5 20.6 %collective-permute-start.1 = (bf16[128,2048]{1,0:T(8,128)(2,1)}, bf16[128,2048]{1,0:T(8,128)(2,1)S(1)}, u32[]{:S(2)}, u32[]{:S(2)}) collective-permute-start(bf16[128,2048]{1,0:T(8,128)(2,1)} %rows_hbm.1), channel_id=1, source_target_pairs={{0,2},{1,3},{2,0},{3,1},{4,6},{5,7},{6,4},{7,5},{8,10},{9,11},{10,... | collective-permute-start | bytes 1572872 | tf_op jit(solution)/shard_map/ppermute | solution.py:411
  6.1 3.1 %copy-start.2 = (bf16[2048,512]{1,0:T(8,128)(2,1)}, bf16[2048,512]{1,0:T(8,128)(2,1)S(1)}, u32[]{:S(2)}) copy-start(bf16[2048,512]{1,0:T(8,128)(2,1)S(1)} %get-tuple-element.37.wk) | copy-start | bytes 6291460
  6.1 3.1 %copy-start.4 = (bf16[2048,512]{1,0:T(8,128)(2,1)}, bf16[2048,512]{1,0:T(8,128)(2,1)S(1)}, u32[]{:S(2)}) copy-start(bf16[2048,512]{1,0:T(8,128)(2,1)S(1)} %get-tuple-element.38.wv) | copy-start | bytes 6291460
  6.2 3.1 %copy-start.6 = (bf16[128,512]{1,0:T(8,128)(2,1)}, bf16[128,512]{1,0:T(8,128)(2,1)S(1)}, u32[]{:S(2)}) copy-start(bf16[128,512]{1,0:T(8,128)(2,1)S(1)} %get-tuple-element.40.values_0.refs_4_) | copy-start | bytes 393220
  9.3 5.8 %copy-start = (bf16[2048,512]{1,0:T(8,128)(2,1)}, bf16[2048,512]{1,0:T(8,128)(2,1)S(1)}, u32[]{:S(2)}) copy-start(bf16[2048,512]{1,0:T(8,128)(2,1)S(1)} %get-tuple-element.41.refs_2_) | copy-start | bytes 6291460
  9.3 5.8 %copy-start.8 = (bf16[128,512]{1,0:T(8,128)(2,1)}, bf16[128,512]{1,0:T(8,128)(2,1)S(1)}, u32[]{:S(2)}) copy-start(bf16[128,512]{1,0:T(8,128)(2,1)S(1)} %get-tuple-element.46.refs_2_) | copy-start | bytes 393220
  9.3 5.8 %copy-start.10 = (bf16[128,512]{1,0:T(8,128)(2,1)}, bf16[128,512]{1,0:T(8,128)(2,1)S(1)}, u32[]{:S(2)}) copy-start(bf16[128,512]{1,0:T(8,128)(2,1)S(1)} %get-tuple-element.48.refs_5_) | copy-start | bytes 393220
  9.3 5.8 %collective-permute-start.2 = (bf16[1,4,32,128]{3,2,1,0:T(8,128)(2,1)S(1)}, bf16[1,4,32,128]{3,2,1,0:T(8,128)(2,1)S(1)}, u32[]{:S(2)}, u32[]{:S(2)}) collective-permute-start(bf16[1,4,32,128]{3,2,1,0:T(8,128)(2,1)S(1)} %bitcast.9), channel_id=1, source_target_pairs={{0,4},{4,0},{8,12},{12,8},{16,20},{20,16},{24,28},{28,24},{1,5},{5... | collective-permute-start | bytes 98312 | tf_op jit(solution)/shard_map/ppermute | solution.py:411
  10.9 5.1 %collective-permute-start.4 = (bf16[1,4,32,128]{3,2,1,0:T(8,128)(2,1)S(1)}, bf16[1,4,32,128]{3,2,1,0:T(8,128)(2,1)S(1)}, u32[]{:S(2)}, u32[]{:S(2)}) collective-permute-start(bf16[1,4,32,128]{3,2,1,0:T(8,128)(2,1)S(1)} %bitcast.6), channel_id=1, source_target_pairs={{0,16},{4,20},{8,24},{12,28},{16,0},{20,4},{24,8},{28,12},{1,17},{... | collective-permute-start | bytes 98312 | tf_op jit(solution)/shard_map/ppermute | solution.py:411
  15.1 5.9 %copy-start.12 = (bf16[256,512]{1,0:T(8,128)(2,1)}, bf16[256,512]{1,0:T(8,128)(2,1)S(1)}, u32[]{:S(2)}) copy-start(bf16[256,512]{1,0:T(8,128)(2,1)S(1)} %get-tuple-element.64.refs_0_) | copy-start | bytes 786436
  15.2 5.7 %collective-permute-start.3 = (bf16[2,4,32,128]{3,2,1,0:T(8,128)(2,1)S(1)}, bf16[2,4,32,128]{3,2,1,0:T(8,128)(2,1)S(1)}, u32[]{:S(2)}, u32[]{:S(2)}) collective-permute-start(bf16[2,4,32,128]{3,2,1,0:T(8,128)(2,1)S(1)} %pad_maximum_fusion.4), channel_id=1, source_target_pairs={{0,16},{4,20},{8,24},{12,28},{16,0},{20,4},{24,8},{28,12},{1,17},{... | collective-permute-start | bytes 196616 | tf_op jit(solution)/shard_map/ppermute | solution.py:411
  16.0 5.0 %collective-permute-start.5 = (bf16[2,4,32,128]{3,2,1,0:T(8,128)(2,1)S(1)}, bf16[2,4,32,128]{3,2,1,0:T(8,128)(2,1)S(1)}, u32[]{:S(2)}, u32[]{:S(2)}) collective-permute-start(bf16[2,4,32,128]{3,2,1,0:T(8,128)(2,1)S(1)} %pad_maximum_fusion.5), channel_id=1, source_target_pairs={{0,8},{4,12},{8,0},{12,4},{16,24},{20,28},{24,16},{28,20},{1,9},{5... | collective-permute-start | bytes 196616 | tf_op jit(solution)/shard_map/ppermute | solution.py:411
  21.1 2.0 %collective-permute-start.6 = (bf16[128,2048]{1,0:T(8,128)(2,1)S(1)}, bf16[128,2048]{1,0:T(8,128)(2,1)S(1)}, u32[]{:S(2)}, u32[]{:S(2)}) collective-permute-start(bf16[128,2048]{1,0:T(8,128)(2,1)S(1)} %collective-permute-done.1.refs_0_.rows_0), channel_id=1, source_target_pairs={{0,1},{1,0},{2,3},{3,2},{4,5},{5,4},{6,7},{7,6},{8,9},{9,8},{10,11... | collective-permute-start | bytes 1572872 | tf_op jit(solution)/shard_map/ppermute | solution.py:411
  23.1 33.0 %collective-permute-start.16 = (bf16[512,2048]{1,0:T(8,128)(2,1)}, bf16[512,2048]{1,0:T(8,128)(2,1)}, u32[]{:S(2)}, u32[]{:S(2)}) collective-permute-start(bf16[512,2048]{1,0:T(8,128)(2,1)} %refs_3_.1), channel_id=1, source_target_pairs={{0,1},{1,0},{2,3},{3,2},{4,5},{5,4},{6,7},{7,6},{8,9},{9,8},{10,11... | collective-permute-start | bytes 6291464 | tf_op jit(solution)/shard_map/ppermute | solution.py:411
  23.2 10.1 %copy-start.1 = (bf16[2048,512]{1,0:T(8,128)(2,1)S(1)}, bf16[2048,512]{1,0:T(8,128)(2,1)}, u32[]{:S(2)}) copy-start(bf16[2048,512]{1,0:T(8,128)(2,1)} %copy-done) | copy-start | bytes 6291460
  23.2 15.1 %collective-permute-start.7 = (bf16[4,4,32,128]{3,2,1,0:T(8,128)(2,1)S(1)}, bf16[4,4,32,128]{3,2,1,0:T(8,128)(2,1)S(1)}, u32[]{:S(2)}, u32[]{:S(2)}) collective-permute-start(bf16[4,4,32,128]{3,2,1,0:T(8,128)(2,1)S(1)} %pad_maximum_fusion.refs_7_), channel_id=1, source_target_pairs={{0,8},{4,12},{8,0},{12,4},{16,24},{20,28},{24,16},{28,20},{1,9},{5... | collective-permute-start | bytes 393224 | tf_op jit(solution)/shard_map/ppermute | solution.py:411
  24.2 14.1 %collective-permute-start.8 = (bf16[4,4,32,128]{3,2,1,0:T(8,128)(2,1)S(1)}, bf16[4,4,32,128]{3,2,1,0:T(8,128)(2,1)S(1)}, u32[]{:S(2)}, u32[]{:S(2)}) collective-permute-start(bf16[4,4,32,128]{3,2,1,0:T(8,128)(2,1)S(1)} %pad_maximum_fusion.1.refs_9_), channel_id=1, source_target_pairs={{0,4},{4,0},{8,12},{12,8},{16,20},{20,16},{24,28},{28,24},{1,5},{5... | collective-permute-start | bytes 393224 | tf_op jit(solution)/shard_map/ppermute | solution.py:411
  30.1 8.1 %copy-start.15 = (s32[8]{0:T(128)S(1)}, s32[8]{0:T(128)}, u32[]{:S(2)}) copy-start(s32[8]{0:T(128)} %param.13) | copy-start | bytes 100
  30.1 8.2 %copy-start.7 = (bf16[128,512]{1,0:T(8,128)(2,1)S(1)}, bf16[128,512]{1,0:T(8,128)(2,1)}, u32[]{:S(2)}) copy-start(bf16[128,512]{1,0:T(8,128)(2,1)} %copy-done.6) | copy-start | bytes 393220
  30.2 8.2 %copy-start.9 = (bf16[128,512]{1,0:T(8,128)(2,1)S(1)}, bf16[128,512]{1,0:T(8,128)(2,1)}, u32[]{:S(2)}) copy-start(bf16[128,512]{1,0:T(8,128)(2,1)} %copy-done.8) | copy-start | bytes 393220
  30.2 8.2 %copy-start.11 = (bf16[128,512]{1,0:T(8,128)(2,1)S(1)}, bf16[128,512]{1,0:T(8,128)(2,1)}, u32[]{:S(2)}) copy-start(bf16[128,512]{1,0:T(8,128)(2,1)} %copy-done.10) | copy-start | bytes 393220
  30.2 4.0 %collective-permute-start.9 = (bf16[1,4,32,128]{3,2,1,0:T(8,128)(2,1)S(1)}, bf16[1,4,32,128]{3,2,1,0:T(8,128)(2,1)S(1)}, u32[]{:S(2)}, u32[]{:S(2)}) collective-permute-start(bf16[1,4,32,128]{3,2,1,0:T(8,128)(2,1)S(1)} %bitcast.14), channel_id=1, source_target_pairs={{0,4},{4,0},{8,12},{12,8},{16,20},{20,16},{24,28},{28,24},{1,5},{5... | collective-permute-start | bytes 98312 | tf_op jit(solution)/shard_map/ppermute | solution.py:411
  30.9 4.8 %collective-permute-start.10 = (bf16[1,4,32,128]{3,2,1,0:T(8,128)(2,1)S(1)}, bf16[1,4,32,128]{3,2,1,0:T(8,128)(2,1)S(1)}, u32[]{:S(2)}, u32[]{:S(2)}) collective-permute-start(bf16[1,4,32,128]{3,2,1,0:T(8,128)(2,1)S(1)} %bitcast.12), channel_id=1, source_target_pairs={{0,16},{4,20},{8,24},{12,28},{16,0},{20,4},{24,8},{28,12},{1,17},{... | collective-permute-start | bytes 98312 | tf_op jit(solution)/shard_map/ppermute | solution.py:411
  35.8 6.0 %collective-permute-start.11 = (bf16[2,4,32,128]{3,2,1,0:T(8,128)(2,1)S(1)}, bf16[2,4,32,128]{3,2,1,0:T(8,128)(2,1)S(1)}, u32[]{:S(2)}, u32[]{:S(2)}) collective-permute-start(bf16[2,4,32,128]{3,2,1,0:T(8,128)(2,1)S(1)} %pad_maximum_fusion.6), channel_id=1, source_target_pairs={{0,16},{4,20},{8,24},{12,28},{16,0},{20,4},{24,8},{28,12},{1,17},{... | collective-permute-start | bytes 196616 | tf_op jit(solution)/shard_map/ppermute | solution.py:411
  41.4 4.7 %collective-permute-start.12 = (bf16[2,4,32,128]{3,2,1,0:T(8,128)(2,1)S(1)}, bf16[2,4,32,128]{3,2,1,0:T(8,128)(2,1)S(1)}, u32[]{:S(2)}, u32[]{:S(2)}) collective-permute-start(bf16[2,4,32,128]{3,2,1,0:T(8,128)(2,1)S(1)} %pad_maximum_fusion.7), channel_id=1, source_target_pairs={{0,8},{4,12},{8,0},{12,4},{16,24},{20,28},{24,16},{28,20},{1,9},{5... | collective-permute-start | bytes 196616 | tf_op jit(solution)/shard_map/ppermute | solution.py:411
  46.1 5.0 %collective-permute-start.13 = (bf16[4,4,32,128]{3,2,1,0:T(8,128)(2,1)S(1)}, bf16[4,4,32,128]{3,2,1,0:T(8,128)(2,1)S(1)}, u32[]{:S(2)}, u32[]{:S(2)}) collective-permute-start(bf16[4,4,32,128]{3,2,1,0:T(8,128)(2,1)S(1)} %pad_maximum_fusion.2.refs_3_.refs_11_), channel_id=1, source_target_pairs={{0,8},{4,12},{8,0},{12,4},{16,24},{20,28},{24,16},{28,20},{1,9},{5... | collective-permute-start | bytes 393224 | tf_op jit(solution)/shard_map/ppermute | solution.py:411
  46.5 5.0 %collective-permute-start.14 = (bf16[4,4,32,128]{3,2,1,0:T(8,128)(2,1)S(1)}, bf16[4,4,32,128]{3,2,1,0:T(8,128)(2,1)S(1)}, u32[]{:S(2)}, u32[]{:S(2)}) collective-permute-start(bf16[4,4,32,128]{3,2,1,0:T(8,128)(2,1)S(1)} %pad_maximum_fusion.3.refs_5_.refs_13_), channel_id=1, source_target_pairs={{0,4},{4,0},{8,12},{12,8},{16,20},{20,16},{24,28},{28,24},{1,5},{5... | collective-permute-start | bytes 393224 | tf_op jit(solution)/shard_map/ppermute | solution.py:411
  54.6 1.4 %collective-permute-start.15 = (bf16[128,512]{1,0:T(8,128)(2,1)S(1)}, bf16[128,512]{1,0:T(8,128)(2,1)S(1)}, u32[]{:S(2)}, u32[]{:S(2)}) collective-permute-start(bf16[128,512]{1,0:T(8,128)(2,1)S(1)} %get-tuple-element.61), channel_id=1, source_target_pairs={{0,1},{1,0},{2,3},{3,2},{4,5},{5,4},{6,7},{7,6},{8,9},{9,8},{10,11... | collective-permute-start | bytes 393224 | tf_op jit(solution)/shard_map/ppermute | solution.py:411
  58.4 14.0 %collective-permute-start.18 = (bf16[128,2048]{1,0:T(8,128)(2,1)S(1)}, bf16[128,2048]{1,0:T(8,128)(2,1)S(1)}, u32[]{:S(2)}, u32[]{:S(2)}) collective-permute-start(bf16[128,2048]{1,0:T(8,128)(2,1)S(1)} %shard_map.80), channel_id=1, source_target_pairs={{0,2},{1,3},{2,0},{3,1},{4,6},{5,7},{6,4},{7,5},{8,10},{9,11},{10,... | collective-permute-start | bytes 1572872 | tf_op jit(solution)/shard_map/ppermute | solution.py:411
  62.3 1.4 %collective-permute-start.17 = (bf16[128,512]{1,0:T(8,128)(2,1)S(1)}, bf16[128,512]{1,0:T(8,128)(2,1)S(1)}, u32[]{:S(2)}, u32[]{:S(2)}) collective-permute-start(bf16[128,512]{1,0:T(8,128)(2,1)S(1)} %get-tuple-element.66), channel_id=1, source_target_pairs={{0,1},{1,0},{2,3},{3,2},{4,5},{5,4},{6,7},{7,6},{8,9},{9,8},{10,11... | collective-permute-start | bytes 393224 | tf_op jit(solution)/shard_map/ppermute | solution.py:411
  (3 other events, 6.2 us)

commit v3 on v2

--- a/solution.py
+++ b/solution.py
@@ -33,8 +33,8 @@
     return lax.dot_general(a, b, (((1,), (1,)), ((), ())), preferred_element_type=F32)
 
 
-def params():
-    return pltpu.CompilerParams(vmem_limit_bytes=40 * 2**20)
+def params(extra=0):
+    return pltpu.CompilerParams(vmem_limit_bytes=16 * 2**20 + extra)
 
 
 def cost(flops, bytes_accessed, transcendentals=0):
@@ -110,11 +110,7 @@
     )(keep_in_hbm(rows), keep_in_hbm(w_key), keep_in_hbm(w_value))
 
 
-def second_kernel(
-    rows, wk, wv, keys_0, values_0, pattern, wq_hbm, wq, keys, values, kept_k, kept_v, sem
-):
-    copy = pltpu.make_async_copy(wq_hbm, wq, sem)
-    copy.start()
+def second_kernel(rows, wk, wv, keys_0, values_0, pattern, keys, values, kept_k, kept_v):
     for part in halves_of(wk.shape[1]):
         keys[:, part] = dot(rows[...], wk[:, part]).astype(BF16)
         values[:, part] = dot(rows[...], wv[:, part]).astype(BF16)
@@ -123,59 +119,73 @@
         lambda head: (head_of(keys, head), head_of(values, head)),
     ]
     pick_dilated(pattern, blocks, kept_k, kept_v)
-    copy.wait()
-
-
-def second(rows, wk, wv, keys_0, values_0, pattern, w_query):
+
+
+def second(rows, wk, wv, keys_0, values_0, pattern):
     count, depth = rows.shape
     width = wk.shape[1]
     kept = (width // HEAD_SIZE, FAR_ROWS, HEAD_SIZE)
     return pl.pallas_call(
         second_kernel,
-        in_specs=[IN_VMEM] * 6 + [IN_HBM],
-        out_specs=[IN_VMEM] * 5,
+        in_specs=[IN_VMEM] * 6,
+        out_specs=[IN_VMEM] * 4,
+        out_shape=[shape((count, width))] * 2 + [shape(kept)] * 2,
+        compiler_params=params(),
+        cost_estimate=cost(4 * count * depth * width, 2 * count * depth),
+    )(rows, wk, wv, keys_0, values_0, pattern)
+
+
+def query_first_kernel(rows_0, rows_1, wq_hbm, w_hbm, queries, wq, w, sems):
+    parts = halves_of(wq.shape[1])
+    copies = [
+        pltpu.make_async_copy(wq_hbm.at[:, part], wq.at[:, part], sems.at[index])
+        for index, part in enumerate(parts)
+    ]
+    copies.append(pltpu.make_async_copy(w_hbm, w, sems.at[len(parts)]))
+    for copy in copies:
+        copy.start()
+    rows = jnp.concatenate([rows_0[...], rows_1[...]], axis=0)
+    for part, copy in zip(parts, copies):
+        copy.wait()
+        queries[:, part] = dot(rows, wq[:, part]).astype(BF16)
+    copies[-1].wait()
+
+
+def query_first(rows_0, rows_1, w_query, w_out):
+    count, depth = rows_0.shape
+    width = w_query.shape[1]
+    return pl.pallas_call(
+        query_first_kernel,
+        in_specs=[IN_VMEM] * 2 + [IN_HBM] * 2,
+        out_specs=[IN_VMEM] * 3,
         out_shape=[
+            shape((2 * count, width)),
             pltpu.VMEM(w_query.shape, BF16),
-            shape((count, width)),
-            shape((count, width)),
-            shape(kept),
-            shape(kept),
+            pltpu.VMEM(w_out.shape, BF16),
         ],
-        scratch_shapes=[pltpu.SemaphoreType.DMA],
-        compiler_params=params(),
-        cost_estimate=cost(4 * count * depth * width, 2 * depth * width),
-    )(rows, wk, wv, keys_0, values_0, pattern, keep_in_hbm(w_query))
-
-
-def query_kernel(carry, *refs):
-    rows_0, rows_1, wq = refs[:3]
-    if carry:
-        w_hbm, queries, w, sem = refs[3:]
-        copy = pltpu.make_async_copy(w_hbm, w, sem)
-        copy.start()
-    else:
-        queries = refs[3]
+        scratch_shapes=[pltpu.SemaphoreType.DMA((1 + len(halves_of(width)),))],
+        compiler_params=params(),
+        cost_estimate=cost(4 * count * depth * width, 4 * depth * width),
+    )(rows_0, rows_1, keep_in_hbm(w_query), keep_in_hbm(w_out))
+
+
+def query_kernel(rows_0, rows_1, wq, queries):
     rows = jnp.concatenate([rows_0[...], rows_1[...]], axis=0)
     for part in halves_of(wq.shape[1]):
         queries[:, part] = dot(rows, wq[:, part]).astype(BF16)
-    if carry:
-        copy.wait()
-
-
-def query(rows_0, rows_1, wq, carried=None):
+
+
+def query(rows_0, rows_1, wq):
     count, depth = rows_0.shape
     width = wq.shape[1]
-    carry = carried is not None
-    return pl.pallas_call(
-        functools.partial(query_kernel, carry),
-        in_specs=[IN_VMEM] * 3 + [IN_HBM] * carry,
-        out_specs=[IN_VMEM] * (1 + carry),
-        out_shape=[shape((2 * count, width))]
-        + ([pltpu.VMEM(carried.shape, BF16)] if carry else []),
-        scratch_shapes=[pltpu.SemaphoreType.DMA] * carry,
-        compiler_params=params(),
-        cost_estimate=cost(4 * count * depth * width, 2 * depth * width * carry),
-    )(rows_0, rows_1, wq, *([keep_in_hbm(carried)] if carry else []))
+    return pl.pallas_call(
+        query_kernel,
+        in_specs=[IN_VMEM] * 3,
+        out_specs=IN_VMEM,
+        out_shape=shape((2 * count, width)),
+        compiler_params=params(),
+        cost_estimate=cost(4 * count * depth * width, 4 * count * depth),
+    )(rows_0, rows_1, wq)
 
 
 def third_kernel(rows_0, rows_1, wk, wv, pattern, keys, values, kept_k, kept_v):
@@ -217,15 +227,38 @@
     return jnp.where(condition, jnp.float32(0), jnp.float32(HIDDEN))
 
 
-def far_bias(place, slides, subs, span_of, blocks, row_slides):
-    column = lax.broadcasted_iota(jnp.int32, (1, GROUP * FAR_ROWS), 1)
-    span = span_of(column // FAR_ROWS)
+def bias_kernel(slides, subs, spans, few, place, out):
+    span, sub = place[slides], place[slides + 1]
+    slide = [slide_of(place, slides, span * subs + (sub ^ r)) for r in range(subs)]
+    for r in range(subs):
+        for c in range(subs):
+            value = hidden_if_not(slide[r] == slide[c])
+            out[r : r + 1, c * BLOCK : (c + 1) * BLOCK] = jnp.full((1, BLOCK), value, F32)
+    count = spans * FAR_ROWS
+    column = lax.broadcasted_iota(jnp.int32, (1, count), 1)
+    far = column // FAR_ROWS
+    if few:
+        far = far ^ span
     upper = (column // DILATED_KEPT) % BLOCKS_HALF
-    me = place[slides + 1]
-    block = span * subs + jnp.where(upper == 0, me ^ blocks[0], me ^ blocks[1])
-    slide = slide_of(place, slides, block)
-    elsewhere = span != place[slides]
-    return [hidden_if_not((slide == mine) & elsewhere) for mine in row_slides]
+    for half in range(subs // BLOCKS_HALF):
+        place_0, place_1 = sub ^ (half * BLOCKS_HALF), sub ^ (half * BLOCKS_HALF + 1)
+        theirs = slide_of(place, slides, far * subs + jnp.where(upper == 0, place_0, place_1))
+        start = subs * BLOCK + half * count
+        for r in range(subs):
+            seen = (theirs == slide[r]) & (far != span)
+            out[r : r + 1, start : start + count] = hidden_if_not(seen)
+
+
+def make_bias(place, slides, subs, spans, few):
+    columns = subs * BLOCK + subs // BLOCKS_HALF * spans * FAR_ROWS
+    return pl.pallas_call(
+        functools.partial(bias_kernel, slides, subs, spans, few),
+        in_specs=[IN_SMEM],
+        out_specs=IN_VMEM,
+        out_shape=shape((subs, columns), F32),
+        compiler_params=params(),
+        cost_estimate=cost(64 * subs * columns, 4 * subs * columns),
+    )(place)
 
 
 def add_rows(scores, bias):
@@ -263,7 +296,7 @@
     return found
 
 
-def attend_kernel(slides, subs, relative, near, halves, few, finish, place, *refs):
+def attend_kernel(relative, near, halves, few, finish, bias, *refs):
     refs = list(refs)
     queries = refs.pop(0)
     if near:
@@ -273,61 +306,49 @@
         gathered_in, stats_in = refs[0:2]
         del refs[:2]
     far = []
-    for blocks in halves:
+    for half in halves:
         size = 2 if few else 1
-        far.append((blocks, refs[:size], refs[size : 2 * size]))
+        far.append((half, refs[:size], refs[size : 2 * size]))
         del refs[: 2 * size]
-    sub = place[slides + 1]
-    slide = [
-        slide_of(place, slides, place[slides] * subs + (sub ^ r)) for r in range(subs)
-    ]
-    mine = [slide[r] for r in relative]
-    if near:
-        near_bias = [
-            jnp.concatenate(
-                [
-                    jnp.full((1, BLOCK), hidden_if_not(slide[r] == slide[c]), F32)
-                    for c in range(subs)
-                ],
-                axis=1,
-            )
-            for r in relative
-        ]
-    if few:
-        biases = [
-            far_bias(place, slides, subs, lambda i: place[slides] ^ i, blocks, mine)
-            for blocks, _, _ in far
-        ]
-    for head in range(queries.shape[1] // HEAD_SIZE):
-        asked = head_of(queries, head)
+    span = bias.shape[0] * BLOCK
+    half_count = (bias.shape[1] - span) * BLOCKS_HALF // bias.shape[0]
+
+    def rows_of_bias(columns):
+        return [bias[r : r + 1, columns] for r in relative]
+
+    def one_head(head, _):
+        columns = pl.ds(pl.multiple_of(head * HEAD_SIZE, HEAD_SIZE), HEAD_SIZE)
+        asked = queries[:, columns]
         if near:
-            near_keys = jnp.concatenate([head_of(ref, head) for ref in keys], axis=0)
-            near_values = jnp.concatenate([head_of(ref, head) for ref in values], axis=0)
-            scores = add_rows(dot_t(asked, near_keys), near_bias)
+            near_keys = jnp.concatenate([ref[:, columns] for ref in keys], axis=0)
+            near_values = jnp.concatenate([ref[:, columns] for ref in values], axis=0)
+            scores = add_rows(dot_t(asked, near_keys), rows_of_bias(slice(0, span)))
             peak = jnp.max(scores, axis=1, keepdims=True)
             weight = jnp.exp2((scores - peak) * SCALE)
             total = jnp.sum(weight, axis=1, keepdims=True)
             state = peak, total, dot(weight.astype(BF16), near_values)
         else:
-            state = stats_in[head, :, 0:1], stats_in[head, :, 1:2], head_of(gathered_in, head)
-        for index, (blocks, far_keys, far_values) in enumerate(far):
+            state = stats_in[head, :, 0:1], stats_in[head, :, 1:2], gathered_in[:, columns]
+        for half, far_keys, far_values in far:
+            start = span + half * half_count
             if few:
                 group = far_group(far_keys, far_values, head)
-                state = far_update(asked, *group, biases[index], state)
+                rows = rows_of_bias(slice(start, start + half_count))
+                state = far_update(asked, *group, rows, state)
                 continue
 
-            def step(number, state, blocks=blocks, k=far_keys[0], v=far_values[0]):
+            def step(number, state, start=start, k=far_keys[0], v=far_values[0]):
                 base = number * GROUP
-                bias = far_bias(place, slides, subs, lambda i: base + i, blocks, mine)
                 group = [
                     jnp.concatenate([ref[base + i, head] for i in range(GROUP)], axis=0)
                     for ref in (k, v)
                 ]
-                return far_update(asked, *group, bias, state)
+                width = GROUP * FAR_ROWS
+                rows = rows_of_bias(pl.ds(pl.multiple_of(start + number * width, width), width))
+                return far_update(asked, *group, rows, state)
 
             state = lax.fori_loop(0, far_keys[0].shape[0] // GROUP, step, state)
         peak, total, gathered = state
-        columns = slice(head * HEAD_SIZE, (head + 1) * HEAD_SIZE)
         if finish:
             keep, send = refs
             context = (gathered / total).astype(BF16)
@@ -338,40 +359,39 @@
             gathered_out[:, columns] = gathered
             lane = lax.broadcasted_iota(jnp.int32, gathered.shape, 1)
             stats_out[head] = jnp.where(lane == 0, peak, total)
-
-
-def attend(place, slides, subs, few, relative, queries, halves, near=None, begun=None, finish=True):
+        return 0
+
+    lax.fori_loop(0, queries.shape[1] // HEAD_SIZE, one_head, 0)
+
+
+def attend(bias, few, relative, queries, halves, near=None, begun=None, finish=True):
     rows, width = queries.shape
     heads = width // HEAD_SIZE
     operands = [queries]
     operands += [*near[0], *near[1]] if near else list(begun)
-    columns = subs * BLOCK if near else 0
+    columns = bias.shape[0] * BLOCK if near else 0
+    spans = 0
     for _, keys, values in halves:
         operands += [*keys, *values]
-        columns += sum(part.shape[0] for part in keys) * FAR_ROWS
+        spans += sum(part.shape[0] for part in keys)
+    columns += spans * FAR_ROWS
     if finish:
         out_shape = [shape((BLOCK, width))] * 2
     else:
         out_shape = [shape((rows, width), F32), shape((heads, rows, HEAD_SIZE), F32)]
+    far_bytes = 4 * spans * FAR_ROWS * width
     return pl.pallas_call(
         functools.partial(
-            attend_kernel,
-            slides,
-            subs,
-            relative,
-            near is not None,
-            [half[0] for half in halves],
-            few,
-            finish,
+            attend_kernel, relative, near is not None, [half[0] for half in halves], few, finish
         ),
-        in_specs=[IN_SMEM] + [IN_VMEM] * len(operands),
+        in_specs=[IN_VMEM] * (1 + len(operands)),
         out_specs=[IN_VMEM] * 2,
         out_shape=out_shape,
-        compiler_params=params(),
+        compiler_params=params(far_bytes),
         cost_estimate=cost(
             4 * rows * columns * width, 4 * rows * width, heads * rows * columns
         ),
-    )(place, *operands)
+    )(bias, *operands)
 
 
 def mix_kernel(rows_0, rows_1, weight_0, weight_1, out):
@@ -413,42 +433,50 @@
     def after(array, *others):
         return lax.optimization_barrier((array, *others))[0]
 
-    def double(parts, bit):
-        return jnp.concatenate([parts, swap(parts, bit, "seq")], axis=0)
-
     def spread(kept, start, middle):
         if not few:
             return [[lax.all_gather(part, "seq", axis=0)] for part in kept]
-        (key_1, key_2, key_3), (value_1, value_2, value_3) = KEY_BITS, VALUE_BITS
-        k, v = start(double(kept[0][None], key_1), double(kept[1][None], value_1))
-        k, v = middle(double(k, key_2), double(v, value_2))
-        return [k, swap(k, key_3, "seq")], [v, swap(v, value_3, "seq")]
+        k, v = kept[0][None], kept[1][None]
+        for key_bit, value_bit, hook in zip(KEY_BITS, VALUE_BITS, (start, middle)):
+            came = hook(swap(k, key_bit, "seq"), swap(v, value_bit, "seq"))
+            k, v = jnp.concatenate([k, came[0]], axis=0), jnp.concatenate([v, came[1]], axis=0)
+        return [k, swap(k, KEY_BITS[-1], "seq")], [v, swap(v, VALUE_BITS[-1], "seq")]
 
     across = swap(normed, 2)
     beside = swap(normed, 1)
     mine, wk, wv, keys_0, values_0 = first(normed, w_key, w_value)
-    wq, keys_1, values_1, *kept = second(beside, wk, wv, keys_0, values_0, pattern, w_query)
-    query_a, wo = query(mine, beside, wq, w_out)
-    held = [across]
+    keys_1, values_1, *kept_a = second(beside, wk, wv, keys_0, values_0, pattern)
+    query_a, wq, wo = query_first(mine, beside, w_query, w_out)
+    bias = make_bias(place, slides, subs, seqs, few)
+    held = [across, query_a, bias]
 
     def before_across(k, v):
-        *held[:], k, v, _ = lax.optimization_barrier((*held, k, v, query_a))
+        *held[:], k, v = lax.optimization_barrier((*held, k, v))
         return k, v
 
-    half_a = (0, 1), *spread(kept, lambda k, v: (k, v), before_across)
-    across = held[0]
-    across_beside = swap(across, 1)
-    wo_beside = swap(after(w_out, across_beside), 1)
-    keys_2, values_2, *kept = third(across, across_beside, wk, wv, pattern)
+    def after_third(k, v):
+        across, query_a, bias = held
+        beyond = swap(across, 1)
+        keys_2, values_2, *kept_b = third(across, beyond, wk, wv, pattern)
+        kept_b[0], kept_b[1], k, v = lax.optimization_barrier((*kept_b, k, v))
+        held[:] = across, beyond, query_a, bias, keys_2, values_2, kept_b
+        return k, v
+
+    def same(k, v):
+        return k, v
+
+    if not few:
+        after_third(across, across)
+    half_a = 0, *spread(kept_a, before_across, after_third)
+    across, beyond, query_a, bias, keys_2, values_2, kept_b = held
+    wo_beside = swap(after(w_out, kept_b[0]), 1)
+    wo_beside = pltpu.with_memory_space_constraint(wo_beside, pltpu.VMEM)
+    query_b = query(across, beyond, wq)
+    half_b = 1, *spread(kept_b, same, same)
     near = [keys_0, keys_1, keys_2], [values_0, values_1, values_2]
-    call = functools.partial(attend, place, slides, subs, few)
-    (query_b,) = query(across, across_beside, wq)
-    begun = call((2, 3), query_b, [half_a], near=near, finish=False)
-    half_b = (2, 3), *spread(
-        kept,
-        lambda k, v: lax.optimization_barrier((k, v, query_b))[:2],
-        lambda k, v: lax.optimization_barrier((k, v, *begun))[:2],
-    )
+    call = functools.partial(attend, bias, few)
+    asked = after(query_b, half_b[1][0], half_b[2][0])
+    begun = call((2, 3), asked, [half_a], near=near, finish=False)
     keep_b, send_b = call((2, 3), query_b, [half_b], begun=begun)
     other_b = swap(send_b, 1)
     leaving = mix(keep_b, other_b, wo, wo_beside, BF16)

time: 73.6 us -> 60.3 us (0.82)
  waiting for transfers between devices: 24.6 us -> 16.1 us
  Pallas kernels: 24 us -> 19.3 us
  local copies, waits for them, and re-layouts: 3.24 us -> 0.01 us
  starting transfers between devices: 20.1 us -> 22.8 us
    ppermute x19, waiting for transfers between devices: 24.6 us -> 16.1 us  [swap(): return lax.ppermute(array, axis, [(i, i ^ bit) for i in range(count)])]
    unnamed x32 -> x4, local copies, waits for them, and re-layouts: 3.24 us -> 0.01 us
    pallas_call x2, Pallas kernels: 4.68 us -> 1.48 us  [mix(): pl.pallas_call(mix_kernel, in_specs=[IN_VMEM] * 4, out_specs=IN_VMEM, out...]
    ppermute x19, starting transfers between devices: 20.1 us -> 22.8 us  [swap(): return lax.ppermute(array, axis, [(i, i ^ bit) for i in range(count)])]
    pallas_call x6 -> x7, Pallas kernels: 14.8 us -> 13.3 us  [the longest x3 8.47 us: attend(): pl.pallas_call(functools.partial(attend_kernel, relative, near is not Non...]
  transfers between devices with their start and end apart: 19 -> 19, of which waited for: 11 -> 9; matrix products, arithmetic and copies ran while one was open for 0% -> 1% of each run, Pallas kernels for 29% -> 31%
where the time goes in v3:
time: 60.3 us; the launch traced here: 60.1 us
  starting transfers between devices  22.8 us (38%)
  Pallas kernels  19.3 us (32%)
  waiting for transfers between devices  16.1 us (27%)
  other arithmetic  1.72 us (3%)
    ppermute x19, starting transfers between devices, swap(): return lax.ppermute(array, axis, [(i, i ^ bit) for i in range(count)])  22.8 us
    ppermute x19, waiting for transfers between devices, swap(): return lax.ppermute(array, axis, [(i, i ^ bit) for i in range(count)])  16.1 us
    pallas_call x3, Pallas kernels, attend(): pl.pallas_call(functools.partial(attend_kernel, relative, near is not Non...  8.47 us
    pallas_call x1, Pallas kernels, first(): pl.pallas_call(first_kernel, in_specs=[IN_HBM] * 3, out_specs=[IN_VMEM] *...  3.14 us
    pallas_call x1, Pallas kernels, query_first(): pl.pallas_call(query_first_kernel, in_specs=[IN_VMEM] * 2 + [IN_HBM] * 2,...  2.63 us
    pallas_call x2, Pallas kernels, mix(): pl.pallas_call(mix_kernel, in_specs=[IN_VMEM] * 4, out_specs=IN_VMEM, out...  1.48 us
    pallas_call x1, Pallas kernels, third(): pl.pallas_call(third_kernel, in_specs=[IN_VMEM] * 5, out_specs=[IN_VMEM]...  1.42 us
  transfers between devices with their start and end apart: 19, of which 9 were waited for; matrix products, arithmetic and copies ran while one was open for 1% of the time, Pallas kernels for 31%

profile of v3, /device:TPU:0, one launch (start us, length us, event | category | flops | bytes accessed | tf_op | source)
XLA Modules:
  0.0 60.1 jit_solution(12000333889810786579)
XLA Ops:
  0.5 2.5 %collective-permute-start = (bf16[128,2048]{1,0:T(8,128)(2,1)}, bf16[128,2048]{1,0:T(8,128)(2,1)S(1)}, u32[]{:S(2)}, u32[]{:S(2)}) collective-permute-start(bf16[128,2048]{1,0:T(8,128)(2,1)} %rows_hbm.1), channel_id=1, source_target_pairs={{0,2},{1,3},{2,0},{3,1},{4,6},{5,7},{6,4},{7,5},{8,10},{9,11},{10,... | collective-permute-start | bytes 1572872 | tf_op jit(solution)/shard_map/ppermute | solution.py:431
  2.9 0.7 %pad_add_fusion.place = s32[10]{0:T(128)S(1)} fusion(s32[1]{0:T(128)} %bitcast.1, s32[1]{0:T(128)} %bitcast, s32[8]{0:T(128)} %param.13), kind=kLoop, calls=%fused_computation.9 | loop fusion | flops 20 | bytes 80 | tf_op jit(solution)/shard_map/concatenate | solution.py:420
  3.7 0.6 shard_map.75.bias
  4.3 3.1 %shard_map.73 = (bf16[128,2048]{1,0:T(8,128)(2,1)S(1)}, bf16[2048,512]{1,0:T(8,128)(2,1)S(1)}, bf16[2048,512]{1,0:T(8,128)(2,1)S(1)}, bf16[128,512]{1,0:T(8,128)(2,1)S(1)}, bf16[128,512]{1,0:T(8,128)(2,1)S(1)}) custom-call(bf16[128,2048]{1,0:T(8,128)(2,1)} %rows_hbm.1, bf16[2048,512]{1,0:T(8,128)(2,1)} %wk_hbm.1, bf16[2048,512]{1,0:T(8,128)(2,1)} %wv_hbm.1), custom_call_target="tpu_custom_call" | custom-call | flops 536870912 | bytes 4194304 | tf_op jit(solution)/shard_map/pallas_call | solution.py:96
  7.5 0.9 %shard_map.76 = (bf16[128,512]{1,0:T(8,128)(2,1)S(1)}, bf16[128,512]{1,0:T(8,128)(2,1)S(1)}, bf16[4,32,128]{2,1,0:T(8,128)(2,1)S(1)}, bf16[4,32,128]{2,1,0:T(8,128)(2,1)S(1)}) custom-call(bf16[128,2048]{1,0:T(8,128)(2,1)S(1)} %collective-permute-done.1.rows_1.rows, bf16[2048,512]{1,0:T(8,128)(2,1)S(1)} %get-tuple-element.41.wk, ...), custom_call_target="tpu_custom_call" | custom-call | flops 536870912 | bytes 524288 | tf_op jit(solution)/shard_map/pallas_call | solution.py:128
  8.4 1.5 %collective-permute-start.2 = (bf16[1,4,32,128]{3,2,1,0:T(8,128)(2,1)S(1)}, bf16[1,4,32,128]{3,2,1,0:T(8,128)(2,1)S(1)}, u32[]{:S(2)}, u32[]{:S(2)}) collective-permute-start(bf16[1,4,32,128]{3,2,1,0:T(8,128)(2,1)S(1)} %bitcast.12), channel_id=1, source_target_pairs={{0,4},{4,0},{8,12},{12,8},{16,20},{20,16},{24,28},{28,24},{1,5},{5... | collective-permute-start | bytes 98312 | tf_op jit(solution)/shard_map/ppermute | solution.py:431
  9.9 2.6 %collective-permute-start.3 = (bf16[1,4,32,128]{3,2,1,0:T(8,128)(2,1)S(1)}, bf16[1,4,32,128]{3,2,1,0:T(8,128)(2,1)S(1)}, u32[]{:S(2)}, u32[]{:S(2)}) collective-permute-start(bf16[1,4,32,128]{3,2,1,0:T(8,128)(2,1)S(1)} %bitcast.6), channel_id=1, source_target_pairs={{0,16},{4,20},{8,24},{12,28},{16,0},{20,4},{24,8},{28,12},{1,17},{... | collective-permute-start | bytes 98312 | tf_op jit(solution)/shard_map/ppermute | solution.py:431
  12.5 2.6 %shard_map.74 = (bf16[256,512]{1,0:T(8,128)(2,1)S(1)}, bf16[2048,512]{1,0:T(8,128)(2,1)S(1)}, bf16[512,2048]{1,0:T(8,128)(2,1)S(1)}) custom-call(bf16[128,2048]{1,0:T(8,128)(2,1)S(1)} %get-tuple-element.39.rows_0, bf16[128,2048]{1,0:T(8,128)(2,1)S(1)} %collective-permute-done.1.rows_1.rows, bf16[2048,512]{1,0:T(8,128)(2,1)} %wq_hbm.1, bf16[512,2048]{1,0:T(8,128)(2,1)} %w_hbm.1), custom_call_target="tpu_custom_call" | custom-call | flops 536870912 | bytes 4194304 | tf_op jit(solution)/shard_map/pallas_call | solution.py:157
  15.1 0.6 %collective-permute-done.rows_0 = bf16[128,2048]{1,0:T(8,128)(2,1)S(1)} collective-permute-done((bf16[128,2048]{1,0:T(8,128)(2,1)}, bf16[128,2048]{1,0:T(8,128)(2,1)S(1)}, u32[]{:S(2)}, u32[]{:S(2)}) %collective-permute-start) | collective-permute-done | bytes 524320 | tf_op jit(solution)/shard_map/ppermute | solution.py:431
  15.8 2.9 %collective-permute-start.5 = (bf16[2,4,32,128]{3,2,1,0:T(8,128)(2,1)S(1)}, bf16[2,4,32,128]{3,2,1,0:T(8,128)(2,1)S(1)}, u32[]{:S(2)}, u32[]{:S(2)}) collective-permute-start(bf16[2,4,32,128]{3,2,1,0:T(8,128)(2,1)S(1)} %pad_maximum_fusion.4), channel_id=1, source_target_pairs={{0,16},{4,20},{8,24},{12,28},{16,0},{20,4},{24,8},{28,12},{1,17},{... | collective-permute-start | bytes 196616 | tf_op jit(solution)/shard_map/ppermute | solution.py:431
  18.7 1.6 %collective-permute-start.6 = (bf16[2,4,32,128]{3,2,1,0:T(8,128)(2,1)S(1)}, bf16[2,4,32,128]{3,2,1,0:T(8,128)(2,1)S(1)}, u32[]{:S(2)}, u32[]{:S(2)}) collective-permute-start(bf16[2,4,32,128]{3,2,1,0:T(8,128)(2,1)S(1)} %pad_maximum_fusion.5), channel_id=1, source_target_pairs={{0,8},{4,12},{8,0},{12,4},{16,24},{20,28},{24,16},{28,20},{1,9},{5... | collective-permute-start | bytes 196616 | tf_op jit(solution)/shard_map/ppermute | solution.py:431
  20.3 1.4 %shard_map.78 = (bf16[256,512]{1,0:T(8,128)(2,1)S(1)}, bf16[256,512]{1,0:T(8,128)(2,1)S(1)}, bf16[4,32,128]{2,1,0:T(8,128)(2,1)S(1)}, bf16[4,32,128]{2,1,0:T(8,128)(2,1)S(1)}) custom-call(bf16[128,2048]{1,0:T(8,128)(2,1)S(1)} %collective-permute-done.rows_0, bf16[128,2048]{1,0:T(8,128)(2,1)S(1)} %collective-permute-done.4.rows_1, ...), custom_call_target="tpu_custom_call" | custom-call | flops 1073741824 | bytes 1048576 | tf_op jit(solution)/shard_map/pallas_call | solution.py:208
  21.8 1.0 %collective-permute-done.5 = bf16[2,4,32,128]{3,2,1,0:T(8,128)(2,1)S(1)} collective-permute-done((bf16[2,4,32,128]{3,2,1,0:T(8,128)(2,1)S(1)}, bf16[2,4,32,128]{3,2,1,0:T(8,128)(2,1)S(1)}, u32[]{:S(2)}, u32[]{:S(2)}) %collective-permute-start.5) | collective-permute-done | bytes 65568 | tf_op jit(solution)/shard_map/ppermute | solution.py:431
  23.2 1.6 %collective-permute-start.7 = (bf16[1,4,32,128]{3,2,1,0:T(8,128)(2,1)S(1)}, bf16[1,4,32,128]{3,2,1,0:T(8,128)(2,1)S(1)}, u32[]{:S(2)}, u32[]{:S(2)}) collective-permute-start(bf16[1,4,32,128]{3,2,1,0:T(8,128)(2,1)S(1)} %bitcast.15), channel_id=1, source_target_pairs={{0,4},{4,0},{8,12},{12,8},{16,20},{20,16},{24,28},{28,24},{1,5},{5... | collective-permute-start | bytes 98312 | tf_op jit(solution)/shard_map/ppermute | solution.py:431
  24.8 1.2 %collective-permute-start.9 = (bf16[1,4,32,128]{3,2,1,0:T(8,128)(2,1)S(1)}, bf16[1,4,32,128]{3,2,1,0:T(8,128)(2,1)S(1)}, u32[]{:S(2)}, u32[]{:S(2)}) collective-permute-start(bf16[1,4,32,128]{3,2,1,0:T(8,128)(2,1)S(1)} %bitcast.9), channel_id=1, source_target_pairs={{0,16},{4,20},{8,24},{12,28},{16,0},{20,4},{24,8},{28,12},{1,17},{... | collective-permute-start | bytes 98312 | tf_op jit(solution)/shard_map/ppermute | solution.py:431
  26.1 2.6 %collective-permute-start.11 = (bf16[4,4,32,128]{3,2,1,0:T(8,128)(2,1)S(1)}, bf16[4,4,32,128]{3,2,1,0:T(8,128)(2,1)S(1)}, u32[]{:S(2)}, u32[]{:S(2)}) collective-permute-start(bf16[4,4,32,128]{3,2,1,0:T(8,128)(2,1)S(1)} %pad_maximum_fusion.2.refs_7_), channel_id=1, source_target_pairs={{0,8},{4,12},{8,0},{12,4},{16,24},{20,28},{24,16},{28,20},{1,9},{5... | collective-permute-start | bytes 393224 | tf_op jit(solution)/shard_map/ppermute | solution.py:431
  28.6 0.6 collective-permute-start.12
  29.2 0.6 collective-permute-start.8
  30.0 1.4 %collective-permute-start.10 = (bf16[2,4,32,128]{3,2,1,0:T(8,128)(2,1)S(1)}, bf16[2,4,32,128]{3,2,1,0:T(8,128)(2,1)S(1)}, u32[]{:S(2)}, u32[]{:S(2)}) collective-permute-start(bf16[2,4,32,128]{3,2,1,0:T(8,128)(2,1)S(1)} %pad_maximum_fusion.7), channel_id=1, source_target_pairs={{0,8},{4,12},{8,0},{12,4},{16,24},{20,28},{24,16},{28,20},{1,9},{5... | collective-permute-start | bytes 196616 | tf_op jit(solution)/shard_map/ppermute | solution.py:431
  31.4 3.7 %collective-permute-done.8 = bf16[2,4,32,128]{3,2,1,0:T(8,128)(2,1)S(1)} collective-permute-done((bf16[2,4,32,128]{3,2,1,0:T(8,128)(2,1)S(1)}, bf16[2,4,32,128]{3,2,1,0:T(8,128)(2,1)S(1)}, u32[]{:S(2)}, u32[]{:S(2)}) %collective-permute-start.8) | collective-permute-done | bytes 65568 | tf_op jit(solution)/shard_map/ppermute | solution.py:431
  35.7 1.0 %collective-permute-start.14 = (bf16[4,4,32,128]{3,2,1,0:T(8,128)(2,1)S(1)}, bf16[4,4,32,128]{3,2,1,0:T(8,128)(2,1)S(1)}, u32[]{:S(2)}, u32[]{:S(2)}) collective-permute-start(bf16[4,4,32,128]{3,2,1,0:T(8,128)(2,1)S(1)} %pad_maximum_fusion.1.refs_5_.refs_13_), channel_id=1, source_target_pairs={{0,4},{4,0},{8,12},{12,8},{16,20},{20,16},{24,28},{28,24},{1,5},{5... | collective-permute-start | bytes 393224 | tf_op jit(solution)/shard_map/ppermute | solution.py:431
  36.7 0.7 %shard_map.77.refs_0_ = bf16[256,512]{1,0:T(8,128)(2,1)S(1)} custom-call(bf16[128,2048]{1,0:T(8,128)(2,1)S(1)} %collective-permute-done.rows_0, bf16[128,2048]{1,0:T(8,128)(2,1)S(1)} %collective-permute-done.4.rows_1, bf16[2048,512]{1,0:T(8,128)(2,1)S(1)} %get-tuple-element.50.wq), custom_call_target="tpu_custom_call" | custom-call | flops 536870912 | bytes 1048576 | tf_op jit(solution)/shard_map/pallas_call | solution.py:181
  37.5 3.0 %shard_map.79 = (f32[256,512]{1,0:T(8,128)S(1)}, f32[4,256,128]{2,1,0:T(8,128)S(1)}) custom-call(f32[4,1024]{1,0:T(4,128)S(1)} %shard_map.75.bias, bf16[256,512]{1,0:T(8,128)(2,1)S(1)} %shard_map.77.refs_0_, bf16[128,512]{1,0:T(8,128)(2,1)S(1)} %get-tuple-element.43.keys_0.refs_1_, bf16[128,512]{1,0:T(8,128)(2,1)S(1)} %get-tuple-element.58.refs_2_, ...), custom_call_target="tpu_custom_call" | custom-call | flops 402653184 | bytes 524288 | tf_op jit(solution)/shard_map/pallas_call | solution.py:383
  40.7 2.3 %shard_map.80 = (bf16[128,512]{1,0:T(8,128)(2,1)S(1)}, bf16[128,512]{1,0:T(8,128)(2,1)S(1)}) custom-call(f32[4,1024]{1,0:T(4,128)S(1)} %shard_map.75.bias, bf16[256,512]{1,0:T(8,128)(2,1)S(1)} %shard_map.77.refs_0_, f32[256,512]{1,0:T(8,128)S(1)} %get-tuple-element.64.refs_1_, f32[4,256,128]{2,1,0:T(8,128)S(1)} %get-tuple-element.65.refs_2_, ...), custom_call_target="tpu_custom_call" | custom-call | flops 134217728 | bytes 524288 | tf_op jit(solution)/shard_map/pallas_call | solution.py:383
  43.1 1.3 %collective-permute-done.15.rows_1 = bf16[128,512]{1,0:T(8,128)(2,1)S(1)} collective-permute-done((bf16[128,512]{1,0:T(8,128)(2,1)S(1)}, bf16[128,512]{1,0:T(8,128)(2,1)S(1)}, u32[]{:S(2)}, u32[]{:S(2)}) %collective-permute-start.15) | collective-permute-done | bytes 131104 | tf_op jit(solution)/shard_map/ppermute | solution.py:431
  44.4 0.7 %shard_map.81 = bf16[128,2048]{1,0:T(8,128)(2,1)S(1)} custom-call(bf16[128,512]{1,0:T(8,128)(2,1)S(1)} %get-tuple-element.66.rows_0, bf16[128,512]{1,0:T(8,128)(2,1)S(1)} %collective-permute-done.15.rows_1, bf16[512,2048]{1,0:T(8,128)(2,1)S(1)} %get-tuple-element.68.weight_0, bf16[512,2048]{1,0:T(8,128)(2,1)S(1)} %collective-permute-done.16.weight_1), custom_call_target="tpu_custom_call" | custom-call | flops 536870912 | bytes 1048576 | tf_op jit(solution)/shard_map/pallas_call | solution.py:408
  45.2 1.6 %collective-permute-start.18 = (bf16[128,2048]{1,0:T(8,128)(2,1)S(1)}, bf16[128,2048]{1,0:T(8,128)(2,1)S(1)}, u32[]{:S(2)}, u32[]{:S(2)}) collective-permute-start(bf16[128,2048]{1,0:T(8,128)(2,1)S(1)} %shard_map.81), channel_id=1, source_target_pairs={{0,2},{1,3},{2,0},{3,1},{4,6},{5,7},{6,4},{7,5},{8,10},{9,11},{10,... | collective-permute-start | bytes 1572872 | tf_op jit(solution)/shard_map/ppermute | solution.py:431
  46.7 3.2 %shard_map.82 = (bf16[128,512]{1,0:T(8,128)(2,1)S(1)}, bf16[128,512]{1,0:T(8,128)(2,1)S(1)}) custom-call(f32[4,1024]{1,0:T(4,128)S(1)} %shard_map.75.bias, bf16[256,512]{1,0:T(8,128)(2,1)S(1)} %get-tuple-element.70.refs_0_, bf16[128,512]{1,0:T(8,128)(2,1)S(1)} %get-tuple-element.43.keys_0.refs_1_, bf16[128,512]{1,0:T(8,128)(2,1)S(1)} %get-tuple-element.58.refs_2_, ...), custom_call_target="tpu_custom_call" | custom-call | flops 536870912 | bytes 524288 | tf_op jit(solution)/shard_map/pallas_call | solution.py:383
  50.1 1.3 %collective-permute-done.17.rows_1 = bf16[128,512]{1,0:T(8,128)(2,1)S(1)} collective-permute-done((bf16[128,512]{1,0:T(8,128)(2,1)S(1)}, bf16[128,512]{1,0:T(8,128)(2,1)S(1)}, u32[]{:S(2)}, u32[]{:S(2)}) %collective-permute-start.17) | collective-permute-done | bytes 131104 | tf_op jit(solution)/shard_map/ppermute | solution.py:431
  51.4 0.7 %shard_map.83 = f32[128,2048]{1,0:T(8,128)S(1)} custom-call(bf16[128,512]{1,0:T(8,128)(2,1)S(1)} %get-tuple-element.71.rows_0, bf16[128,512]{1,0:T(8,128)(2,1)S(1)} %collective-permute-done.17.rows_1, bf16[512,2048]{1,0:T(8,128)(2,1)S(1)} %get-tuple-element.68.weight_0, bf16[512,2048]{1,0:T(8,128)(2,1)S(1)} %collective-permute-done.16.weight_1), custom_call_target="tpu_custom_call" | custom-call | flops 536870912 | bytes 1048576 | tf_op jit(solution)/shard_map/pallas_call | solution.py:408
  52.1 7.1 %collective-permute-done.18 = bf16[128,2048]{1,0:T(8,128)(2,1)S(1)} collective-permute-done((bf16[128,2048]{1,0:T(8,128)(2,1)S(1)}, bf16[128,2048]{1,0:T(8,128)(2,1)S(1)}, u32[]{:S(2)}, u32[]{:S(2)}) %collective-permute-start.18) | collective-permute-done | bytes 524320 | tf_op jit(solution)/shard_map/ppermute | solution.py:431
  59.2 0.9 %add_convert_fusion = bf16[128,2048]{1,0:T(8,128)(2,1)} fusion(f32[128,2048]{1,0:T(8,128)S(1)} %shard_map.83, bf16[128,2048]{1,0:T(8,128)(2,1)S(1)} %collective-permute-done.18), kind=kLoop, calls=%fused_computation | loop fusion | flops 786432 | bytes 2097152 | tf_op jit(solution)/shard_map/convert_element_type | solution.py:488
  (31 shorter events, 2.3 us)
Async XLA Ops:
  0.0 7.4 %collective-permute-start.1 = (bf16[128,2048]{1,0:T(8,128)(2,1)}, bf16[128,2048]{1,0:T(8,128)(2,1)S(1)}, u32[]{:S(2)}, u32[]{:S(2)}) collective-permute-start(bf16[128,2048]{1,0:T(8,128)(2,1)} %rows_hbm.1), channel_id=1, source_target_pairs={{0,1},{1,0},{2,3},{3,2},{4,5},{5,4},{6,7},{7,6},{8,9},{9,8},{10,11... | collective-permute-start | bytes 1572872 | tf_op jit(solution)/shard_map/ppermute | solution.py:431
  0.5 15.3 %collective-permute-start = (bf16[128,2048]{1,0:T(8,128)(2,1)}, bf16[128,2048]{1,0:T(8,128)(2,1)S(1)}, u32[]{:S(2)}, u32[]{:S(2)}) collective-permute-start(bf16[128,2048]{1,0:T(8,128)(2,1)} %rows_hbm.1), channel_id=1, source_target_pairs={{0,2},{1,3},{2,0},{3,1},{4,6},{5,7},{6,4},{7,5},{8,10},{9,11},{10,... | collective-permute-start | bytes 1572872 | tf_op jit(solution)/shard_map/ppermute | solution.py:431
  4.3 3.2 %copy-start = (s32[4,128]{1,0:T(4,128)S(1)}, s32[4,128]{1,0:T(4,128)}, u32[]{:S(2)}) copy-start(s32[4,128]{1,0:T(4,128)} %pattern.3) | copy-start | bytes 6148
  8.4 7.4 %collective-permute-start.2 = (bf16[1,4,32,128]{3,2,1,0:T(8,128)(2,1)S(1)}, bf16[1,4,32,128]{3,2,1,0:T(8,128)(2,1)S(1)}, u32[]{:S(2)}, u32[]{:S(2)}) collective-permute-start(bf16[1,4,32,128]{3,2,1,0:T(8,128)(2,1)S(1)} %bitcast.12), channel_id=1, source_target_pairs={{0,4},{4,0},{8,12},{12,8},{16,20},{20,16},{24,28},{28,24},{1,5},{5... | collective-permute-start | bytes 98312 | tf_op jit(solution)/shard_map/ppermute | solution.py:431
  9.9 5.9 %collective-permute-start.3 = (bf16[1,4,32,128]{3,2,1,0:T(8,128)(2,1)S(1)}, bf16[1,4,32,128]{3,2,1,0:T(8,128)(2,1)S(1)}, u32[]{:S(2)}, u32[]{:S(2)}) collective-permute-start(bf16[1,4,32,128]{3,2,1,0:T(8,128)(2,1)S(1)} %bitcast.6), channel_id=1, source_target_pairs={{0,16},{4,20},{8,24},{12,28},{16,0},{20,4},{24,8},{28,12},{1,17},{... | collective-permute-start | bytes 98312 | tf_op jit(solution)/shard_map/ppermute | solution.py:431
  15.8 4.6 %collective-permute-start.4 = (bf16[128,2048]{1,0:T(8,128)(2,1)S(1)}, bf16[128,2048]{1,0:T(8,128)(2,1)S(1)}, u32[]{:S(2)}, u32[]{:S(2)}) collective-permute-start(bf16[128,2048]{1,0:T(8,128)(2,1)S(1)} %collective-permute-done.rows_0), channel_id=1, source_target_pairs={{0,1},{1,0},{2,3},{3,2},{4,5},{5,4},{6,7},{7,6},{8,9},{9,8},{10,11... | collective-permute-start | bytes 1572872 | tf_op jit(solution)/shard_map/ppermute | solution.py:431
  15.8 6.9 %collective-permute-start.5 = (bf16[2,4,32,128]{3,2,1,0:T(8,128)(2,1)S(1)}, bf16[2,4,32,128]{3,2,1,0:T(8,128)(2,1)S(1)}, u32[]{:S(2)}, u32[]{:S(2)}) collective-permute-start(bf16[2,4,32,128]{3,2,1,0:T(8,128)(2,1)S(1)} %pad_maximum_fusion.4), channel_id=1, source_target_pairs={{0,16},{4,20},{8,24},{12,28},{16,0},{20,4},{24,8},{28,12},{1,17},{... | collective-permute-start | bytes 196616 | tf_op jit(solution)/shard_map/ppermute | solution.py:431
  18.7 4.5 %copy-start.1 = (bf16[512,2048]{1,0:T(8,128)(2,1)S(1)}, bf16[512,2048]{1,0:T(8,128)(2,1)}, u32[]{:S(2)}) copy-start(bf16[512,2048]{1,0:T(8,128)(2,1)} %w_hbm.1) | copy-start | bytes 6291460
  18.7 4.5 %collective-permute-start.6 = (bf16[2,4,32,128]{3,2,1,0:T(8,128)(2,1)S(1)}, bf16[2,4,32,128]{3,2,1,0:T(8,128)(2,1)S(1)}, u32[]{:S(2)}, u32[]{:S(2)}) collective-permute-start(bf16[2,4,32,128]{3,2,1,0:T(8,128)(2,1)S(1)} %pad_maximum_fusion.5), channel_id=1, source_target_pairs={{0,8},{4,12},{8,0},{12,4},{16,24},{20,28},{24,16},{28,20},{1,9},{5... | collective-permute-start | bytes 196616 | tf_op jit(solution)/shard_map/ppermute | solution.py:431
  23.2 21.2 %collective-permute-start.16 = (bf16[512,2048]{1,0:T(8,128)(2,1)S(1)}, bf16[512,2048]{1,0:T(8,128)(2,1)S(1)}, u32[]{:S(2)}, u32[]{:S(2)}) collective-permute-start(bf16[512,2048]{1,0:T(8,128)(2,1)S(1)} %copy-done.1), channel_id=1, source_target_pairs={{0,1},{1,0},{2,3},{3,2},{4,5},{5,4},{6,7},{7,6},{8,9},{9,8},{10,11... | collective-permute-start | bytes 6291464 | tf_op jit(solution)/shard_map/ppermute | solution.py:431
  23.2 6.0 %collective-permute-start.7 = (bf16[1,4,32,128]{3,2,1,0:T(8,128)(2,1)S(1)}, bf16[1,4,32,128]{3,2,1,0:T(8,128)(2,1)S(1)}, u32[]{:S(2)}, u32[]{:S(2)}) collective-permute-start(bf16[1,4,32,128]{3,2,1,0:T(8,128)(2,1)S(1)} %bitcast.15), channel_id=1, source_target_pairs={{0,4},{4,0},{8,12},{12,8},{16,20},{20,16},{24,28},{28,24},{1,5},{5... | collective-permute-start | bytes 98312 | tf_op jit(solution)/shard_map/ppermute | solution.py:431
  24.8 5.2 %collective-permute-start.9 = (bf16[1,4,32,128]{3,2,1,0:T(8,128)(2,1)S(1)}, bf16[1,4,32,128]{3,2,1,0:T(8,128)(2,1)S(1)}, u32[]{:S(2)}, u32[]{:S(2)}) collective-permute-start(bf16[1,4,32,128]{3,2,1,0:T(8,128)(2,1)S(1)} %bitcast.9), channel_id=1, source_target_pairs={{0,16},{4,20},{8,24},{12,28},{16,0},{20,4},{24,8},{28,12},{1,17},{... | collective-permute-start | bytes 98312 | tf_op jit(solution)/shard_map/ppermute | solution.py:431
  26.1 11.4 %collective-permute-start.11 = (bf16[4,4,32,128]{3,2,1,0:T(8,128)(2,1)S(1)}, bf16[4,4,32,128]{3,2,1,0:T(8,128)(2,1)S(1)}, u32[]{:S(2)}, u32[]{:S(2)}) collective-permute-start(bf16[4,4,32,128]{3,2,1,0:T(8,128)(2,1)S(1)} %pad_maximum_fusion.2.refs_7_), channel_id=1, source_target_pairs={{0,8},{4,12},{8,0},{12,4},{16,24},{20,28},{24,16},{28,20},{1,9},{5... | collective-permute-start | bytes 393224 | tf_op jit(solution)/shard_map/ppermute | solution.py:431
  28.6 8.8 %collective-permute-start.12 = (bf16[4,4,32,128]{3,2,1,0:T(8,128)(2,1)S(1)}, bf16[4,4,32,128]{3,2,1,0:T(8,128)(2,1)S(1)}, u32[]{:S(2)}, u32[]{:S(2)}) collective-permute-start(bf16[4,4,32,128]{3,2,1,0:T(8,128)(2,1)S(1)} %pad_maximum_fusion.3.refs_9_), channel_id=1, source_target_pairs={{0,4},{4,0},{8,12},{12,8},{16,20},{20,16},{24,28},{28,24},{1,5},{5... | collective-permute-start | bytes 393224 | tf_op jit(solution)/shard_map/ppermute | solution.py:431
  29.2 5.9 %collective-permute-start.8 = (bf16[2,4,32,128]{3,2,1,0:T(8,128)(2,1)S(1)}, bf16[2,4,32,128]{3,2,1,0:T(8,128)(2,1)S(1)}, u32[]{:S(2)}, u32[]{:S(2)}) collective-permute-start(bf16[2,4,32,128]{3,2,1,0:T(8,128)(2,1)S(1)} %pad_maximum_fusion.6), channel_id=1, source_target_pairs={{0,16},{4,20},{8,24},{12,28},{16,0},{20,4},{24,8},{28,12},{1,17},{... | collective-permute-start | bytes 196616 | tf_op jit(solution)/shard_map/ppermute | solution.py:431
  30.0 5.7 %collective-permute-start.10 = (bf16[2,4,32,128]{3,2,1,0:T(8,128)(2,1)S(1)}, bf16[2,4,32,128]{3,2,1,0:T(8,128)(2,1)S(1)}, u32[]{:S(2)}, u32[]{:S(2)}) collective-permute-start(bf16[2,4,32,128]{3,2,1,0:T(8,128)(2,1)S(1)} %pad_maximum_fusion.7), channel_id=1, source_target_pairs={{0,8},{4,12},{8,0},{12,4},{16,24},{20,28},{24,16},{28,20},{1,9},{5... | collective-permute-start | bytes 196616 | tf_op jit(solution)/shard_map/ppermute | solution.py:431
  35.1 5.3 %collective-permute-start.13 = (bf16[4,4,32,128]{3,2,1,0:T(8,128)(2,1)S(1)}, bf16[4,4,32,128]{3,2,1,0:T(8,128)(2,1)S(1)}, u32[]{:S(2)}, u32[]{:S(2)}) collective-permute-start(bf16[4,4,32,128]{3,2,1,0:T(8,128)(2,1)S(1)} %pad_maximum_fusion.refs_3_.refs_11_), channel_id=1, source_target_pairs={{0,8},{4,12},{8,0},{12,4},{16,24},{20,28},{24,16},{28,20},{1,9},{5... | collective-permute-start | bytes 393224 | tf_op jit(solution)/shard_map/ppermute | solution.py:431
  35.7 5.0 %collective-permute-start.14 = (bf16[4,4,32,128]{3,2,1,0:T(8,128)(2,1)S(1)}, bf16[4,4,32,128]{3,2,1,0:T(8,128)(2,1)S(1)}, u32[]{:S(2)}, u32[]{:S(2)}) collective-permute-start(bf16[4,4,32,128]{3,2,1,0:T(8,128)(2,1)S(1)} %pad_maximum_fusion.1.refs_5_.refs_13_), channel_id=1, source_target_pairs={{0,4},{4,0},{8,12},{12,8},{16,20},{20,16},{24,28},{28,24},{1,5},{5... | collective-permute-start | bytes 393224 | tf_op jit(solution)/shard_map/ppermute | solution.py:431
  43.0 1.4 %collective-permute-start.15 = (bf16[128,512]{1,0:T(8,128)(2,1)S(1)}, bf16[128,512]{1,0:T(8,128)(2,1)S(1)}, u32[]{:S(2)}, u32[]{:S(2)}) collective-permute-start(bf16[128,512]{1,0:T(8,128)(2,1)S(1)} %get-tuple-element.67), channel_id=1, source_target_pairs={{0,1},{1,0},{2,3},{3,2},{4,5},{5,4},{6,7},{7,6},{8,9},{9,8},{10,11... | collective-permute-start | bytes 393224 | tf_op jit(solution)/shard_map/ppermute | solution.py:431
  45.2 14.0 %collective-permute-start.18 = (bf16[128,2048]{1,0:T(8,128)(2,1)S(1)}, bf16[128,2048]{1,0:T(8,128)(2,1)S(1)}, u32[]{:S(2)}, u32[]{:S(2)}) collective-permute-start(bf16[128,2048]{1,0:T(8,128)(2,1)S(1)} %shard_map.81), channel_id=1, source_target_pairs={{0,2},{1,3},{2,0},{3,1},{4,6},{5,7},{6,4},{7,5},{8,10},{9,11},{10,... | collective-permute-start | bytes 1572872 | tf_op jit(solution)/shard_map/ppermute | solution.py:431
  50.0 1.4 %collective-permute-start.17 = (bf16[128,512]{1,0:T(8,128)(2,1)S(1)}, bf16[128,512]{1,0:T(8,128)(2,1)S(1)}, u32[]{:S(2)}, u32[]{:S(2)}) collective-permute-start(bf16[128,512]{1,0:T(8,128)(2,1)S(1)} %get-tuple-element.72), channel_id=1, source_target_pairs={{0,1},{1,0},{2,3},{3,2},{4,5},{5,4},{6,7},{7,6},{8,9},{9,8},{10,11... | collective-permute-start | bytes 393224 | tf_op jit(solution)/shard_map/ppermute | solution.py:431

commit v4 on v3

--- a/solution.py
+++ b/solution.py
@@ -21,8 +21,9 @@
 IN_VMEM = pl.BlockSpec(memory_space=pltpu.VMEM)
 IN_HBM = pl.BlockSpec(memory_space=pltpu.HBM)
 IN_SMEM = pl.BlockSpec(memory_space=pltpu.SMEM)
-KEY_BITS = (1, 4, 2)
-VALUE_BITS = (4, 2, 1)
+BOTH_BITS = (4, 2, 1)
+KEY_BITS = (4, 1, 2)
+VALUE_BITS = (2, 4, 1)
 
 
 def dot(a, b):
@@ -56,16 +57,17 @@
     return [slice(i * tile, (i + 1) * tile) for i in range(width // tile)]
 
 
-def pick_dilated(pattern, blocks, kept_keys, kept_values):
+def pick_dilated(pattern, blocks, kept):
+    (keys, key_slot), (values, value_slot) = kept
     positions = lax.broadcasted_iota(jnp.int32, (BLOCK, BLOCK), 0)
-    for head in range(kept_keys.shape[0]):
+    for head in range(keys.shape[1]):
         row = pattern[head : head + 1, :]
         chosen = (positions == row).astype(F32).T[:DILATED_KEPT].astype(BF16)
         for index, block in enumerate(blocks):
             picked = dot(chosen, jnp.concatenate(block(head), axis=1)).astype(BF16)
             spot = slice(index * DILATED_KEPT, (index + 1) * DILATED_KEPT)
-            kept_keys[head, spot, :] = picked[:, :HEAD_SIZE]
-            kept_values[head, spot, :] = picked[:, HEAD_SIZE:]
+            keys[key_slot, head, spot, :] = picked[:, :HEAD_SIZE]
+            values[value_slot, head, spot, :] = picked[:, HEAD_SIZE:]
 
 
 def head_of(ref, head, rows=slice(None)):
@@ -110,7 +112,7 @@
     )(keep_in_hbm(rows), keep_in_hbm(w_key), keep_in_hbm(w_value))
 
 
-def second_kernel(rows, wk, wv, keys_0, values_0, pattern, keys, values, kept_k, kept_v):
+def second_kernel(rows, wk, wv, keys_0, values_0, pattern, keys, values, kept):
     for part in halves_of(wk.shape[1]):
         keys[:, part] = dot(rows[...], wk[:, part]).astype(BF16)
         values[:, part] = dot(rows[...], wv[:, part]).astype(BF16)
@@ -118,18 +120,18 @@
         lambda head: (head_of(keys_0, head), head_of(values_0, head)),
         lambda head: (head_of(keys, head), head_of(values, head)),
     ]
-    pick_dilated(pattern, blocks, kept_k, kept_v)
+    pick_dilated(pattern, blocks, ((kept, 0), (kept, 1)))
 
 
 def second(rows, wk, wv, keys_0, values_0, pattern):
     count, depth = rows.shape
     width = wk.shape[1]
-    kept = (width // HEAD_SIZE, FAR_ROWS, HEAD_SIZE)
+    kept = (2, width // HEAD_SIZE, FAR_ROWS, HEAD_SIZE)
     return pl.pallas_call(
         second_kernel,
         in_specs=[IN_VMEM] * 6,
-        out_specs=[IN_VMEM] * 4,
-        out_shape=[shape((count, width))] * 2 + [shape(kept)] * 2,
+        out_specs=[IN_VMEM] * 3,
+        out_shape=[shape((count, width))] * 2 + [shape(kept)],
         compiler_params=params(),
         cost_estimate=cost(4 * count * depth * width, 2 * count * depth),
     )(rows, wk, wv, keys_0, values_0, pattern)
@@ -198,13 +200,13 @@
         return lambda head: (head_of(keys, head, where), head_of(values, head, where))
 
     blocks = [block(slice(i * BLOCK, (i + 1) * BLOCK)) for i in range(BLOCKS_HALF)]
-    pick_dilated(pattern, blocks, kept_k, kept_v)
+    pick_dilated(pattern, blocks, ((kept_k, 0), (kept_v, 0)))
 
 
 def third(rows_0, rows_1, wk, wv, pattern):
     count, depth = rows_0.shape
     width = wk.shape[1]
-    kept = (width // HEAD_SIZE, FAR_ROWS, HEAD_SIZE)
+    kept = (1, width // HEAD_SIZE, FAR_ROWS, HEAD_SIZE)
     return pl.pallas_call(
         third_kernel,
         in_specs=[IN_VMEM] * 5,
@@ -277,22 +279,16 @@
     return higher, total, gathered * shrink + dot(weight.astype(BF16), values)
 
 
-def far_group(keys, values, head):
+def far_group(parts, head):
     found = []
-    for refs, bits in ((keys, KEY_BITS), (values, VALUE_BITS)):
+    for refs, slot, bits in parts:
         order = [0]
         for bit in bits:
             order += [place ^ bit for place in order]
         half = len(order) // 2
-        found.append(
-            jnp.concatenate(
-                [
-                    refs[order.index(i) // half][order.index(i) % half, head]
-                    for i in range(len(order))
-                ],
-                axis=0,
-            )
-        )
+        spots = [order.index(i) for i in range(len(order))]
+        pieces = [refs[spot // half][spot % half, slot, head] for spot in spots]
+        found.append(jnp.concatenate(pieces, axis=0))
     return found
 
 
@@ -308,8 +304,12 @@
     far = []
     for half in halves:
         size = 2 if few else 1
-        far.append((half, refs[:size], refs[size : 2 * size]))
-        del refs[: 2 * size]
+        if half == 0:
+            parts = [(refs[:size], slot, BOTH_BITS) for slot in range(2)]
+        else:
+            parts = [(refs[:size], 0, KEY_BITS), (refs[size : 2 * size], 0, VALUE_BITS)]
+        del refs[: size * (half + 1)]
+        far.append((half, parts))
     span = bias.shape[0] * BLOCK
     half_count = (bias.shape[1] - span) * BLOCKS_HALF // bias.shape[0]
 
@@ -329,25 +329,25 @@
             state = peak, total, dot(weight.astype(BF16), near_values)
         else:
             state = stats_in[head, :, 0:1], stats_in[head, :, 1:2], gathered_in[:, columns]
-        for half, far_keys, far_values in far:
+        for half, parts in far:
             start = span + half * half_count
             if few:
-                group = far_group(far_keys, far_values, head)
+                group = far_group(parts, head)
                 rows = rows_of_bias(slice(start, start + half_count))
                 state = far_update(asked, *group, rows, state)
                 continue
 
-            def step(number, state, start=start, k=far_keys[0], v=far_values[0]):
+            def step(number, state, start=start, parts=parts):
                 base = number * GROUP
                 group = [
-                    jnp.concatenate([ref[base + i, head] for i in range(GROUP)], axis=0)
-                    for ref in (k, v)
+                    jnp.concatenate([refs[0][base + i, slot, head] for i in range(GROUP)], axis=0)
+                    for refs, slot, _ in parts
                 ]
                 width = GROUP * FAR_ROWS
                 rows = rows_of_bias(pl.ds(pl.multiple_of(start + number * width, width), width))
                 return far_update(asked, *group, rows, state)
 
-            state = lax.fori_loop(0, far_keys[0].shape[0] // GROUP, step, state)
+            state = lax.fori_loop(0, parts[0][0][0].shape[0] // GROUP, step, state)
         peak, total, gathered = state
         if finish:
             keep, send = refs
@@ -371,9 +371,9 @@
     operands += [*near[0], *near[1]] if near else list(begun)
     columns = bias.shape[0] * BLOCK if near else 0
     spans = 0
-    for _, keys, values in halves:
-        operands += [*keys, *values]
-        spans += sum(part.shape[0] for part in keys)
+    for _, *parts in halves:
+        operands += sum(parts, [])
+        spans += sum(part.shape[0] for part in parts[0])
     columns += spans * FAR_ROWS
     if finish:
         out_shape = [shape((BLOCK, width))] * 2
@@ -417,13 +417,7 @@
 
 def shards(seqs, subs, normed, w_query, w_key, w_value, w_out, pattern, slide_lengths):
     slides = slide_lengths.shape[0]
-    place = jnp.concatenate(
-        [
-            slide_lengths,
-            lax.axis_index("seq").astype(jnp.int32)[None],
-            lax.axis_index("sub").astype(jnp.int32)[None],
-        ]
-    )
+    axes = [lax.axis_index(name).astype(jnp.int32)[None] for name in ("seq", "sub")]
     few = seqs == GROUP
 
     def swap(array, bit, axis="sub"):
@@ -433,46 +427,39 @@
     def after(array, *others):
         return lax.optimization_barrier((array, *others))[0]
 
-    def spread(kept, start, middle):
-        if not few:
-            return [[lax.all_gather(part, "seq", axis=0)] for part in kept]
-        k, v = kept[0][None], kept[1][None]
-        for key_bit, value_bit, hook in zip(KEY_BITS, VALUE_BITS, (start, middle)):
-            came = hook(swap(k, key_bit, "seq"), swap(v, value_bit, "seq"))
-            k, v = jnp.concatenate([k, came[0]], axis=0), jnp.concatenate([v, came[1]], axis=0)
-        return [k, swap(k, KEY_BITS[-1], "seq")], [v, swap(v, VALUE_BITS[-1], "seq")]
+    def double(parts, bit, hook=lambda came: came):
+        return jnp.concatenate([parts, hook(swap(parts, bit, "seq"))], axis=0)
 
     across = swap(normed, 2)
     beside = swap(normed, 1)
     mine, wk, wv, keys_0, values_0 = first(normed, w_key, w_value)
-    keys_1, values_1, *kept_a = second(beside, wk, wv, keys_0, values_0, pattern)
+    keys_1, values_1, kept_a = second(beside, wk, wv, keys_0, values_0, pattern)
+    place = jnp.concatenate([after(slide_lengths, kept_a), *axes])
+    bias = make_bias(place, slides, subs, seqs, few)
+    if few:
+        kept_a = double(kept_a[None], BOTH_BITS[0], lambda came: after(came, bias))
+        mine = after(mine, kept_a)
     query_a, wq, wo = query_first(mine, beside, w_query, w_out)
-    bias = make_bias(place, slides, subs, seqs, few)
-    held = [across, query_a, bias]
-
-    def before_across(k, v):
-        *held[:], k, v = lax.optimization_barrier((*held, k, v))
-        return k, v
-
-    def after_third(k, v):
-        across, query_a, bias = held
-        beyond = swap(across, 1)
-        keys_2, values_2, *kept_b = third(across, beyond, wk, wv, pattern)
-        kept_b[0], kept_b[1], k, v = lax.optimization_barrier((*kept_b, k, v))
-        held[:] = across, beyond, query_a, bias, keys_2, values_2, kept_b
-        return k, v
-
-    def same(k, v):
-        return k, v
-
-    if not few:
-        after_third(across, across)
-    half_a = 0, *spread(kept_a, before_across, after_third)
-    across, beyond, query_a, bias, keys_2, values_2, kept_b = held
+    if few:
+        came = swap(kept_a, BOTH_BITS[1], "seq")
+        across, came, query_a = lax.optimization_barrier((across, came, query_a))
+        kept_a = jnp.concatenate([kept_a, came], axis=0)
+        half_a = 0, [kept_a, swap(kept_a, BOTH_BITS[2], "seq")]
+    else:
+        half_a = 0, [lax.all_gather(kept_a, "seq", axis=0)]
+    beyond = swap(across, 1)
+    keys_2, values_2, *kept_b = third(across, beyond, wk, wv, pattern)
     wo_beside = swap(after(w_out, kept_b[0]), 1)
     wo_beside = pltpu.with_memory_space_constraint(wo_beside, pltpu.VMEM)
     query_b = query(across, beyond, wq)
-    half_b = 1, *spread(kept_b, same, same)
+    if few:
+        k, v = double(kept_b[0][None], KEY_BITS[0]), double(kept_b[1][None], VALUE_BITS[0])
+        came = swap(k, KEY_BITS[1], "seq"), swap(v, VALUE_BITS[1], "seq")
+        *came, query_b, half_a[1][1] = lax.optimization_barrier((*came, query_b, half_a[1][1]))
+        k, v = jnp.concatenate([k, came[0]], axis=0), jnp.concatenate([v, came[1]], axis=0)
+        half_b = 1, [k, swap(k, KEY_BITS[2], "seq")], [v, swap(v, VALUE_BITS[2], "seq")]
+    else:
+        half_b = 1, *[[lax.all_gather(part, "seq", axis=0)] for part in kept_b]
     near = [keys_0, keys_1, keys_2], [values_0, values_1, values_2]
     call = functools.partial(attend, bias, few)
     asked = after(query_b, half_b[1][0], half_b[2][0])

time: 60.3 us -> 60.3 us (level)
  waiting for transfers between devices: 16.1 us -> 23 us
  starting transfers between devices: 22.8 us -> 16.3 us
  other arithmetic: 1.72 us -> 1.06 us
    ppermute x19 -> x16, waiting for transfers between devices: 16.1 us -> 23 us  [swap(): return lax.ppermute(array, axis, [(i, i ^ bit) for i in range(count)])]
    ppermute x19 -> x16, starting transfers between devices: 22.8 us -> 16.3 us  [swap(): return lax.ppermute(array, axis, [(i, i ^ bit) for i in range(count)])]
    concatenate x9 -> x7, other arithmetic: 0.82 us -> 0.16 us  [the longest x1 0.08 us: shards(): place = jnp.concatenate([after(slide_lengths, kept_a), *axes])]
  transfers between devices with their start and end apart: 19 -> 16, of which waited for: 9 -> 11; matrix products, arithmetic and copies ran while one was open for 1% -> 0% of each run, Pallas kernels for 31% -> 29%
where the time goes in v4:
time: 60.3 us; the launch traced here: 59.8 us
  waiting for transfers between devices  23 us (38%)
  Pallas kernels  19.3 us (32%)
  starting transfers between devices  16.3 us (27%)
  other arithmetic  1.06 us (2%)
    ppermute x16, waiting for transfers between devices, swap(): return lax.ppermute(array, axis, [(i, i ^ bit) for i in range(count)])  23 us
    ppermute x16, starting transfers between devices, swap(): return lax.ppermute(array, axis, [(i, i ^ bit) for i in range(count)])  16.3 us
    pallas_call x3, Pallas kernels, attend(): pl.pallas_call(functools.partial(attend_kernel, relative, near is not Non...  8.46 us
    pallas_call x1, Pallas kernels, first(): pl.pallas_call(first_kernel, in_specs=[IN_HBM] * 3, out_specs=[IN_VMEM] *...  3.12 us
    pallas_call x1, Pallas kernels, query_first(): pl.pallas_call(query_first_kernel, in_specs=[IN_VMEM] * 2 + [IN_HBM] * 2,...  2.63 us
    pallas_call x2, Pallas kernels, mix(): pl.pallas_call(mix_kernel, in_specs=[IN_VMEM] * 4, out_specs=IN_VMEM, out...  1.47 us
    pallas_call x1, Pallas kernels, third(): pl.pallas_call(third_kernel, in_specs=[IN_VMEM] * 5, out_specs=[IN_VMEM]...  1.42 us
  transfers between devices with their start and end apart: 16, of which 11 were waited for; matrix products, arithmetic and copies ran while one was open for 0% of the time, Pallas kernels for 29%

profile of v4, /device:TPU:0, one launch (start us, length us, event | category | flops | bytes accessed | tf_op | source)
XLA Modules:
  0.0 59.8 jit_solution(581508150150334709)
XLA Ops:
  0.5 2.5 %collective-permute-start.1 = (bf16[128,2048]{1,0:T(8,128)(2,1)}, bf16[128,2048]{1,0:T(8,128)(2,1)S(1)}, u32[]{:S(2)}, u32[]{:S(2)}) collective-permute-start(bf16[128,2048]{1,0:T(8,128)(2,1)} %rows_hbm.1), channel_id=1, source_target_pairs={{0,2},{1,3},{2,0},{3,1},{4,6},{5,7},{6,4},{7,5},{8,10},{9,11},{10,... | collective-permute-start | bytes 1572872 | tf_op jit(solution)/shard_map/ppermute | solution.py:425
  2.9 3.1 %shard_map.73 = (bf16[128,2048]{1,0:T(8,128)(2,1)S(1)}, bf16[2048,512]{1,0:T(8,128)(2,1)S(1)}, bf16[2048,512]{1,0:T(8,128)(2,1)S(1)}, bf16[128,512]{1,0:T(8,128)(2,1)S(1)}, bf16[128,512]{1,0:T(8,128)(2,1)S(1)}) custom-call(bf16[128,2048]{1,0:T(8,128)(2,1)} %rows_hbm.1, bf16[2048,512]{1,0:T(8,128)(2,1)} %wk_hbm.1, bf16[2048,512]{1,0:T(8,128)(2,1)} %wv_hbm.1), custom_call_target="tpu_custom_call" | custom-call | flops 536870912 | bytes 4194304 | tf_op jit(solution)/shard_map/pallas_call | solution.py:98
  6.1 0.9 %shard_map.74 = (bf16[128,512]{1,0:T(8,128)(2,1)S(1)}, bf16[128,512]{1,0:T(8,128)(2,1)S(1)}, bf16[2,4,32,128]{3,2,1,0:T(8,128)(2,1)S(1)}) custom-call(bf16[128,2048]{1,0:T(8,128)(2,1)S(1)} %collective-permute-done.rows.rows_1, bf16[2048,512]{1,0:T(8,128)(2,1)S(1)} %get-tuple-element.39.wk, bf16[2048,512]{1,0:T(8,128)(2,1)S(1)} %get-tuple-element.40.wv, ...), custom_call_target="tpu_custom_call" | custom-call | flops 536870912 | bytes 524288 | tf_op jit(solution)/shard_map/pallas_call | solution.py:130
  7.0 2.6 %collective-permute-start.2 = (bf16[1,2,4,32,128]{4,3,2,1,0:T(8,128)(2,1)S(1)}, bf16[1,2,4,32,128]{4,3,2,1,0:T(8,128)(2,1)S(1)}, u32[]{:S(2)}, u32[]{:S(2)}) collective-permute-start(bf16[1,2,4,32,128]{4,3,2,1,0:T(8,128)(2,1)S(1)} %bitcast.5), channel_id=1, source_target_pairs={{0,16},{4,20},{8,24},{12,28},{16,0},{20,4},{24,8},{28,12},{1,17},{... | collective-permute-start | bytes 196616 | tf_op jit(solution)/shard_map/ppermute | solution.py:425
  9.7 0.6 shard_map.75.bias
  10.3 3.3 %collective-permute-done.2 = bf16[1,2,4,32,128]{4,3,2,1,0:T(8,128)(2,1)S(1)} collective-permute-done((bf16[1,2,4,32,128]{4,3,2,1,0:T(8,128)(2,1)S(1)}, bf16[1,2,4,32,128]{4,3,2,1,0:T(8,128)(2,1)S(1)}, u32[]{:S(2)}, u32[]{:S(2)}) %collective-permute-start.2) | collective-permute-done | bytes 65568 | tf_op jit(solution)/shard_map/ppermute | solution.py:425
  13.6 0.7 %collective-permute-start.3 = (bf16[2,2,4,32,128]{4,3,2,1,0:T(8,128)(2,1)S(1)}, bf16[2,2,4,32,128]{4,3,2,1,0:T(8,128)(2,1)S(1)}, u32[]{:S(2)}, u32[]{:S(2)}) collective-permute-start(bf16[2,2,4,32,128]{4,3,2,1,0:T(8,128)(2,1)S(1)} %pad_maximum_fusion.1), channel_id=1, source_target_pairs={{0,8},{4,12},{8,0},{12,4},{16,24},{20,28},{24,16},{28,20},{1,9},{5... | collective-permute-start | bytes 393224 | tf_op jit(solution)/shard_map/ppermute | solution.py:425
  14.3 2.6 %shard_map.76 = (bf16[256,512]{1,0:T(8,128)(2,1)S(1)}, bf16[2048,512]{1,0:T(8,128)(2,1)S(1)}, bf16[512,2048]{1,0:T(8,128)(2,1)S(1)}) custom-call(bf16[128,2048]{1,0:T(8,128)(2,1)S(1)} %get-tuple-element.47.rows_0, bf16[128,2048]{1,0:T(8,128)(2,1)S(1)} %collective-permute-done.rows.rows_1, bf16[2048,512]{1,0:T(8,128)(2,1)} %wq_hbm.1, bf16[512,2048]{1,0:T(8,128)(2,1)} %w_hbm.1), custom_call_target="tpu_custom_call" | custom-call | flops 536870912 | bytes 4194304 | tf_op jit(solution)/shard_map/pallas_call | solution.py:159
  17.0 1.7 %collective-permute-done.3 = bf16[2,2,4,32,128]{4,3,2,1,0:T(8,128)(2,1)S(1)} collective-permute-done((bf16[2,2,4,32,128]{4,3,2,1,0:T(8,128)(2,1)S(1)}, bf16[2,2,4,32,128]{4,3,2,1,0:T(8,128)(2,1)S(1)}, u32[]{:S(2)}, u32[]{:S(2)}) %collective-permute-start.3) | collective-permute-done | bytes 131104 | tf_op jit(solution)/shard_map/ppermute | solution.py:425
  18.7 1.9 %collective-permute-done.4.rows_1 = bf16[128,2048]{1,0:T(8,128)(2,1)S(1)} collective-permute-done((bf16[128,2048]{1,0:T(8,128)(2,1)S(1)}, bf16[128,2048]{1,0:T(8,128)(2,1)S(1)}, u32[]{:S(2)}, u32[]{:S(2)}) %collective-permute-start.4) | collective-permute-done | bytes 524320 | tf_op jit(solution)/shard_map/ppermute | solution.py:425
  20.6 1.4 %shard_map.77 = (bf16[256,512]{1,0:T(8,128)(2,1)S(1)}, bf16[256,512]{1,0:T(8,128)(2,1)S(1)}, bf16[1,4,32,128]{3,2,1,0:T(8,128)(2,1)S(1)}, bf16[1,4,32,128]{3,2,1,0:T(8,128)(2,1)S(1)}) custom-call(bf16[128,2048]{1,0:T(8,128)(2,1)S(1)} %collective-permute-done.1.rows_0, bf16[128,2048]{1,0:T(8,128)(2,1)S(1)} %collective-permute-done.4.rows_1, ...), custom_call_target="tpu_custom_call" | custom-call | flops 1073741824 | bytes 1048576 | tf_op jit(solution)/shard_map/pallas_call | solution.py:210
  22.2 1.1 %collective-permute-start.7 = (bf16[1,1,4,32,128]{4,3,2,1,0:T(8,128)(2,1)S(1)}, bf16[1,1,4,32,128]{4,3,2,1,0:T(8,128)(2,1)S(1)}, u32[]{:S(2)}, u32[]{:S(2)}) collective-permute-start(bf16[1,1,4,32,128]{4,3,2,1,0:T(8,128)(2,1)S(1)} %bitcast.11), channel_id=1, source_target_pairs={{0,8},{4,12},{8,0},{12,4},{16,24},{20,28},{24,16},{28,20},{1,9},{5... | collective-permute-start | bytes 98312 | tf_op jit(solution)/shard_map/ppermute | solution.py:425
  23.4 1.6 %collective-permute-start.9 = (bf16[4,2,4,32,128]{4,3,2,1,0:T(8,128)(2,1)S(1)}, bf16[4,2,4,32,128]{4,3,2,1,0:T(8,128)(2,1)S(1)}, u32[]{:S(2)}, u32[]{:S(2)}) collective-permute-start(bf16[4,2,4,32,128]{4,3,2,1,0:T(8,128)(2,1)S(1)} %pad_maximum_fusion.refs_7_), channel_id=1, source_target_pairs={{0,4},{4,0},{8,12},{12,8},{16,20},{20,16},{24,28},{28,24},{1,5},{5... | collective-permute-start | bytes 786440 | tf_op jit(solution)/shard_map/ppermute | solution.py:425
  24.9 3.4 %collective-permute-start.5 = (bf16[1,1,4,32,128]{4,3,2,1,0:T(8,128)(2,1)S(1)}, bf16[1,1,4,32,128]{4,3,2,1,0:T(8,128)(2,1)S(1)}, u32[]{:S(2)}, u32[]{:S(2)}) collective-permute-start(bf16[1,1,4,32,128]{4,3,2,1,0:T(8,128)(2,1)S(1)} %bitcast.8), channel_id=1, source_target_pairs={{0,16},{4,20},{8,24},{12,28},{16,0},{20,4},{24,8},{28,12},{1,17},{... | collective-permute-start | bytes 98312 | tf_op jit(solution)/shard_map/ppermute | solution.py:425
  28.3 0.6 %collective-permute-start.8 = (bf16[2,1,4,32,128]{4,3,2,1,0:T(8,128)(2,1)S(1)}, bf16[2,1,4,32,128]{4,3,2,1,0:T(8,128)(2,1)S(1)}, u32[]{:S(2)}, u32[]{:S(2)}) collective-permute-start(bf16[2,1,4,32,128]{4,3,2,1,0:T(8,128)(2,1)S(1)} %pad_maximum_fusion.5), channel_id=1, source_target_pairs={{0,16},{4,20},{8,24},{12,28},{16,0},{20,4},{24,8},{28,12},{1,17},{... | collective-permute-start | bytes 196616 | tf_op jit(solution)/shard_map/ppermute | solution.py:425
  29.0 1.5 %collective-permute-done.5 = bf16[1,1,4,32,128]{4,3,2,1,0:T(8,128)(2,1)S(1)} collective-permute-done((bf16[1,1,4,32,128]{4,3,2,1,0:T(8,128)(2,1)S(1)}, bf16[1,1,4,32,128]{4,3,2,1,0:T(8,128)(2,1)S(1)}, u32[]{:S(2)}, u32[]{:S(2)}) %collective-permute-start.5) | collective-permute-done | bytes 32800 | tf_op jit(solution)/shard_map/ppermute | solution.py:425
  30.5 0.6 collective-permute-start.6
  31.0 0.7 %shard_map.78.refs_0_ = bf16[256,512]{1,0:T(8,128)(2,1)S(1)} custom-call(bf16[128,2048]{1,0:T(8,128)(2,1)S(1)} %collective-permute-done.1.rows_0, bf16[128,2048]{1,0:T(8,128)(2,1)S(1)} %collective-permute-done.4.rows_1, bf16[2048,512]{1,0:T(8,128)(2,1)S(1)} %get-tuple-element.53.wq), custom_call_target="tpu_custom_call" | custom-call | flops 536870912 | bytes 1048576 | tf_op jit(solution)/shard_map/pallas_call | solution.py:183
  31.8 2.2 %collective-permute-done.8 = bf16[2,1,4,32,128]{4,3,2,1,0:T(8,128)(2,1)S(1)} collective-permute-done((bf16[2,1,4,32,128]{4,3,2,1,0:T(8,128)(2,1)S(1)}, bf16[2,1,4,32,128]{4,3,2,1,0:T(8,128)(2,1)S(1)}, u32[]{:S(2)}, u32[]{:S(2)}) %collective-permute-start.8) | collective-permute-done | bytes 65568 | tf_op jit(solution)/shard_map/ppermute | solution.py:425
  34.0 0.8 %collective-permute-done.6 = bf16[2,1,4,32,128]{4,3,2,1,0:T(8,128)(2,1)S(1)} collective-permute-done((bf16[2,1,4,32,128]{4,3,2,1,0:T(8,128)(2,1)S(1)}, bf16[2,1,4,32,128]{4,3,2,1,0:T(8,128)(2,1)S(1)}, u32[]{:S(2)}, u32[]{:S(2)}) %collective-permute-start.6) | collective-permute-done | bytes 65568 | tf_op jit(solution)/shard_map/ppermute | solution.py:425
  34.8 0.6 collective-permute-start.11
  35.4 1.3 %collective-permute-start.10 = (bf16[4,1,4,32,128]{4,3,2,1,0:T(8,128)(2,1)S(1)}, bf16[4,1,4,32,128]{4,3,2,1,0:T(8,128)(2,1)S(1)}, u32[]{:S(2)}, u32[]{:S(2)}) collective-permute-start(bf16[4,1,4,32,128]{4,3,2,1,0:T(8,128)(2,1)S(1)} %pad_maximum_fusion.2.refs_3_.refs_9_), channel_id=1, source_target_pairs={{0,8},{4,12},{8,0},{12,4},{16,24},{20,28},{24,16},{28,20},{1,9},{5... | collective-permute-start | bytes 393224 | tf_op jit(solution)/shard_map/ppermute | solution.py:425
  36.7 2.9 %shard_map.79 = (f32[256,512]{1,0:T(8,128)S(1)}, f32[4,256,128]{2,1,0:T(8,128)S(1)}) custom-call(f32[4,1024]{1,0:T(4,128)S(1)} %shard_map.75.bias, bf16[256,512]{1,0:T(8,128)(2,1)S(1)} %shard_map.78.refs_0_, bf16[128,512]{1,0:T(8,128)(2,1)S(1)} %get-tuple-element.41.keys_0.refs_1_, bf16[128,512]{1,0:T(8,128)(2,1)S(1)} %get-tuple-element.59.refs_2_, ...), custom_call_target="tpu_custom_call" | custom-call | flops 402653184 | bytes 524288 | tf_op jit(solution)/shard_map/pallas_call | solution.py:383
  39.9 0.6 collective-permute-done.10.refs_4_.refs_10_
  40.4 2.3 %shard_map.80 = (bf16[128,512]{1,0:T(8,128)(2,1)S(1)}, bf16[128,512]{1,0:T(8,128)(2,1)S(1)}) custom-call(f32[4,1024]{1,0:T(4,128)S(1)} %shard_map.75.bias, bf16[256,512]{1,0:T(8,128)(2,1)S(1)} %shard_map.78.refs_0_, f32[256,512]{1,0:T(8,128)S(1)} %get-tuple-element.64.refs_1_, f32[4,256,128]{2,1,0:T(8,128)S(1)} %get-tuple-element.65.refs_2_, ...), custom_call_target="tpu_custom_call" | custom-call | flops 134217728 | bytes 524288 | tf_op jit(solution)/shard_map/pallas_call | solution.py:383
  42.8 1.3 %collective-permute-done.12.rows_1 = bf16[128,512]{1,0:T(8,128)(2,1)S(1)} collective-permute-done((bf16[128,512]{1,0:T(8,128)(2,1)S(1)}, bf16[128,512]{1,0:T(8,128)(2,1)S(1)}, u32[]{:S(2)}, u32[]{:S(2)}) %collective-permute-start.12) | collective-permute-done | bytes 131104 | tf_op jit(solution)/shard_map/ppermute | solution.py:425
  44.1 0.7 %shard_map.81 = bf16[128,2048]{1,0:T(8,128)(2,1)S(1)} custom-call(bf16[128,512]{1,0:T(8,128)(2,1)S(1)} %get-tuple-element.66.rows_0, bf16[128,512]{1,0:T(8,128)(2,1)S(1)} %collective-permute-done.12.rows_1, bf16[512,2048]{1,0:T(8,128)(2,1)S(1)} %get-tuple-element.68.weight_0, bf16[512,2048]{1,0:T(8,128)(2,1)S(1)} %collective-permute-done.13.weight_1), custom_call_target="tpu_custom_call" | custom-call | flops 536870912 | bytes 1048576 | tf_op jit(solution)/shard_map/pallas_call | solution.py:408
  45.4 3.2 %shard_map.82 = (bf16[128,512]{1,0:T(8,128)(2,1)S(1)}, bf16[128,512]{1,0:T(8,128)(2,1)S(1)}) custom-call(f32[4,1024]{1,0:T(4,128)S(1)} %shard_map.75.bias, bf16[256,512]{1,0:T(8,128)(2,1)S(1)} %get-tuple-element.70.refs_0_, bf16[128,512]{1,0:T(8,128)(2,1)S(1)} %get-tuple-element.41.keys_0.refs_1_, bf16[128,512]{1,0:T(8,128)(2,1)S(1)} %get-tuple-element.59.refs_2_, ...), custom_call_target="tpu_custom_call" | custom-call | flops 536870912 | bytes 524288 | tf_op jit(solution)/shard_map/pallas_call | solution.py:383
  48.7 1.3 %collective-permute-done.14.rows_1 = bf16[128,512]{1,0:T(8,128)(2,1)S(1)} collective-permute-done((bf16[128,512]{1,0:T(8,128)(2,1)S(1)}, bf16[128,512]{1,0:T(8,128)(2,1)S(1)}, u32[]{:S(2)}, u32[]{:S(2)}) %collective-permute-start.14) | collective-permute-done | bytes 131104 | tf_op jit(solution)/shard_map/ppermute | solution.py:425
  50.1 0.7 %shard_map.83 = f32[128,2048]{1,0:T(8,128)S(1)} custom-call(bf16[128,512]{1,0:T(8,128)(2,1)S(1)} %get-tuple-element.71.rows_0, bf16[128,512]{1,0:T(8,128)(2,1)S(1)} %collective-permute-done.14.rows_1, bf16[512,2048]{1,0:T(8,128)(2,1)S(1)} %get-tuple-element.68.weight_0, bf16[512,2048]{1,0:T(8,128)(2,1)S(1)} %collective-permute-done.13.weight_1), custom_call_target="tpu_custom_call" | custom-call | flops 536870912 | bytes 1048576 | tf_op jit(solution)/shard_map/pallas_call | solution.py:408
  50.8 8.1 %collective-permute-done.15 = bf16[128,2048]{1,0:T(8,128)(2,1)S(1)} collective-permute-done((bf16[128,2048]{1,0:T(8,128)(2,1)S(1)}, bf16[128,2048]{1,0:T(8,128)(2,1)S(1)}, u32[]{:S(2)}, u32[]{:S(2)}) %collective-permute-start.15) | collective-permute-done | bytes 524320 | tf_op jit(solution)/shard_map/ppermute | solution.py:425
  58.9 0.9 %add_convert_fusion = bf16[128,2048]{1,0:T(8,128)(2,1)} fusion(f32[128,2048]{1,0:T(8,128)S(1)} %shard_map.83, bf16[128,2048]{1,0:T(8,128)(2,1)S(1)} %collective-permute-done.15), kind=kLoop, calls=%fused_computation | loop fusion | flops 786432 | bytes 2097152 | tf_op jit(solution)/shard_map/convert_element_type | solution.py:475
  (25 shorter events, 1.7 us)
Async XLA Ops:
  0.0 6.1 %collective-permute-start = (bf16[128,2048]{1,0:T(8,128)(2,1)}, bf16[128,2048]{1,0:T(8,128)(2,1)S(1)}, u32[]{:S(2)}, u32[]{:S(2)}) collective-permute-start(bf16[128,2048]{1,0:T(8,128)(2,1)} %rows_hbm.1), channel_id=1, source_target_pairs={{0,1},{1,0},{2,3},{3,2},{4,5},{5,4},{6,7},{7,6},{8,9},{9,8},{10,11... | collective-permute-start | bytes 1572872 | tf_op jit(solution)/shard_map/ppermute | solution.py:425
  0.5 16.5 %collective-permute-start.1 = (bf16[128,2048]{1,0:T(8,128)(2,1)}, bf16[128,2048]{1,0:T(8,128)(2,1)S(1)}, u32[]{:S(2)}, u32[]{:S(2)}) collective-permute-start(bf16[128,2048]{1,0:T(8,128)(2,1)} %rows_hbm.1), channel_id=1, source_target_pairs={{0,2},{1,3},{2,0},{3,1},{4,6},{5,7},{6,4},{7,5},{8,10},{9,11},{10,... | collective-permute-start | bytes 1572872 | tf_op jit(solution)/shard_map/ppermute | solution.py:425
  2.9 3.1 %copy-start = (s32[4,128]{1,0:T(4,128)S(1)}, s32[4,128]{1,0:T(4,128)}, u32[]{:S(2)}) copy-start(s32[4,128]{1,0:T(4,128)} %pattern.3) | copy-start | bytes 6148
  6.1 3.5 %copy-start.2 = (s32[8]{0:T(128)S(1)}, s32[8]{0:T(128)}, u32[]{:S(2)}) copy-start(s32[8]{0:T(128)} %param.13) | copy-start | bytes 100
  7.0 6.6 %collective-permute-start.2 = (bf16[1,2,4,32,128]{4,3,2,1,0:T(8,128)(2,1)S(1)}, bf16[1,2,4,32,128]{4,3,2,1,0:T(8,128)(2,1)S(1)}, u32[]{:S(2)}, u32[]{:S(2)}) collective-permute-start(bf16[1,2,4,32,128]{4,3,2,1,0:T(8,128)(2,1)S(1)} %bitcast.5), channel_id=1, source_target_pairs={{0,16},{4,20},{8,24},{12,28},{16,0},{20,4},{24,8},{28,12},{1,17},{... | collective-permute-start | bytes 196616 | tf_op jit(solution)/shard_map/ppermute | solution.py:425
  13.6 5.0 %collective-permute-start.3 = (bf16[2,2,4,32,128]{4,3,2,1,0:T(8,128)(2,1)S(1)}, bf16[2,2,4,32,128]{4,3,2,1,0:T(8,128)(2,1)S(1)}, u32[]{:S(2)}, u32[]{:S(2)}) collective-permute-start(bf16[2,2,4,32,128]{4,3,2,1,0:T(8,128)(2,1)S(1)} %pad_maximum_fusion.1), channel_id=1, source_target_pairs={{0,8},{4,12},{8,0},{12,4},{16,24},{20,28},{24,16},{28,20},{1,9},{5... | collective-permute-start | bytes 393224 | tf_op jit(solution)/shard_map/ppermute | solution.py:425
  18.6 3.3 %copy-start.1 = (bf16[512,2048]{1,0:T(8,128)(2,1)S(1)}, bf16[512,2048]{1,0:T(8,128)(2,1)}, u32[]{:S(2)}) copy-start(bf16[512,2048]{1,0:T(8,128)(2,1)} %w_hbm.1) | copy-start | bytes 6291460
  18.6 1.9 %collective-permute-start.4 = (bf16[128,2048]{1,0:T(8,128)(2,1)S(1)}, bf16[128,2048]{1,0:T(8,128)(2,1)S(1)}, u32[]{:S(2)}, u32[]{:S(2)}) collective-permute-start(bf16[128,2048]{1,0:T(8,128)(2,1)S(1)} %collective-permute-done.1.rows_0), channel_id=1, source_target_pairs={{0,1},{1,0},{2,3},{3,2},{4,5},{5,4},{6,7},{7,6},{8,9},{9,8},{10,11... | collective-permute-start | bytes 1572872 | tf_op jit(solution)/shard_map/ppermute | solution.py:425
  22.0 22.2 %collective-permute-start.13 = (bf16[512,2048]{1,0:T(8,128)(2,1)S(1)}, bf16[512,2048]{1,0:T(8,128)(2,1)S(1)}, u32[]{:S(2)}, u32[]{:S(2)}) collective-permute-start(bf16[512,2048]{1,0:T(8,128)(2,1)S(1)} %copy-done.1), channel_id=1, source_target_pairs={{0,1},{1,0},{2,3},{3,2},{4,5},{5,4},{6,7},{7,6},{8,9},{9,8},{10,11... | collective-permute-start | bytes 6291464 | tf_op jit(solution)/shard_map/ppermute | solution.py:425
  22.2 6.1 %collective-permute-start.7 = (bf16[1,1,4,32,128]{4,3,2,1,0:T(8,128)(2,1)S(1)}, bf16[1,1,4,32,128]{4,3,2,1,0:T(8,128)(2,1)S(1)}, u32[]{:S(2)}, u32[]{:S(2)}) collective-permute-start(bf16[1,1,4,32,128]{4,3,2,1,0:T(8,128)(2,1)S(1)} %bitcast.11), channel_id=1, source_target_pairs={{0,8},{4,12},{8,0},{12,4},{16,24},{20,28},{24,16},{28,20},{1,9},{5... | collective-permute-start | bytes 98312 | tf_op jit(solution)/shard_map/ppermute | solution.py:425
  23.4 8.4 %collective-permute-start.9 = (bf16[4,2,4,32,128]{4,3,2,1,0:T(8,128)(2,1)S(1)}, bf16[4,2,4,32,128]{4,3,2,1,0:T(8,128)(2,1)S(1)}, u32[]{:S(2)}, u32[]{:S(2)}) collective-permute-start(bf16[4,2,4,32,128]{4,3,2,1,0:T(8,128)(2,1)S(1)} %pad_maximum_fusion.refs_7_), channel_id=1, source_target_pairs={{0,4},{4,0},{8,12},{12,8},{16,20},{20,16},{24,28},{28,24},{1,5},{5... | collective-permute-start | bytes 786440 | tf_op jit(solution)/shard_map/ppermute | solution.py:425
  24.9 5.5 %collective-permute-start.5 = (bf16[1,1,4,32,128]{4,3,2,1,0:T(8,128)(2,1)S(1)}, bf16[1,1,4,32,128]{4,3,2,1,0:T(8,128)(2,1)S(1)}, u32[]{:S(2)}, u32[]{:S(2)}) collective-permute-start(bf16[1,1,4,32,128]{4,3,2,1,0:T(8,128)(2,1)S(1)} %bitcast.8), channel_id=1, source_target_pairs={{0,16},{4,20},{8,24},{12,28},{16,0},{20,4},{24,8},{28,12},{1,17},{... | collective-permute-start | bytes 98312 | tf_op jit(solution)/shard_map/ppermute | solution.py:425
  28.3 5.6 %collective-permute-start.8 = (bf16[2,1,4,32,128]{4,3,2,1,0:T(8,128)(2,1)S(1)}, bf16[2,1,4,32,128]{4,3,2,1,0:T(8,128)(2,1)S(1)}, u32[]{:S(2)}, u32[]{:S(2)}) collective-permute-start(bf16[2,1,4,32,128]{4,3,2,1,0:T(8,128)(2,1)S(1)} %pad_maximum_fusion.5), channel_id=1, source_target_pairs={{0,16},{4,20},{8,24},{12,28},{16,0},{20,4},{24,8},{28,12},{1,17},{... | collective-permute-start | bytes 196616 | tf_op jit(solution)/shard_map/ppermute | solution.py:425
  30.5 4.3 %collective-permute-start.6 = (bf16[2,1,4,32,128]{4,3,2,1,0:T(8,128)(2,1)S(1)}, bf16[2,1,4,32,128]{4,3,2,1,0:T(8,128)(2,1)S(1)}, u32[]{:S(2)}, u32[]{:S(2)}) collective-permute-start(bf16[2,1,4,32,128]{4,3,2,1,0:T(8,128)(2,1)S(1)} %pad_maximum_fusion.4), channel_id=1, source_target_pairs={{0,4},{4,0},{8,12},{12,8},{16,20},{20,16},{24,28},{28,24},{1,5},{5... | collective-permute-start | bytes 196616 | tf_op jit(solution)/shard_map/ppermute | solution.py:425
  34.8 5.0 %collective-permute-start.11 = (bf16[4,1,4,32,128]{4,3,2,1,0:T(8,128)(2,1)S(1)}, bf16[4,1,4,32,128]{4,3,2,1,0:T(8,128)(2,1)S(1)}, u32[]{:S(2)}, u32[]{:S(2)}) collective-permute-start(bf16[4,1,4,32,128]{4,3,2,1,0:T(8,128)(2,1)S(1)} %pad_maximum_fusion.3.refs_5_.refs_11_), channel_id=1, source_target_pairs={{0,4},{4,0},{8,12},{12,8},{16,20},{20,16},{24,28},{28,24},{1,5},{5... | collective-permute-start | bytes 393224 | tf_op jit(solution)/shard_map/ppermute | solution.py:425
  35.4 5.0 %collective-permute-start.10 = (bf16[4,1,4,32,128]{4,3,2,1,0:T(8,128)(2,1)S(1)}, bf16[4,1,4,32,128]{4,3,2,1,0:T(8,128)(2,1)S(1)}, u32[]{:S(2)}, u32[]{:S(2)}) collective-permute-start(bf16[4,1,4,32,128]{4,3,2,1,0:T(8,128)(2,1)S(1)} %pad_maximum_fusion.2.refs_3_.refs_9_), channel_id=1, source_target_pairs={{0,8},{4,12},{8,0},{12,4},{16,24},{20,28},{24,16},{28,20},{1,9},{5... | collective-permute-start | bytes 393224 | tf_op jit(solution)/shard_map/ppermute | solution.py:425
  42.7 1.4 %collective-permute-start.12 = (bf16[128,512]{1,0:T(8,128)(2,1)S(1)}, bf16[128,512]{1,0:T(8,128)(2,1)S(1)}, u32[]{:S(2)}, u32[]{:S(2)}) collective-permute-start(bf16[128,512]{1,0:T(8,128)(2,1)S(1)} %get-tuple-element.67), channel_id=1, source_target_pairs={{0,1},{1,0},{2,3},{3,2},{4,5},{5,4},{6,7},{7,6},{8,9},{9,8},{10,11... | collective-permute-start | bytes 393224 | tf_op jit(solution)/shard_map/ppermute | solution.py:425
  44.9 14.0 %collective-permute-start.15 = (bf16[128,2048]{1,0:T(8,128)(2,1)S(1)}, bf16[128,2048]{1,0:T(8,128)(2,1)S(1)}, u32[]{:S(2)}, u32[]{:S(2)}) collective-permute-start(bf16[128,2048]{1,0:T(8,128)(2,1)S(1)} %shard_map.81), channel_id=1, source_target_pairs={{0,2},{1,3},{2,0},{3,1},{4,6},{5,7},{6,4},{7,5},{8,10},{9,11},{10,... | collective-permute-start | bytes 1572872 | tf_op jit(solution)/shard_map/ppermute | solution.py:425
  48.6 1.4 %collective-permute-start.14 = (bf16[128,512]{1,0:T(8,128)(2,1)S(1)}, bf16[128,512]{1,0:T(8,128)(2,1)S(1)}, u32[]{:S(2)}, u32[]{:S(2)}) collective-permute-start(bf16[128,512]{1,0:T(8,128)(2,1)S(1)} %get-tuple-element.72), channel_id=1, source_target_pairs={{0,1},{1,0},{2,3},{3,2},{4,5},{5,4},{6,7},{7,6},{8,9},{9,8},{10,11... | collective-permute-start | bytes 393224 | tf_op jit(solution)/shard_map/ppermute | solution.py:425

commit v5 on v4

--- a/solution.py
+++ b/solution.py
@@ -21,9 +21,8 @@
 IN_VMEM = pl.BlockSpec(memory_space=pltpu.VMEM)
 IN_HBM = pl.BlockSpec(memory_space=pltpu.HBM)
 IN_SMEM = pl.BlockSpec(memory_space=pltpu.SMEM)
-BOTH_BITS = (4, 2, 1)
-KEY_BITS = (4, 1, 2)
-VALUE_BITS = (2, 4, 1)
+Y_BIT = 1
+Z_BITS = (2, 4, 6)
 
 
 def dot(a, b):
@@ -58,16 +57,15 @@
 
 
 def pick_dilated(pattern, blocks, kept):
-    (keys, key_slot), (values, value_slot) = kept
     positions = lax.broadcasted_iota(jnp.int32, (BLOCK, BLOCK), 0)
-    for head in range(keys.shape[1]):
+    for head in range(kept.shape[1]):
         row = pattern[head : head + 1, :]
         chosen = (positions == row).astype(F32).T[:DILATED_KEPT].astype(BF16)
         for index, block in enumerate(blocks):
             picked = dot(chosen, jnp.concatenate(block(head), axis=1)).astype(BF16)
             spot = slice(index * DILATED_KEPT, (index + 1) * DILATED_KEPT)
-            keys[key_slot, head, spot, :] = picked[:, :HEAD_SIZE]
-            values[value_slot, head, spot, :] = picked[:, HEAD_SIZE:]
+            kept[0, head, spot, :] = picked[:, :HEAD_SIZE]
+            kept[1, head, spot, :] = picked[:, HEAD_SIZE:]
 
 
 def head_of(ref, head, rows=slice(None)):
@@ -120,7 +118,7 @@
         lambda head: (head_of(keys_0, head), head_of(values_0, head)),
         lambda head: (head_of(keys, head), head_of(values, head)),
     ]
-    pick_dilated(pattern, blocks, ((kept, 0), (kept, 1)))
+    pick_dilated(pattern, blocks, kept)
 
 
 def second(rows, wk, wv, keys_0, values_0, pattern):
@@ -190,7 +188,7 @@
     )(rows_0, rows_1, wq)
 
 
-def third_kernel(rows_0, rows_1, wk, wv, pattern, keys, values, kept_k, kept_v):
+def third_kernel(rows_0, rows_1, wk, wv, pattern, keys, values, kept):
     rows = jnp.concatenate([rows_0[...], rows_1[...]], axis=0)
     for part in halves_of(wk.shape[1]):
         keys[:, part] = dot(rows, wk[:, part]).astype(BF16)
@@ -200,18 +198,18 @@
         return lambda head: (head_of(keys, head, where), head_of(values, head, where))
 
     blocks = [block(slice(i * BLOCK, (i + 1) * BLOCK)) for i in range(BLOCKS_HALF)]
-    pick_dilated(pattern, blocks, ((kept_k, 0), (kept_v, 0)))
+    pick_dilated(pattern, blocks, kept)
 
 
 def third(rows_0, rows_1, wk, wv, pattern):
     count, depth = rows_0.shape
     width = wk.shape[1]
-    kept = (1, width // HEAD_SIZE, FAR_ROWS, HEAD_SIZE)
+    kept = (2, width // HEAD_SIZE, FAR_ROWS, HEAD_SIZE)
     return pl.pallas_call(
         third_kernel,
         in_specs=[IN_VMEM] * 5,
-        out_specs=[IN_VMEM] * 4,
-        out_shape=[shape((2 * count, width))] * 2 + [shape(kept)] * 2,
+        out_specs=[IN_VMEM] * 3,
+        out_shape=[shape((2 * count, width))] * 2 + [shape(kept)],
         compiler_params=params(),
         cost_estimate=cost(8 * count * depth * width, 4 * count * depth),
     )(rows_0, rows_1, wk, wv, pattern)
@@ -279,15 +277,13 @@
     return higher, total, gathered * shrink + dot(weight.astype(BF16), values)
 
 
-def far_group(parts, head):
+def far_group(refs, head):
+    mine, along_z, along_y, beyond = refs
     found = []
-    for refs, slot, bits in parts:
-        order = [0]
-        for bit in bits:
-            order += [place ^ bit for place in order]
-        half = len(order) // 2
-        spots = [order.index(i) for i in range(len(order))]
-        pieces = [refs[spot // half][spot % half, slot, head] for spot in spots]
+    for slot in range(2):
+        pieces = [mine[slot, head], along_y[slot, head]]
+        for step in range(len(Z_BITS)):
+            pieces += [along_z[step, slot, head], beyond[step, slot, head]]
         found.append(jnp.concatenate(pieces, axis=0))
     return found
 
@@ -303,13 +299,9 @@
         del refs[:2]
     far = []
     for half in halves:
-        size = 2 if few else 1
-        if half == 0:
-            parts = [(refs[:size], slot, BOTH_BITS) for slot in range(2)]
-        else:
-            parts = [(refs[:size], 0, KEY_BITS), (refs[size : 2 * size], 0, VALUE_BITS)]
-        del refs[: size * (half + 1)]
-        far.append((half, parts))
+        size = 4 if few else 1
+        far.append((half, refs[:size]))
+        del refs[:size]
     span = bias.shape[0] * BLOCK
     half_count = (bias.shape[1] - span) * BLOCKS_HALF // bias.shape[0]
 
@@ -337,17 +329,17 @@
                 state = far_update(asked, *group, rows, state)
                 continue
 
-            def step(number, state, start=start, parts=parts):
+            def step(number, state, start=start, part=parts[0]):
                 base = number * GROUP
                 group = [
-                    jnp.concatenate([refs[0][base + i, slot, head] for i in range(GROUP)], axis=0)
-                    for refs, slot, _ in parts
+                    jnp.concatenate([part[base + i, slot, head] for i in range(GROUP)], axis=0)
+                    for slot in range(2)
                 ]
                 width = GROUP * FAR_ROWS
                 rows = rows_of_bias(pl.ds(pl.multiple_of(start + number * width, width), width))
                 return far_update(asked, *group, rows, state)
 
-            state = lax.fori_loop(0, parts[0][0][0].shape[0] // GROUP, step, state)
+            state = lax.fori_loop(0, parts[0].shape[0] // GROUP, step, state)
         peak, total, gathered = state
         if finish:
             keep, send = refs
@@ -370,16 +362,15 @@
     operands = [queries]
     operands += [*near[0], *near[1]] if near else list(begun)
     columns = bias.shape[0] * BLOCK if near else 0
-    spans = 0
-    for _, *parts in halves:
-        operands += sum(parts, [])
-        spans += sum(part.shape[0] for part in parts[0])
+    for _, parts in halves:
+        operands += parts
+    far_bytes = sum(2 * part.size for _, parts in halves for part in parts)
+    spans = far_bytes // (4 * FAR_ROWS * width)
     columns += spans * FAR_ROWS
     if finish:
         out_shape = [shape((BLOCK, width))] * 2
     else:
         out_shape = [shape((rows, width), F32), shape((heads, rows, HEAD_SIZE), F32)]
-    far_bytes = 4 * spans * FAR_ROWS * width
     return pl.pallas_call(
         functools.partial(
             attend_kernel, relative, near is not None, [half[0] for half in halves], few, finish
@@ -427,8 +418,12 @@
     def after(array, *others):
         return lax.optimization_barrier((array, *others))[0]
 
-    def double(parts, bit, hook=lambda came: came):
-        return jnp.concatenate([parts, hook(swap(parts, bit, "seq"))], axis=0)
+    def first_round(kept):
+        return [swap(kept, bit, "seq") for bit in Z_BITS], swap(kept, Y_BIT, "seq")
+
+    def second_round(kept, along_z, along_y):
+        along_z = jnp.stack(along_z)
+        return [kept, along_z, along_y, swap(along_z, Y_BIT, "seq")]
 
     across = swap(normed, 2)
     beside = swap(normed, 1)
@@ -436,33 +431,33 @@
     keys_1, values_1, kept_a = second(beside, wk, wv, keys_0, values_0, pattern)
     place = jnp.concatenate([after(slide_lengths, kept_a), *axes])
     bias = make_bias(place, slides, subs, seqs, few)
-    if few:
-        kept_a = double(kept_a[None], BOTH_BITS[0], lambda came: after(came, bias))
-        mine = after(mine, kept_a)
     query_a, wq, wo = query_first(mine, beside, w_query, w_out)
     if few:
-        came = swap(kept_a, BOTH_BITS[1], "seq")
-        across, came, query_a = lax.optimization_barrier((across, came, query_a))
-        kept_a = jnp.concatenate([kept_a, came], axis=0)
-        half_a = 0, [kept_a, swap(kept_a, BOTH_BITS[2], "seq")]
+        along_z, along_y = first_round(kept_a)
+        *along_z, along_y, query_a, bias = lax.optimization_barrier(
+            (*along_z, along_y, query_a, bias)
+        )
+        half_a = 0, second_round(kept_a, along_z, along_y)
+        across = after(across, half_a[1][1])
     else:
         half_a = 0, [lax.all_gather(kept_a, "seq", axis=0)]
     beyond = swap(across, 1)
-    keys_2, values_2, *kept_b = third(across, beyond, wk, wv, pattern)
-    wo_beside = swap(after(w_out, kept_b[0]), 1)
-    wo_beside = pltpu.with_memory_space_constraint(wo_beside, pltpu.VMEM)
+    keys_2, values_2, kept_b = third(across, beyond, wk, wv, pattern)
     query_b = query(across, beyond, wq)
     if few:
-        k, v = double(kept_b[0][None], KEY_BITS[0]), double(kept_b[1][None], VALUE_BITS[0])
-        came = swap(k, KEY_BITS[1], "seq"), swap(v, VALUE_BITS[1], "seq")
-        *came, query_b, half_a[1][1] = lax.optimization_barrier((*came, query_b, half_a[1][1]))
-        k, v = jnp.concatenate([k, came[0]], axis=0), jnp.concatenate([v, came[1]], axis=0)
-        half_b = 1, [k, swap(k, KEY_BITS[2], "seq")], [v, swap(v, VALUE_BITS[2], "seq")]
+        along_z, along_y = first_round(kept_b)
+        *along_z, along_y, query_b, half_a[1][3] = lax.optimization_barrier(
+            (*along_z, along_y, query_b, half_a[1][3])
+        )
+        half_b = 1, second_round(kept_b, along_z, along_y)
+        asked = after(query_b, half_b[1][1])
     else:
-        half_b = 1, *[[lax.all_gather(part, "seq", axis=0)] for part in kept_b]
+        half_b = 1, [lax.all_gather(kept_b, "seq", axis=0)]
+        asked = query_b
+    wo_beside = swap(after(w_out, asked), 1)
+    wo_beside = pltpu.with_memory_space_constraint(wo_beside, pltpu.VMEM)
     near = [keys_0, keys_1, keys_2], [values_0, values_1, values_2]
     call = functools.partial(attend, bias, few)
-    asked = after(query_b, half_b[1][0], half_b[2][0])
     begun = call((2, 3), asked, [half_a], near=near, finish=False)
     keep_b, send_b = call((2, 3), query_b, [half_b], begun=begun)
     other_b = swap(send_b, 1)

time: 60.3 us -> 58.3 us (0.967)
  waiting for transfers between devices: 23 us -> 18.6 us
  starting transfers between devices: 16.3 us -> 19 us
    ppermute x16 -> x17, waiting for transfers between devices: 23 us -> 18.6 us  [swap(): return lax.ppermute(array, axis, [(i, i ^ bit) for i in range(count)])]
    ppermute x16 -> x17, starting transfers between devices: 16.3 us -> 19 us  [swap(): return lax.ppermute(array, axis, [(i, i ^ bit) for i in range(count)])]
  transfers between devices with their start and end apart: 16 -> 17, of which waited for: 11 -> 7; matrix products, arithmetic and copies ran while one was open for 0% -> 0% of each run, Pallas kernels for 29% -> 32%
where the time goes in v5:
time: 58.3 us; the launch traced here: 58.2 us
  Pallas kernels  19.3 us (33%)
  starting transfers between devices  19 us (33%)
  waiting for transfers between devices  18.6 us (32%)
  other arithmetic  1.02 us (2%)
    ppermute x17, starting transfers between devices, swap(): return lax.ppermute(array, axis, [(i, i ^ bit) for i in range(count)])  19 us
    ppermute x17, waiting for transfers between devices, swap(): return lax.ppermute(array, axis, [(i, i ^ bit) for i in range(count)])  18.6 us
    pallas_call x3, Pallas kernels, attend(): pl.pallas_call(functools.partial(attend_kernel, relative, near is not Non...  8.45 us
    pallas_call x1, Pallas kernels, first(): pl.pallas_call(first_kernel, in_specs=[IN_HBM] * 3, out_specs=[IN_VMEM] *...  3.12 us
    pallas_call x1, Pallas kernels, query_first(): pl.pallas_call(query_first_kernel, in_specs=[IN_VMEM] * 2 + [IN_HBM] * 2,...  2.64 us
    pallas_call x2, Pallas kernels, mix(): pl.pallas_call(mix_kernel, in_specs=[IN_VMEM] * 4, out_specs=IN_VMEM, out...  1.48 us
    pallas_call x1, Pallas kernels, third(): pl.pallas_call(third_kernel, in_specs=[IN_VMEM] * 5, out_specs=[IN_VMEM]...  1.42 us
  transfers between devices with their start and end apart: 17, of which 7 were waited for; matrix products, arithmetic and copies ran while one was open for 0% of the time, Pallas kernels for 32%

profile of v5, /device:TPU:0, one launch (start us, length us, event | category | flops | bytes accessed | tf_op | source)
XLA Modules:
  0.0 58.2 jit_solution(14199022157978764877)
XLA Ops:
  0.0 0.5 collective-permute-start
  0.5 2.5 %collective-permute-start.5 = (bf16[128,2048]{1,0:T(8,128)(2,1)}, bf16[128,2048]{1,0:T(8,128)(2,1)S(1)}, u32[]{:S(2)}, u32[]{:S(2)}) collective-permute-start(bf16[128,2048]{1,0:T(8,128)(2,1)} %rows_hbm.1), channel_id=1, source_target_pairs={{0,2},{1,3},{2,0},{3,1},{4,6},{5,7},{6,4},{7,5},{8,10},{9,11},{10,... | collective-permute-start | bytes 1572872 | tf_op jit(solution)/shard_map/ppermute | solution.py:416
  2.9 3.1 %shard_map.73 = (bf16[128,2048]{1,0:T(8,128)(2,1)S(1)}, bf16[2048,512]{1,0:T(8,128)(2,1)S(1)}, bf16[2048,512]{1,0:T(8,128)(2,1)S(1)}, bf16[128,512]{1,0:T(8,128)(2,1)S(1)}, bf16[128,512]{1,0:T(8,128)(2,1)S(1)}) custom-call(bf16[128,2048]{1,0:T(8,128)(2,1)} %rows_hbm.1, bf16[2048,512]{1,0:T(8,128)(2,1)} %wk_hbm.1, bf16[2048,512]{1,0:T(8,128)(2,1)} %wv_hbm.1), custom_call_target="tpu_custom_call" | custom-call | flops 536870912 | bytes 4194304 | tf_op jit(solution)/shard_map/pallas_call | solution.py:96
  6.1 0.9 %shard_map.74 = (bf16[128,512]{1,0:T(8,128)(2,1)S(1)}, bf16[128,512]{1,0:T(8,128)(2,1)S(1)}, bf16[2,4,32,128]{3,2,1,0:T(8,128)(2,1)S(1)}) custom-call(bf16[128,2048]{1,0:T(8,128)(2,1)S(1)} %collective-permute-done.rows.rows_1, bf16[2048,512]{1,0:T(8,128)(2,1)S(1)} %get-tuple-element.42.wk, bf16[2048,512]{1,0:T(8,128)(2,1)S(1)} %get-tuple-element.43.wv, ...), custom_call_target="tpu_custom_call" | custom-call | flops 536870912 | bytes 524288 | tf_op jit(solution)/shard_map/pallas_call | solution.py:128
  7.0 1.6 %collective-permute-start.1 = (bf16[2,4,32,128]{3,2,1,0:T(8,128)(2,1)S(1)}, bf16[2,4,32,128]{3,2,1,0:T(8,128)(2,1)S(1)}, u32[]{:S(2)}, u32[]{:S(2)}) collective-permute-start(bf16[2,4,32,128]{3,2,1,0:T(8,128)(2,1)S(1)} %get-tuple-element.46.refs_7_), channel_id=1, source_target_pairs={{0,8},{4,12},{8,0},{12,4},{16,24},{20,28},{24,16},{28,20},{1,9},{5... | collective-permute-start | bytes 196616 | tf_op jit(solution)/shard_map/ppermute | solution.py:416
  8.6 2.6 %collective-permute-start.2 = (bf16[2,4,32,128]{3,2,1,0:T(8,128)(2,1)S(1)}, bf16[2,4,32,128]{3,2,1,0:T(8,128)(2,1)S(1)}, u32[]{:S(2)}, u32[]{:S(2)}) collective-permute-start(bf16[2,4,32,128]{3,2,1,0:T(8,128)(2,1)S(1)} %get-tuple-element.46.refs_7_), channel_id=1, source_target_pairs={{0,16},{4,20},{8,24},{12,28},{16,0},{20,4},{24,8},{28,12},{1,17},{... | collective-permute-start | bytes 196616 | tf_op jit(solution)/shard_map/ppermute | solution.py:416
  11.2 0.2 collective-permute-start.3
  11.4 1.5 %collective-permute-start.4 = (bf16[2,4,32,128]{3,2,1,0:T(8,128)(2,1)S(1)}, bf16[2,4,32,128]{3,2,1,0:T(8,128)(2,1)S(1)}, u32[]{:S(2)}, u32[]{:S(2)}) collective-permute-start(bf16[2,4,32,128]{3,2,1,0:T(8,128)(2,1)S(1)} %get-tuple-element.46.refs_7_), channel_id=1, source_target_pairs={{0,4},{4,0},{8,12},{12,8},{16,20},{20,16},{24,28},{28,24},{1,5},{5... | collective-permute-start | bytes 196616 | tf_op jit(solution)/shard_map/ppermute | solution.py:416
  13.0 0.6 %shard_map.76.bias = f32[4,1024]{1,0:T(4,128)S(1)} custom-call(s32[10]{0:T(128)S(1)} %pad_add_fusion.place), custom_call_target="tpu_custom_call" | custom-call | flops 262144 | bytes 16384 | tf_op jit(solution)/shard_map/pallas_call | solution.py:254
  13.6 2.6 %shard_map.75 = (bf16[256,512]{1,0:T(8,128)(2,1)S(1)}, bf16[2048,512]{1,0:T(8,128)(2,1)S(1)}, bf16[512,2048]{1,0:T(8,128)(2,1)S(1)}) custom-call(bf16[128,2048]{1,0:T(8,128)(2,1)S(1)} %get-tuple-element.47.rows_0, bf16[128,2048]{1,0:T(8,128)(2,1)S(1)} %collective-permute-done.rows.rows_1, bf16[2048,512]{1,0:T(8,128)(2,1)} %wq_hbm.1, bf16[512,2048]{1,0:T(8,128)(2,1)} %w_hbm.1), custom_call_target="tpu_custom_call" | custom-call | flops 536870912 | bytes 4194304 | tf_op jit(solution)/shard_map/pallas_call | solution.py:157
  16.3 1.1 %collective-permute-done.3 = bf16[2,4,32,128]{3,2,1,0:T(8,128)(2,1)S(1)} collective-permute-done((bf16[2,4,32,128]{3,2,1,0:T(8,128)(2,1)S(1)}, bf16[2,4,32,128]{3,2,1,0:T(8,128)(2,1)S(1)}, u32[]{:S(2)}, u32[]{:S(2)}) %collective-permute-start.3) | collective-permute-done | bytes 65568 | tf_op jit(solution)/shard_map/ppermute | solution.py:416
  17.5 1.6 %collective-permute-start.11 = (bf16[3,2,4,32,128]{4,3,2,1,0:T(8,128)(2,1)S(1)}, bf16[3,2,4,32,128]{4,3,2,1,0:T(8,128)(2,1)S(1)}, u32[]{:S(2)}, u32[]{:S(2)}) collective-permute-start(bf16[3,2,4,32,128]{4,3,2,1,0:T(8,128)(2,1)S(1)} %pad_maximum_fusion.refs_8_), channel_id=1, source_target_pairs={{0,4},{4,0},{8,12},{12,8},{16,20},{20,16},{24,28},{28,24},{1,5},{5... | collective-permute-start | bytes 589832 | tf_op jit(solution)/shard_map/ppermute | solution.py:416
  19.1 0.3 collective-permute-done.6.rows_1
  19.4 1.4 %shard_map.77 = (bf16[256,512]{1,0:T(8,128)(2,1)S(1)}, bf16[256,512]{1,0:T(8,128)(2,1)S(1)}, bf16[2,4,32,128]{3,2,1,0:T(8,128)(2,1)S(1)}) custom-call(bf16[128,2048]{1,0:T(8,128)(2,1)S(1)} %collective-permute-done.5.rows_0, bf16[128,2048]{1,0:T(8,128)(2,1)S(1)} %collective-permute-done.6.rows_1, bf16[2048,512]{1,0:T(8,128)(2,1)S(1)} %get-tuple-element.42.wk, ...), custom_call_target="tpu_custom_call" | custom-call | flops 1073741824 | bytes 1048576 | tf_op jit(solution)/shard_map/pallas_call | solution.py:208
  20.8 1.6 %collective-permute-start.10 = (bf16[2,4,32,128]{3,2,1,0:T(8,128)(2,1)S(1)}, bf16[2,4,32,128]{3,2,1,0:T(8,128)(2,1)S(1)}, u32[]{:S(2)}, u32[]{:S(2)}) collective-permute-start(bf16[2,4,32,128]{3,2,1,0:T(8,128)(2,1)S(1)} %get-tuple-element.56.refs_3_.refs_11_), channel_id=1, source_target_pairs={{0,4},{4,0},{8,12},{12,8},{16,20},{20,16},{24,28},{28,24},{1,5},{5... | collective-permute-start | bytes 196616 | tf_op jit(solution)/shard_map/ppermute | solution.py:416
  22.4 0.9 %collective-permute-start.7 = (bf16[2,4,32,128]{3,2,1,0:T(8,128)(2,1)S(1)}, bf16[2,4,32,128]{3,2,1,0:T(8,128)(2,1)S(1)}, u32[]{:S(2)}, u32[]{:S(2)}) collective-permute-start(bf16[2,4,32,128]{3,2,1,0:T(8,128)(2,1)S(1)} %get-tuple-element.56.refs_3_.refs_11_), channel_id=1, source_target_pairs={{0,8},{4,12},{8,0},{12,4},{16,24},{20,28},{24,16},{28,20},{1,9},{5... | collective-permute-start | bytes 196616 | tf_op jit(solution)/shard_map/ppermute | solution.py:416
  23.3 1.8 %collective-permute-start.8 = (bf16[2,4,32,128]{3,2,1,0:T(8,128)(2,1)S(1)}, bf16[2,4,32,128]{3,2,1,0:T(8,128)(2,1)S(1)}, u32[]{:S(2)}, u32[]{:S(2)}) collective-permute-start(bf16[2,4,32,128]{3,2,1,0:T(8,128)(2,1)S(1)} %get-tuple-element.56.refs_3_.refs_11_), channel_id=1, source_target_pairs={{0,16},{4,20},{8,24},{12,28},{16,0},{20,4},{24,8},{28,12},{1,17},{... | collective-permute-start | bytes 196616 | tf_op jit(solution)/shard_map/ppermute | solution.py:416
  25.1 1.7 %collective-permute-start.9 = (bf16[2,4,32,128]{3,2,1,0:T(8,128)(2,1)S(1)}, bf16[2,4,32,128]{3,2,1,0:T(8,128)(2,1)S(1)}, u32[]{:S(2)}, u32[]{:S(2)}) collective-permute-start(bf16[2,4,32,128]{3,2,1,0:T(8,128)(2,1)S(1)} %get-tuple-element.56.refs_3_.refs_11_), channel_id=1, source_target_pairs={{0,24},{4,28},{8,16},{12,20},{16,8},{20,12},{24,0},{28,4},{1,25},{... | collective-permute-start | bytes 196616 | tf_op jit(solution)/shard_map/ppermute | solution.py:416
  26.8 0.7 %shard_map.78.refs_0_ = bf16[256,512]{1,0:T(8,128)(2,1)S(1)} custom-call(bf16[128,2048]{1,0:T(8,128)(2,1)S(1)} %collective-permute-done.5.rows_0, bf16[128,2048]{1,0:T(8,128)(2,1)S(1)} %collective-permute-done.6.rows_1, bf16[2048,512]{1,0:T(8,128)(2,1)S(1)} %get-tuple-element.57.wq), custom_call_target="tpu_custom_call" | custom-call | flops 536870912 | bytes 1048576 | tf_op jit(solution)/shard_map/pallas_call | solution.py:181
  27.5 3.8 %collective-permute-done.8 = bf16[2,4,32,128]{3,2,1,0:T(8,128)(2,1)S(1)} collective-permute-done((bf16[2,4,32,128]{3,2,1,0:T(8,128)(2,1)S(1)}, bf16[2,4,32,128]{3,2,1,0:T(8,128)(2,1)S(1)}, u32[]{:S(2)}, u32[]{:S(2)}) %collective-permute-start.8) | collective-permute-done | bytes 65568 | tf_op jit(solution)/shard_map/ppermute | solution.py:416
  31.4 0.9 %collective-permute-start.12 = (bf16[3,2,4,32,128]{4,3,2,1,0:T(8,128)(2,1)S(1)}, bf16[3,2,4,32,128]{4,3,2,1,0:T(8,128)(2,1)S(1)}, u32[]{:S(2)}, u32[]{:S(2)}) collective-permute-start(bf16[3,2,4,32,128]{4,3,2,1,0:T(8,128)(2,1)S(1)} %pad_maximum_fusion.1.refs_4_.refs_12_), channel_id=1, source_target_pairs={{0,4},{4,0},{8,12},{12,8},{16,20},{20,16},{24,28},{28,24},{1,5},{5... | collective-permute-start | bytes 589832 | tf_op jit(solution)/shard_map/ppermute | solution.py:416
  32.4 2.9 %shard_map.79 = (f32[256,512]{1,0:T(8,128)S(1)}, f32[4,256,128]{2,1,0:T(8,128)S(1)}) custom-call(f32[4,1024]{1,0:T(4,128)S(1)} %shard_map.76.bias, bf16[256,512]{1,0:T(8,128)(2,1)S(1)} %shard_map.78.refs_0_, bf16[128,512]{1,0:T(8,128)(2,1)S(1)} %get-tuple-element.44.keys_0.refs_1_, bf16[128,512]{1,0:T(8,128)(2,1)S(1)} %get-tuple-element.63.refs_2_, ...), custom_call_target="tpu_custom_call" | custom-call | flops 402653184 | bytes 524288 | tf_op jit(solution)/shard_map/pallas_call | solution.py:374
  35.3 3.4 %collective-permute-done.12.refs_6_.refs_14_ = bf16[3,2,4,32,128]{4,3,2,1,0:T(8,128)(2,1)S(1)} collective-permute-done((bf16[3,2,4,32,128]{4,3,2,1,0:T(8,128)(2,1)S(1)}, bf16[3,2,4,32,128]{4,3,2,1,0:T(8,128)(2,1)S(1)}, u32[]{:S(2)}, u32[]{:S(2)}) %collective-permute-start.12) | collective-permute-done | bytes 196640 | tf_op jit(solution)/shard_map/ppermute | solution.py:416
  38.8 2.3 %shard_map.80 = (bf16[128,512]{1,0:T(8,128)(2,1)S(1)}, bf16[128,512]{1,0:T(8,128)(2,1)S(1)}) custom-call(f32[4,1024]{1,0:T(4,128)S(1)} %shard_map.76.bias, bf16[256,512]{1,0:T(8,128)(2,1)S(1)} %shard_map.78.refs_0_, f32[256,512]{1,0:T(8,128)S(1)} %get-tuple-element.69.refs_1_, f32[4,256,128]{2,1,0:T(8,128)S(1)} %get-tuple-element.70.refs_2_, ...), custom_call_target="tpu_custom_call" | custom-call | flops 134217728 | bytes 524288 | tf_op jit(solution)/shard_map/pallas_call | solution.py:374
  41.1 1.3 %collective-permute-done.13.rows_1 = bf16[128,512]{1,0:T(8,128)(2,1)S(1)} collective-permute-done((bf16[128,512]{1,0:T(8,128)(2,1)S(1)}, bf16[128,512]{1,0:T(8,128)(2,1)S(1)}, u32[]{:S(2)}, u32[]{:S(2)}) %collective-permute-start.13) | collective-permute-done | bytes 131104 | tf_op jit(solution)/shard_map/ppermute | solution.py:416
  42.5 0.7 %shard_map.81 = bf16[128,2048]{1,0:T(8,128)(2,1)S(1)} custom-call(bf16[128,512]{1,0:T(8,128)(2,1)S(1)} %get-tuple-element.72.rows_0, bf16[128,512]{1,0:T(8,128)(2,1)S(1)} %collective-permute-done.13.rows_1, bf16[512,2048]{1,0:T(8,128)(2,1)S(1)} %get-tuple-element.74.weight_0, bf16[512,2048]{1,0:T(8,128)(2,1)S(1)} %collective-permute-done.14.weight_1), custom_call_target="tpu_custom_call" | custom-call | flops 536870912 | bytes 1048576 | tf_op jit(solution)/shard_map/pallas_call | solution.py:399
  43.2 1.4 %collective-permute-start.16 = (bf16[128,2048]{1,0:T(8,128)(2,1)S(1)}, bf16[128,2048]{1,0:T(8,128)(2,1)S(1)}, u32[]{:S(2)}, u32[]{:S(2)}) collective-permute-start(bf16[128,2048]{1,0:T(8,128)(2,1)S(1)} %shard_map.81), channel_id=1, source_target_pairs={{0,2},{1,3},{2,0},{3,1},{4,6},{5,7},{6,4},{7,5},{8,10},{9,11},{10,... | collective-permute-start | bytes 1572872 | tf_op jit(solution)/shard_map/ppermute | solution.py:416
  44.6 3.2 %shard_map.82 = (bf16[128,512]{1,0:T(8,128)(2,1)S(1)}, bf16[128,512]{1,0:T(8,128)(2,1)S(1)}) custom-call(f32[4,1024]{1,0:T(4,128)S(1)} %shard_map.76.bias, bf16[256,512]{1,0:T(8,128)(2,1)S(1)} %get-tuple-element.76.refs_0_, bf16[128,512]{1,0:T(8,128)(2,1)S(1)} %get-tuple-element.44.keys_0.refs_1_, bf16[128,512]{1,0:T(8,128)(2,1)S(1)} %get-tuple-element.63.refs_2_, ...), custom_call_target="tpu_custom_call" | custom-call | flops 536870912 | bytes 524288 | tf_op jit(solution)/shard_map/pallas_call | solution.py:374
  47.9 1.3 %collective-permute-done.15.rows_1 = bf16[128,512]{1,0:T(8,128)(2,1)S(1)} collective-permute-done((bf16[128,512]{1,0:T(8,128)(2,1)S(1)}, bf16[128,512]{1,0:T(8,128)(2,1)S(1)}, u32[]{:S(2)}, u32[]{:S(2)}) %collective-permute-start.15) | collective-permute-done | bytes 131104 | tf_op jit(solution)/shard_map/ppermute | solution.py:416
  49.3 0.7 %shard_map.83 = f32[128,2048]{1,0:T(8,128)S(1)} custom-call(bf16[128,512]{1,0:T(8,128)(2,1)S(1)} %get-tuple-element.77.rows_0, bf16[128,512]{1,0:T(8,128)(2,1)S(1)} %collective-permute-done.15.rows_1, bf16[512,2048]{1,0:T(8,128)(2,1)S(1)} %get-tuple-element.74.weight_0, bf16[512,2048]{1,0:T(8,128)(2,1)S(1)} %collective-permute-done.14.weight_1), custom_call_target="tpu_custom_call" | custom-call | flops 536870912 | bytes 1048576 | tf_op jit(solution)/shard_map/pallas_call | solution.py:399
  50.0 7.2 %collective-permute-done.16 = bf16[128,2048]{1,0:T(8,128)(2,1)S(1)} collective-permute-done((bf16[128,2048]{1,0:T(8,128)(2,1)S(1)}, bf16[128,2048]{1,0:T(8,128)(2,1)S(1)}, u32[]{:S(2)}, u32[]{:S(2)}) %collective-permute-start.16) | collective-permute-done | bytes 524320 | tf_op jit(solution)/shard_map/ppermute | solution.py:416
  57.3 0.9 %add_convert_fusion = bf16[128,2048]{1,0:T(8,128)(2,1)} fusion(f32[128,2048]{1,0:T(8,128)S(1)} %shard_map.83, bf16[128,2048]{1,0:T(8,128)(2,1)S(1)} %collective-permute-done.16), kind=kLoop, calls=%fused_computation | loop fusion | flops 786432 | bytes 2097152 | tf_op jit(solution)/shard_map/convert_element_type | solution.py:470
  (23 shorter events, 0.4 us)
Async XLA Ops:
  0.0 6.1 %collective-permute-start = (bf16[128,2048]{1,0:T(8,128)(2,1)}, bf16[128,2048]{1,0:T(8,128)(2,1)S(1)}, u32[]{:S(2)}, u32[]{:S(2)}) collective-permute-start(bf16[128,2048]{1,0:T(8,128)(2,1)} %rows_hbm.1), channel_id=1, source_target_pairs={{0,1},{1,0},{2,3},{3,2},{4,5},{5,4},{6,7},{7,6},{8,9},{9,8},{10,11... | collective-permute-start | bytes 1572872 | tf_op jit(solution)/shard_map/ppermute | solution.py:416
  0.5 16.9 %collective-permute-start.5 = (bf16[128,2048]{1,0:T(8,128)(2,1)}, bf16[128,2048]{1,0:T(8,128)(2,1)S(1)}, u32[]{:S(2)}, u32[]{:S(2)}) collective-permute-start(bf16[128,2048]{1,0:T(8,128)(2,1)} %rows_hbm.1), channel_id=1, source_target_pairs={{0,2},{1,3},{2,0},{3,1},{4,6},{5,7},{6,4},{7,5},{8,10},{9,11},{10,... | collective-permute-start | bytes 1572872 | tf_op jit(solution)/shard_map/ppermute | solution.py:416
  2.9 3.1 %copy-start = (s32[4,128]{1,0:T(4,128)S(1)}, s32[4,128]{1,0:T(4,128)}, u32[]{:S(2)}) copy-start(s32[4,128]{1,0:T(4,128)} %pattern.3) | copy-start | bytes 6148
  6.1 6.8 %copy-start.2 = (s32[8]{0:T(128)S(1)}, s32[8]{0:T(128)}, u32[]{:S(2)}) copy-start(s32[8]{0:T(128)} %param.13) | copy-start | bytes 100
  7.0 9.3 %collective-permute-start.1 = (bf16[2,4,32,128]{3,2,1,0:T(8,128)(2,1)S(1)}, bf16[2,4,32,128]{3,2,1,0:T(8,128)(2,1)S(1)}, u32[]{:S(2)}, u32[]{:S(2)}) collective-permute-start(bf16[2,4,32,128]{3,2,1,0:T(8,128)(2,1)S(1)} %get-tuple-element.46.refs_7_), channel_id=1, source_target_pairs={{0,8},{4,12},{8,0},{12,4},{16,24},{20,28},{24,16},{28,20},{1,9},{5... | collective-permute-start | bytes 196616 | tf_op jit(solution)/shard_map/ppermute | solution.py:416
  8.6 7.7 %collective-permute-start.2 = (bf16[2,4,32,128]{3,2,1,0:T(8,128)(2,1)S(1)}, bf16[2,4,32,128]{3,2,1,0:T(8,128)(2,1)S(1)}, u32[]{:S(2)}, u32[]{:S(2)}) collective-permute-start(bf16[2,4,32,128]{3,2,1,0:T(8,128)(2,1)S(1)} %get-tuple-element.46.refs_7_), channel_id=1, source_target_pairs={{0,16},{4,20},{8,24},{12,28},{16,0},{20,4},{24,8},{28,12},{1,17},{... | collective-permute-start | bytes 196616 | tf_op jit(solution)/shard_map/ppermute | solution.py:416
  11.2 6.2 %collective-permute-start.3 = (bf16[2,4,32,128]{3,2,1,0:T(8,128)(2,1)S(1)}, bf16[2,4,32,128]{3,2,1,0:T(8,128)(2,1)S(1)}, u32[]{:S(2)}, u32[]{:S(2)}) collective-permute-start(bf16[2,4,32,128]{3,2,1,0:T(8,128)(2,1)S(1)} %get-tuple-element.46.refs_7_), channel_id=1, source_target_pairs={{0,24},{4,28},{8,16},{12,20},{16,8},{20,12},{24,0},{28,4},{1,25},{... | collective-permute-start | bytes 196616 | tf_op jit(solution)/shard_map/ppermute | solution.py:416
  11.4 6.0 %collective-permute-start.4 = (bf16[2,4,32,128]{3,2,1,0:T(8,128)(2,1)S(1)}, bf16[2,4,32,128]{3,2,1,0:T(8,128)(2,1)S(1)}, u32[]{:S(2)}, u32[]{:S(2)}) collective-permute-start(bf16[2,4,32,128]{3,2,1,0:T(8,128)(2,1)S(1)} %get-tuple-element.46.refs_7_), channel_id=1, source_target_pairs={{0,4},{4,0},{8,12},{12,8},{16,20},{20,16},{24,28},{28,24},{1,5},{5... | collective-permute-start | bytes 196616 | tf_op jit(solution)/shard_map/ppermute | solution.py:416
  17.4 2.0 %collective-permute-start.6 = (bf16[128,2048]{1,0:T(8,128)(2,1)S(1)}, bf16[128,2048]{1,0:T(8,128)(2,1)S(1)}, u32[]{:S(2)}, u32[]{:S(2)}) collective-permute-start(bf16[128,2048]{1,0:T(8,128)(2,1)S(1)} %collective-permute-done.5.rows_0), channel_id=1, source_target_pairs={{0,1},{1,0},{2,3},{3,2},{4,5},{5,4},{6,7},{7,6},{8,9},{9,8},{10,11... | collective-permute-start | bytes 1572872 | tf_op jit(solution)/shard_map/ppermute | solution.py:416
  17.5 10.0 %collective-permute-start.11 = (bf16[3,2,4,32,128]{4,3,2,1,0:T(8,128)(2,1)S(1)}, bf16[3,2,4,32,128]{4,3,2,1,0:T(8,128)(2,1)S(1)}, u32[]{:S(2)}, u32[]{:S(2)}) collective-permute-start(bf16[3,2,4,32,128]{4,3,2,1,0:T(8,128)(2,1)S(1)} %pad_maximum_fusion.refs_8_), channel_id=1, source_target_pairs={{0,4},{4,0},{8,12},{12,8},{16,20},{20,16},{24,28},{28,24},{1,5},{5... | collective-permute-start | bytes 589832 | tf_op jit(solution)/shard_map/ppermute | solution.py:416
  20.8 10.5 %copy-start.1 = (bf16[512,2048]{1,0:T(8,128)(2,1)S(1)}, bf16[512,2048]{1,0:T(8,128)(2,1)}, u32[]{:S(2)}) copy-start(bf16[512,2048]{1,0:T(8,128)(2,1)} %w_hbm.1) | copy-start | bytes 6291460
  20.8 6.7 %collective-permute-start.10 = (bf16[2,4,32,128]{3,2,1,0:T(8,128)(2,1)S(1)}, bf16[2,4,32,128]{3,2,1,0:T(8,128)(2,1)S(1)}, u32[]{:S(2)}, u32[]{:S(2)}) collective-permute-start(bf16[2,4,32,128]{3,2,1,0:T(8,128)(2,1)S(1)} %get-tuple-element.56.refs_3_.refs_11_), channel_id=1, source_target_pairs={{0,4},{4,0},{8,12},{12,8},{16,20},{20,16},{24,28},{28,24},{1,5},{5... | collective-permute-start | bytes 196616 | tf_op jit(solution)/shard_map/ppermute | solution.py:416
  22.4 5.1 %collective-permute-start.7 = (bf16[2,4,32,128]{3,2,1,0:T(8,128)(2,1)S(1)}, bf16[2,4,32,128]{3,2,1,0:T(8,128)(2,1)S(1)}, u32[]{:S(2)}, u32[]{:S(2)}) collective-permute-start(bf16[2,4,32,128]{3,2,1,0:T(8,128)(2,1)S(1)} %get-tuple-element.56.refs_3_.refs_11_), channel_id=1, source_target_pairs={{0,8},{4,12},{8,0},{12,4},{16,24},{20,28},{24,16},{28,20},{1,9},{5... | collective-permute-start | bytes 196616 | tf_op jit(solution)/shard_map/ppermute | solution.py:416
  23.3 8.0 %collective-permute-start.8 = (bf16[2,4,32,128]{3,2,1,0:T(8,128)(2,1)S(1)}, bf16[2,4,32,128]{3,2,1,0:T(8,128)(2,1)S(1)}, u32[]{:S(2)}, u32[]{:S(2)}) collective-permute-start(bf16[2,4,32,128]{3,2,1,0:T(8,128)(2,1)S(1)} %get-tuple-element.56.refs_3_.refs_11_), channel_id=1, source_target_pairs={{0,16},{4,20},{8,24},{12,28},{16,0},{20,4},{24,8},{28,12},{1,17},{... | collective-permute-start | bytes 196616 | tf_op jit(solution)/shard_map/ppermute | solution.py:416
  25.1 6.2 %collective-permute-start.9 = (bf16[2,4,32,128]{3,2,1,0:T(8,128)(2,1)S(1)}, bf16[2,4,32,128]{3,2,1,0:T(8,128)(2,1)S(1)}, u32[]{:S(2)}, u32[]{:S(2)}) collective-permute-start(bf16[2,4,32,128]{3,2,1,0:T(8,128)(2,1)S(1)} %get-tuple-element.56.refs_3_.refs_11_), channel_id=1, source_target_pairs={{0,24},{4,28},{8,16},{12,20},{16,8},{20,12},{24,0},{28,4},{1,25},{... | collective-permute-start | bytes 196616 | tf_op jit(solution)/shard_map/ppermute | solution.py:416
  31.4 11.1 %collective-permute-start.14 = (bf16[512,2048]{1,0:T(8,128)(2,1)S(1)}, bf16[512,2048]{1,0:T(8,128)(2,1)S(1)}, u32[]{:S(2)}, u32[]{:S(2)}) collective-permute-start(bf16[512,2048]{1,0:T(8,128)(2,1)S(1)} %copy-done.1), channel_id=1, source_target_pairs={{0,1},{1,0},{2,3},{3,2},{4,5},{5,4},{6,7},{7,6},{8,9},{9,8},{10,11... | collective-permute-start | bytes 6291464 | tf_op jit(solution)/shard_map/ppermute | solution.py:416
  31.4 7.3 %collective-permute-start.12 = (bf16[3,2,4,32,128]{4,3,2,1,0:T(8,128)(2,1)S(1)}, bf16[3,2,4,32,128]{4,3,2,1,0:T(8,128)(2,1)S(1)}, u32[]{:S(2)}, u32[]{:S(2)}) collective-permute-start(bf16[3,2,4,32,128]{4,3,2,1,0:T(8,128)(2,1)S(1)} %pad_maximum_fusion.1.refs_4_.refs_12_), channel_id=1, source_target_pairs={{0,4},{4,0},{8,12},{12,8},{16,20},{20,16},{24,28},{28,24},{1,5},{5... | collective-permute-start | bytes 589832 | tf_op jit(solution)/shard_map/ppermute | solution.py:416
  41.0 1.4 %collective-permute-start.13 = (bf16[128,512]{1,0:T(8,128)(2,1)S(1)}, bf16[128,512]{1,0:T(8,128)(2,1)S(1)}, u32[]{:S(2)}, u32[]{:S(2)}) collective-permute-start(bf16[128,512]{1,0:T(8,128)(2,1)S(1)} %get-tuple-element.73), channel_id=1, source_target_pairs={{0,1},{1,0},{2,3},{3,2},{4,5},{5,4},{6,7},{7,6},{8,9},{9,8},{10,11... | collective-permute-start | bytes 393224 | tf_op jit(solution)/shard_map/ppermute | solution.py:416
  43.2 14.0 %collective-permute-start.16 = (bf16[128,2048]{1,0:T(8,128)(2,1)S(1)}, bf16[128,2048]{1,0:T(8,128)(2,1)S(1)}, u32[]{:S(2)}, u32[]{:S(2)}) collective-permute-start(bf16[128,2048]{1,0:T(8,128)(2,1)S(1)} %shard_map.81), channel_id=1, source_target_pairs={{0,2},{1,3},{2,0},{3,1},{4,6},{5,7},{6,4},{7,5},{8,10},{9,11},{10,... | collective-permute-start | bytes 1572872 | tf_op jit(solution)/shard_map/ppermute | solution.py:416
  47.9 1.4 %collective-permute-start.15 = (bf16[128,512]{1,0:T(8,128)(2,1)S(1)}, bf16[128,512]{1,0:T(8,128)(2,1)S(1)}, u32[]{:S(2)}, u32[]{:S(2)}) collective-permute-start(bf16[128,512]{1,0:T(8,128)(2,1)S(1)} %get-tuple-element.78), channel_id=1, source_target_pairs={{0,1},{1,0},{2,3},{3,2},{4,5},{5,4},{6,7},{7,6},{8,9},{9,8},{10,11... | collective-permute-start | bytes 393224 | tf_op jit(solution)/shard_map/ppermute | solution.py:416

commit v6 on v5

--- a/solution.py
+++ b/solution.py
@@ -21,8 +21,6 @@
 IN_VMEM = pl.BlockSpec(memory_space=pltpu.VMEM)
 IN_HBM = pl.BlockSpec(memory_space=pltpu.HBM)
 IN_SMEM = pl.BlockSpec(memory_space=pltpu.SMEM)
-Y_BIT = 1
-Z_BITS = (2, 4, 6)
 
 
 def dot(a, b):
@@ -227,7 +225,7 @@
     return jnp.where(condition, jnp.float32(0), jnp.float32(HIDDEN))
 
 
-def bias_kernel(slides, subs, spans, few, place, out):
+def bias_kernel(slides, subs, spans, place, out):
     span, sub = place[slides], place[slides + 1]
     slide = [slide_of(place, slides, span * subs + (sub ^ r)) for r in range(subs)]
     for r in range(subs):
@@ -237,8 +235,6 @@
     count = spans * FAR_ROWS
     column = lax.broadcasted_iota(jnp.int32, (1, count), 1)
     far = column // FAR_ROWS
-    if few:
-        far = far ^ span
     upper = (column // DILATED_KEPT) % BLOCKS_HALF
     for half in range(subs // BLOCKS_HALF):
         place_0, place_1 = sub ^ (half * BLOCKS_HALF), sub ^ (half * BLOCKS_HALF + 1)
@@ -249,10 +245,10 @@
             out[r : r + 1, start : start + count] = hidden_if_not(seen)
 
 
-def make_bias(place, slides, subs, spans, few):
+def make_bias(place, slides, subs, spans):
     columns = subs * BLOCK + subs // BLOCKS_HALF * spans * FAR_ROWS
     return pl.pallas_call(
-        functools.partial(bias_kernel, slides, subs, spans, few),
+        functools.partial(bias_kernel, slides, subs, spans),
         in_specs=[IN_SMEM],
         out_specs=IN_VMEM,
         out_shape=shape((subs, columns), F32),
@@ -277,18 +273,7 @@
     return higher, total, gathered * shrink + dot(weight.astype(BF16), values)
 
 
-def far_group(refs, head):
-    mine, along_z, along_y, beyond = refs
-    found = []
-    for slot in range(2):
-        pieces = [mine[slot, head], along_y[slot, head]]
-        for step in range(len(Z_BITS)):
-            pieces += [along_z[step, slot, head], beyond[step, slot, head]]
-        found.append(jnp.concatenate(pieces, axis=0))
-    return found
-
-
-def attend_kernel(relative, near, halves, few, finish, bias, *refs):
+def attend_kernel(relative, near, halves, finish, bias, *refs):
     refs = list(refs)
     queries = refs.pop(0)
     if near:
@@ -299,9 +284,7 @@
         del refs[:2]
     far = []
     for half in halves:
-        size = 4 if few else 1
-        far.append((half, refs[:size]))
-        del refs[:size]
+        far.append((half, refs.pop(0)))
     span = bias.shape[0] * BLOCK
     half_count = (bias.shape[1] - span) * BLOCKS_HALF // bias.shape[0]
 
@@ -321,25 +304,23 @@
             state = peak, total, dot(weight.astype(BF16), near_values)
         else:
             state = stats_in[head, :, 0:1], stats_in[head, :, 1:2], gathered_in[:, columns]
-        for half, parts in far:
+        for half, part in far:
             start = span + half * half_count
-            if few:
-                group = far_group(parts, head)
-                rows = rows_of_bias(slice(start, start + half_count))
-                state = far_update(asked, *group, rows, state)
-                continue
-
-            def step(number, state, start=start, part=parts[0]):
+            width = GROUP * FAR_ROWS
+
+            def step(number, state, start=start, part=part):
                 base = number * GROUP
                 group = [
                     jnp.concatenate([part[base + i, slot, head] for i in range(GROUP)], axis=0)
                     for slot in range(2)
                 ]
-                width = GROUP * FAR_ROWS
-                rows = rows_of_bias(pl.ds(pl.multiple_of(start + number * width, width), width))
-                return far_update(asked, *group, rows, state)
-
-            state = lax.fori_loop(0, parts[0].shape[0] // GROUP, step, state)
+                first_column = start + number * width
+                if not isinstance(first_column, int):
+                    first_column = pl.multiple_of(first_column, width)
+                return far_update(asked, *group, rows_of_bias(pl.ds(first_column, width)), state)
+
+            steps = part.shape[0] // GROUP
+            state = step(0, state) if steps == 1 else lax.fori_loop(0, steps, step, state)
         peak, total, gathered = state
         if finish:
             keep, send = refs
@@ -356,15 +337,14 @@
     lax.fori_loop(0, queries.shape[1] // HEAD_SIZE, one_head, 0)
 
 
-def attend(bias, few, relative, queries, halves, near=None, begun=None, finish=True):
+def attend(bias, relative, queries, halves, near=None, begun=None, finish=True):
     rows, width = queries.shape
     heads = width // HEAD_SIZE
     operands = [queries]
     operands += [*near[0], *near[1]] if near else list(begun)
     columns = bias.shape[0] * BLOCK if near else 0
-    for _, parts in halves:
-        operands += parts
-    far_bytes = sum(2 * part.size for _, parts in halves for part in parts)
+    operands += [part for _, part in halves]
+    far_bytes = sum(2 * part.size for _, part in halves)
     spans = far_bytes // (4 * FAR_ROWS * width)
     columns += spans * FAR_ROWS
     if finish:
@@ -373,7 +353,7 @@
         out_shape = [shape((rows, width), F32), shape((heads, rows, HEAD_SIZE), F32)]
     return pl.pallas_call(
         functools.partial(
-            attend_kernel, relative, near is not None, [half[0] for half in halves], few, finish
+            attend_kernel, relative, near is not None, [half[0] for half in halves], finish
         ),
         in_specs=[IN_VMEM] * (1 + len(operands)),
         out_specs=[IN_VMEM] * 2,
@@ -418,47 +398,30 @@
     def after(array, *others):
         return lax.optimization_barrier((array, *others))[0]
 
-    def first_round(kept):
-        return [swap(kept, bit, "seq") for bit in Z_BITS], swap(kept, Y_BIT, "seq")
-
-    def second_round(kept, along_z, along_y):
-        along_z = jnp.stack(along_z)
-        return [kept, along_z, along_y, swap(along_z, Y_BIT, "seq")]
+    def spread(kept):
+        if not few:
+            return lax.all_gather(kept, "seq", axis=0)
+        copies = jnp.broadcast_to(kept[None], (seqs, *kept.shape))
+        return lax.all_to_all(copies, "seq", 0, 0)
 
     across = swap(normed, 2)
     beside = swap(normed, 1)
     mine, wk, wv, keys_0, values_0 = first(normed, w_key, w_value)
     keys_1, values_1, kept_a = second(beside, wk, wv, keys_0, values_0, pattern)
     place = jnp.concatenate([after(slide_lengths, kept_a), *axes])
-    bias = make_bias(place, slides, subs, seqs, few)
+    bias = make_bias(place, slides, subs, seqs)
     query_a, wq, wo = query_first(mine, beside, w_query, w_out)
-    if few:
-        along_z, along_y = first_round(kept_a)
-        *along_z, along_y, query_a, bias = lax.optimization_barrier(
-            (*along_z, along_y, query_a, bias)
-        )
-        half_a = 0, second_round(kept_a, along_z, along_y)
-        across = after(across, half_a[1][1])
-    else:
-        half_a = 0, [lax.all_gather(kept_a, "seq", axis=0)]
+    half_a = 0, spread(kept_a)
+    across = after(across, query_a, bias)
     beyond = swap(across, 1)
     keys_2, values_2, kept_b = third(across, beyond, wk, wv, pattern)
     query_b = query(across, beyond, wq)
-    if few:
-        along_z, along_y = first_round(kept_b)
-        *along_z, along_y, query_b, half_a[1][3] = lax.optimization_barrier(
-            (*along_z, along_y, query_b, half_a[1][3])
-        )
-        half_b = 1, second_round(kept_b, along_z, along_y)
-        asked = after(query_b, half_b[1][1])
-    else:
-        half_b = 1, [lax.all_gather(kept_b, "seq", axis=0)]
-        asked = query_b
-    wo_beside = swap(after(w_out, asked), 1)
+    half_b = 1, spread(kept_b)
+    wo_beside = swap(after(w_out, kept_b), 1)
     wo_beside = pltpu.with_memory_space_constraint(wo_beside, pltpu.VMEM)
     near = [keys_0, keys_1, keys_2], [values_0, values_1, values_2]
-    call = functools.partial(attend, bias, few)
-    begun = call((2, 3), asked, [half_a], near=near, finish=False)
+    call = functools.partial(attend, bias)
+    begun = call((2, 3), query_b, [half_a], near=near, finish=False)
     keep_b, send_b = call((2, 3), query_b, [half_b], begun=begun)
     other_b = swap(send_b, 1)
     leaving = mix(keep_b, other_b, wo, wo_beside, BF16)

time: 58.3 us -> 83.8 us (1.44)
  blocking collectives: 0 us -> 20.9 us
  local copies, waits for them, and re-layouts: 0.01 us -> 11.1 us
  starting transfers between devices: 19 us -> 8.41 us
  Pallas kernels: 19.3 us -> 22.5 us
    all_to_all x0 -> x1, blocking collectives: none -> 20.9 us  [spread(): return lax.all_to_all(copies, 'seq', 0, 0)]
    ppermute x17 -> x7, starting transfers between devices: 19 us -> 4.77 us  [swap(): return lax.ppermute(array, axis, [(i, i ^ bit) for i in range(count)])]
    unnamed x6 -> x58, local copies, waits for them, and re-layouts: 0.01 us -> 10.1 us
    all_to_all x0 -> x1, waiting for transfers between devices: none -> 4.31 us  [spread(): return lax.all_to_all(copies, 'seq', 0, 0)]
    ppermute x17 -> x7, waiting for transfers between devices: 18.6 us -> 14.7 us  [swap(): return lax.ppermute(array, axis, [(i, i ^ bit) for i in range(count)])]
    all_to_all x0 -> x1, starting transfers between devices: none -> 3.64 us  [spread(): return lax.all_to_all(copies, 'seq', 0, 0)]
    pallas_call x2, Pallas kernels: 1.48 us -> 4.7 us  [mix(): pl.pallas_call(mix_kernel, in_specs=[IN_VMEM] * 4, out_specs=IN_VMEM, out...]
    broadcast_in_dim x0 -> x2, local copies, waits for them, and re-layouts: none -> 0.99 us  [spread(): copies = jnp.broadcast_to(kept[None], (seqs, *kept.shape))]
  transfers between devices with their start and end apart: 17 -> 8, of which waited for: 7 -> 6; matrix products, arithmetic and copies ran while one was open for 0% -> 1% of each run, Pallas kernels for 32% -> 22%
where the time goes in v6:
time: 83.8 us; the launch traced here: 83.2 us
  Pallas kernels  22.5 us (27%)
  blocking collectives  20.9 us (25%)
  waiting for transfers between devices  19 us (23%)
  local copies, waits for them, and re-layouts  11.1 us (13%)
  starting transfers between devices  8.41 us (10%)
  other arithmetic  0.98 us (1%)
    all_to_all x1, blocking collectives, spread(): return lax.all_to_all(copies, 'seq', 0, 0)  20.9 us
    ppermute x7, waiting for transfers between devices, swap(): return lax.ppermute(array, axis, [(i, i ^ bit) for i in range(count)])  14.7 us
    unnamed x58, local copies, waits for them, and re-layouts  10.1 us
    pallas_call x3, Pallas kernels, attend(): pl.pallas_call(functools.partial(attend_kernel, relative, near is not Non...  8.46 us
    ppermute x7, starting transfers between devices, swap(): return lax.ppermute(array, axis, [(i, i ^ bit) for i in range(count)])  4.77 us
    pallas_call x2, Pallas kernels, mix(): pl.pallas_call(mix_kernel, in_specs=[IN_VMEM] * 4, out_specs=IN_VMEM, out...  4.7 us
    all_to_all x1, waiting for transfers between devices, spread(): return lax.all_to_all(copies, 'seq', 0, 0)  4.31 us
    all_to_all x1, starting transfers between devices, spread(): return lax.all_to_all(copies, 'seq', 0, 0)  3.64 us
  transfers between devices with their start and end apart: 8, of which 6 were waited for; matrix products, arithmetic and copies ran while one was open for 1% of the time, Pallas kernels for 22%

profile of v6, /device:TPU:0, one launch (start us, length us, event | category | flops | bytes accessed | tf_op | source)
XLA Modules:
  0.0 83.2 jit_solution(15160142321503599969)
XLA Ops:
  0.5 2.5 %collective-permute-start.1 = (bf16[128,2048]{1,0:T(8,128)(2,1)}, bf16[128,2048]{1,0:T(8,128)(2,1)S(1)}, u32[]{:S(2)}, u32[]{:S(2)}) collective-permute-start(bf16[128,2048]{1,0:T(8,128)(2,1)} %rows_hbm.1), channel_id=1, source_target_pairs={{0,2},{1,3},{2,0},{3,1},{4,6},{5,7},{6,4},{7,5},{8,10},{9,11},{10,... | collective-permute-start | bytes 1572872 | tf_op jit(solution)/shard_map/ppermute | solution.py:396
  2.9 3.1 %shard_map.73 = (bf16[128,2048]{1,0:T(8,128)(2,1)S(1)}, bf16[2048,512]{1,0:T(8,128)(2,1)S(1)}, bf16[2048,512]{1,0:T(8,128)(2,1)S(1)}, bf16[128,512]{1,0:T(8,128)(2,1)S(1)}, bf16[128,512]{1,0:T(8,128)(2,1)S(1)}) custom-call(bf16[128,2048]{1,0:T(8,128)(2,1)} %rows_hbm.1, bf16[2048,512]{1,0:T(8,128)(2,1)} %wk_hbm.1, bf16[2048,512]{1,0:T(8,128)(2,1)} %wv_hbm.1), custom_call_target="tpu_custom_call" | custom-call | flops 536870912 | bytes 4194304 | tf_op jit(solution)/shard_map/pallas_call | solution.py:94
  6.1 0.9 %shard_map.74 = (bf16[128,512]{1,0:T(8,128)(2,1)S(1)}, bf16[128,512]{1,0:T(8,128)(2,1)S(1)}, bf16[2,4,32,128]{3,2,1,0:T(8,128)(2,1)S(1)}) custom-call(bf16[128,2048]{1,0:T(8,128)(2,1)S(1)} %collective-permute-done.rows.rows_1, bf16[2048,512]{1,0:T(8,128)(2,1)S(1)} %get-tuple-element.29.wk, bf16[2048,512]{1,0:T(8,128)(2,1)S(1)} %get-tuple-element.30.wv, ...), custom_call_target="tpu_custom_call" | custom-call | flops 536870912 | bytes 524288 | tf_op jit(solution)/shard_map/pallas_call | solution.py:126
  7.7 2.6 %shard_map.76 = (bf16[256,512]{1,0:T(8,128)(2,1)S(1)}, bf16[2048,512]{1,0:T(8,128)(2,1)S(1)}, bf16[512,2048]{1,0:T(8,128)(2,1)S(1)}) custom-call(bf16[128,2048]{1,0:T(8,128)(2,1)S(1)} %get-tuple-element.35.rows_0, bf16[128,2048]{1,0:T(8,128)(2,1)S(1)} %collective-permute-done.rows.rows_1, bf16[2048,512]{1,0:T(8,128)(2,1)} %wq_hbm.1, bf16[512,2048]{1,0:T(8,128)(2,1)} %w_hbm.1), custom_call_target="tpu_custom_call" | custom-call | flops 536870912 | bytes 4194304 | tf_op jit(solution)/shard_map/pallas_call | solution.py:155
  10.4 0.7 copy-done.25
  11.1 4.7 %collective-permute-done.1.rows_0 = bf16[128,2048]{1,0:T(8,128)(2,1)S(1)} collective-permute-done((bf16[128,2048]{1,0:T(8,128)(2,1)}, bf16[128,2048]{1,0:T(8,128)(2,1)S(1)}, u32[]{:S(2)}, u32[]{:S(2)}) %collective-permute-start.1) | collective-permute-done | bytes 524320 | tf_op jit(solution)/shard_map/ppermute | solution.py:396
  15.8 1.9 %collective-permute-done.2.rows_1 = bf16[128,2048]{1,0:T(8,128)(2,1)S(1)} collective-permute-done((bf16[128,2048]{1,0:T(8,128)(2,1)S(1)}, bf16[128,2048]{1,0:T(8,128)(2,1)S(1)}, u32[]{:S(2)}, u32[]{:S(2)}) %collective-permute-start.2) | collective-permute-done | bytes 524320 | tf_op jit(solution)/shard_map/ppermute | solution.py:396
  17.7 1.4 %shard_map.78 = (bf16[256,512]{1,0:T(8,128)(2,1)S(1)}, bf16[256,512]{1,0:T(8,128)(2,1)S(1)}, bf16[2,4,32,128]{3,2,1,0:T(8,128)(2,1)S(1)}) custom-call(bf16[128,2048]{1,0:T(8,128)(2,1)S(1)} %collective-permute-done.1.rows_0, bf16[128,2048]{1,0:T(8,128)(2,1)S(1)} %collective-permute-done.2.rows_1, bf16[2048,512]{1,0:T(8,128)(2,1)S(1)} %get-tuple-element.29.wk, ...), custom_call_target="tpu_custom_call" | custom-call | flops 1073741824 | bytes 1048576 | tf_op jit(solution)/shard_map/pallas_call | solution.py:206
  19.1 0.7 copy-done.12
  20.0 20.9 %all_to_all.10.refs_7_ = bf16[8,2,4,32,128]{4,3,2,1,0:T(8,128)(2,1)S(1)} all-to-all(bf16[8,2,4,32,128]{4,3,2,1,0:T(8,128)(2,1)S(1)} %broadcast_in_dim.20), channel_id=1, replica_groups=mesh['seq'=8,'sub'=4] {'seq'}, dimensions={0} | all-to-all | bytes 1048576 | tf_op jit(solution)/shard_map/all_to_all | solution.py:405
  40.9 0.9 %broadcast_in_dim.21 = bf16[8,2,4,32,128]{4,3,2,1,0:T(8,128)(2,1)} broadcast(bf16[2,4,32,128]{3,2,1,0:T(8,128)(2,1)S(1)} %get-tuple-element.45), dimensions={1,2,3,4} | broadcast | bytes 589824 | tf_op jit(solution)/shard_map/broadcast_in_dim | solution.py:404
  41.8 3.6 %all-to-all-start.1 = ((bf16[8,2,4,32,128]{4,3,2,1,0:T(8,128)(2,1)}), bf16[8,2,4,32,128]{4,3,2,1,0:T(8,128)(2,1)S(1)}, u32[]{:S(2)}, u32[]{:S(2)}) async-start(bf16[8,2,4,32,128]{4,3,2,1,0:T(8,128)(2,1)} %broadcast_in_dim.21), calls=%async_computation.1 | async-start | bytes 1048576 | tf_op jit(solution)/shard_map/all_to_all | solution.py:405
  45.5 1.0 %copy-done.1 = bf16[128,2048]{1,0:T(8,128)(2,1)S(1)} copy-done((bf16[128,2048]{1,0:T(8,128)(2,1)S(1)}, bf16[128,2048]{1,0:T(8,128)(2,1)}, u32[]{:S(2)}) %copy-start.1) | copy-done | bytes 524312
  46.5 1.0 %copy-done.3 = bf16[128,2048]{1,0:T(8,128)(2,1)S(1)} copy-done((bf16[128,2048]{1,0:T(8,128)(2,1)S(1)}, bf16[128,2048]{1,0:T(8,128)(2,1)}, u32[]{:S(2)}) %copy-start.3) | copy-done | bytes 524312
  47.6 1.6 %copy-done.5 = bf16[2048,512]{1,0:T(8,128)(2,1)S(1)} copy-done((bf16[2048,512]{1,0:T(8,128)(2,1)S(1)}, bf16[2048,512]{1,0:T(8,128)(2,1)}, u32[]{:S(2)}) %copy-start.5) | copy-done | bytes 2097176
  49.2 0.7 shard_map.77.refs_0_
  50.3 0.9 %copy-done.7 = bf16[128,512]{1,0:T(8,128)(2,1)S(1)} copy-done((bf16[128,512]{1,0:T(8,128)(2,1)S(1)}, bf16[128,512]{1,0:T(8,128)(2,1)}, u32[]{:S(2)}) %copy-start.7) | copy-done | bytes 131096
  51.2 2.9 %shard_map.79 = (f32[256,512]{1,0:T(8,128)S(1)}, f32[4,256,128]{2,1,0:T(8,128)S(1)}) custom-call(f32[4,1024]{1,0:T(4,128)S(1)} %shard_map.75.bias, bf16[256,512]{1,0:T(8,128)(2,1)S(1)} %shard_map.77.refs_0_, bf16[128,512]{1,0:T(8,128)(2,1)S(1)} %get-tuple-element.31.keys_0.refs_1_, bf16[128,512]{1,0:T(8,128)(2,1)S(1)} %copy-done.16, ...), custom_call_target="tpu_custom_call" | custom-call | flops 402653184 | bytes 524288 | tf_op jit(solution)/shard_map/pallas_call | solution.py:354
  54.1 0.8 copy-done.21
  54.9 0.8 copy-done.23
  55.7 4.3 %all-to-all-done.1.refs_3_.refs_8_ = bf16[8,2,4,32,128]{4,3,2,1,0:T(8,128)(2,1)S(1)} async-done(((bf16[8,2,4,32,128]{4,3,2,1,0:T(8,128)(2,1)}), bf16[8,2,4,32,128]{4,3,2,1,0:T(8,128)(2,1)S(1)}, u32[]{:S(2)}, u32[]{:S(2)}) %all-to-all-start.1) | async-done | bytes 524320 | tf_op jit(solution)/shard_map/all_to_all | solution.py:405
  60.1 1.0 %copy-done.22 = f32[256,512]{1,0:T(8,128)S(1)} copy-done((f32[256,512]{1,0:T(8,128)S(1)}, f32[256,512]{1,0:T(8,128)}, u32[]{:S(2)}) %copy-start.22) | copy-done | bytes 524312
  61.1 1.0 %copy-done.24 = f32[4,256,128]{2,1,0:T(8,128)S(1)} copy-done((f32[4,256,128]{2,1,0:T(8,128)S(1)}, f32[4,256,128]{2,1,0:T(8,128)}, u32[]{:S(2)}) %copy-start.24) | copy-done | bytes 524312
  62.1 2.3 %shard_map.80 = (bf16[128,512]{1,0:T(8,128)(2,1)S(1)}, bf16[128,512]{1,0:T(8,128)(2,1)S(1)}) custom-call(f32[4,1024]{1,0:T(4,128)S(1)} %shard_map.75.bias, bf16[256,512]{1,0:T(8,128)(2,1)S(1)} %shard_map.77.refs_0_, f32[256,512]{1,0:T(8,128)S(1)} %copy-done.22, f32[4,256,128]{2,1,0:T(8,128)S(1)} %copy-done.24, ...), custom_call_target="tpu_custom_call" | custom-call | flops 134217728 | bytes 524288 | tf_op jit(solution)/shard_map/pallas_call | solution.py:354
  64.5 1.3 %collective-permute-done.3.rows_1 = bf16[128,512]{1,0:T(8,128)(2,1)S(1)} collective-permute-done((bf16[128,512]{1,0:T(8,128)(2,1)S(1)}, bf16[128,512]{1,0:T(8,128)(2,1)S(1)}, u32[]{:S(2)}, u32[]{:S(2)}) %collective-permute-start.3) | collective-permute-done | bytes 131104 | tf_op jit(solution)/shard_map/ppermute | solution.py:396
  65.9 2.4 %shard_map.81 = bf16[128,2048]{1,0:T(8,128)(2,1)S(1)} custom-call(bf16[128,512]{1,0:T(8,128)(2,1)S(1)} %get-tuple-element.46.rows_0, bf16[128,512]{1,0:T(8,128)(2,1)S(1)} %collective-permute-done.3.rows_1, bf16[512,2048]{1,0:T(8,128)(2,1)S(1)} %get-tuple-element.48.weight_0, bf16[512,2048]{1,0:T(8,128)(2,1)} %collective-permute-done.4.weight_1), custom_call_target="tpu_custom_call" | custom-call | flops 536870912 | bytes 1048576 | tf_op jit(solution)/shard_map/pallas_call | solution.py:379
  68.3 1.6 %collective-permute-start.6 = (bf16[128,2048]{1,0:T(8,128)(2,1)S(1)}, bf16[128,2048]{1,0:T(8,128)(2,1)S(1)}, u32[]{:S(2)}, u32[]{:S(2)}) collective-permute-start(bf16[128,2048]{1,0:T(8,128)(2,1)S(1)} %shard_map.81), channel_id=1, source_target_pairs={{0,2},{1,3},{2,0},{3,1},{4,6},{5,7},{6,4},{7,5},{8,10},{9,11},{10,... | collective-permute-start | bytes 1572872 | tf_op jit(solution)/shard_map/ppermute | solution.py:396
  69.9 3.2 %shard_map.82 = (bf16[128,512]{1,0:T(8,128)(2,1)S(1)}, bf16[128,512]{1,0:T(8,128)(2,1)S(1)}) custom-call(f32[4,1024]{1,0:T(4,128)S(1)} %shard_map.75.bias, bf16[256,512]{1,0:T(8,128)(2,1)S(1)} %copy-done.26, bf16[128,512]{1,0:T(8,128)(2,1)S(1)} %get-tuple-element.31.keys_0.refs_1_, bf16[128,512]{1,0:T(8,128)(2,1)S(1)} %copy-done.17, ...), custom_call_target="tpu_custom_call" | custom-call | flops 536870912 | bytes 524288 | tf_op jit(solution)/shard_map/pallas_call | solution.py:354
  73.2 1.3 %collective-permute-done.5.rows_1 = bf16[128,512]{1,0:T(8,128)(2,1)S(1)} collective-permute-done((bf16[128,512]{1,0:T(8,128)(2,1)S(1)}, bf16[128,512]{1,0:T(8,128)(2,1)S(1)}, u32[]{:S(2)}, u32[]{:S(2)}) %collective-permute-start.5) | collective-permute-done | bytes 131104 | tf_op jit(solution)/shard_map/ppermute | solution.py:396
  74.5 2.3 %shard_map.83 = f32[128,2048]{1,0:T(8,128)S(1)} custom-call(bf16[128,512]{1,0:T(8,128)(2,1)S(1)} %get-tuple-element.51.rows_0, bf16[128,512]{1,0:T(8,128)(2,1)S(1)} %collective-permute-done.5.rows_1, bf16[512,2048]{1,0:T(8,128)(2,1)S(1)} %get-tuple-element.48.weight_0, bf16[512,2048]{1,0:T(8,128)(2,1)} %collective-permute-done.4.weight_1), custom_call_target="tpu_custom_call" | custom-call | flops 536870912 | bytes 1048576 | tf_op jit(solution)/shard_map/pallas_call | solution.py:379
  76.8 5.5 %collective-permute-done.6 = bf16[128,2048]{1,0:T(8,128)(2,1)S(1)} collective-permute-done((bf16[128,2048]{1,0:T(8,128)(2,1)S(1)}, bf16[128,2048]{1,0:T(8,128)(2,1)S(1)}, u32[]{:S(2)}, u32[]{:S(2)}) %collective-permute-start.6) | collective-permute-done | bytes 524320 | tf_op jit(solution)/shard_map/ppermute | solution.py:396
  82.3 0.9 %add_convert_fusion = bf16[128,2048]{1,0:T(8,128)(2,1)} fusion(f32[128,2048]{1,0:T(8,128)S(1)} %shard_map.83, bf16[128,2048]{1,0:T(8,128)(2,1)S(1)} %collective-permute-done.6), kind=kLoop, calls=%fused_computation | loop fusion | flops 786432 | bytes 2097152 | tf_op jit(solution)/shard_map/convert_element_type | solution.py:433
  (58 shorter events, 2.0 us)
Async XLA Ops:
  0.0 6.1 %collective-permute-start = (bf16[128,2048]{1,0:T(8,128)(2,1)}, bf16[128,2048]{1,0:T(8,128)(2,1)S(1)}, u32[]{:S(2)}, u32[]{:S(2)}) collective-permute-start(bf16[128,2048]{1,0:T(8,128)(2,1)} %rows_hbm.1), channel_id=1, source_target_pairs={{0,1},{1,0},{2,3},{3,2},{4,5},{5,4},{6,7},{7,6},{8,9},{9,8},{10,11... | collective-permute-start | bytes 1572872 | tf_op jit(solution)/shard_map/ppermute | solution.py:396
  0.5 15.3 %collective-permute-start.1 = (bf16[128,2048]{1,0:T(8,128)(2,1)}, bf16[128,2048]{1,0:T(8,128)(2,1)S(1)}, u32[]{:S(2)}, u32[]{:S(2)}) collective-permute-start(bf16[128,2048]{1,0:T(8,128)(2,1)} %rows_hbm.1), channel_id=1, source_target_pairs={{0,2},{1,3},{2,0},{3,1},{4,6},{5,7},{6,4},{7,5},{8,10},{9,11},{10,... | collective-permute-start | bytes 1572872 | tf_op jit(solution)/shard_map/ppermute | solution.py:396
  2.9 3.2 %copy-start.27 = (s32[4,128]{1,0:T(4,128)S(1)}, s32[4,128]{1,0:T(4,128)}, u32[]{:S(2)}) copy-start(s32[4,128]{1,0:T(4,128)} %pattern.3) | copy-start | bytes 6148
  6.1 0.9 %copy-start.6 = (bf16[128,512]{1,0:T(8,128)(2,1)}, bf16[128,512]{1,0:T(8,128)(2,1)S(1)}, u32[]{:S(2)}) copy-start(bf16[128,512]{1,0:T(8,128)(2,1)S(1)} %get-tuple-element.32.values_0.refs_4_) | copy-start | bytes 393220
  7.0 3.4 %copy-start.15 = (bf16[128,512]{1,0:T(8,128)(2,1)}, bf16[128,512]{1,0:T(8,128)(2,1)S(1)}, u32[]{:S(2)}) copy-start(bf16[128,512]{1,0:T(8,128)(2,1)S(1)} %get-tuple-element.39.refs_2_) | copy-start | bytes 393220
  7.0 3.4 %copy-start.18 = (bf16[128,512]{1,0:T(8,128)(2,1)}, bf16[128,512]{1,0:T(8,128)(2,1)S(1)}, u32[]{:S(2)}) copy-start(bf16[128,512]{1,0:T(8,128)(2,1)S(1)} %get-tuple-element.41.refs_5_) | copy-start | bytes 393220
  11.1 8.0 %copy-start.4 = (bf16[2048,512]{1,0:T(8,128)(2,1)}, bf16[2048,512]{1,0:T(8,128)(2,1)S(1)}, u32[]{:S(2)}) copy-start(bf16[2048,512]{1,0:T(8,128)(2,1)S(1)} %get-tuple-element.38.wq) | copy-start | bytes 6291460
  15.7 3.3 %copy-start = (bf16[128,2048]{1,0:T(8,128)(2,1)}, bf16[128,2048]{1,0:T(8,128)(2,1)S(1)}, u32[]{:S(2)}) copy-start(bf16[128,2048]{1,0:T(8,128)(2,1)S(1)} %collective-permute-done.1.rows_0) | copy-start | bytes 1572868
  15.7 1.9 %collective-permute-start.2 = (bf16[128,2048]{1,0:T(8,128)(2,1)S(1)}, bf16[128,2048]{1,0:T(8,128)(2,1)S(1)}, u32[]{:S(2)}, u32[]{:S(2)}) collective-permute-start(bf16[128,2048]{1,0:T(8,128)(2,1)S(1)} %collective-permute-done.1.rows_0), channel_id=1, source_target_pairs={{0,1},{1,0},{2,3},{3,2},{4,5},{5,4},{6,7},{7,6},{8,9},{9,8},{10,11... | collective-permute-start | bytes 1572872 | tf_op jit(solution)/shard_map/ppermute | solution.py:396
  17.7 1.4 %copy-start.2 = (bf16[128,2048]{1,0:T(8,128)(2,1)}, bf16[128,2048]{1,0:T(8,128)(2,1)S(1)}, u32[]{:S(2)}) copy-start(bf16[128,2048]{1,0:T(8,128)(2,1)S(1)} %collective-permute-done.2.rows_1) | copy-start | bytes 1572868
  19.8 25.7 %copy-start.9 = (bf16[256,512]{1,0:T(8,128)(2,1)}, bf16[256,512]{1,0:T(8,128)(2,1)S(1)}, u32[]{:S(2)}) copy-start(bf16[256,512]{1,0:T(8,128)(2,1)S(1)} %get-tuple-element.40.refs_3_) | copy-start | bytes 786436
  19.8 46.1 %collective-permute-start.4 = (bf16[512,2048]{1,0:T(8,128)(2,1)}, bf16[512,2048]{1,0:T(8,128)(2,1)}, u32[]{:S(2)}, u32[]{:S(2)}) collective-permute-start(bf16[512,2048]{1,0:T(8,128)(2,1)} %w_hbm.1), channel_id=1, source_target_pairs={{0,1},{1,0},{2,3},{3,2},{4,5},{5,4},{6,7},{7,6},{8,9},{9,8},{10,11... | collective-permute-start | bytes 6291464 | tf_op jit(solution)/shard_map/ppermute | solution.py:396
  41.8 18.2 %all-to-all-start.1 = ((bf16[8,2,4,32,128]{4,3,2,1,0:T(8,128)(2,1)}), bf16[8,2,4,32,128]{4,3,2,1,0:T(8,128)(2,1)S(1)}, u32[]{:S(2)}, u32[]{:S(2)}) async-start(bf16[8,2,4,32,128]{4,3,2,1,0:T(8,128)(2,1)} %broadcast_in_dim.21), calls=%async_computation.1 | async-start | bytes 1048576 | tf_op jit(solution)/shard_map/all_to_all | solution.py:405
  45.5 1.0 %copy-start.1 = (bf16[128,2048]{1,0:T(8,128)(2,1)S(1)}, bf16[128,2048]{1,0:T(8,128)(2,1)}, u32[]{:S(2)}) copy-start(bf16[128,2048]{1,0:T(8,128)(2,1)} %copy-done) | copy-start | bytes 1572868
  46.5 1.0 %copy-start.3 = (bf16[128,2048]{1,0:T(8,128)(2,1)S(1)}, bf16[128,2048]{1,0:T(8,128)(2,1)}, u32[]{:S(2)}) copy-start(bf16[128,2048]{1,0:T(8,128)(2,1)} %copy-done.2) | copy-start | bytes 1572868
  47.6 1.6 %copy-start.5 = (bf16[2048,512]{1,0:T(8,128)(2,1)S(1)}, bf16[2048,512]{1,0:T(8,128)(2,1)}, u32[]{:S(2)}) copy-start(bf16[2048,512]{1,0:T(8,128)(2,1)} %copy-done.4) | copy-start | bytes 6291460
  49.2 0.9 %copy-start.10 = (bf16[256,512]{1,0:T(8,128)(2,1)S(1)}, bf16[256,512]{1,0:T(8,128)(2,1)}, u32[]{:S(2)}) copy-start(bf16[256,512]{1,0:T(8,128)(2,1)} %copy-done.9) | copy-start | bytes 786436
  49.2 1.0 %copy-start.13 = (bf16[256,512]{1,0:T(8,128)(2,1)S(1)}, bf16[256,512]{1,0:T(8,128)(2,1)}, u32[]{:S(2)}) copy-start(bf16[256,512]{1,0:T(8,128)(2,1)} %copy-done.12) | copy-start | bytes 786436
  49.2 1.1 %copy-start.16 = (bf16[128,512]{1,0:T(8,128)(2,1)S(1)}, bf16[128,512]{1,0:T(8,128)(2,1)}, u32[]{:S(2)}) copy-start(bf16[128,512]{1,0:T(8,128)(2,1)} %copy-done.15) | copy-start | bytes 393220
  49.2 1.1 %copy-start.19 = (bf16[128,512]{1,0:T(8,128)(2,1)S(1)}, bf16[128,512]{1,0:T(8,128)(2,1)}, u32[]{:S(2)}) copy-start(bf16[128,512]{1,0:T(8,128)(2,1)} %copy-done.18) | copy-start | bytes 393220
  50.3 0.9 %copy-start.7 = (bf16[128,512]{1,0:T(8,128)(2,1)S(1)}, bf16[128,512]{1,0:T(8,128)(2,1)}, u32[]{:S(2)}) copy-start(bf16[128,512]{1,0:T(8,128)(2,1)} %copy-done.6) | copy-start | bytes 393220
  60.0 1.0 %copy-start.22 = (f32[256,512]{1,0:T(8,128)S(1)}, f32[256,512]{1,0:T(8,128)}, u32[]{:S(2)}) copy-start(f32[256,512]{1,0:T(8,128)} %copy-done.21) | copy-start | bytes 1572868
  61.1 1.0 %copy-start.24 = (f32[4,256,128]{2,1,0:T(8,128)S(1)}, f32[4,256,128]{2,1,0:T(8,128)}, u32[]{:S(2)}) copy-start(f32[4,256,128]{2,1,0:T(8,128)} %copy-done.23) | copy-start | bytes 1572868
  64.4 1.4 %collective-permute-start.3 = (bf16[128,512]{1,0:T(8,128)(2,1)S(1)}, bf16[128,512]{1,0:T(8,128)(2,1)S(1)}, u32[]{:S(2)}, u32[]{:S(2)}) collective-permute-start(bf16[128,512]{1,0:T(8,128)(2,1)S(1)} %get-tuple-element.47), channel_id=1, source_target_pairs={{0,1},{1,0},{2,3},{3,2},{4,5},{5,4},{6,7},{7,6},{8,9},{9,8},{10,11... | collective-permute-start | bytes 393224 | tf_op jit(solution)/shard_map/ppermute | solution.py:396
  65.8 4.0 %copy-start.8 = (bf16[128,512]{1,0:T(8,128)(2,1)S(1)}, bf16[128,512]{1,0:T(8,128)(2,1)}, u32[]{:S(2)}) copy-start(bf16[128,512]{1,0:T(8,128)(2,1)} %copy-done.6) | copy-start | bytes 393220
  65.8 4.0 %copy-start.11 = (bf16[256,512]{1,0:T(8,128)(2,1)S(1)}, bf16[256,512]{1,0:T(8,128)(2,1)}, u32[]{:S(2)}) copy-start(bf16[256,512]{1,0:T(8,128)(2,1)} %copy-done.9) | copy-start | bytes 786436
  65.8 4.0 %copy-start.14 = (bf16[256,512]{1,0:T(8,128)(2,1)S(1)}, bf16[256,512]{1,0:T(8,128)(2,1)}, u32[]{:S(2)}) copy-start(bf16[256,512]{1,0:T(8,128)(2,1)} %copy-done.12) | copy-start | bytes 786436
  65.9 4.0 %copy-start.17 = (bf16[128,512]{1,0:T(8,128)(2,1)S(1)}, bf16[128,512]{1,0:T(8,128)(2,1)}, u32[]{:S(2)}) copy-start(bf16[128,512]{1,0:T(8,128)(2,1)} %copy-done.15) | copy-start | bytes 393220
  65.9 4.0 %copy-start.20 = (bf16[128,512]{1,0:T(8,128)(2,1)S(1)}, bf16[128,512]{1,0:T(8,128)(2,1)}, u32[]{:S(2)}) copy-start(bf16[128,512]{1,0:T(8,128)(2,1)} %copy-done.18) | copy-start | bytes 393220
  65.9 4.0 %copy-start.26 = (bf16[256,512]{1,0:T(8,128)(2,1)S(1)}, bf16[256,512]{1,0:T(8,128)(2,1)}, u32[]{:S(2)}) copy-start(bf16[256,512]{1,0:T(8,128)(2,1)} %copy-done.25) | copy-start | bytes 786436
  68.3 14.0 %collective-permute-start.6 = (bf16[128,2048]{1,0:T(8,128)(2,1)S(1)}, bf16[128,2048]{1,0:T(8,128)(2,1)S(1)}, u32[]{:S(2)}, u32[]{:S(2)}) collective-permute-start(bf16[128,2048]{1,0:T(8,128)(2,1)S(1)} %shard_map.81), channel_id=1, source_target_pairs={{0,2},{1,3},{2,0},{3,1},{4,6},{5,7},{6,4},{7,5},{8,10},{9,11},{10,... | collective-permute-start | bytes 1572872 | tf_op jit(solution)/shard_map/ppermute | solution.py:396
  73.1 1.4 %collective-permute-start.5 = (bf16[128,512]{1,0:T(8,128)(2,1)S(1)}, bf16[128,512]{1,0:T(8,128)(2,1)S(1)}, u32[]{:S(2)}, u32[]{:S(2)}) collective-permute-start(bf16[128,512]{1,0:T(8,128)(2,1)S(1)} %get-tuple-element.52), channel_id=1, source_target_pairs={{0,1},{1,0},{2,3},{3,2},{4,5},{5,4},{6,7},{7,6},{8,9},{9,8},{10,11... | collective-permute-start | bytes 393224 | tf_op jit(solution)/shard_map/ppermute | solution.py:396
  (5 other events, 3.9 us)

commit v7 on v5

--- a/solution.py
+++ b/solution.py
@@ -22,7 +22,7 @@
 IN_HBM = pl.BlockSpec(memory_space=pltpu.HBM)
 IN_SMEM = pl.BlockSpec(memory_space=pltpu.SMEM)
 Y_BIT = 1
-Z_BITS = (2, 4, 6)
+Z_BITS = (4, 6, 2)
 
 
 def dot(a, b):
@@ -39,7 +39,9 @@
 
 def cost(flops, bytes_accessed, transcendentals=0):
     return pl.CostEstimate(
-        flops=flops, bytes_accessed=bytes_accessed, transcendentals=transcendentals
+        flops=flops // 100,
+        bytes_accessed=bytes_accessed // 100,
+        transcendentals=transcendentals // 100,
     )
 
 
@@ -188,31 +190,23 @@
     )(rows_0, rows_1, wq)
 
 
-def third_kernel(rows_0, rows_1, wk, wv, pattern, keys, values, kept):
-    rows = jnp.concatenate([rows_0[...], rows_1[...]], axis=0)
+def across_kernel(rows, wk, wv, keys, values):
     for part in halves_of(wk.shape[1]):
-        keys[:, part] = dot(rows, wk[:, part]).astype(BF16)
-        values[:, part] = dot(rows, wv[:, part]).astype(BF16)
-
-    def block(where):
-        return lambda head: (head_of(keys, head, where), head_of(values, head, where))
-
-    blocks = [block(slice(i * BLOCK, (i + 1) * BLOCK)) for i in range(BLOCKS_HALF)]
-    pick_dilated(pattern, blocks, kept)
-
-
-def third(rows_0, rows_1, wk, wv, pattern):
-    count, depth = rows_0.shape
+        keys[:, part] = dot(rows[...], wk[:, part]).astype(BF16)
+        values[:, part] = dot(rows[...], wv[:, part]).astype(BF16)
+
+
+def keys_and_values(rows, wk, wv):
+    count, depth = rows.shape
     width = wk.shape[1]
-    kept = (2, width // HEAD_SIZE, FAR_ROWS, HEAD_SIZE)
-    return pl.pallas_call(
-        third_kernel,
-        in_specs=[IN_VMEM] * 5,
-        out_specs=[IN_VMEM] * 3,
-        out_shape=[shape((2 * count, width))] * 2 + [shape(kept)],
-        compiler_params=params(),
-        cost_estimate=cost(8 * count * depth * width, 4 * count * depth),
-    )(rows_0, rows_1, wk, wv, pattern)
+    return pl.pallas_call(
+        across_kernel,
+        in_specs=[IN_VMEM] * 3,
+        out_specs=[IN_VMEM] * 2,
+        out_shape=[shape((count, width))] * 2,
+        compiler_params=params(),
+        cost_estimate=cost(4 * count * depth * width, 2 * count * depth),
+    )(rows, wk, wv)
 
 
 def slide_of(place, slides, block):
@@ -238,7 +232,11 @@
     column = lax.broadcasted_iota(jnp.int32, (1, count), 1)
     far = column // FAR_ROWS
     if few:
-        far = far ^ span
+        order = [bit | y for y in (0, Y_BIT) for bit in (0, *Z_BITS)]
+        place_of = jnp.zeros_like(far)
+        for index, bits in enumerate(order):
+            place_of = jnp.where(far == index, bits, place_of)
+        far = place_of ^ span
     upper = (column // DILATED_KEPT) % BLOCKS_HALF
     for half in range(subs // BLOCKS_HALF):
         place_0, place_1 = sub ^ (half * BLOCKS_HALF), sub ^ (half * BLOCKS_HALF + 1)
@@ -278,28 +276,26 @@
 
 
 def far_group(refs, head):
-    mine, along_z, along_y, beyond = refs
-    found = []
-    for slot in range(2):
-        pieces = [mine[slot, head], along_y[slot, head]]
-        for step in range(len(Z_BITS)):
-            pieces += [along_z[step, slot, head], beyond[step, slot, head]]
-        found.append(jnp.concatenate(pieces, axis=0))
-    return found
+    return [
+        jnp.concatenate(
+            [ref[step, slot, head] for ref in refs for step in range(GROUP // 2)], axis=0
+        )
+        for slot in range(2)
+    ]
 
 
 def attend_kernel(relative, near, halves, few, finish, bias, *refs):
     refs = list(refs)
     queries = refs.pop(0)
     if near:
-        keys, values = refs[0:3], refs[3:6]
-        del refs[:6]
+        keys, values = refs[0:4], refs[4:8]
+        del refs[:8]
     else:
         gathered_in, stats_in = refs[0:2]
         del refs[:2]
     far = []
     for half in halves:
-        size = 4 if few else 1
+        size = 2 if few else 1
         far.append((half, refs[:size]))
         del refs[:size]
     span = bias.shape[0] * BLOCK
@@ -419,11 +415,11 @@
         return lax.optimization_barrier((array, *others))[0]
 
     def first_round(kept):
-        return [swap(kept, bit, "seq") for bit in Z_BITS], swap(kept, Y_BIT, "seq")
-
-    def second_round(kept, along_z, along_y):
-        along_z = jnp.stack(along_z)
-        return [kept, along_z, along_y, swap(along_z, Y_BIT, "seq")]
+        return [swap(kept, bit, "seq") for bit in Z_BITS]
+
+    def second_round(kept, along_z):
+        column = jnp.stack([kept, *along_z])
+        return [column, swap(column, Y_BIT, "seq")]
 
     across = swap(normed, 2)
     beside = swap(normed, 1)
@@ -432,31 +428,30 @@
     place = jnp.concatenate([after(slide_lengths, kept_a), *axes])
     bias = make_bias(place, slides, subs, seqs, few)
     query_a, wq, wo = query_first(mine, beside, w_query, w_out)
+    wo_beside = swap(w_out, 1)
     if few:
-        along_z, along_y = first_round(kept_a)
-        *along_z, along_y, query_a, bias = lax.optimization_barrier(
-            (*along_z, along_y, query_a, bias)
-        )
-        half_a = 0, second_round(kept_a, along_z, along_y)
-        across = after(across, half_a[1][1])
+        along_z = first_round(kept_a)
+        *along_z, query_a, bias = lax.optimization_barrier((*along_z, query_a, bias))
+        half_a = 0, second_round(kept_a, along_z)
+        across = after(across, half_a[1][0], wo_beside)
     else:
         half_a = 0, [lax.all_gather(kept_a, "seq", axis=0)]
+    wo_beside = pltpu.with_memory_space_constraint(wo_beside, pltpu.VMEM)
     beyond = swap(across, 1)
-    keys_2, values_2, kept_b = third(across, beyond, wk, wv, pattern)
+    keys_2, values_2 = keys_and_values(across, wk, wv)
+    keys_3, values_3, kept_b = second(after(beyond, keys_2), wk, wv, keys_2, values_2, pattern)
     query_b = query(across, beyond, wq)
     if few:
-        along_z, along_y = first_round(kept_b)
-        *along_z, along_y, query_b, half_a[1][3] = lax.optimization_barrier(
-            (*along_z, along_y, query_b, half_a[1][3])
+        along_z = first_round(kept_b)
+        *along_z, query_b, half_a[1][1] = lax.optimization_barrier(
+            (*along_z, query_b, half_a[1][1])
         )
-        half_b = 1, second_round(kept_b, along_z, along_y)
-        asked = after(query_b, half_b[1][1])
+        half_b = 1, second_round(kept_b, along_z)
+        asked = after(query_b, half_b[1][0])
     else:
         half_b = 1, [lax.all_gather(kept_b, "seq", axis=0)]
         asked = query_b
-    wo_beside = swap(after(w_out, asked), 1)
-    wo_beside = pltpu.with_memory_space_constraint(wo_beside, pltpu.VMEM)
-    near = [keys_0, keys_1, keys_2], [values_0, values_1, values_2]
+    near = [keys_0, keys_1, keys_2, keys_3], [values_0, values_1, values_2, values_3]
     call = functools.partial(attend, bias, few)
     begun = call((2, 3), asked, [half_a], near=near, finish=False)
     keep_b, send_b = call((2, 3), query_b, [half_b], begun=begun)

time: 58.3 us -> 56.4 us (0.967)
  starting transfers between devices: 19 us -> 15.7 us
  waiting for transfers between devices: 18.6 us -> 20 us
    ppermute x17 -> x15, starting transfers between devices: 19 us -> 15.7 us  [swap(): return lax.ppermute(array, axis, [(i, i ^ bit) for i in range(count)])]
    ppermute x17 -> x15, waiting for transfers between devices: 18.6 us -> 20 us  [swap(): return lax.ppermute(array, axis, [(i, i ^ bit) for i in range(count)])]
    pallas_call x1 -> x2, Pallas kernels: 0.9 us -> 1.72 us  [second(): pl.pallas_call(second_kernel, in_specs=[IN_VMEM] * 6, out_specs=[IN_VMEM]...]
    pallas_call x1, Pallas kernels: 1.42 us -> 0.71 us  [keys_and_values(): pl.pallas_call(across_kernel, in_specs=[IN_VMEM] * 3, out_specs=[IN_VMEM]...]
  transfers between devices with their start and end apart: 17 -> 15, of which waited for: 7 -> 11; matrix products, arithmetic and copies ran while one was open for 0% -> 0% of each run, Pallas kernels for 32% -> 29%
where the time goes in v7:
time: 56.4 us; the launch traced here: 56.3 us
  waiting for transfers between devices  20 us (35%)
  Pallas kernels  19.4 us (34%)
  starting transfers between devices  15.7 us (28%)
  other arithmetic  1.05 us (2%)
    ppermute x15, waiting for transfers between devices, swap(): return lax.ppermute(array, axis, [(i, i ^ bit) for i in range(count)])  20 us
    ppermute x15, starting transfers between devices, swap(): return lax.ppermute(array, axis, [(i, i ^ bit) for i in range(count)])  15.7 us
    pallas_call x3, Pallas kernels, attend(): pl.pallas_call(functools.partial(attend_kernel, relative, near is not Non...  8.47 us
    pallas_call x1, Pallas kernels, first(): pl.pallas_call(first_kernel, in_specs=[IN_HBM] * 3, out_specs=[IN_VMEM] *...  3.12 us
    pallas_call x1, Pallas kernels, query_first(): pl.pallas_call(query_first_kernel, in_specs=[IN_VMEM] * 2 + [IN_HBM] * 2,...  2.63 us
    pallas_call x2, Pallas kernels, second(): pl.pallas_call(second_kernel, in_specs=[IN_VMEM] * 6, out_specs=[IN_VMEM]...  1.72 us
    pallas_call x2, Pallas kernels, mix(): pl.pallas_call(mix_kernel, in_specs=[IN_VMEM] * 4, out_specs=IN_VMEM, out...  1.43 us
  transfers between devices with their start and end apart: 15, of which 11 were waited for; matrix products, arithmetic and copies ran while one was open for 0% of the time, Pallas kernels for 29%

profile of v7, /device:TPU:0, one launch (start us, length us, event | category | flops | bytes accessed | tf_op | source)
XLA Modules:
  0.0 56.3 jit_solution(13071840621042819596)
XLA Ops:
  0.0 0.5 collective-permute-start.5
  0.5 2.9 %collective-permute-start.4 = (bf16[128,2048]{1,0:T(8,128)(2,1)}, bf16[128,2048]{1,0:T(8,128)(2,1)S(1)}, u32[]{:S(2)}, u32[]{:S(2)}) collective-permute-start(bf16[128,2048]{1,0:T(8,128)(2,1)} %rows_hbm.1), channel_id=1, source_target_pairs={{0,2},{1,3},{2,0},{3,1},{4,6},{5,7},{6,4},{7,5},{8,10},{9,11},{10,... | collective-permute-start | bytes 1572872 | tf_op jit(solution)/shard_map/ppermute | solution.py:412
  3.5 3.1 %shard_map.73 = (bf16[128,2048]{1,0:T(8,128)(2,1)S(1)}, bf16[2048,512]{1,0:T(8,128)(2,1)S(1)}, bf16[2048,512]{1,0:T(8,128)(2,1)S(1)}, bf16[128,512]{1,0:T(8,128)(2,1)S(1)}, bf16[128,512]{1,0:T(8,128)(2,1)S(1)}) custom-call(bf16[128,2048]{1,0:T(8,128)(2,1)} %rows_hbm.1, bf16[2048,512]{1,0:T(8,128)(2,1)} %wk_hbm.1, bf16[2048,512]{1,0:T(8,128)(2,1)} %wv_hbm.1), custom_call_target="tpu_custom_call" | custom-call | flops 5368709 | bytes 41943 | tf_op jit(solution)/shard_map/pallas_call | solution.py:98
  6.6 0.9 %shard_map.74 = (bf16[128,512]{1,0:T(8,128)(2,1)S(1)}, bf16[128,512]{1,0:T(8,128)(2,1)S(1)}, bf16[2,4,32,128]{3,2,1,0:T(8,128)(2,1)S(1)}) custom-call(bf16[128,2048]{1,0:T(8,128)(2,1)S(1)} %collective-permute-done.rows.rows_1, bf16[2048,512]{1,0:T(8,128)(2,1)S(1)} %get-tuple-element.42.wk, bf16[2048,512]{1,0:T(8,128)(2,1)S(1)} %get-tuple-element.43.wv, ...), custom_call_target="tpu_custom_call" | custom-call | flops 5368709 | bytes 5242 | tf_op jit(solution)/shard_map/pallas_call | solution.py:130
  7.5 2.6 %collective-permute-start.1 = (bf16[2,4,32,128]{3,2,1,0:T(8,128)(2,1)S(1)}, bf16[2,4,32,128]{3,2,1,0:T(8,128)(2,1)S(1)}, u32[]{:S(2)}, u32[]{:S(2)}) collective-permute-start(bf16[2,4,32,128]{3,2,1,0:T(8,128)(2,1)S(1)} %get-tuple-element.46), channel_id=1, source_target_pairs={{0,16},{4,20},{8,24},{12,28},{16,0},{20,4},{24,8},{28,12},{1,17},{... | collective-permute-start | bytes 196616 | tf_op jit(solution)/shard_map/ppermute | solution.py:412
  10.1 1.3 %collective-permute-start.2 = (bf16[2,4,32,128]{3,2,1,0:T(8,128)(2,1)S(1)}, bf16[2,4,32,128]{3,2,1,0:T(8,128)(2,1)S(1)}, u32[]{:S(2)}, u32[]{:S(2)}) collective-permute-start(bf16[2,4,32,128]{3,2,1,0:T(8,128)(2,1)S(1)} %get-tuple-element.46), channel_id=1, source_target_pairs={{0,24},{4,28},{8,16},{12,20},{16,8},{20,12},{24,0},{28,4},{1,25},{... | collective-permute-start | bytes 196616 | tf_op jit(solution)/shard_map/ppermute | solution.py:412
  11.7 0.6 %shard_map.76.bias = f32[4,1024]{1,0:T(4,128)S(1)} custom-call(s32[10]{0:T(128)S(1)} %pad_add_fusion.place), custom_call_target="tpu_custom_call" | custom-call | flops 2621 | bytes 163 | tf_op jit(solution)/shard_map/pallas_call | solution.py:252
  12.3 2.6 %shard_map.75 = (bf16[256,512]{1,0:T(8,128)(2,1)S(1)}, bf16[2048,512]{1,0:T(8,128)(2,1)S(1)}, bf16[512,2048]{1,0:T(8,128)(2,1)S(1)}) custom-call(bf16[128,2048]{1,0:T(8,128)(2,1)S(1)} %get-tuple-element.47.rows_0, bf16[128,2048]{1,0:T(8,128)(2,1)S(1)} %collective-permute-done.rows.rows_1, bf16[2048,512]{1,0:T(8,128)(2,1)} %wq_hbm.1, bf16[512,2048]{1,0:T(8,128)(2,1)} %w_hbm.1), custom_call_target="tpu_custom_call" | custom-call | flops 5368709 | bytes 41943 | tf_op jit(solution)/shard_map/pallas_call | solution.py:159
  15.2 1.3 %collective-permute-done.2 = bf16[2,4,32,128]{3,2,1,0:T(8,128)(2,1)S(1)} collective-permute-done((bf16[2,4,32,128]{3,2,1,0:T(8,128)(2,1)S(1)}, bf16[2,4,32,128]{3,2,1,0:T(8,128)(2,1)S(1)}, u32[]{:S(2)}, u32[]{:S(2)}) %collective-permute-start.2) | collective-permute-done | bytes 65568 | tf_op jit(solution)/shard_map/ppermute | solution.py:412
  16.4 0.3 collective-permute-done.3
  16.9 1.6 %collective-permute-start.10 = (bf16[4,2,4,32,128]{4,3,2,1,0:T(8,128)(2,1)S(1)}, bf16[4,2,4,32,128]{4,3,2,1,0:T(8,128)(2,1)S(1)}, u32[]{:S(2)}, u32[]{:S(2)}) collective-permute-start(bf16[4,2,4,32,128]{4,3,2,1,0:T(8,128)(2,1)S(1)} %pad_maximum_fusion.refs_9_), channel_id=1, source_target_pairs={{0,4},{4,0},{8,12},{12,8},{16,20},{20,16},{24,28},{28,24},{1,5},{5... | collective-permute-start | bytes 786440 | tf_op jit(solution)/shard_map/ppermute | solution.py:412
  18.5 0.7 %shard_map.77 = (bf16[128,512]{1,0:T(8,128)(2,1)S(1)}, bf16[128,512]{1,0:T(8,128)(2,1)S(1)}) custom-call(bf16[128,2048]{1,0:T(8,128)(2,1)S(1)} %collective-permute-done.4.rows.rows_0, bf16[2048,512]{1,0:T(8,128)(2,1)S(1)} %get-tuple-element.42.wk, bf16[2048,512]{1,0:T(8,128)(2,1)S(1)} %get-tuple-element.43.wv), custom_call_target="tpu_custom_call" | custom-call | flops 5368709 | bytes 5242 | tf_op jit(solution)/shard_map/pallas_call | solution.py:202
  19.2 0.9 %shard_map.78 = (bf16[128,512]{1,0:T(8,128)(2,1)S(1)}, bf16[128,512]{1,0:T(8,128)(2,1)S(1)}, bf16[2,4,32,128]{3,2,1,0:T(8,128)(2,1)S(1)}) custom-call(bf16[128,2048]{1,0:T(8,128)(2,1)S(1)} %collective-permute-done.6.rows.rows_1, bf16[2048,512]{1,0:T(8,128)(2,1)S(1)} %get-tuple-element.42.wk, bf16[2048,512]{1,0:T(8,128)(2,1)S(1)} %get-tuple-element.43.wv, ...), custom_call_target="tpu_custom_call" | custom-call | flops 5368709 | bytes 5242 | tf_op jit(solution)/shard_map/pallas_call | solution.py:130
  20.1 2.6 %collective-permute-start.7 = (bf16[2,4,32,128]{3,2,1,0:T(8,128)(2,1)S(1)}, bf16[2,4,32,128]{3,2,1,0:T(8,128)(2,1)S(1)}, u32[]{:S(2)}, u32[]{:S(2)}) collective-permute-start(bf16[2,4,32,128]{3,2,1,0:T(8,128)(2,1)S(1)} %get-tuple-element.59), channel_id=1, source_target_pairs={{0,16},{4,20},{8,24},{12,28},{16,0},{20,4},{24,8},{28,12},{1,17},{... | collective-permute-start | bytes 196616 | tf_op jit(solution)/shard_map/ppermute | solution.py:412
  22.7 0.6 %collective-permute-start.8 = (bf16[2,4,32,128]{3,2,1,0:T(8,128)(2,1)S(1)}, bf16[2,4,32,128]{3,2,1,0:T(8,128)(2,1)S(1)}, u32[]{:S(2)}, u32[]{:S(2)}) collective-permute-start(bf16[2,4,32,128]{3,2,1,0:T(8,128)(2,1)S(1)} %get-tuple-element.59), channel_id=1, source_target_pairs={{0,24},{4,28},{8,16},{12,20},{16,8},{20,12},{24,0},{28,4},{1,25},{... | collective-permute-start | bytes 196616 | tf_op jit(solution)/shard_map/ppermute | solution.py:412
  23.3 0.5 collective-permute-start.9
  23.8 0.7 %shard_map.79.refs_0_ = bf16[256,512]{1,0:T(8,128)(2,1)S(1)} custom-call(bf16[128,2048]{1,0:T(8,128)(2,1)S(1)} %collective-permute-done.4.rows.rows_0, bf16[128,2048]{1,0:T(8,128)(2,1)S(1)} %collective-permute-done.6.rows.rows_1, bf16[2048,512]{1,0:T(8,128)(2,1)S(1)} %get-tuple-element.60.wq), custom_call_target="tpu_custom_call" | custom-call | flops 5368709 | bytes 10485 | tf_op jit(solution)/shard_map/pallas_call | solution.py:183
  24.5 1.1 %collective-permute-done.10.refs_10_ = bf16[4,2,4,32,128]{4,3,2,1,0:T(8,128)(2,1)S(1)} collective-permute-done((bf16[4,2,4,32,128]{4,3,2,1,0:T(8,128)(2,1)S(1)}, bf16[4,2,4,32,128]{4,3,2,1,0:T(8,128)(2,1)S(1)}, u32[]{:S(2)}, u32[]{:S(2)}) %collective-permute-start.10) | collective-permute-done | bytes 262176 | tf_op jit(solution)/shard_map/ppermute | solution.py:412
  25.6 2.2 %collective-permute-done.7 = bf16[2,4,32,128]{3,2,1,0:T(8,128)(2,1)S(1)} collective-permute-done((bf16[2,4,32,128]{3,2,1,0:T(8,128)(2,1)S(1)}, bf16[2,4,32,128]{3,2,1,0:T(8,128)(2,1)S(1)}, u32[]{:S(2)}, u32[]{:S(2)}) %collective-permute-start.7) | collective-permute-done | bytes 65568 | tf_op jit(solution)/shard_map/ppermute | solution.py:412
  27.8 1.3 %collective-permute-done.8 = bf16[2,4,32,128]{3,2,1,0:T(8,128)(2,1)S(1)} collective-permute-done((bf16[2,4,32,128]{3,2,1,0:T(8,128)(2,1)S(1)}, bf16[2,4,32,128]{3,2,1,0:T(8,128)(2,1)S(1)}, u32[]{:S(2)}, u32[]{:S(2)}) %collective-permute-start.8) | collective-permute-done | bytes 65568 | tf_op jit(solution)/shard_map/ppermute | solution.py:412
  29.4 1.1 %collective-permute-start.11 = (bf16[4,2,4,32,128]{4,3,2,1,0:T(8,128)(2,1)S(1)}, bf16[4,2,4,32,128]{4,3,2,1,0:T(8,128)(2,1)S(1)}, u32[]{:S(2)}, u32[]{:S(2)}) collective-permute-start(bf16[4,2,4,32,128]{4,3,2,1,0:T(8,128)(2,1)S(1)} %pad_maximum_fusion.1.refs_3_.refs_11_), channel_id=1, source_target_pairs={{0,4},{4,0},{8,12},{12,8},{16,20},{20,16},{24,28},{28,24},{1,5},{5... | collective-permute-start | bytes 786440 | tf_op jit(solution)/shard_map/ppermute | solution.py:412
  30.5 2.9 %shard_map.80 = (f32[256,512]{1,0:T(8,128)S(1)}, f32[4,256,128]{2,1,0:T(8,128)S(1)}) custom-call(f32[4,1024]{1,0:T(4,128)S(1)} %shard_map.76.bias, bf16[256,512]{1,0:T(8,128)(2,1)S(1)} %shard_map.79.refs_0_, bf16[128,512]{1,0:T(8,128)(2,1)S(1)} %get-tuple-element.44.keys_0.refs_1_, bf16[128,512]{1,0:T(8,128)(2,1)S(1)} %get-tuple-element.66.refs_2_, ...), custom_call_target="tpu_custom_call" | custom-call | flops 4026531 | bytes 5242 | tf_op jit(solution)/shard_map/pallas_call | solution.py:370
  33.5 3.4 %collective-permute-done.11.refs_4_.refs_12_ = bf16[4,2,4,32,128]{4,3,2,1,0:T(8,128)(2,1)S(1)} collective-permute-done((bf16[4,2,4,32,128]{4,3,2,1,0:T(8,128)(2,1)S(1)}, bf16[4,2,4,32,128]{4,3,2,1,0:T(8,128)(2,1)S(1)}, u32[]{:S(2)}, u32[]{:S(2)}) %collective-permute-start.11) | collective-permute-done | bytes 262176 | tf_op jit(solution)/shard_map/ppermute | solution.py:412
  36.9 2.3 %shard_map.81 = (bf16[128,512]{1,0:T(8,128)(2,1)S(1)}, bf16[128,512]{1,0:T(8,128)(2,1)S(1)}) custom-call(f32[4,1024]{1,0:T(4,128)S(1)} %shard_map.76.bias, bf16[256,512]{1,0:T(8,128)(2,1)S(1)} %shard_map.79.refs_0_, f32[256,512]{1,0:T(8,128)S(1)} %get-tuple-element.71.refs_1_, f32[4,256,128]{2,1,0:T(8,128)S(1)} %get-tuple-element.72.refs_2_, ...), custom_call_target="tpu_custom_call" | custom-call | flops 1342177 | bytes 5242 | tf_op jit(solution)/shard_map/pallas_call | solution.py:370
  39.3 1.3 %collective-permute-done.12.rows_1 = bf16[128,512]{1,0:T(8,128)(2,1)S(1)} collective-permute-done((bf16[128,512]{1,0:T(8,128)(2,1)S(1)}, bf16[128,512]{1,0:T(8,128)(2,1)S(1)}, u32[]{:S(2)}, u32[]{:S(2)}) %collective-permute-start.12) | collective-permute-done | bytes 131104 | tf_op jit(solution)/shard_map/ppermute | solution.py:412
  40.6 0.7 %shard_map.82 = bf16[128,2048]{1,0:T(8,128)(2,1)S(1)} custom-call(bf16[128,512]{1,0:T(8,128)(2,1)S(1)} %get-tuple-element.73.rows_0, bf16[128,512]{1,0:T(8,128)(2,1)S(1)} %collective-permute-done.12.rows_1, bf16[512,2048]{1,0:T(8,128)(2,1)S(1)} %get-tuple-element.75.weight_0, bf16[512,2048]{1,0:T(8,128)(2,1)S(1)} %collective-permute-done.5.weight_1), custom_call_target="tpu_custom_call" | custom-call | flops 5368709 | bytes 10485 | tf_op jit(solution)/shard_map/pallas_call | solution.py:395
  41.3 1.5 %collective-permute-start.14 = (bf16[128,2048]{1,0:T(8,128)(2,1)S(1)}, bf16[128,2048]{1,0:T(8,128)(2,1)S(1)}, u32[]{:S(2)}, u32[]{:S(2)}) collective-permute-start(bf16[128,2048]{1,0:T(8,128)(2,1)S(1)} %shard_map.82), channel_id=1, source_target_pairs={{0,2},{1,3},{2,0},{3,1},{4,6},{5,7},{6,4},{7,5},{8,10},{9,11},{10,... | collective-permute-start | bytes 1572872 | tf_op jit(solution)/shard_map/ppermute | solution.py:412
  42.8 3.2 %shard_map.83 = (bf16[128,512]{1,0:T(8,128)(2,1)S(1)}, bf16[128,512]{1,0:T(8,128)(2,1)S(1)}) custom-call(f32[4,1024]{1,0:T(4,128)S(1)} %shard_map.76.bias, bf16[256,512]{1,0:T(8,128)(2,1)S(1)} %get-tuple-element.76.refs_0_, bf16[128,512]{1,0:T(8,128)(2,1)S(1)} %get-tuple-element.44.keys_0.refs_1_, bf16[128,512]{1,0:T(8,128)(2,1)S(1)} %get-tuple-element.66.refs_2_, ...), custom_call_target="tpu_custom_call" | custom-call | flops 5368709 | bytes 5242 | tf_op jit(solution)/shard_map/pallas_call | solution.py:370
  46.1 1.3 %collective-permute-done.13.rows_1 = bf16[128,512]{1,0:T(8,128)(2,1)S(1)} collective-permute-done((bf16[128,512]{1,0:T(8,128)(2,1)S(1)}, bf16[128,512]{1,0:T(8,128)(2,1)S(1)}, u32[]{:S(2)}, u32[]{:S(2)}) %collective-permute-start.13) | collective-permute-done | bytes 131104 | tf_op jit(solution)/shard_map/ppermute | solution.py:412
  47.5 0.7 %shard_map.84 = f32[128,2048]{1,0:T(8,128)S(1)} custom-call(bf16[128,512]{1,0:T(8,128)(2,1)S(1)} %get-tuple-element.77.rows_0, bf16[128,512]{1,0:T(8,128)(2,1)S(1)} %collective-permute-done.13.rows_1, bf16[512,2048]{1,0:T(8,128)(2,1)S(1)} %get-tuple-element.75.weight_0, bf16[512,2048]{1,0:T(8,128)(2,1)S(1)} %collective-permute-done.5.weight_1), custom_call_target="tpu_custom_call" | custom-call | flops 5368709 | bytes 10485 | tf_op jit(solution)/shard_map/pallas_call | solution.py:395
  48.2 7.2 %collective-permute-done.14 = bf16[128,2048]{1,0:T(8,128)(2,1)S(1)} collective-permute-done((bf16[128,2048]{1,0:T(8,128)(2,1)S(1)}, bf16[128,2048]{1,0:T(8,128)(2,1)S(1)}, u32[]{:S(2)}, u32[]{:S(2)}) %collective-permute-start.14) | collective-permute-done | bytes 524320 | tf_op jit(solution)/shard_map/ppermute | solution.py:412
  55.4 0.9 %add_convert_fusion = bf16[128,2048]{1,0:T(8,128)(2,1)} fusion(f32[128,2048]{1,0:T(8,128)S(1)} %shard_map.84, bf16[128,2048]{1,0:T(8,128)(2,1)S(1)} %collective-permute-done.14), kind=kLoop, calls=%fused_computation | loop fusion | flops 786432 | bytes 2097152 | tf_op jit(solution)/shard_map/convert_element_type | solution.py:465
  (18 shorter events, 1.1 us)
Async XLA Ops:
  0.0 16.8 %collective-permute-start.5 = (bf16[512,2048]{1,0:T(8,128)(2,1)}, bf16[512,2048]{1,0:T(8,128)(2,1)S(1)}, u32[]{:S(2)}, u32[]{:S(2)}) collective-permute-start(bf16[512,2048]{1,0:T(8,128)(2,1)} %w_hbm.1), channel_id=1, source_target_pairs={{0,1},{1,0},{2,3},{3,2},{4,5},{5,4},{6,7},{7,6},{8,9},{9,8},{10,11... | collective-permute-start | bytes 6291464 | tf_op jit(solution)/shard_map/ppermute | solution.py:412
  0.5 6.1 %collective-permute-start = (bf16[128,2048]{1,0:T(8,128)(2,1)}, bf16[128,2048]{1,0:T(8,128)(2,1)S(1)}, u32[]{:S(2)}, u32[]{:S(2)}) collective-permute-start(bf16[128,2048]{1,0:T(8,128)(2,1)} %rows_hbm.1), channel_id=1, source_target_pairs={{0,1},{1,0},{2,3},{3,2},{4,5},{5,4},{6,7},{7,6},{8,9},{9,8},{10,11... | collective-permute-start | bytes 1572872 | tf_op jit(solution)/shard_map/ppermute | solution.py:412
  0.5 16.3 %collective-permute-start.4 = (bf16[128,2048]{1,0:T(8,128)(2,1)}, bf16[128,2048]{1,0:T(8,128)(2,1)S(1)}, u32[]{:S(2)}, u32[]{:S(2)}) collective-permute-start(bf16[128,2048]{1,0:T(8,128)(2,1)} %rows_hbm.1), channel_id=1, source_target_pairs={{0,2},{1,3},{2,0},{3,1},{4,6},{5,7},{6,4},{7,5},{8,10},{9,11},{10,... | collective-permute-start | bytes 1572872 | tf_op jit(solution)/shard_map/ppermute | solution.py:412
  3.5 3.1 %copy-start = (s32[4,128]{1,0:T(4,128)S(1)}, s32[4,128]{1,0:T(4,128)}, u32[]{:S(2)}) copy-start(s32[4,128]{1,0:T(4,128)} %pattern.3) | copy-start | bytes 6148
  6.6 5.1 %copy-start.1 = (s32[8]{0:T(128)S(1)}, s32[8]{0:T(128)}, u32[]{:S(2)}) copy-start(s32[8]{0:T(128)} %param.13) | copy-start | bytes 100
  7.5 7.7 %collective-permute-start.1 = (bf16[2,4,32,128]{3,2,1,0:T(8,128)(2,1)S(1)}, bf16[2,4,32,128]{3,2,1,0:T(8,128)(2,1)S(1)}, u32[]{:S(2)}, u32[]{:S(2)}) collective-permute-start(bf16[2,4,32,128]{3,2,1,0:T(8,128)(2,1)S(1)} %get-tuple-element.46), channel_id=1, source_target_pairs={{0,16},{4,20},{8,24},{12,28},{16,0},{20,4},{24,8},{28,12},{1,17},{... | collective-permute-start | bytes 196616 | tf_op jit(solution)/shard_map/ppermute | solution.py:412
  10.1 6.4 %collective-permute-start.2 = (bf16[2,4,32,128]{3,2,1,0:T(8,128)(2,1)S(1)}, bf16[2,4,32,128]{3,2,1,0:T(8,128)(2,1)S(1)}, u32[]{:S(2)}, u32[]{:S(2)}) collective-permute-start(bf16[2,4,32,128]{3,2,1,0:T(8,128)(2,1)S(1)} %get-tuple-element.46), channel_id=1, source_target_pairs={{0,24},{4,28},{8,16},{12,20},{16,8},{20,12},{24,0},{28,4},{1,25},{... | collective-permute-start | bytes 196616 | tf_op jit(solution)/shard_map/ppermute | solution.py:412
  11.4 5.3 %collective-permute-start.3 = (bf16[2,4,32,128]{3,2,1,0:T(8,128)(2,1)S(1)}, bf16[2,4,32,128]{3,2,1,0:T(8,128)(2,1)S(1)}, u32[]{:S(2)}, u32[]{:S(2)}) collective-permute-start(bf16[2,4,32,128]{3,2,1,0:T(8,128)(2,1)S(1)} %get-tuple-element.46), channel_id=1, source_target_pairs={{0,8},{4,12},{8,0},{12,4},{16,24},{20,28},{24,16},{28,20},{1,9},{5... | collective-permute-start | bytes 196616 | tf_op jit(solution)/shard_map/ppermute | solution.py:412
  16.8 2.4 %collective-permute-start.6 = (bf16[128,2048]{1,0:T(8,128)(2,1)S(1)}, bf16[128,2048]{1,0:T(8,128)(2,1)S(1)}, u32[]{:S(2)}, u32[]{:S(2)}) collective-permute-start(bf16[128,2048]{1,0:T(8,128)(2,1)S(1)} %collective-permute-done.4.rows.rows_0), channel_id=1, source_target_pairs={{0,1},{1,0},{2,3},{3,2},{4,5},{5,4},{6,7},{7,6},{8,9},{9,8},{10,11... | collective-permute-start | bytes 1572872 | tf_op jit(solution)/shard_map/ppermute | solution.py:412
  16.9 8.7 %collective-permute-start.10 = (bf16[4,2,4,32,128]{4,3,2,1,0:T(8,128)(2,1)S(1)}, bf16[4,2,4,32,128]{4,3,2,1,0:T(8,128)(2,1)S(1)}, u32[]{:S(2)}, u32[]{:S(2)}) collective-permute-start(bf16[4,2,4,32,128]{4,3,2,1,0:T(8,128)(2,1)S(1)} %pad_maximum_fusion.refs_9_), channel_id=1, source_target_pairs={{0,4},{4,0},{8,12},{12,8},{16,20},{20,16},{24,28},{28,24},{1,5},{5... | collective-permute-start | bytes 786440 | tf_op jit(solution)/shard_map/ppermute | solution.py:412
  20.1 7.8 %collective-permute-start.7 = (bf16[2,4,32,128]{3,2,1,0:T(8,128)(2,1)S(1)}, bf16[2,4,32,128]{3,2,1,0:T(8,128)(2,1)S(1)}, u32[]{:S(2)}, u32[]{:S(2)}) collective-permute-start(bf16[2,4,32,128]{3,2,1,0:T(8,128)(2,1)S(1)} %get-tuple-element.59), channel_id=1, source_target_pairs={{0,16},{4,20},{8,24},{12,28},{16,0},{20,4},{24,8},{28,12},{1,17},{... | collective-permute-start | bytes 196616 | tf_op jit(solution)/shard_map/ppermute | solution.py:412
  22.7 6.4 %collective-permute-start.8 = (bf16[2,4,32,128]{3,2,1,0:T(8,128)(2,1)S(1)}, bf16[2,4,32,128]{3,2,1,0:T(8,128)(2,1)S(1)}, u32[]{:S(2)}, u32[]{:S(2)}) collective-permute-start(bf16[2,4,32,128]{3,2,1,0:T(8,128)(2,1)S(1)} %get-tuple-element.59), channel_id=1, source_target_pairs={{0,24},{4,28},{8,16},{12,20},{16,8},{20,12},{24,0},{28,4},{1,25},{... | collective-permute-start | bytes 196616 | tf_op jit(solution)/shard_map/ppermute | solution.py:412
  23.3 6.1 %collective-permute-start.9 = (bf16[2,4,32,128]{3,2,1,0:T(8,128)(2,1)S(1)}, bf16[2,4,32,128]{3,2,1,0:T(8,128)(2,1)S(1)}, u32[]{:S(2)}, u32[]{:S(2)}) collective-permute-start(bf16[2,4,32,128]{3,2,1,0:T(8,128)(2,1)S(1)} %get-tuple-element.59), channel_id=1, source_target_pairs={{0,8},{4,12},{8,0},{12,4},{16,24},{20,28},{24,16},{28,20},{1,9},{5... | collective-permute-start | bytes 196616 | tf_op jit(solution)/shard_map/ppermute | solution.py:412
  29.4 7.5 %collective-permute-start.11 = (bf16[4,2,4,32,128]{4,3,2,1,0:T(8,128)(2,1)S(1)}, bf16[4,2,4,32,128]{4,3,2,1,0:T(8,128)(2,1)S(1)}, u32[]{:S(2)}, u32[]{:S(2)}) collective-permute-start(bf16[4,2,4,32,128]{4,3,2,1,0:T(8,128)(2,1)S(1)} %pad_maximum_fusion.1.refs_3_.refs_11_), channel_id=1, source_target_pairs={{0,4},{4,0},{8,12},{12,8},{16,20},{20,16},{24,28},{28,24},{1,5},{5... | collective-permute-start | bytes 786440 | tf_op jit(solution)/shard_map/ppermute | solution.py:412
  39.2 1.4 %collective-permute-start.12 = (bf16[128,512]{1,0:T(8,128)(2,1)S(1)}, bf16[128,512]{1,0:T(8,128)(2,1)S(1)}, u32[]{:S(2)}, u32[]{:S(2)}) collective-permute-start(bf16[128,512]{1,0:T(8,128)(2,1)S(1)} %get-tuple-element.74), channel_id=1, source_target_pairs={{0,1},{1,0},{2,3},{3,2},{4,5},{5,4},{6,7},{7,6},{8,9},{9,8},{10,11... | collective-permute-start | bytes 393224 | tf_op jit(solution)/shard_map/ppermute | solution.py:412
  41.3 14.0 %collective-permute-start.14 = (bf16[128,2048]{1,0:T(8,128)(2,1)S(1)}, bf16[128,2048]{1,0:T(8,128)(2,1)S(1)}, u32[]{:S(2)}, u32[]{:S(2)}) collective-permute-start(bf16[128,2048]{1,0:T(8,128)(2,1)S(1)} %shard_map.82), channel_id=1, source_target_pairs={{0,2},{1,3},{2,0},{3,1},{4,6},{5,7},{6,4},{7,5},{8,10},{9,11},{10,... | collective-permute-start | bytes 1572872 | tf_op jit(solution)/shard_map/ppermute | solution.py:412
  46.1 1.4 %collective-permute-start.13 = (bf16[128,512]{1,0:T(8,128)(2,1)S(1)}, bf16[128,512]{1,0:T(8,128)(2,1)S(1)}, u32[]{:S(2)}, u32[]{:S(2)}) collective-permute-start(bf16[128,512]{1,0:T(8,128)(2,1)S(1)} %get-tuple-element.78), channel_id=1, source_target_pairs={{0,1},{1,0},{2,3},{3,2},{4,5},{5,4},{6,7},{7,6},{8,9},{9,8},{10,11... | collective-permute-start | bytes 393224 | tf_op jit(solution)/shard_map/ppermute | solution.py:412

commit v8 on v7

--- a/solution.py
+++ b/solution.py
@@ -217,74 +217,77 @@
     return total
 
 
-def hidden_if_not(condition):
-    return jnp.where(condition, jnp.float32(0), jnp.float32(HIDDEN))
-
-
-def bias_kernel(slides, subs, spans, few, place, out):
+def mask_kernel(slides, subs, spans, few, place, asking, asked):
     span, sub = place[slides], place[slides + 1]
     slide = [slide_of(place, slides, span * subs + (sub ^ r)) for r in range(subs)]
+    lane = lax.broadcasted_iota(jnp.int32, (BLOCK, HEAD_SIZE), 1)
     for r in range(subs):
-        for c in range(subs):
-            value = hidden_if_not(slide[r] == slide[c])
-            out[r : r + 1, c * BLOCK : (c + 1) * BLOCK] = jnp.full((1, BLOCK), value, F32)
-    count = spans * FAR_ROWS
-    column = lax.broadcasted_iota(jnp.int32, (1, count), 1)
-    far = column // FAR_ROWS
-    if few:
-        order = [bit | y for y in (0, Y_BIT) for bit in (0, *Z_BITS)]
-        place_of = jnp.zeros_like(far)
-        for index, bits in enumerate(order):
-            place_of = jnp.where(far == index, bits, place_of)
-        far = place_of ^ span
-    upper = (column // DILATED_KEPT) % BLOCKS_HALF
+        rows = slice(r * BLOCK, (r + 1) * BLOCK)
+        apart = (lane <= slides) & (lane != slide[r])
+        asking[rows, :] = jnp.where(apart, HIDDEN, 0.0).astype(BF16)
+        asked[rows, :] = jnp.where(lane == slide[r], 1.0, 0.0).astype(BF16)
+    count = min(spans, GROUP) * FAR_ROWS
+    row = lax.broadcasted_iota(jnp.int32, (count, HEAD_SIZE), 0)
+    lane = lax.broadcasted_iota(jnp.int32, (count, HEAD_SIZE), 1)
+    upper = (row // DILATED_KEPT) % BLOCKS_HALF
     for half in range(subs // BLOCKS_HALF):
         place_0, place_1 = sub ^ (half * BLOCKS_HALF), sub ^ (half * BLOCKS_HALF + 1)
-        theirs = slide_of(place, slides, far * subs + jnp.where(upper == 0, place_0, place_1))
-        start = subs * BLOCK + half * count
-        for r in range(subs):
-            seen = (theirs == slide[r]) & (far != span)
-            out[r : r + 1, start : start + count] = hidden_if_not(seen)
-
-
-def make_bias(place, slides, subs, spans, few):
-    columns = subs * BLOCK + subs // BLOCKS_HALF * spans * FAR_ROWS
-    return pl.pallas_call(
-        functools.partial(bias_kernel, slides, subs, spans, few),
+        for group in range(spans * FAR_ROWS // count):
+            far = row // FAR_ROWS
+            if few:
+                order = [bit | y for y in (0, Y_BIT) for bit in (0, *Z_BITS)]
+                place_of = jnp.zeros_like(far)
+                for index, bits in enumerate(order):
+                    place_of = jnp.where(far == index, bits, place_of)
+                far = place_of ^ span
+            else:
+                far = far + group * GROUP
+            theirs = slide_of(place, slides, far * subs + jnp.where(upper == 0, place_0, place_1))
+            marked = (lane == theirs) | ((lane == slides) & (far == span))
+            start = subs * BLOCK + (half * spans * FAR_ROWS + group * count)
+            asked[start : start + count, :] = jnp.where(marked, 1.0, 0.0).astype(BF16)
+
+
+def make_masks(place, slides, subs, spans, few):
+    keys = subs * BLOCK + subs // BLOCKS_HALF * spans * FAR_ROWS
+    return pl.pallas_call(
+        functools.partial(mask_kernel, slides, subs, spans, few),
         in_specs=[IN_SMEM],
-        out_specs=IN_VMEM,
-        out_shape=shape((subs, columns), F32),
-        compiler_params=params(),
-        cost_estimate=cost(64 * subs * columns, 4 * subs * columns),
+        out_specs=[IN_VMEM] * 2,
+        out_shape=[shape((subs * BLOCK, HEAD_SIZE)), shape((keys, HEAD_SIZE))],
+        compiler_params=params(),
+        cost_estimate=cost(64 * keys * HEAD_SIZE, 2 * keys * HEAD_SIZE),
     )(place)
 
 
-def add_rows(scores, bias):
-    return jnp.concatenate(
-        [scores[i * BLOCK : (i + 1) * BLOCK] + row for i, row in enumerate(bias)], axis=0
+def scores_of(keys, queries):
+    return dot_t(keys, queries)
+
+
+def gather(values, weight):
+    return lax.dot_general(
+        values, weight.astype(BF16), (((0,), (0,)), ((), ())), preferred_element_type=F32
     )
 
 
-def far_update(queries, keys, values, bias, state):
-    scores = add_rows(dot_t(queries, keys), bias)
+def begin(queries, keys, values):
+    scores = scores_of(keys, queries)
+    peak = jnp.max(scores, axis=0, keepdims=True)
+    weight = jnp.exp2((scores - peak) * SCALE)
+    return peak, jnp.sum(weight, axis=0, keepdims=True), gather(values, weight)
+
+
+def update(queries, keys, values, state):
     peak, total, gathered = state
-    higher = jnp.maximum(peak, jnp.max(scores, axis=1, keepdims=True))
+    scores = scores_of(keys, queries)
+    higher = jnp.maximum(peak, jnp.max(scores, axis=0, keepdims=True))
     shrink = jnp.exp2((peak - higher) * SCALE)
     weight = jnp.exp2((scores - higher) * SCALE)
-    total = total * shrink + jnp.sum(weight, axis=1, keepdims=True)
-    return higher, total, gathered * shrink + dot(weight.astype(BF16), values)
-
-
-def far_group(refs, head):
-    return [
-        jnp.concatenate(
-            [ref[step, slot, head] for ref in refs for step in range(GROUP // 2)], axis=0
-        )
-        for slot in range(2)
-    ]
-
-
-def attend_kernel(relative, near, halves, few, finish, bias, *refs):
+    total = total * shrink + jnp.sum(weight, axis=0, keepdims=True)
+    return higher, total, gathered * shrink + gather(values, weight)
+
+
+def attend_kernel(first_row, near, halves, few, finish, asking, asked_of, *refs):
     refs = list(refs)
     queries = refs.pop(0)
     if near:
@@ -294,91 +297,102 @@
         gathered_in, stats_in = refs[0:2]
         del refs[:2]
     far = []
-    for half in halves:
-        size = 2 if few else 1
+    for half, size in halves:
         far.append((half, refs[:size]))
         del refs[:size]
-    span = bias.shape[0] * BLOCK
-    half_count = (bias.shape[1] - span) * BLOCKS_HALF // bias.shape[0]
-
-    def rows_of_bias(columns):
-        return [bias[r : r + 1, columns] for r in relative]
+    rows = queries.shape[0]
+    span = asking.shape[0]
+    half_count = (asked_of.shape[0] - span) // BLOCKS_HALF
 
     def one_head(head, _):
         columns = pl.ds(pl.multiple_of(head * HEAD_SIZE, HEAD_SIZE), HEAD_SIZE)
-        asked = queries[:, columns]
+        asked = jnp.concatenate(
+            [queries[:, columns], asking[first_row : first_row + rows, :]], axis=1
+        )
+
+        def marked(parts, where):
+            return jnp.concatenate([jnp.concatenate(parts, axis=0), asked_of[where, :]], axis=1)
+
+        keyed, valued = [], []
         if near:
-            near_keys = jnp.concatenate([ref[:, columns] for ref in keys], axis=0)
-            near_values = jnp.concatenate([ref[:, columns] for ref in values], axis=0)
-            scores = add_rows(dot_t(asked, near_keys), rows_of_bias(slice(0, span)))
-            peak = jnp.max(scores, axis=1, keepdims=True)
-            weight = jnp.exp2((scores - peak) * SCALE)
-            total = jnp.sum(weight, axis=1, keepdims=True)
-            state = peak, total, dot(weight.astype(BF16), near_values)
+            keyed.append(marked([ref[:, columns] for ref in keys], slice(0, span)))
+            valued += [ref[:, columns] for ref in values]
+        if few:
+            for half, parts in far:
+                start = span + half * half_count
+                pieces = [(ref, i) for ref in parts for i in range(ref.shape[0])]
+                keyed.append(
+                    marked([ref[i, 0, head] for ref, i in pieces], slice(start, start + half_count))
+                )
+                valued += [ref[i, 1, head] for ref, i in pieces]
+        if near:
+            ready = asked, jnp.concatenate(keyed, axis=0), jnp.concatenate(valued, axis=0)
+            state = begin(*ready)
         else:
-            state = stats_in[head, :, 0:1], stats_in[head, :, 1:2], gathered_in[:, columns]
-        for half, parts in far:
-            start = span + half * half_count
+            state = stats_in[head, 0:1, :], stats_in[head, 1:2, :], gathered_in[head]
             if few:
-                group = far_group(parts, head)
-                rows = rows_of_bias(slice(start, start + half_count))
-                state = far_update(asked, *group, rows, state)
-                continue
-
-            def step(number, state, start=start, part=parts[0]):
-                base = number * GROUP
-                group = [
-                    jnp.concatenate([part[base + i, slot, head] for i in range(GROUP)], axis=0)
-                    for slot in range(2)
-                ]
-                width = GROUP * FAR_ROWS
-                rows = rows_of_bias(pl.ds(pl.multiple_of(start + number * width, width), width))
-                return far_update(asked, *group, rows, state)
-
-            state = lax.fori_loop(0, parts[0].shape[0] // GROUP, step, state)
+                ready = asked, jnp.concatenate(keyed, axis=0), jnp.concatenate(valued, axis=0)
+                state = update(*ready, state)
+        if not few:
+            for half, (part,) in far:
+                start = span + half * half_count
+
+                def step(number, state, start=start, part=part):
+                    base = number * GROUP
+                    width = GROUP * FAR_ROWS
+                    where = pl.ds(pl.multiple_of(start + number * width, width), width)
+                    keyed = marked([part[base + i, 0, head] for i in range(GROUP)], where)
+                    valued = jnp.concatenate([part[base + i, 1, head] for i in range(GROUP)], axis=0)
+                    return update(asked, keyed, valued, state)
+
+                state = lax.fori_loop(0, part.shape[0] // GROUP, step, state)
         peak, total, gathered = state
         if finish:
             keep, send = refs
-            context = (gathered / total).astype(BF16)
+            context = (gathered / total).T.astype(BF16)
             keep[:, columns] = context[:BLOCK]
             send[:, columns] = context[BLOCK:]
         else:
             gathered_out, stats_out = refs
-            gathered_out[:, columns] = gathered
-            lane = lax.broadcasted_iota(jnp.int32, gathered.shape, 1)
-            stats_out[head] = jnp.where(lane == 0, peak, total)
+            gathered_out[head] = gathered
+            stats_out[head, 0:1, :] = peak
+            stats_out[head, 1:2, :] = total
         return 0
 
     lax.fori_loop(0, queries.shape[1] // HEAD_SIZE, one_head, 0)
 
 
-def attend(bias, few, relative, queries, halves, near=None, begun=None, finish=True):
+def attend(masks, few, first_row, queries, halves, near=None, begun=None, finish=True):
     rows, width = queries.shape
     heads = width // HEAD_SIZE
-    operands = [queries]
+    operands = [*masks, queries]
     operands += [*near[0], *near[1]] if near else list(begun)
-    columns = bias.shape[0] * BLOCK if near else 0
+    columns = masks[0].shape[0] if near else 0
     for _, parts in halves:
         operands += parts
     far_bytes = sum(2 * part.size for _, parts in halves for part in parts)
-    spans = far_bytes // (4 * FAR_ROWS * width)
-    columns += spans * FAR_ROWS
+    columns += far_bytes // (4 * width)
     if finish:
         out_shape = [shape((BLOCK, width))] * 2
     else:
-        out_shape = [shape((rows, width), F32), shape((heads, rows, HEAD_SIZE), F32)]
+        out_shape = [shape((heads, HEAD_SIZE, rows), F32), shape((heads, 8, rows), F32)]
     return pl.pallas_call(
         functools.partial(
-            attend_kernel, relative, near is not None, [half[0] for half in halves], few, finish
+            attend_kernel,
+            first_row,
+            near is not None,
+            [(half, len(parts)) for half, parts in halves],
+            few,
+            finish,
         ),
-        in_specs=[IN_VMEM] * (1 + len(operands)),
+        in_specs=[IN_VMEM] * len(operands),
         out_specs=[IN_VMEM] * 2,
         out_shape=out_shape,
         compiler_params=params(far_bytes),
         cost_estimate=cost(
             4 * rows * columns * width, 4 * rows * width, heads * rows * columns
         ),
-    )(bias, *operands)
+    )(*operands)
 
 
 def mix_kernel(rows_0, rows_1, weight_0, weight_1, out):
@@ -426,12 +440,12 @@
     mine, wk, wv, keys_0, values_0 = first(normed, w_key, w_value)
     keys_1, values_1, kept_a = second(beside, wk, wv, keys_0, values_0, pattern)
     place = jnp.concatenate([after(slide_lengths, kept_a), *axes])
-    bias = make_bias(place, slides, subs, seqs, few)
+    masks = list(make_masks(place, slides, subs, seqs, few))
     query_a, wq, wo = query_first(mine, beside, w_query, w_out)
     wo_beside = swap(w_out, 1)
     if few:
         along_z = first_round(kept_a)
-        *along_z, query_a, bias = lax.optimization_barrier((*along_z, query_a, bias))
+        *along_z, query_a, masks[0] = lax.optimization_barrier((*along_z, query_a, masks[0]))
         half_a = 0, second_round(kept_a, along_z)
         across = after(across, half_a[1][0], wo_beside)
     else:
@@ -441,25 +455,26 @@
     keys_2, values_2 = keys_and_values(across, wk, wv)
     keys_3, values_3, kept_b = second(after(beyond, keys_2), wk, wv, keys_2, values_2, pattern)
     query_b = query(across, beyond, wq)
+    near = [keys_0, keys_1, keys_2, keys_3], [values_0, values_1, values_2, values_3]
+    call = functools.partial(attend, masks, few)
     if few:
-        along_z = first_round(kept_b)
-        *along_z, query_b, half_a[1][1] = lax.optimization_barrier(
-            (*along_z, query_b, half_a[1][1])
-        )
-        half_b = 1, second_round(kept_b, along_z)
-        asked = after(query_b, half_b[1][0])
+        two, *along_z = first_round(kept_b)
+        two, query_b, half_a[1][1] = lax.optimization_barrier((two, query_b, half_a[1][1]))
+        soon = second_round(kept_b, [two])
+        *along_z, soon[1] = lax.optimization_barrier((*along_z, soon[1]))
+        late = second_round(along_z[0], along_z[1:])
+        asked = after(query_b, late[0])
+        half_b = 1, [soon[0], late[0], soon[1], late[1]]
+        begun = call(2 * BLOCK, asked, [half_a], near=near, finish=False)
     else:
         half_b = 1, [lax.all_gather(kept_b, "seq", axis=0)]
-        asked = query_b
-    near = [keys_0, keys_1, keys_2, keys_3], [values_0, values_1, values_2, values_3]
-    call = functools.partial(attend, bias, few)
-    begun = call((2, 3), asked, [half_a], near=near, finish=False)
-    keep_b, send_b = call((2, 3), query_b, [half_b], begun=begun)
+        begun = call(2 * BLOCK, query_b, [half_a], near=near, finish=False)
+    keep_b, send_b = call(2 * BLOCK, query_b, [half_b], begun=begun)
     other_b = swap(send_b, 1)
     leaving = mix(keep_b, other_b, wo, wo_beside, BF16)
     arriving = swap(leaving, 2)
     query_a = after(query_a, leaving)
-    keep_a, send_a = call((0, 1), query_a, [half_a, half_b], near=near)
+    keep_a, send_a = call(0, query_a, [half_a, half_b], near=near)
     other_a = swap(send_a, 1)
     own = mix(keep_a, other_a, wo, wo_beside, F32)
     return (own + arriving.astype(F32)).astype(BF16)

time: 56.4 us -> 58.7 us (1.041)
  starting transfers between devices: 15.7 us -> 19.2 us
  waiting for transfers between devices: 20 us -> 18.8 us
    ppermute x15 -> x16, starting transfers between devices: 15.7 us -> 19.2 us  [swap(): return lax.ppermute(array, axis, [(i, i ^ bit) for i in range(count)])]
    ppermute x15 -> x16, waiting for transfers between devices: 20 us -> 18.8 us  [swap(): return lax.ppermute(array, axis, [(i, i ^ bit) for i in range(count)])]
  transfers between devices with their start and end apart: 15 -> 16, of which waited for: 11 -> 11; matrix products, arithmetic and copies ran while one was open for 0% -> 0% of each run, Pallas kernels for 29% -> 28%
where the time goes in v8:
time: 58.7 us; the launch traced here: 58.6 us
  Pallas kernels  19.4 us (33%)
  starting transfers between devices  19.2 us (33%)
  waiting for transfers between devices  18.8 us (32%)
  other arithmetic  1.04 us (2%)
    ppermute x16, starting transfers between devices, swap(): return lax.ppermute(array, axis, [(i, i ^ bit) for i in range(count)])  19.2 us
    ppermute x16, waiting for transfers between devices, swap(): return lax.ppermute(array, axis, [(i, i ^ bit) for i in range(count)])  18.8 us
    pallas_call x3, Pallas kernels, attend(): pl.pallas_call(functools.partial(attend_kernel, first_row, near is not No...  8.42 us
    pallas_call x1, Pallas kernels, first(): pl.pallas_call(first_kernel, in_specs=[IN_HBM] * 3, out_specs=[IN_VMEM] *...  3.12 us
    pallas_call x1, Pallas kernels, query_first(): pl.pallas_call(query_first_kernel, in_specs=[IN_VMEM] * 2 + [IN_HBM] * 2,...  2.64 us
    pallas_call x2, Pallas kernels, second(): pl.pallas_call(second_kernel, in_specs=[IN_VMEM] * 6, out_specs=[IN_VMEM]...  1.72 us
    pallas_call x2, Pallas kernels, mix(): pl.pallas_call(mix_kernel, in_specs=[IN_VMEM] * 4, out_specs=IN_VMEM, out...  1.43 us
  transfers between devices with their start and end apart: 16, of which 11 were waited for; matrix products, arithmetic and copies ran while one was open for 0% of the time, Pallas kernels for 28%

profile of v8, /device:TPU:0, one launch (start us, length us, event | category | flops | bytes accessed | tf_op | source)
XLA Modules:
  0.0 58.6 jit_solution(16262274884092806830)
XLA Ops:
  0.0 0.5 collective-permute-start.5
  0.5 2.9 %collective-permute-start.4 = (bf16[128,2048]{1,0:T(8,128)(2,1)}, bf16[128,2048]{1,0:T(8,128)(2,1)S(1)}, u32[]{:S(2)}, u32[]{:S(2)}) collective-permute-start(bf16[128,2048]{1,0:T(8,128)(2,1)} %rows_hbm.1), channel_id=1, source_target_pairs={{0,2},{1,3},{2,0},{3,1},{4,6},{5,7},{6,4},{7,5},{8,10},{9,11},{10,... | collective-permute-start | bytes 1572872 | tf_op jit(solution)/shard_map/ppermute | solution.py:426
  3.5 3.1 %shard_map.73 = (bf16[128,2048]{1,0:T(8,128)(2,1)S(1)}, bf16[2048,512]{1,0:T(8,128)(2,1)S(1)}, bf16[2048,512]{1,0:T(8,128)(2,1)S(1)}, bf16[128,512]{1,0:T(8,128)(2,1)S(1)}, bf16[128,512]{1,0:T(8,128)(2,1)S(1)}) custom-call(bf16[128,2048]{1,0:T(8,128)(2,1)} %rows_hbm.1, bf16[2048,512]{1,0:T(8,128)(2,1)} %wk_hbm.1, bf16[2048,512]{1,0:T(8,128)(2,1)} %wv_hbm.1), custom_call_target="tpu_custom_call" | custom-call | flops 5368709 | bytes 41943 | tf_op jit(solution)/shard_map/pallas_call | solution.py:98
  6.6 0.9 %shard_map.74 = (bf16[128,512]{1,0:T(8,128)(2,1)S(1)}, bf16[128,512]{1,0:T(8,128)(2,1)S(1)}, bf16[2,4,32,128]{3,2,1,0:T(8,128)(2,1)S(1)}) custom-call(bf16[128,2048]{1,0:T(8,128)(2,1)S(1)} %collective-permute-done.rows.rows_1, bf16[2048,512]{1,0:T(8,128)(2,1)S(1)} %get-tuple-element.45.wk, bf16[2048,512]{1,0:T(8,128)(2,1)S(1)} %get-tuple-element.46.wv, ...), custom_call_target="tpu_custom_call" | custom-call | flops 5368709 | bytes 5242 | tf_op jit(solution)/shard_map/pallas_call | solution.py:130
  7.5 2.6 %collective-permute-start.1 = (bf16[2,4,32,128]{3,2,1,0:T(8,128)(2,1)S(1)}, bf16[2,4,32,128]{3,2,1,0:T(8,128)(2,1)S(1)}, u32[]{:S(2)}, u32[]{:S(2)}) collective-permute-start(bf16[2,4,32,128]{3,2,1,0:T(8,128)(2,1)S(1)} %get-tuple-element.49), channel_id=1, source_target_pairs={{0,16},{4,20},{8,24},{12,28},{16,0},{20,4},{24,8},{28,12},{1,17},{... | collective-permute-start | bytes 196616 | tf_op jit(solution)/shard_map/ppermute | solution.py:426
  10.1 1.3 %collective-permute-start.2 = (bf16[2,4,32,128]{3,2,1,0:T(8,128)(2,1)S(1)}, bf16[2,4,32,128]{3,2,1,0:T(8,128)(2,1)S(1)}, u32[]{:S(2)}, u32[]{:S(2)}) collective-permute-start(bf16[2,4,32,128]{3,2,1,0:T(8,128)(2,1)S(1)} %get-tuple-element.49), channel_id=1, source_target_pairs={{0,24},{4,28},{8,16},{12,20},{16,8},{20,12},{24,0},{28,4},{1,25},{... | collective-permute-start | bytes 196616 | tf_op jit(solution)/shard_map/ppermute | solution.py:426
  11.7 0.7 %shard_map.76 = (bf16[512,128]{1,0:T(8,128)(2,1)S(1)}, bf16[1024,128]{1,0:T(8,128)(2,1)S(1)}) custom-call(s32[10]{0:T(128)S(1)} %pad_add_fusion.place), custom_call_target="tpu_custom_call" | custom-call | flops 83886 | bytes 2621 | tf_op jit(solution)/shard_map/pallas_call | solution.py:253
  12.4 2.6 %shard_map.75 = (bf16[256,512]{1,0:T(8,128)(2,1)S(1)}, bf16[2048,512]{1,0:T(8,128)(2,1)S(1)}, bf16[512,2048]{1,0:T(8,128)(2,1)S(1)}) custom-call(bf16[128,2048]{1,0:T(8,128)(2,1)S(1)} %get-tuple-element.50.rows_0, bf16[128,2048]{1,0:T(8,128)(2,1)S(1)} %collective-permute-done.rows.rows_1, bf16[2048,512]{1,0:T(8,128)(2,1)} %wq_hbm.1, bf16[512,2048]{1,0:T(8,128)(2,1)} %w_hbm.1), custom_call_target="tpu_custom_call" | custom-call | flops 5368709 | bytes 41943 | tf_op jit(solution)/shard_map/pallas_call | solution.py:159
  15.2 1.3 %collective-permute-done.2 = bf16[2,4,32,128]{3,2,1,0:T(8,128)(2,1)S(1)} collective-permute-done((bf16[2,4,32,128]{3,2,1,0:T(8,128)(2,1)S(1)}, bf16[2,4,32,128]{3,2,1,0:T(8,128)(2,1)S(1)}, u32[]{:S(2)}, u32[]{:S(2)}) %collective-permute-start.2) | collective-permute-done | bytes 65568 | tf_op jit(solution)/shard_map/ppermute | solution.py:426
  16.9 1.6 %collective-permute-start.8 = (bf16[4,2,4,32,128]{4,3,2,1,0:T(8,128)(2,1)S(1)}, bf16[4,2,4,32,128]{4,3,2,1,0:T(8,128)(2,1)S(1)}, u32[]{:S(2)}, u32[]{:S(2)}) collective-permute-start(bf16[4,2,4,32,128]{4,3,2,1,0:T(8,128)(2,1)S(1)} %pad_maximum_fusion.refs_9_), channel_id=1, source_target_pairs={{0,4},{4,0},{8,12},{12,8},{16,20},{20,16},{24,28},{28,24},{1,5},{5... | collective-permute-start | bytes 786440 | tf_op jit(solution)/shard_map/ppermute | solution.py:426
  18.5 0.7 %shard_map.77 = (bf16[128,512]{1,0:T(8,128)(2,1)S(1)}, bf16[128,512]{1,0:T(8,128)(2,1)S(1)}) custom-call(bf16[128,2048]{1,0:T(8,128)(2,1)S(1)} %collective-permute-done.4.rows.rows_0, bf16[2048,512]{1,0:T(8,128)(2,1)S(1)} %get-tuple-element.45.wk, bf16[2048,512]{1,0:T(8,128)(2,1)S(1)} %get-tuple-element.46.wv), custom_call_target="tpu_custom_call" | custom-call | flops 5368709 | bytes 5242 | tf_op jit(solution)/shard_map/pallas_call | solution.py:202
  19.2 0.9 %shard_map.78 = (bf16[128,512]{1,0:T(8,128)(2,1)S(1)}, bf16[128,512]{1,0:T(8,128)(2,1)S(1)}, bf16[2,4,32,128]{3,2,1,0:T(8,128)(2,1)S(1)}) custom-call(bf16[128,2048]{1,0:T(8,128)(2,1)S(1)} %collective-permute-done.6.rows.rows_1, bf16[2048,512]{1,0:T(8,128)(2,1)S(1)} %get-tuple-element.45.wk, bf16[2048,512]{1,0:T(8,128)(2,1)S(1)} %get-tuple-element.46.wv, ...), custom_call_target="tpu_custom_call" | custom-call | flops 5368709 | bytes 5242 | tf_op jit(solution)/shard_map/pallas_call | solution.py:130
  20.1 2.6 %collective-permute-start.7 = (bf16[2,4,32,128]{3,2,1,0:T(8,128)(2,1)S(1)}, bf16[2,4,32,128]{3,2,1,0:T(8,128)(2,1)S(1)}, u32[]{:S(2)}, u32[]{:S(2)}) collective-permute-start(bf16[2,4,32,128]{3,2,1,0:T(8,128)(2,1)S(1)} %get-tuple-element.64), channel_id=1, source_target_pairs={{0,16},{4,20},{8,24},{12,28},{16,0},{20,4},{24,8},{28,12},{1,17},{... | collective-permute-start | bytes 196616 | tf_op jit(solution)/shard_map/ppermute | solution.py:426
  22.7 0.7 %shard_map.79.refs_0_ = bf16[256,512]{1,0:T(8,128)(2,1)S(1)} custom-call(bf16[128,2048]{1,0:T(8,128)(2,1)S(1)} %collective-permute-done.4.rows.rows_0, bf16[128,2048]{1,0:T(8,128)(2,1)S(1)} %collective-permute-done.6.rows.rows_1, bf16[2048,512]{1,0:T(8,128)(2,1)S(1)} %get-tuple-element.65.wq), custom_call_target="tpu_custom_call" | custom-call | flops 5368709 | bytes 10485 | tf_op jit(solution)/shard_map/pallas_call | solution.py:183
  23.4 2.3 %collective-permute-done.8.refs_10_ = bf16[4,2,4,32,128]{4,3,2,1,0:T(8,128)(2,1)S(1)} collective-permute-done((bf16[4,2,4,32,128]{4,3,2,1,0:T(8,128)(2,1)S(1)}, bf16[4,2,4,32,128]{4,3,2,1,0:T(8,128)(2,1)S(1)}, u32[]{:S(2)}, u32[]{:S(2)}) %collective-permute-start.8) | collective-permute-done | bytes 262176 | tf_op jit(solution)/shard_map/ppermute | solution.py:426
  25.6 0.9 %collective-permute-done.7 = bf16[2,4,32,128]{3,2,1,0:T(8,128)(2,1)S(1)} collective-permute-done((bf16[2,4,32,128]{3,2,1,0:T(8,128)(2,1)S(1)}, bf16[2,4,32,128]{3,2,1,0:T(8,128)(2,1)S(1)}, u32[]{:S(2)}, u32[]{:S(2)}) %collective-permute-start.7) | collective-permute-done | bytes 65568 | tf_op jit(solution)/shard_map/ppermute | solution.py:426
  26.6 1.1 %collective-permute-start.11 = (bf16[2,2,4,32,128]{4,3,2,1,0:T(8,128)(2,1)S(1)}, bf16[2,2,4,32,128]{4,3,2,1,0:T(8,128)(2,1)S(1)}, u32[]{:S(2)}, u32[]{:S(2)}) collective-permute-start(bf16[2,2,4,32,128]{4,3,2,1,0:T(8,128)(2,1)S(1)} %pad_maximum_fusion.1.refs_3_.refs_11_), channel_id=1, source_target_pairs={{0,4},{4,0},{8,12},{12,8},{16,20},{20,16},{24,28},{28,24},{1,5},{5... | collective-permute-start | bytes 393224 | tf_op jit(solution)/shard_map/ppermute | solution.py:426
  28.0 3.3 %collective-permute-start.9 = (bf16[2,4,32,128]{3,2,1,0:T(8,128)(2,1)S(1)}, bf16[2,4,32,128]{3,2,1,0:T(8,128)(2,1)S(1)}, u32[]{:S(2)}, u32[]{:S(2)}) collective-permute-start(bf16[2,4,32,128]{3,2,1,0:T(8,128)(2,1)S(1)} %get-tuple-element.64), channel_id=1, source_target_pairs={{0,24},{4,28},{8,16},{12,20},{16,8},{20,12},{24,0},{28,4},{1,25},{... | collective-permute-start | bytes 196616 | tf_op jit(solution)/shard_map/ppermute | solution.py:426
  31.3 0.7 %collective-permute-done.10 = bf16[2,4,32,128]{3,2,1,0:T(8,128)(2,1)S(1)} collective-permute-done((bf16[2,4,32,128]{3,2,1,0:T(8,128)(2,1)S(1)}, bf16[2,4,32,128]{3,2,1,0:T(8,128)(2,1)S(1)}, u32[]{:S(2)}, u32[]{:S(2)}) %collective-permute-start.10) | collective-permute-done | bytes 65568 | tf_op jit(solution)/shard_map/ppermute | solution.py:426
  32.0 2.3 %collective-permute-done.9 = bf16[2,4,32,128]{3,2,1,0:T(8,128)(2,1)S(1)} collective-permute-done((bf16[2,4,32,128]{3,2,1,0:T(8,128)(2,1)S(1)}, bf16[2,4,32,128]{3,2,1,0:T(8,128)(2,1)S(1)}, u32[]{:S(2)}, u32[]{:S(2)}) %collective-permute-start.9) | collective-permute-done | bytes 65568 | tf_op jit(solution)/shard_map/ppermute | solution.py:426
  34.3 0.9 %collective-permute-start.12 = (bf16[2,2,4,32,128]{4,3,2,1,0:T(8,128)(2,1)S(1)}, bf16[2,2,4,32,128]{4,3,2,1,0:T(8,128)(2,1)S(1)}, u32[]{:S(2)}, u32[]{:S(2)}) collective-permute-start(bf16[2,2,4,32,128]{4,3,2,1,0:T(8,128)(2,1)S(1)} %pad_maximum_fusion.2.refs_4_.refs_12_), channel_id=1, source_target_pairs={{0,4},{4,0},{8,12},{12,8},{16,20},{20,16},{24,28},{28,24},{1,5},{5... | collective-permute-start | bytes 393224 | tf_op jit(solution)/shard_map/ppermute | solution.py:426
  35.2 2.8 %shard_map.80 = (f32[4,128,256]{2,1,0:T(8,128)S(1)}, f32[4,8,256]{2,1,0:T(8,128)S(1)}) custom-call(bf16[512,128]{1,0:T(8,128)(2,1)S(1)} %get-tuple-element.54.asking, bf16[1024,128]{1,0:T(8,128)(2,1)S(1)} %get-tuple-element.55.asked_of, bf16[256,512]{1,0:T(8,128)(2,1)S(1)} %shard_map.79.refs_0_, bf16[128,512]{1,0:T(8,128)(2,1)S(1)} %get-tuple-element.47.keys_0.refs_1_, ...), custom_call_target="tpu_custom_call" | custom-call | flops 4026531 | bytes 5242 | tf_op jit(solution)/shard_map/pallas_call | solution.py:379
  38.0 1.4 %collective-permute-done.12.refs_6_.refs_14_ = bf16[2,2,4,32,128]{4,3,2,1,0:T(8,128)(2,1)S(1)} collective-permute-done((bf16[2,2,4,32,128]{4,3,2,1,0:T(8,128)(2,1)S(1)}, bf16[2,2,4,32,128]{4,3,2,1,0:T(8,128)(2,1)S(1)}, u32[]{:S(2)}, u32[]{:S(2)}) %collective-permute-start.12) | collective-permute-done | bytes 131104 | tf_op jit(solution)/shard_map/ppermute | solution.py:426
  39.4 2.1 %shard_map.81 = (bf16[128,512]{1,0:T(8,128)(2,1)S(1)}, bf16[128,512]{1,0:T(8,128)(2,1)S(1)}) custom-call(bf16[512,128]{1,0:T(8,128)(2,1)S(1)} %get-tuple-element.54.asking, bf16[1024,128]{1,0:T(8,128)(2,1)S(1)} %get-tuple-element.55.asked_of, bf16[256,512]{1,0:T(8,128)(2,1)S(1)} %shard_map.79.refs_0_, f32[4,128,256]{2,1,0:T(8,128)S(1)} %get-tuple-element.76.refs_1_, ...), custom_call_target="tpu_custom_call" | custom-call | flops 1342177 | bytes 5242 | tf_op jit(solution)/shard_map/pallas_call | solution.py:379
  41.6 1.3 %collective-permute-done.13.rows_1 = bf16[128,512]{1,0:T(8,128)(2,1)S(1)} collective-permute-done((bf16[128,512]{1,0:T(8,128)(2,1)S(1)}, bf16[128,512]{1,0:T(8,128)(2,1)S(1)}, u32[]{:S(2)}, u32[]{:S(2)}) %collective-permute-start.13) | collective-permute-done | bytes 131104 | tf_op jit(solution)/shard_map/ppermute | solution.py:426
  42.9 0.7 %shard_map.82 = bf16[128,2048]{1,0:T(8,128)(2,1)S(1)} custom-call(bf16[128,512]{1,0:T(8,128)(2,1)S(1)} %get-tuple-element.79.rows_0, bf16[128,512]{1,0:T(8,128)(2,1)S(1)} %collective-permute-done.13.rows_1, bf16[512,2048]{1,0:T(8,128)(2,1)S(1)} %get-tuple-element.81.weight_0, bf16[512,2048]{1,0:T(8,128)(2,1)S(1)} %collective-permute-done.5.weight_1), custom_call_target="tpu_custom_call" | custom-call | flops 5368709 | bytes 10485 | tf_op jit(solution)/shard_map/pallas_call | solution.py:409
  43.6 1.6 %collective-permute-start.15 = (bf16[128,2048]{1,0:T(8,128)(2,1)S(1)}, bf16[128,2048]{1,0:T(8,128)(2,1)S(1)}, u32[]{:S(2)}, u32[]{:S(2)}) collective-permute-start(bf16[128,2048]{1,0:T(8,128)(2,1)S(1)} %shard_map.82), channel_id=1, source_target_pairs={{0,2},{1,3},{2,0},{3,1},{4,6},{5,7},{6,4},{7,5},{8,10},{9,11},{10,... | collective-permute-start | bytes 1572872 | tf_op jit(solution)/shard_map/ppermute | solution.py:426
  45.2 3.5 %shard_map.83 = (bf16[128,512]{1,0:T(8,128)(2,1)S(1)}, bf16[128,512]{1,0:T(8,128)(2,1)S(1)}) custom-call(bf16[512,128]{1,0:T(8,128)(2,1)S(1)} %get-tuple-element.54.asking, bf16[1024,128]{1,0:T(8,128)(2,1)S(1)} %get-tuple-element.55.asked_of, bf16[256,512]{1,0:T(8,128)(2,1)S(1)} %get-tuple-element.82.refs_0_, ...), custom_call_target="tpu_custom_call" | custom-call | flops 5368709 | bytes 5242 | tf_op jit(solution)/shard_map/pallas_call | solution.py:379
  48.8 1.3 %collective-permute-done.14.rows_1 = bf16[128,512]{1,0:T(8,128)(2,1)S(1)} collective-permute-done((bf16[128,512]{1,0:T(8,128)(2,1)S(1)}, bf16[128,512]{1,0:T(8,128)(2,1)S(1)}, u32[]{:S(2)}, u32[]{:S(2)}) %collective-permute-start.14) | collective-permute-done | bytes 131104 | tf_op jit(solution)/shard_map/ppermute | solution.py:426
  50.1 0.7 %shard_map.84 = f32[128,2048]{1,0:T(8,128)S(1)} custom-call(bf16[128,512]{1,0:T(8,128)(2,1)S(1)} %get-tuple-element.83.rows_0, bf16[128,512]{1,0:T(8,128)(2,1)S(1)} %collective-permute-done.14.rows_1, bf16[512,2048]{1,0:T(8,128)(2,1)S(1)} %get-tuple-element.81.weight_0, bf16[512,2048]{1,0:T(8,128)(2,1)S(1)} %collective-permute-done.5.weight_1), custom_call_target="tpu_custom_call" | custom-call | flops 5368709 | bytes 10485 | tf_op jit(solution)/shard_map/pallas_call | solution.py:409
  50.9 6.8 %collective-permute-done.15 = bf16[128,2048]{1,0:T(8,128)(2,1)S(1)} collective-permute-done((bf16[128,2048]{1,0:T(8,128)(2,1)S(1)}, bf16[128,2048]{1,0:T(8,128)(2,1)S(1)}, u32[]{:S(2)}, u32[]{:S(2)}) %collective-permute-start.15) | collective-permute-done | bytes 524320 | tf_op jit(solution)/shard_map/ppermute | solution.py:426
  57.7 0.9 %add_convert_fusion = bf16[128,2048]{1,0:T(8,128)(2,1)} fusion(f32[128,2048]{1,0:T(8,128)S(1)} %shard_map.84, bf16[128,2048]{1,0:T(8,128)(2,1)S(1)} %collective-permute-done.15), kind=kLoop, calls=%fused_computation | loop fusion | flops 786432 | bytes 2097152 | tf_op jit(solution)/shard_map/convert_element_type | solution.py:480
  (21 shorter events, 1.4 us)
Async XLA Ops:
  0.0 16.8 %collective-permute-start.5 = (bf16[512,2048]{1,0:T(8,128)(2,1)}, bf16[512,2048]{1,0:T(8,128)(2,1)S(1)}, u32[]{:S(2)}, u32[]{:S(2)}) collective-permute-start(bf16[512,2048]{1,0:T(8,128)(2,1)} %w_hbm.1), channel_id=1, source_target_pairs={{0,1},{1,0},{2,3},{3,2},{4,5},{5,4},{6,7},{7,6},{8,9},{9,8},{10,11... | collective-permute-start | bytes 6291464 | tf_op jit(solution)/shard_map/ppermute | solution.py:426
  0.5 6.1 %collective-permute-start = (bf16[128,2048]{1,0:T(8,128)(2,1)}, bf16[128,2048]{1,0:T(8,128)(2,1)S(1)}, u32[]{:S(2)}, u32[]{:S(2)}) collective-permute-start(bf16[128,2048]{1,0:T(8,128)(2,1)} %rows_hbm.1), channel_id=1, source_target_pairs={{0,1},{1,0},{2,3},{3,2},{4,5},{5,4},{6,7},{7,6},{8,9},{9,8},{10,11... | collective-permute-start | bytes 1572872 | tf_op jit(solution)/shard_map/ppermute | solution.py:426
  0.5 16.3 %collective-permute-start.4 = (bf16[128,2048]{1,0:T(8,128)(2,1)}, bf16[128,2048]{1,0:T(8,128)(2,1)S(1)}, u32[]{:S(2)}, u32[]{:S(2)}) collective-permute-start(bf16[128,2048]{1,0:T(8,128)(2,1)} %rows_hbm.1), channel_id=1, source_target_pairs={{0,2},{1,3},{2,0},{3,1},{4,6},{5,7},{6,4},{7,5},{8,10},{9,11},{10,... | collective-permute-start | bytes 1572872 | tf_op jit(solution)/shard_map/ppermute | solution.py:426
  3.5 3.1 %copy-start = (s32[4,128]{1,0:T(4,128)S(1)}, s32[4,128]{1,0:T(4,128)}, u32[]{:S(2)}) copy-start(s32[4,128]{1,0:T(4,128)} %pattern.3) | copy-start | bytes 6148
  6.6 5.1 %copy-start.1 = (s32[8]{0:T(128)S(1)}, s32[8]{0:T(128)}, u32[]{:S(2)}) copy-start(s32[8]{0:T(128)} %param.13) | copy-start | bytes 100
  7.5 7.7 %collective-permute-start.1 = (bf16[2,4,32,128]{3,2,1,0:T(8,128)(2,1)S(1)}, bf16[2,4,32,128]{3,2,1,0:T(8,128)(2,1)S(1)}, u32[]{:S(2)}, u32[]{:S(2)}) collective-permute-start(bf16[2,4,32,128]{3,2,1,0:T(8,128)(2,1)S(1)} %get-tuple-element.49), channel_id=1, source_target_pairs={{0,16},{4,20},{8,24},{12,28},{16,0},{20,4},{24,8},{28,12},{1,17},{... | collective-permute-start | bytes 196616 | tf_op jit(solution)/shard_map/ppermute | solution.py:426
  10.1 6.4 %collective-permute-start.2 = (bf16[2,4,32,128]{3,2,1,0:T(8,128)(2,1)S(1)}, bf16[2,4,32,128]{3,2,1,0:T(8,128)(2,1)S(1)}, u32[]{:S(2)}, u32[]{:S(2)}) collective-permute-start(bf16[2,4,32,128]{3,2,1,0:T(8,128)(2,1)S(1)} %get-tuple-element.49), channel_id=1, source_target_pairs={{0,24},{4,28},{8,16},{12,20},{16,8},{20,12},{24,0},{28,4},{1,25},{... | collective-permute-start | bytes 196616 | tf_op jit(solution)/shard_map/ppermute | solution.py:426
  11.4 5.3 %collective-permute-start.3 = (bf16[2,4,32,128]{3,2,1,0:T(8,128)(2,1)S(1)}, bf16[2,4,32,128]{3,2,1,0:T(8,128)(2,1)S(1)}, u32[]{:S(2)}, u32[]{:S(2)}) collective-permute-start(bf16[2,4,32,128]{3,2,1,0:T(8,128)(2,1)S(1)} %get-tuple-element.49), channel_id=1, source_target_pairs={{0,8},{4,12},{8,0},{12,4},{16,24},{20,28},{24,16},{28,20},{1,9},{5... | collective-permute-start | bytes 196616 | tf_op jit(solution)/shard_map/ppermute | solution.py:426
  16.8 2.4 %collective-permute-start.6 = (bf16[128,2048]{1,0:T(8,128)(2,1)S(1)}, bf16[128,2048]{1,0:T(8,128)(2,1)S(1)}, u32[]{:S(2)}, u32[]{:S(2)}) collective-permute-start(bf16[128,2048]{1,0:T(8,128)(2,1)S(1)} %collective-permute-done.4.rows.rows_0), channel_id=1, source_target_pairs={{0,1},{1,0},{2,3},{3,2},{4,5},{5,4},{6,7},{7,6},{8,9},{9,8},{10,11... | collective-permute-start | bytes 1572872 | tf_op jit(solution)/shard_map/ppermute | solution.py:426
  16.9 8.7 %collective-permute-start.8 = (bf16[4,2,4,32,128]{4,3,2,1,0:T(8,128)(2,1)S(1)}, bf16[4,2,4,32,128]{4,3,2,1,0:T(8,128)(2,1)S(1)}, u32[]{:S(2)}, u32[]{:S(2)}) collective-permute-start(bf16[4,2,4,32,128]{4,3,2,1,0:T(8,128)(2,1)S(1)} %pad_maximum_fusion.refs_9_), channel_id=1, source_target_pairs={{0,4},{4,0},{8,12},{12,8},{16,20},{20,16},{24,28},{28,24},{1,5},{5... | collective-permute-start | bytes 786440 | tf_op jit(solution)/shard_map/ppermute | solution.py:426
  20.1 6.5 %collective-permute-start.7 = (bf16[2,4,32,128]{3,2,1,0:T(8,128)(2,1)S(1)}, bf16[2,4,32,128]{3,2,1,0:T(8,128)(2,1)S(1)}, u32[]{:S(2)}, u32[]{:S(2)}) collective-permute-start(bf16[2,4,32,128]{3,2,1,0:T(8,128)(2,1)S(1)} %get-tuple-element.64), channel_id=1, source_target_pairs={{0,16},{4,20},{8,24},{12,28},{16,0},{20,4},{24,8},{28,12},{1,17},{... | collective-permute-start | bytes 196616 | tf_op jit(solution)/shard_map/ppermute | solution.py:426
  26.6 7.7 %collective-permute-start.11 = (bf16[2,2,4,32,128]{4,3,2,1,0:T(8,128)(2,1)S(1)}, bf16[2,2,4,32,128]{4,3,2,1,0:T(8,128)(2,1)S(1)}, u32[]{:S(2)}, u32[]{:S(2)}) collective-permute-start(bf16[2,2,4,32,128]{4,3,2,1,0:T(8,128)(2,1)S(1)} %pad_maximum_fusion.1.refs_3_.refs_11_), channel_id=1, source_target_pairs={{0,4},{4,0},{8,12},{12,8},{16,20},{20,16},{24,28},{28,24},{1,5},{5... | collective-permute-start | bytes 393224 | tf_op jit(solution)/shard_map/ppermute | solution.py:426
  27.7 4.3 %collective-permute-start.10 = (bf16[2,4,32,128]{3,2,1,0:T(8,128)(2,1)S(1)}, bf16[2,4,32,128]{3,2,1,0:T(8,128)(2,1)S(1)}, u32[]{:S(2)}, u32[]{:S(2)}) collective-permute-start(bf16[2,4,32,128]{3,2,1,0:T(8,128)(2,1)S(1)} %get-tuple-element.64), channel_id=1, source_target_pairs={{0,8},{4,12},{8,0},{12,4},{16,24},{20,28},{24,16},{28,20},{1,9},{5... | collective-permute-start | bytes 196616 | tf_op jit(solution)/shard_map/ppermute | solution.py:426
  28.0 6.3 %collective-permute-start.9 = (bf16[2,4,32,128]{3,2,1,0:T(8,128)(2,1)S(1)}, bf16[2,4,32,128]{3,2,1,0:T(8,128)(2,1)S(1)}, u32[]{:S(2)}, u32[]{:S(2)}) collective-permute-start(bf16[2,4,32,128]{3,2,1,0:T(8,128)(2,1)S(1)} %get-tuple-element.64), channel_id=1, source_target_pairs={{0,24},{4,28},{8,16},{12,20},{16,8},{20,12},{24,0},{28,4},{1,25},{... | collective-permute-start | bytes 196616 | tf_op jit(solution)/shard_map/ppermute | solution.py:426
  34.3 5.0 %collective-permute-start.12 = (bf16[2,2,4,32,128]{4,3,2,1,0:T(8,128)(2,1)S(1)}, bf16[2,2,4,32,128]{4,3,2,1,0:T(8,128)(2,1)S(1)}, u32[]{:S(2)}, u32[]{:S(2)}) collective-permute-start(bf16[2,2,4,32,128]{4,3,2,1,0:T(8,128)(2,1)S(1)} %pad_maximum_fusion.2.refs_4_.refs_12_), channel_id=1, source_target_pairs={{0,4},{4,0},{8,12},{12,8},{16,20},{20,16},{24,28},{28,24},{1,5},{5... | collective-permute-start | bytes 393224 | tf_op jit(solution)/shard_map/ppermute | solution.py:426
  41.5 1.4 %collective-permute-start.13 = (bf16[128,512]{1,0:T(8,128)(2,1)S(1)}, bf16[128,512]{1,0:T(8,128)(2,1)S(1)}, u32[]{:S(2)}, u32[]{:S(2)}) collective-permute-start(bf16[128,512]{1,0:T(8,128)(2,1)S(1)} %get-tuple-element.80), channel_id=1, source_target_pairs={{0,1},{1,0},{2,3},{3,2},{4,5},{5,4},{6,7},{7,6},{8,9},{9,8},{10,11... | collective-permute-start | bytes 393224 | tf_op jit(solution)/shard_map/ppermute | solution.py:426
  43.6 14.0 %collective-permute-start.15 = (bf16[128,2048]{1,0:T(8,128)(2,1)S(1)}, bf16[128,2048]{1,0:T(8,128)(2,1)S(1)}, u32[]{:S(2)}, u32[]{:S(2)}) collective-permute-start(bf16[128,2048]{1,0:T(8,128)(2,1)S(1)} %shard_map.82), channel_id=1, source_target_pairs={{0,2},{1,3},{2,0},{3,1},{4,6},{5,7},{6,4},{7,5},{8,10},{9,11},{10,... | collective-permute-start | bytes 1572872 | tf_op jit(solution)/shard_map/ppermute | solution.py:426
  48.7 1.4 %collective-permute-start.14 = (bf16[128,512]{1,0:T(8,128)(2,1)S(1)}, bf16[128,512]{1,0:T(8,128)(2,1)S(1)}, u32[]{:S(2)}, u32[]{:S(2)}) collective-permute-start(bf16[128,512]{1,0:T(8,128)(2,1)S(1)} %get-tuple-element.84), channel_id=1, source_target_pairs={{0,1},{1,0},{2,3},{3,2},{4,5},{5,4},{6,7},{7,6},{8,9},{9,8},{10,11... | collective-permute-start | bytes 393224 | tf_op jit(solution)/shard_map/ppermute | solution.py:426

commit v9 on v8

--- a/solution.py
+++ b/solution.py
@@ -137,7 +137,9 @@
     )(rows, wk, wv, keys_0, values_0, pattern)
 
 
-def query_first_kernel(rows_0, rows_1, wq_hbm, w_hbm, queries, wq, w, sems):
+def query_kernel(*refs):
+    rows, (wq_hbm, w_hbm), outs, (wq, sems) = refs[:4], refs[4:6], refs[6:9], refs[9:]
+    w = outs[2]
     parts = halves_of(wq.shape[1])
     copies = [
         pltpu.make_async_copy(wq_hbm.at[:, part], wq.at[:, part], sems.at[index])
@@ -146,48 +148,29 @@
     copies.append(pltpu.make_async_copy(w_hbm, w, sems.at[len(parts)]))
     for copy in copies:
         copy.start()
-    rows = jnp.concatenate([rows_0[...], rows_1[...]], axis=0)
     for part, copy in zip(parts, copies):
         copy.wait()
-        queries[:, part] = dot(rows, wq[:, part]).astype(BF16)
+        for pair, out in ((rows[:2], outs[0]), (rows[2:], outs[1])):
+            both = jnp.concatenate([ref[...] for ref in pair], axis=0)
+            out[:, part] = dot(both, wq[:, part]).astype(BF16)
     copies[-1].wait()
 
 
-def query_first(rows_0, rows_1, w_query, w_out):
-    count, depth = rows_0.shape
+def query(rows, w_query, w_out):
+    count, depth = rows[0].shape
     width = w_query.shape[1]
     return pl.pallas_call(
-        query_first_kernel,
-        in_specs=[IN_VMEM] * 2 + [IN_HBM] * 2,
+        query_kernel,
+        in_specs=[IN_VMEM] * 4 + [IN_HBM] * 2,
         out_specs=[IN_VMEM] * 3,
-        out_shape=[
-            shape((2 * count, width)),
+        out_shape=[shape((2 * count, width))] * 2 + [pltpu.VMEM(w_out.shape, BF16)],
+        scratch_shapes=[
             pltpu.VMEM(w_query.shape, BF16),
-            pltpu.VMEM(w_out.shape, BF16),
+            pltpu.SemaphoreType.DMA((1 + len(halves_of(width)),)),
         ],
-        scratch_shapes=[pltpu.SemaphoreType.DMA((1 + len(halves_of(width)),))],
         compiler_params=params(),
-        cost_estimate=cost(4 * count * depth * width, 4 * depth * width),
-    )(rows_0, rows_1, keep_in_hbm(w_query), keep_in_hbm(w_out))
-
-
-def query_kernel(rows_0, rows_1, wq, queries):
-    rows = jnp.concatenate([rows_0[...], rows_1[...]], axis=0)
-    for part in halves_of(wq.shape[1]):
-        queries[:, part] = dot(rows, wq[:, part]).astype(BF16)
-
-
-def query(rows_0, rows_1, wq):
-    count, depth = rows_0.shape
-    width = wq.shape[1]
-    return pl.pallas_call(
-        query_kernel,
-        in_specs=[IN_VMEM] * 3,
-        out_specs=IN_VMEM,
-        out_shape=shape((2 * count, width)),
-        compiler_params=params(),
-        cost_estimate=cost(4 * count * depth * width, 4 * count * depth),
-    )(rows_0, rows_1, wq)
+        cost_estimate=cost(8 * count * depth * width, 4 * depth * width),
+    )(*rows, keep_in_hbm(w_query), keep_in_hbm(w_out))
 
 
 def across_kernel(rows, wk, wv, keys, values):
@@ -271,20 +254,27 @@
 
 
 def begin(queries, keys, values):
-    scores = scores_of(keys, queries)
-    peak = jnp.max(scores, axis=0, keepdims=True)
-    weight = jnp.exp2((scores - peak) * SCALE)
-    return peak, jnp.sum(weight, axis=0, keepdims=True), gather(values, weight)
+    scores = [scores_of(k, q) for k, q in zip(keys, queries)]
+    peak = [jnp.max(each, axis=0, keepdims=True) for each in scores]
+    weight = [jnp.exp2((each - top) * SCALE) for each, top in zip(scores, peak)]
+    total = [jnp.sum(each, axis=0, keepdims=True) for each in weight]
+    return peak, total, [gather(v, each) for v, each in zip(values, weight)]
 
 
 def update(queries, keys, values, state):
-    peak, total, gathered = state
-    scores = scores_of(keys, queries)
-    higher = jnp.maximum(peak, jnp.max(scores, axis=0, keepdims=True))
-    shrink = jnp.exp2((peak - higher) * SCALE)
-    weight = jnp.exp2((scores - higher) * SCALE)
-    total = total * shrink + jnp.sum(weight, axis=0, keepdims=True)
-    return higher, total, gathered * shrink + gather(values, weight)
+    scores = [scores_of(k, q) for k, q in zip(keys, queries)]
+    higher = [
+        jnp.maximum(top, jnp.max(each, axis=0, keepdims=True))
+        for top, each in zip(state[0], scores)
+    ]
+    shrink = [jnp.exp2((top - new) * SCALE) for top, new in zip(state[0], higher)]
+    weight = [jnp.exp2((each - new) * SCALE) for each, new in zip(scores, higher)]
+    total = [
+        old * less + jnp.sum(each, axis=0, keepdims=True)
+        for old, less, each in zip(state[1], shrink, weight)
+    ]
+    added = [gather(v, each) for v, each in zip(values, weight)]
+    return higher, total, [old * less + new for old, less, new in zip(state[2], shrink, added)]
 
 
 def attend_kernel(first_row, near, halves, few, finish, asking, asked_of, *refs):
@@ -304,35 +294,47 @@
     span = asking.shape[0]
     half_count = (asked_of.shape[0] - span) // BLOCKS_HALF
 
-    def one_head(head, _):
-        columns = pl.ds(pl.multiple_of(head * HEAD_SIZE, HEAD_SIZE), HEAD_SIZE)
-        asked = jnp.concatenate(
-            [queries[:, columns], asking[first_row : first_row + rows, :]], axis=1
-        )
+    heads = queries.shape[1] // HEAD_SIZE
+    group = heads if few and not near else 1
+
+    def some_heads(turn, _):
+        those = [turn * group + i for i in range(group)]
+        columns = [
+            pl.ds(pl.multiple_of(head * HEAD_SIZE, HEAD_SIZE), HEAD_SIZE)
+            if group < heads
+            else slice(head * HEAD_SIZE, (head + 1) * HEAD_SIZE)
+            for head in those
+        ]
+        row_marks = asking[first_row : first_row + rows, :]
+        asked = [jnp.concatenate([queries[:, each], row_marks], axis=1) for each in columns]
 
         def marked(parts, where):
             return jnp.concatenate([jnp.concatenate(parts, axis=0), asked_of[where, :]], axis=1)
 
-        keyed, valued = [], []
+        def ready(head, each):
+            keyed, valued = [], []
+            if near:
+                keyed.append(marked([ref[:, each] for ref in keys], slice(0, span)))
+                valued += [ref[:, each] for ref in values]
+            if few:
+                for half, parts in far:
+                    start = span + half * half_count
+                    pieces = [(ref, i) for ref in parts for i in range(ref.shape[0])]
+                    where = slice(start, start + half_count)
+                    keyed.append(marked([ref[i, 0, head] for ref, i in pieces], where))
+                    valued += [ref[i, 1, head] for ref, i in pieces]
+            return jnp.concatenate(keyed, axis=0), jnp.concatenate(valued, axis=0)
+
         if near:
-            keyed.append(marked([ref[:, columns] for ref in keys], slice(0, span)))
-            valued += [ref[:, columns] for ref in values]
-        if few:
-            for half, parts in far:
-                start = span + half * half_count
-                pieces = [(ref, i) for ref in parts for i in range(ref.shape[0])]
-                keyed.append(
-                    marked([ref[i, 0, head] for ref, i in pieces], slice(start, start + half_count))
-                )
-                valued += [ref[i, 1, head] for ref, i in pieces]
-        if near:
-            ready = asked, jnp.concatenate(keyed, axis=0), jnp.concatenate(valued, axis=0)
-            state = begin(*ready)
+            state = begin(asked, *zip(*map(ready, those, columns)))
         else:
-            state = stats_in[head, 0:1, :], stats_in[head, 1:2, :], gathered_in[head]
+            state = (
+                [stats_in[head, 0:1, :] for head in those],
+                [stats_in[head, 1:2, :] for head in those],
+                [gathered_in[head] for head in those],
+            )
             if few:
-                ready = asked, jnp.concatenate(keyed, axis=0), jnp.concatenate(valued, axis=0)
-                state = update(*ready, state)
+                state = update(asked, *zip(*map(ready, those, columns)), state)
         if not few:
             for half, (part,) in far:
                 start = span + half * half_count
@@ -341,25 +343,36 @@
                     base = number * GROUP
                     width = GROUP * FAR_ROWS
                     where = pl.ds(pl.multiple_of(start + number * width, width), width)
-                    keyed = marked([part[base + i, 0, head] for i in range(GROUP)], where)
-                    valued = jnp.concatenate([part[base + i, 1, head] for i in range(GROUP)], axis=0)
-                    return update(asked, keyed, valued, state)
+                    found = [
+                        [
+                            marked([part[base + i, 0, head] for i in range(GROUP)], where)
+                            for head in those
+                        ],
+                        [
+                            jnp.concatenate([part[base + i, 1, head] for i in range(GROUP)], axis=0)
+                            for head in those
+                        ],
+                    ]
+                    return update(asked, *found, state)
 
                 state = lax.fori_loop(0, part.shape[0] // GROUP, step, state)
-        peak, total, gathered = state
-        if finish:
-            keep, send = refs
-            context = (gathered / total).T.astype(BF16)
-            keep[:, columns] = context[:BLOCK]
-            send[:, columns] = context[BLOCK:]
-        else:
-            gathered_out, stats_out = refs
-            gathered_out[head] = gathered
-            stats_out[head, 0:1, :] = peak
-            stats_out[head, 1:2, :] = total
+        for head, each, peak, total, gathered in zip(those, columns, *state):
+            if finish:
+                keep, send = refs
+                context = (gathered / total).T.astype(BF16)
+                keep[:, each] = context[:BLOCK]
+                send[:, each] = context[BLOCK:]
+            else:
+                gathered_out, stats_out = refs
+                gathered_out[head] = gathered
+                stats_out[head, 0:1, :] = peak
+                stats_out[head, 1:2, :] = total
         return 0
 
-    lax.fori_loop(0, queries.shape[1] // HEAD_SIZE, one_head, 0)
+    if group == heads:
+        some_heads(0, 0)
+    else:
+        lax.fori_loop(0, heads // group, some_heads, 0)
 
 
 def attend(masks, few, first_row, queries, halves, near=None, begun=None, finish=True):
@@ -441,11 +454,10 @@
     keys_1, values_1, kept_a = second(beside, wk, wv, keys_0, values_0, pattern)
     place = jnp.concatenate([after(slide_lengths, kept_a), *axes])
     masks = list(make_masks(place, slides, subs, seqs, few))
-    query_a, wq, wo = query_first(mine, beside, w_query, w_out)
     wo_beside = swap(w_out, 1)
     if few:
         along_z = first_round(kept_a)
-        *along_z, query_a, masks[0] = lax.optimization_barrier((*along_z, query_a, masks[0]))
+        *along_z, masks[0] = lax.optimization_barrier((*along_z, masks[0]))
         half_a = 0, second_round(kept_a, along_z)
         across = after(across, half_a[1][0], wo_beside)
     else:
@@ -454,17 +466,16 @@
     beyond = swap(across, 1)
     keys_2, values_2 = keys_and_values(across, wk, wv)
     keys_3, values_3, kept_b = second(after(beyond, keys_2), wk, wv, keys_2, values_2, pattern)
-    query_b = query(across, beyond, wq)
+    query_a, query_b, wo = query([mine, beside, across, beyond], w_query, w_out)
     near = [keys_0, keys_1, keys_2, keys_3], [values_0, values_1, values_2, values_3]
     call = functools.partial(attend, masks, few)
     if few:
-        two, *along_z = first_round(kept_b)
-        two, query_b, half_a[1][1] = lax.optimization_barrier((two, query_b, half_a[1][1]))
-        soon = second_round(kept_b, [two])
-        *along_z, soon[1] = lax.optimization_barrier((*along_z, soon[1]))
-        late = second_round(along_z[0], along_z[1:])
-        asked = after(query_b, late[0])
-        half_b = 1, [soon[0], late[0], soon[1], late[1]]
+        along_z = first_round(kept_b)
+        *along_z, query_b, half_a[1][1] = lax.optimization_barrier(
+            (*along_z, query_b, half_a[1][1])
+        )
+        half_b = 1, second_round(kept_b, along_z)
+        asked = after(query_b, half_b[1][0])
         begun = call(2 * BLOCK, asked, [half_a], near=near, finish=False)
     else:
         half_b = 1, [lax.all_gather(kept_b, "seq", axis=0)]

time: 58.7 us -> 55.1 us (0.939)
  starting transfers between devices: 19.2 us -> 15.6 us
  waiting for transfers between devices: 18.8 us -> 20.6 us
  Pallas kernels: 19.4 us -> 17.6 us
    ppermute x16 -> x15, starting transfers between devices: 19.2 us -> 15.6 us  [swap(): return lax.ppermute(array, axis, [(i, i ^ bit) for i in range(count)])]
    ppermute x16 -> x15, waiting for transfers between devices: 18.8 us -> 20.6 us  [swap(): return lax.ppermute(array, axis, [(i, i ^ bit) for i in range(count)])]
    pallas_call x3, Pallas kernels: 8.42 us -> 7.06 us  [attend(): pl.pallas_call(functools.partial(attend_kernel, first_row, near is not No...]
    pallas_call x2 -> x1, Pallas kernels: 3.34 us -> 2.67 us  [query(): pl.pallas_call(query_kernel, in_specs=[IN_VMEM] * 4 + [IN_HBM] * 2, out_s...]
  transfers between devices with their start and end apart: 16 -> 15, of which waited for: 11 -> 10; matrix products, arithmetic and copies ran while one was open for 0% -> 0% of each run, Pallas kernels for 28% -> 29%
where the time goes in v9:
time: 55.1 us; the launch traced here: 55 us
  waiting for transfers between devices  20.6 us (37%)
  Pallas kernels  17.6 us (32%)
  starting transfers between devices  15.6 us (28%)
  other arithmetic  1.05 us (2%)
    ppermute x15, waiting for transfers between devices, swap(): return lax.ppermute(array, axis, [(i, i ^ bit) for i in range(count)])  20.6 us
    ppermute x15, starting transfers between devices, swap(): return lax.ppermute(array, axis, [(i, i ^ bit) for i in range(count)])  15.6 us
    pallas_call x3, Pallas kernels, attend(): pl.pallas_call(functools.partial(attend_kernel, first_row, near is not No...  7.06 us
    pallas_call x1, Pallas kernels, first(): pl.pallas_call(first_kernel, in_specs=[IN_HBM] * 3, out_specs=[IN_VMEM] *...  3.14 us
    pallas_call x1, Pallas kernels, query(): pl.pallas_call(query_kernel, in_specs=[IN_VMEM] * 4 + [IN_HBM] * 2, out_s...  2.67 us
    pallas_call x2, Pallas kernels, second(): pl.pallas_call(second_kernel, in_specs=[IN_VMEM] * 6, out_specs=[IN_VMEM]...  1.81 us
    pallas_call x2, Pallas kernels, mix(): pl.pallas_call(mix_kernel, in_specs=[IN_VMEM] * 4, out_specs=IN_VMEM, out...  1.43 us
  transfers between devices with their start and end apart: 15, of which 10 were waited for; matrix products, arithmetic and copies ran while one was open for 0% of the time, Pallas kernels for 29%

profile of v9, /device:TPU:0, one launch (start us, length us, event | category | flops | bytes accessed | tf_op | source)
XLA Modules:
  0.0 55.0 jit_solution(16270501224540402716)
XLA Ops:
  0.0 0.5 collective-permute-start.5
  0.5 2.9 %collective-permute-start.4 = (bf16[128,2048]{1,0:T(8,128)(2,1)}, bf16[128,2048]{1,0:T(8,128)(2,1)S(1)}, u32[]{:S(2)}, u32[]{:S(2)}) collective-permute-start(bf16[128,2048]{1,0:T(8,128)(2,1)} %rows_hbm.1), channel_id=1, source_target_pairs={{0,2},{1,3},{2,0},{3,1},{4,6},{5,7},{6,4},{7,5},{8,10},{9,11},{10,... | collective-permute-start | bytes 1572872 | tf_op jit(solution)/shard_map/ppermute | solution.py:439
  3.5 3.1 %shard_map.73 = (bf16[128,2048]{1,0:T(8,128)(2,1)S(1)}, bf16[2048,512]{1,0:T(8,128)(2,1)S(1)}, bf16[2048,512]{1,0:T(8,128)(2,1)S(1)}, bf16[128,512]{1,0:T(8,128)(2,1)S(1)}, bf16[128,512]{1,0:T(8,128)(2,1)S(1)}) custom-call(bf16[128,2048]{1,0:T(8,128)(2,1)} %rows_hbm.1, bf16[2048,512]{1,0:T(8,128)(2,1)} %wk_hbm.1, bf16[2048,512]{1,0:T(8,128)(2,1)} %wv_hbm.1), custom_call_target="tpu_custom_call" | custom-call | flops 5368709 | bytes 41943 | tf_op jit(solution)/shard_map/pallas_call | solution.py:98
  6.6 0.9 %shard_map.74 = (bf16[128,512]{1,0:T(8,128)(2,1)S(1)}, bf16[128,512]{1,0:T(8,128)(2,1)S(1)}, bf16[2,4,32,128]{3,2,1,0:T(8,128)(2,1)S(1)}) custom-call(bf16[128,2048]{1,0:T(8,128)(2,1)S(1)} %collective-permute-done.rows.refs_1_, bf16[2048,512]{1,0:T(8,128)(2,1)S(1)} %get-tuple-element.43.wk, bf16[2048,512]{1,0:T(8,128)(2,1)S(1)} %get-tuple-element.44.wv, ...), custom_call_target="tpu_custom_call" | custom-call | flops 5368709 | bytes 5242 | tf_op jit(solution)/shard_map/pallas_call | solution.py:130
  7.5 2.6 %collective-permute-start.1 = (bf16[2,4,32,128]{3,2,1,0:T(8,128)(2,1)S(1)}, bf16[2,4,32,128]{3,2,1,0:T(8,128)(2,1)S(1)}, u32[]{:S(2)}, u32[]{:S(2)}) collective-permute-start(bf16[2,4,32,128]{3,2,1,0:T(8,128)(2,1)S(1)} %get-tuple-element.47), channel_id=1, source_target_pairs={{0,16},{4,20},{8,24},{12,28},{16,0},{20,4},{24,8},{28,12},{1,17},{... | collective-permute-start | bytes 196616 | tf_op jit(solution)/shard_map/ppermute | solution.py:439
  10.1 1.3 %collective-permute-start.2 = (bf16[2,4,32,128]{3,2,1,0:T(8,128)(2,1)S(1)}, bf16[2,4,32,128]{3,2,1,0:T(8,128)(2,1)S(1)}, u32[]{:S(2)}, u32[]{:S(2)}) collective-permute-start(bf16[2,4,32,128]{3,2,1,0:T(8,128)(2,1)S(1)} %get-tuple-element.47), channel_id=1, source_target_pairs={{0,24},{4,28},{8,16},{12,20},{16,8},{20,12},{24,0},{28,4},{1,25},{... | collective-permute-start | bytes 196616 | tf_op jit(solution)/shard_map/ppermute | solution.py:439
  11.8 0.7 %shard_map.75 = (bf16[512,128]{1,0:T(8,128)(2,1)S(1)}, bf16[1024,128]{1,0:T(8,128)(2,1)S(1)}) custom-call(s32[10]{0:T(128)S(1)} %pad_add_fusion.place), custom_call_target="tpu_custom_call" | custom-call | flops 83886 | bytes 2621 | tf_op jit(solution)/shard_map/pallas_call | solution.py:236
  12.5 2.7 %collective-permute-done.1 = bf16[2,4,32,128]{3,2,1,0:T(8,128)(2,1)S(1)} collective-permute-done((bf16[2,4,32,128]{3,2,1,0:T(8,128)(2,1)S(1)}, bf16[2,4,32,128]{3,2,1,0:T(8,128)(2,1)S(1)}, u32[]{:S(2)}, u32[]{:S(2)}) %collective-permute-start.1) | collective-permute-done | bytes 65568 | tf_op jit(solution)/shard_map/ppermute | solution.py:439
  15.2 1.3 %collective-permute-done.2 = bf16[2,4,32,128]{3,2,1,0:T(8,128)(2,1)S(1)} collective-permute-done((bf16[2,4,32,128]{3,2,1,0:T(8,128)(2,1)S(1)}, bf16[2,4,32,128]{3,2,1,0:T(8,128)(2,1)S(1)}, u32[]{:S(2)}, u32[]{:S(2)}) %collective-permute-start.2) | collective-permute-done | bytes 65568 | tf_op jit(solution)/shard_map/ppermute | solution.py:439
  16.5 0.3 collective-permute-done.3
  16.9 1.6 %collective-permute-start.10 = (bf16[4,2,4,32,128]{4,3,2,1,0:T(8,128)(2,1)S(1)}, bf16[4,2,4,32,128]{4,3,2,1,0:T(8,128)(2,1)S(1)}, u32[]{:S(2)}, u32[]{:S(2)}) collective-permute-start(bf16[4,2,4,32,128]{4,3,2,1,0:T(8,128)(2,1)S(1)} %pad_maximum_fusion.refs_9_), channel_id=1, source_target_pairs={{0,4},{4,0},{8,12},{12,8},{16,20},{20,16},{24,28},{28,24},{1,5},{5... | collective-permute-start | bytes 786440 | tf_op jit(solution)/shard_map/ppermute | solution.py:439
  18.5 0.8 %shard_map.77 = (bf16[128,512]{1,0:T(8,128)(2,1)S(1)}, bf16[128,512]{1,0:T(8,128)(2,1)S(1)}) custom-call(bf16[128,2048]{1,0:T(8,128)(2,1)S(1)} %collective-permute-done.4.refs_2_.rows, bf16[2048,512]{1,0:T(8,128)(2,1)S(1)} %get-tuple-element.43.wk, bf16[2048,512]{1,0:T(8,128)(2,1)S(1)} %get-tuple-element.44.wv), custom_call_target="tpu_custom_call" | custom-call | flops 5368709 | bytes 5242 | tf_op jit(solution)/shard_map/pallas_call | solution.py:185
  19.3 0.9 %shard_map.78 = (bf16[128,512]{1,0:T(8,128)(2,1)S(1)}, bf16[128,512]{1,0:T(8,128)(2,1)S(1)}, bf16[2,4,32,128]{3,2,1,0:T(8,128)(2,1)S(1)}) custom-call(bf16[128,2048]{1,0:T(8,128)(2,1)S(1)} %collective-permute-done.6.refs_3_.rows, bf16[2048,512]{1,0:T(8,128)(2,1)S(1)} %get-tuple-element.43.wk, bf16[2048,512]{1,0:T(8,128)(2,1)S(1)} %get-tuple-element.44.wv, ...), custom_call_target="tpu_custom_call" | custom-call | flops 5368709 | bytes 5242 | tf_op jit(solution)/shard_map/pallas_call | solution.py:130
  20.2 2.6 %collective-permute-start.7 = (bf16[2,4,32,128]{3,2,1,0:T(8,128)(2,1)S(1)}, bf16[2,4,32,128]{3,2,1,0:T(8,128)(2,1)S(1)}, u32[]{:S(2)}, u32[]{:S(2)}) collective-permute-start(bf16[2,4,32,128]{3,2,1,0:T(8,128)(2,1)S(1)} %get-tuple-element.61), channel_id=1, source_target_pairs={{0,16},{4,20},{8,24},{12,28},{16,0},{20,4},{24,8},{28,12},{1,17},{... | collective-permute-start | bytes 196616 | tf_op jit(solution)/shard_map/ppermute | solution.py:439
  22.8 0.6 %collective-permute-start.8 = (bf16[2,4,32,128]{3,2,1,0:T(8,128)(2,1)S(1)}, bf16[2,4,32,128]{3,2,1,0:T(8,128)(2,1)S(1)}, u32[]{:S(2)}, u32[]{:S(2)}) collective-permute-start(bf16[2,4,32,128]{3,2,1,0:T(8,128)(2,1)S(1)} %get-tuple-element.61), channel_id=1, source_target_pairs={{0,24},{4,28},{8,16},{12,20},{16,8},{20,12},{24,0},{28,4},{1,25},{... | collective-permute-start | bytes 196616 | tf_op jit(solution)/shard_map/ppermute | solution.py:439
  23.4 0.5 collective-permute-start.9
  23.9 2.7 %shard_map.76 = (bf16[256,512]{1,0:T(8,128)(2,1)S(1)}, bf16[256,512]{1,0:T(8,128)(2,1)S(1)}, bf16[512,2048]{1,0:T(8,128)(2,1)S(1)}) custom-call(bf16[128,2048]{1,0:T(8,128)(2,1)S(1)} %get-tuple-element.52.refs_0_, bf16[128,2048]{1,0:T(8,128)(2,1)S(1)} %collective-permute-done.rows.refs_1_, bf16[128,2048]{1,0:T(8,128)(2,1)S(1)} %collective-permute-done.4.refs_2_.rows, ...), custom_call_target="tpu_custom_call" | custom-call | flops 10737418 | bytes 41943 | tf_op jit(solution)/shard_map/pallas_call | solution.py:162
  26.6 1.4 %collective-permute-done.7 = bf16[2,4,32,128]{3,2,1,0:T(8,128)(2,1)S(1)} collective-permute-done((bf16[2,4,32,128]{3,2,1,0:T(8,128)(2,1)S(1)}, bf16[2,4,32,128]{3,2,1,0:T(8,128)(2,1)S(1)}, u32[]{:S(2)}, u32[]{:S(2)}) %collective-permute-start.7) | collective-permute-done | bytes 65568 | tf_op jit(solution)/shard_map/ppermute | solution.py:439
  27.9 1.3 %collective-permute-done.8 = bf16[2,4,32,128]{3,2,1,0:T(8,128)(2,1)S(1)} collective-permute-done((bf16[2,4,32,128]{3,2,1,0:T(8,128)(2,1)S(1)}, bf16[2,4,32,128]{3,2,1,0:T(8,128)(2,1)S(1)}, u32[]{:S(2)}, u32[]{:S(2)}) %collective-permute-start.8) | collective-permute-done | bytes 65568 | tf_op jit(solution)/shard_map/ppermute | solution.py:439
  29.2 0.3 collective-permute-done.9
  29.6 1.1 %collective-permute-start.11 = (bf16[4,2,4,32,128]{4,3,2,1,0:T(8,128)(2,1)S(1)}, bf16[4,2,4,32,128]{4,3,2,1,0:T(8,128)(2,1)S(1)}, u32[]{:S(2)}, u32[]{:S(2)}) collective-permute-start(bf16[4,2,4,32,128]{4,3,2,1,0:T(8,128)(2,1)S(1)} %pad_maximum_fusion.1.refs_3_.refs_11_), channel_id=1, source_target_pairs={{0,4},{4,0},{8,12},{12,8},{16,20},{20,16},{24,28},{28,24},{1,5},{5... | collective-permute-start | bytes 786440 | tf_op jit(solution)/shard_map/ppermute | solution.py:439
  30.6 2.8 %shard_map.79 = (f32[4,128,256]{2,1,0:T(8,128)S(1)}, f32[4,8,256]{2,1,0:T(8,128)S(1)}) custom-call(bf16[512,128]{1,0:T(8,128)(2,1)S(1)} %get-tuple-element.50.asking, bf16[1024,128]{1,0:T(8,128)(2,1)S(1)} %get-tuple-element.51.asked_of, bf16[256,512]{1,0:T(8,128)(2,1)S(1)} %get-tuple-element.67.refs_0_, ...), custom_call_target="tpu_custom_call" | custom-call | flops 4026531 | bytes 5242 | tf_op jit(solution)/shard_map/pallas_call | solution.py:392
  33.4 3.7 %collective-permute-done.11.refs_4_.refs_12_ = bf16[4,2,4,32,128]{4,3,2,1,0:T(8,128)(2,1)S(1)} collective-permute-done((bf16[4,2,4,32,128]{4,3,2,1,0:T(8,128)(2,1)S(1)}, bf16[4,2,4,32,128]{4,3,2,1,0:T(8,128)(2,1)S(1)}, u32[]{:S(2)}, u32[]{:S(2)}) %collective-permute-start.11) | collective-permute-done | bytes 262176 | tf_op jit(solution)/shard_map/ppermute | solution.py:439
  37.1 0.8 %shard_map.80 = (bf16[128,512]{1,0:T(8,128)(2,1)S(1)}, bf16[128,512]{1,0:T(8,128)(2,1)S(1)}) custom-call(bf16[512,128]{1,0:T(8,128)(2,1)S(1)} %get-tuple-element.50.asking, bf16[1024,128]{1,0:T(8,128)(2,1)S(1)} %get-tuple-element.51.asked_of, bf16[256,512]{1,0:T(8,128)(2,1)S(1)} %get-tuple-element.67.refs_0_, f32[4,128,256]{2,1,0:T(8,128)S(1)} %get-tuple-element.73.refs_1_, ...), custom_call_target="tpu_custom_call" | custom-call | flops 1342177 | bytes 5242 | tf_op jit(solution)/shard_map/pallas_call | solution.py:392
  38.0 1.3 %collective-permute-done.12.rows_1 = bf16[128,512]{1,0:T(8,128)(2,1)S(1)} collective-permute-done((bf16[128,512]{1,0:T(8,128)(2,1)S(1)}, bf16[128,512]{1,0:T(8,128)(2,1)S(1)}, u32[]{:S(2)}, u32[]{:S(2)}) %collective-permute-start.12) | collective-permute-done | bytes 131104 | tf_op jit(solution)/shard_map/ppermute | solution.py:439
  39.3 0.7 %shard_map.81 = bf16[128,2048]{1,0:T(8,128)(2,1)S(1)} custom-call(bf16[128,512]{1,0:T(8,128)(2,1)S(1)} %get-tuple-element.75.rows_0, bf16[128,512]{1,0:T(8,128)(2,1)S(1)} %collective-permute-done.12.rows_1, bf16[512,2048]{1,0:T(8,128)(2,1)S(1)} %get-tuple-element.77.weight_0, bf16[512,2048]{1,0:T(8,128)(2,1)S(1)} %collective-permute-done.5.weight_1), custom_call_target="tpu_custom_call" | custom-call | flops 5368709 | bytes 10485 | tf_op jit(solution)/shard_map/pallas_call | solution.py:422
  40.0 1.4 %collective-permute-start.14 = (bf16[128,2048]{1,0:T(8,128)(2,1)S(1)}, bf16[128,2048]{1,0:T(8,128)(2,1)S(1)}, u32[]{:S(2)}, u32[]{:S(2)}) collective-permute-start(bf16[128,2048]{1,0:T(8,128)(2,1)S(1)} %shard_map.81), channel_id=1, source_target_pairs={{0,2},{1,3},{2,0},{3,1},{4,6},{5,7},{6,4},{7,5},{8,10},{9,11},{10,... | collective-permute-start | bytes 1572872 | tf_op jit(solution)/shard_map/ppermute | solution.py:439
  41.4 3.5 %shard_map.82 = (bf16[128,512]{1,0:T(8,128)(2,1)S(1)}, bf16[128,512]{1,0:T(8,128)(2,1)S(1)}) custom-call(bf16[512,128]{1,0:T(8,128)(2,1)S(1)} %get-tuple-element.50.asking, bf16[1024,128]{1,0:T(8,128)(2,1)S(1)} %get-tuple-element.51.asked_of, bf16[256,512]{1,0:T(8,128)(2,1)S(1)} %get-tuple-element.78.refs_0_, ...), custom_call_target="tpu_custom_call" | custom-call | flops 5368709 | bytes 5242 | tf_op jit(solution)/shard_map/pallas_call | solution.py:392
  45.0 1.3 %collective-permute-done.13.rows_1 = bf16[128,512]{1,0:T(8,128)(2,1)S(1)} collective-permute-done((bf16[128,512]{1,0:T(8,128)(2,1)S(1)}, bf16[128,512]{1,0:T(8,128)(2,1)S(1)}, u32[]{:S(2)}, u32[]{:S(2)}) %collective-permute-start.13) | collective-permute-done | bytes 131104 | tf_op jit(solution)/shard_map/ppermute | solution.py:439
  46.4 0.7 %shard_map.83 = f32[128,2048]{1,0:T(8,128)S(1)} custom-call(bf16[128,512]{1,0:T(8,128)(2,1)S(1)} %get-tuple-element.79.rows_0, bf16[128,512]{1,0:T(8,128)(2,1)S(1)} %collective-permute-done.13.rows_1, bf16[512,2048]{1,0:T(8,128)(2,1)S(1)} %get-tuple-element.77.weight_0, bf16[512,2048]{1,0:T(8,128)(2,1)S(1)} %collective-permute-done.5.weight_1), custom_call_target="tpu_custom_call" | custom-call | flops 5368709 | bytes 10485 | tf_op jit(solution)/shard_map/pallas_call | solution.py:422
  47.1 7.0 %collective-permute-done.14 = bf16[128,2048]{1,0:T(8,128)(2,1)S(1)} collective-permute-done((bf16[128,2048]{1,0:T(8,128)(2,1)S(1)}, bf16[128,2048]{1,0:T(8,128)(2,1)S(1)}, u32[]{:S(2)}, u32[]{:S(2)}) %collective-permute-start.14) | collective-permute-done | bytes 524320 | tf_op jit(solution)/shard_map/ppermute | solution.py:439
  54.1 0.9 %add_convert_fusion = bf16[128,2048]{1,0:T(8,128)(2,1)} fusion(f32[128,2048]{1,0:T(8,128)S(1)} %shard_map.83, bf16[128,2048]{1,0:T(8,128)(2,1)S(1)} %collective-permute-done.14), kind=kLoop, calls=%fused_computation | loop fusion | flops 786432 | bytes 2097152 | tf_op jit(solution)/shard_map/convert_element_type | solution.py:491
  (17 shorter events, 0.7 us)
Async XLA Ops:
  0.0 16.9 %collective-permute-start.5 = (bf16[512,2048]{1,0:T(8,128)(2,1)}, bf16[512,2048]{1,0:T(8,128)(2,1)S(1)}, u32[]{:S(2)}, u32[]{:S(2)}) collective-permute-start(bf16[512,2048]{1,0:T(8,128)(2,1)} %refs_5_.1), channel_id=1, source_target_pairs={{0,1},{1,0},{2,3},{3,2},{4,5},{5,4},{6,7},{7,6},{8,9},{9,8},{10,11... | collective-permute-start | bytes 6291464 | tf_op jit(solution)/shard_map/ppermute | solution.py:439
  0.5 6.2 %collective-permute-start = (bf16[128,2048]{1,0:T(8,128)(2,1)}, bf16[128,2048]{1,0:T(8,128)(2,1)S(1)}, u32[]{:S(2)}, u32[]{:S(2)}) collective-permute-start(bf16[128,2048]{1,0:T(8,128)(2,1)} %rows_hbm.1), channel_id=1, source_target_pairs={{0,1},{1,0},{2,3},{3,2},{4,5},{5,4},{6,7},{7,6},{8,9},{9,8},{10,11... | collective-permute-start | bytes 1572872 | tf_op jit(solution)/shard_map/ppermute | solution.py:439
  0.5 16.3 %collective-permute-start.4 = (bf16[128,2048]{1,0:T(8,128)(2,1)}, bf16[128,2048]{1,0:T(8,128)(2,1)S(1)}, u32[]{:S(2)}, u32[]{:S(2)}) collective-permute-start(bf16[128,2048]{1,0:T(8,128)(2,1)} %rows_hbm.1), channel_id=1, source_target_pairs={{0,2},{1,3},{2,0},{3,1},{4,6},{5,7},{6,4},{7,5},{8,10},{9,11},{10,... | collective-permute-start | bytes 1572872 | tf_op jit(solution)/shard_map/ppermute | solution.py:439
  3.5 3.2 %copy-start = (s32[4,128]{1,0:T(4,128)S(1)}, s32[4,128]{1,0:T(4,128)}, u32[]{:S(2)}) copy-start(s32[4,128]{1,0:T(4,128)} %pattern.3) | copy-start | bytes 6148
  6.6 5.1 %copy-start.1 = (s32[8]{0:T(128)S(1)}, s32[8]{0:T(128)}, u32[]{:S(2)}) copy-start(s32[8]{0:T(128)} %param.13) | copy-start | bytes 100
  7.5 7.7 %collective-permute-start.1 = (bf16[2,4,32,128]{3,2,1,0:T(8,128)(2,1)S(1)}, bf16[2,4,32,128]{3,2,1,0:T(8,128)(2,1)S(1)}, u32[]{:S(2)}, u32[]{:S(2)}) collective-permute-start(bf16[2,4,32,128]{3,2,1,0:T(8,128)(2,1)S(1)} %get-tuple-element.47), channel_id=1, source_target_pairs={{0,16},{4,20},{8,24},{12,28},{16,0},{20,4},{24,8},{28,12},{1,17},{... | collective-permute-start | bytes 196616 | tf_op jit(solution)/shard_map/ppermute | solution.py:439
  10.1 6.4 %collective-permute-start.2 = (bf16[2,4,32,128]{3,2,1,0:T(8,128)(2,1)S(1)}, bf16[2,4,32,128]{3,2,1,0:T(8,128)(2,1)S(1)}, u32[]{:S(2)}, u32[]{:S(2)}) collective-permute-start(bf16[2,4,32,128]{3,2,1,0:T(8,128)(2,1)S(1)} %get-tuple-element.47), channel_id=1, source_target_pairs={{0,24},{4,28},{8,16},{12,20},{16,8},{20,12},{24,0},{28,4},{1,25},{... | collective-permute-start | bytes 196616 | tf_op jit(solution)/shard_map/ppermute | solution.py:439
  11.5 5.3 %collective-permute-start.3 = (bf16[2,4,32,128]{3,2,1,0:T(8,128)(2,1)S(1)}, bf16[2,4,32,128]{3,2,1,0:T(8,128)(2,1)S(1)}, u32[]{:S(2)}, u32[]{:S(2)}) collective-permute-start(bf16[2,4,32,128]{3,2,1,0:T(8,128)(2,1)S(1)} %get-tuple-element.47), channel_id=1, source_target_pairs={{0,8},{4,12},{8,0},{12,4},{16,24},{20,28},{24,16},{28,20},{1,9},{5... | collective-permute-start | bytes 196616 | tf_op jit(solution)/shard_map/ppermute | solution.py:439
  16.9 2.4 %collective-permute-start.6 = (bf16[128,2048]{1,0:T(8,128)(2,1)S(1)}, bf16[128,2048]{1,0:T(8,128)(2,1)S(1)}, u32[]{:S(2)}, u32[]{:S(2)}) collective-permute-start(bf16[128,2048]{1,0:T(8,128)(2,1)S(1)} %collective-permute-done.4.refs_2_.rows), channel_id=1, source_target_pairs={{0,1},{1,0},{2,3},{3,2},{4,5},{5,4},{6,7},{7,6},{8,9},{9,8},{10,11... | collective-permute-start | bytes 1572872 | tf_op jit(solution)/shard_map/ppermute | solution.py:439
  16.9 9.6 %collective-permute-start.10 = (bf16[4,2,4,32,128]{4,3,2,1,0:T(8,128)(2,1)S(1)}, bf16[4,2,4,32,128]{4,3,2,1,0:T(8,128)(2,1)S(1)}, u32[]{:S(2)}, u32[]{:S(2)}) collective-permute-start(bf16[4,2,4,32,128]{4,3,2,1,0:T(8,128)(2,1)S(1)} %pad_maximum_fusion.refs_9_), channel_id=1, source_target_pairs={{0,4},{4,0},{8,12},{12,8},{16,20},{20,16},{24,28},{28,24},{1,5},{5... | collective-permute-start | bytes 786440 | tf_op jit(solution)/shard_map/ppermute | solution.py:439
  20.2 7.7 %collective-permute-start.7 = (bf16[2,4,32,128]{3,2,1,0:T(8,128)(2,1)S(1)}, bf16[2,4,32,128]{3,2,1,0:T(8,128)(2,1)S(1)}, u32[]{:S(2)}, u32[]{:S(2)}) collective-permute-start(bf16[2,4,32,128]{3,2,1,0:T(8,128)(2,1)S(1)} %get-tuple-element.61), channel_id=1, source_target_pairs={{0,16},{4,20},{8,24},{12,28},{16,0},{20,4},{24,8},{28,12},{1,17},{... | collective-permute-start | bytes 196616 | tf_op jit(solution)/shard_map/ppermute | solution.py:439
  22.8 6.4 %collective-permute-start.8 = (bf16[2,4,32,128]{3,2,1,0:T(8,128)(2,1)S(1)}, bf16[2,4,32,128]{3,2,1,0:T(8,128)(2,1)S(1)}, u32[]{:S(2)}, u32[]{:S(2)}) collective-permute-start(bf16[2,4,32,128]{3,2,1,0:T(8,128)(2,1)S(1)} %get-tuple-element.61), channel_id=1, source_target_pairs={{0,24},{4,28},{8,16},{12,20},{16,8},{20,12},{24,0},{28,4},{1,25},{... | collective-permute-start | bytes 196616 | tf_op jit(solution)/shard_map/ppermute | solution.py:439
  23.4 6.1 %collective-permute-start.9 = (bf16[2,4,32,128]{3,2,1,0:T(8,128)(2,1)S(1)}, bf16[2,4,32,128]{3,2,1,0:T(8,128)(2,1)S(1)}, u32[]{:S(2)}, u32[]{:S(2)}) collective-permute-start(bf16[2,4,32,128]{3,2,1,0:T(8,128)(2,1)S(1)} %get-tuple-element.61), channel_id=1, source_target_pairs={{0,8},{4,12},{8,0},{12,4},{16,24},{20,28},{24,16},{28,20},{1,9},{5... | collective-permute-start | bytes 196616 | tf_op jit(solution)/shard_map/ppermute | solution.py:439
  29.6 7.6 %collective-permute-start.11 = (bf16[4,2,4,32,128]{4,3,2,1,0:T(8,128)(2,1)S(1)}, bf16[4,2,4,32,128]{4,3,2,1,0:T(8,128)(2,1)S(1)}, u32[]{:S(2)}, u32[]{:S(2)}) collective-permute-start(bf16[4,2,4,32,128]{4,3,2,1,0:T(8,128)(2,1)S(1)} %pad_maximum_fusion.1.refs_3_.refs_11_), channel_id=1, source_target_pairs={{0,4},{4,0},{8,12},{12,8},{16,20},{20,16},{24,28},{28,24},{1,5},{5... | collective-permute-start | bytes 786440 | tf_op jit(solution)/shard_map/ppermute | solution.py:439
  37.9 1.4 %collective-permute-start.12 = (bf16[128,512]{1,0:T(8,128)(2,1)S(1)}, bf16[128,512]{1,0:T(8,128)(2,1)S(1)}, u32[]{:S(2)}, u32[]{:S(2)}) collective-permute-start(bf16[128,512]{1,0:T(8,128)(2,1)S(1)} %get-tuple-element.76), channel_id=1, source_target_pairs={{0,1},{1,0},{2,3},{3,2},{4,5},{5,4},{6,7},{7,6},{8,9},{9,8},{10,11... | collective-permute-start | bytes 393224 | tf_op jit(solution)/shard_map/ppermute | solution.py:439
  40.0 14.0 %collective-permute-start.14 = (bf16[128,2048]{1,0:T(8,128)(2,1)S(1)}, bf16[128,2048]{1,0:T(8,128)(2,1)S(1)}, u32[]{:S(2)}, u32[]{:S(2)}) collective-permute-start(bf16[128,2048]{1,0:T(8,128)(2,1)S(1)} %shard_map.81), channel_id=1, source_target_pairs={{0,2},{1,3},{2,0},{3,1},{4,6},{5,7},{6,4},{7,5},{8,10},{9,11},{10,... | collective-permute-start | bytes 1572872 | tf_op jit(solution)/shard_map/ppermute | solution.py:439
  45.0 1.4 %collective-permute-start.13 = (bf16[128,512]{1,0:T(8,128)(2,1)S(1)}, bf16[128,512]{1,0:T(8,128)(2,1)S(1)}, u32[]{:S(2)}, u32[]{:S(2)}) collective-permute-start(bf16[128,512]{1,0:T(8,128)(2,1)S(1)} %get-tuple-element.80), channel_id=1, source_target_pairs={{0,1},{1,0},{2,3},{3,2},{4,5},{5,4},{6,7},{7,6},{8,9},{9,8},{10,11... | collective-permute-start | bytes 393224 | tf_op jit(solution)/shard_map/ppermute | solution.py:439

commit v10 on v9

--- a/solution.py
+++ b/solution.py
@@ -138,7 +138,7 @@
 
 
 def query_kernel(*refs):
-    rows, (wq_hbm, w_hbm), outs, (wq, sems) = refs[:4], refs[4:6], refs[6:9], refs[9:]
+    rows, (wq_hbm, w_hbm, kept), outs, (wq, sems) = refs[:4], refs[4:7], refs[7:11], refs[11:]
     w = outs[2]
     parts = halves_of(wq.shape[1])
     copies = [
@@ -153,24 +153,26 @@
         for pair, out in ((rows[:2], outs[0]), (rows[2:], outs[1])):
             both = jnp.concatenate([ref[...] for ref in pair], axis=0)
             out[:, part] = dot(both, wq[:, part]).astype(BF16)
+    outs[3][...] = kept[...]
     copies[-1].wait()
 
 
-def query(rows, w_query, w_out):
+def query(rows, w_query, w_out, kept):
     count, depth = rows[0].shape
     width = w_query.shape[1]
     return pl.pallas_call(
         query_kernel,
-        in_specs=[IN_VMEM] * 4 + [IN_HBM] * 2,
-        out_specs=[IN_VMEM] * 3,
-        out_shape=[shape((2 * count, width))] * 2 + [pltpu.VMEM(w_out.shape, BF16)],
+        in_specs=[IN_VMEM] * 4 + [IN_HBM] * 2 + [IN_VMEM],
+        out_specs=[IN_VMEM] * 4,
+        out_shape=[shape((2 * count, width))] * 2
+        + [pltpu.VMEM(w_out.shape, BF16), shape(kept.shape)],
         scratch_shapes=[
             pltpu.VMEM(w_query.shape, BF16),
             pltpu.SemaphoreType.DMA((1 + len(halves_of(width)),)),
         ],
         compiler_params=params(),
         cost_estimate=cost(8 * count * depth * width, 4 * depth * width),
-    )(*rows, keep_in_hbm(w_query), keep_in_hbm(w_out))
+    )(*rows, keep_in_hbm(w_query), keep_in_hbm(w_out), kept)
 
 
 def across_kernel(rows, wk, wv, keys, values):
@@ -444,8 +446,8 @@
     def first_round(kept):
         return [swap(kept, bit, "seq") for bit in Z_BITS]
 
-    def second_round(kept, along_z):
-        column = jnp.stack([kept, *along_z])
+    def second_round(pieces):
+        column = jnp.stack(pieces)
         return [column, swap(column, Y_BIT, "seq")]
 
     across = swap(normed, 2)
@@ -458,24 +460,29 @@
     if few:
         along_z = first_round(kept_a)
         *along_z, masks[0] = lax.optimization_barrier((*along_z, masks[0]))
-        half_a = 0, second_round(kept_a, along_z)
-        across = after(across, half_a[1][0], wo_beside)
+        half_a = 0, second_round([kept_a, *along_z])
+        across = after(across, masks[0], wo_beside)
     else:
         half_a = 0, [lax.all_gather(kept_a, "seq", axis=0)]
     wo_beside = pltpu.with_memory_space_constraint(wo_beside, pltpu.VMEM)
     beyond = swap(across, 1)
+    if few:
+        beyond = after(beyond, half_a[1][0])
     keys_2, values_2 = keys_and_values(across, wk, wv)
     keys_3, values_3, kept_b = second(after(beyond, keys_2), wk, wv, keys_2, values_2, pattern)
-    query_a, query_b, wo = query([mine, beside, across, beyond], w_query, w_out)
+    rows = [mine, beside, across, beyond]
+    query_a, query_b, wo, kept_again = query(rows, w_query, w_out, kept_b)
     near = [keys_0, keys_1, keys_2, keys_3], [values_0, values_1, values_2, values_3]
     call = functools.partial(attend, masks, few)
     if few:
         along_z = first_round(kept_b)
-        *along_z, query_b, half_a[1][1] = lax.optimization_barrier(
-            (*along_z, query_b, half_a[1][1])
+        along_y = swap(kept_again, Y_BIT, "seq")
+        *along_z, along_y, query_b, half_a[1][1] = lax.optimization_barrier(
+            (*along_z, along_y, query_b, half_a[1][1])
         )
-        half_b = 1, second_round(kept_b, along_z)
-        asked = after(query_b, half_b[1][0])
+        column, other = second_round(along_z)
+        half_b = 1, [kept_b[None], column, along_y[None], other]
+        asked = after(query_b, column)
         begun = call(2 * BLOCK, asked, [half_a], near=near, finish=False)
     else:
         half_b = 1, [lax.all_gather(kept_b, "seq", axis=0)]

time: 55.1 us -> 54.6 us (level)
  waiting for transfers between devices: 20.6 us -> 18.9 us
  starting transfers between devices: 15.6 us -> 16.8 us
    ppermute x15 -> x16, waiting for transfers between devices: 20.6 us -> 18.9 us  [swap(): return lax.ppermute(array, axis, [(i, i ^ bit) for i in range(count)])]
    ppermute x15 -> x16, starting transfers between devices: 15.6 us -> 16.8 us  [swap(): return lax.ppermute(array, axis, [(i, i ^ bit) for i in range(count)])]
  transfers between devices with their start and end apart: 15 -> 16, of which waited for: 10 -> 10; matrix products, arithmetic and copies ran while one was open for 0% -> 0% of each run, Pallas kernels for 29% -> 30%
where the time goes in v10:
time: 54.6 us; the launch traced here: 54.4 us
  waiting for transfers between devices  18.9 us (35%)
  Pallas kernels  17.5 us (32%)
  starting transfers between devices  16.8 us (31%)
  other arithmetic  1.04 us (2%)
    ppermute x16, waiting for transfers between devices, swap(): return lax.ppermute(array, axis, [(i, i ^ bit) for i in range(count)])  18.9 us
    ppermute x16, starting transfers between devices, swap(): return lax.ppermute(array, axis, [(i, i ^ bit) for i in range(count)])  16.8 us
    pallas_call x3, Pallas kernels, attend(): pl.pallas_call(functools.partial(attend_kernel, first_row, near is not No...  7.03 us
    pallas_call x1, Pallas kernels, first(): pl.pallas_call(first_kernel, in_specs=[IN_HBM] * 3, out_specs=[IN_VMEM] *...  3.14 us
    pallas_call x1, Pallas kernels, query(): pl.pallas_call(query_kernel, in_specs=[IN_VMEM] * 4 + [IN_HBM] * 2 + [IN_...  2.67 us
    pallas_call x2, Pallas kernels, second(): pl.pallas_call(second_kernel, in_specs=[IN_VMEM] * 6, out_specs=[IN_VMEM]...  1.81 us
    pallas_call x2, Pallas kernels, mix(): pl.pallas_call(mix_kernel, in_specs=[IN_VMEM] * 4, out_specs=IN_VMEM, out...  1.44 us
  transfers between devices with their start and end apart: 16, of which 10 were waited for; matrix products, arithmetic and copies ran while one was open for 0% of the time, Pallas kernels for 30%

profile of v10, /device:TPU:0, one launch (start us, length us, event | category | flops | bytes accessed | tf_op | source)
XLA Modules:
  0.0 54.4 jit_solution(6617401613629531154)
XLA Ops:
  0.0 0.5 collective-permute-start.5
  0.5 2.9 %collective-permute-start.4 = (bf16[128,2048]{1,0:T(8,128)(2,1)}, bf16[128,2048]{1,0:T(8,128)(2,1)S(1)}, u32[]{:S(2)}, u32[]{:S(2)}) collective-permute-start(bf16[128,2048]{1,0:T(8,128)(2,1)} %rows_hbm.1), channel_id=1, source_target_pairs={{0,2},{1,3},{2,0},{3,1},{4,6},{5,7},{6,4},{7,5},{8,10},{9,11},{10,... | collective-permute-start | bytes 1572872 | tf_op jit(solution)/shard_map/ppermute | solution.py:441
  3.5 3.1 %shard_map.73 = (bf16[128,2048]{1,0:T(8,128)(2,1)S(1)}, bf16[2048,512]{1,0:T(8,128)(2,1)S(1)}, bf16[2048,512]{1,0:T(8,128)(2,1)S(1)}, bf16[128,512]{1,0:T(8,128)(2,1)S(1)}, bf16[128,512]{1,0:T(8,128)(2,1)S(1)}) custom-call(bf16[128,2048]{1,0:T(8,128)(2,1)} %rows_hbm.1, bf16[2048,512]{1,0:T(8,128)(2,1)} %wk_hbm.1, bf16[2048,512]{1,0:T(8,128)(2,1)} %wv_hbm.1), custom_call_target="tpu_custom_call" | custom-call | flops 5368709 | bytes 41943 | tf_op jit(solution)/shard_map/pallas_call | solution.py:98
  6.6 0.9 %shard_map.74 = (bf16[128,512]{1,0:T(8,128)(2,1)S(1)}, bf16[128,512]{1,0:T(8,128)(2,1)S(1)}, bf16[2,4,32,128]{3,2,1,0:T(8,128)(2,1)S(1)}) custom-call(bf16[128,2048]{1,0:T(8,128)(2,1)S(1)} %collective-permute-done.rows.refs_1_, bf16[2048,512]{1,0:T(8,128)(2,1)S(1)} %get-tuple-element.46.wk, bf16[2048,512]{1,0:T(8,128)(2,1)S(1)} %get-tuple-element.47.wv, ...), custom_call_target="tpu_custom_call" | custom-call | flops 5368709 | bytes 5242 | tf_op jit(solution)/shard_map/pallas_call | solution.py:130
  7.5 2.6 %collective-permute-start.1 = (bf16[2,4,32,128]{3,2,1,0:T(8,128)(2,1)S(1)}, bf16[2,4,32,128]{3,2,1,0:T(8,128)(2,1)S(1)}, u32[]{:S(2)}, u32[]{:S(2)}) collective-permute-start(bf16[2,4,32,128]{3,2,1,0:T(8,128)(2,1)S(1)} %get-tuple-element.50), channel_id=1, source_target_pairs={{0,16},{4,20},{8,24},{12,28},{16,0},{20,4},{24,8},{28,12},{1,17},{... | collective-permute-start | bytes 196616 | tf_op jit(solution)/shard_map/ppermute | solution.py:441
  10.1 1.3 %collective-permute-start.2 = (bf16[2,4,32,128]{3,2,1,0:T(8,128)(2,1)S(1)}, bf16[2,4,32,128]{3,2,1,0:T(8,128)(2,1)S(1)}, u32[]{:S(2)}, u32[]{:S(2)}) collective-permute-start(bf16[2,4,32,128]{3,2,1,0:T(8,128)(2,1)S(1)} %get-tuple-element.50), channel_id=1, source_target_pairs={{0,24},{4,28},{8,16},{12,20},{16,8},{20,12},{24,0},{28,4},{1,25},{... | collective-permute-start | bytes 196616 | tf_op jit(solution)/shard_map/ppermute | solution.py:441
  11.8 0.7 %shard_map.75 = (bf16[512,128]{1,0:T(8,128)(2,1)S(1)}, bf16[1024,128]{1,0:T(8,128)(2,1)S(1)}) custom-call(s32[10]{0:T(128)S(1)} %pad_add_fusion.place), custom_call_target="tpu_custom_call" | custom-call | flops 83886 | bytes 2621 | tf_op jit(solution)/shard_map/pallas_call | solution.py:238
  12.5 2.7 %collective-permute-done.1 = bf16[2,4,32,128]{3,2,1,0:T(8,128)(2,1)S(1)} collective-permute-done((bf16[2,4,32,128]{3,2,1,0:T(8,128)(2,1)S(1)}, bf16[2,4,32,128]{3,2,1,0:T(8,128)(2,1)S(1)}, u32[]{:S(2)}, u32[]{:S(2)}) %collective-permute-start.1) | collective-permute-done | bytes 65568 | tf_op jit(solution)/shard_map/ppermute | solution.py:441
  15.2 1.3 %collective-permute-done.2 = bf16[2,4,32,128]{3,2,1,0:T(8,128)(2,1)S(1)} collective-permute-done((bf16[2,4,32,128]{3,2,1,0:T(8,128)(2,1)S(1)}, bf16[2,4,32,128]{3,2,1,0:T(8,128)(2,1)S(1)}, u32[]{:S(2)}, u32[]{:S(2)}) %collective-permute-start.2) | collective-permute-done | bytes 65568 | tf_op jit(solution)/shard_map/ppermute | solution.py:441
  16.5 0.3 collective-permute-done.3
  16.9 1.6 %collective-permute-start.11 = (bf16[4,2,4,32,128]{4,3,2,1,0:T(8,128)(2,1)S(1)}, bf16[4,2,4,32,128]{4,3,2,1,0:T(8,128)(2,1)S(1)}, u32[]{:S(2)}, u32[]{:S(2)}) collective-permute-start(bf16[4,2,4,32,128]{4,3,2,1,0:T(8,128)(2,1)S(1)} %pad_maximum_fusion.refs_9_), channel_id=1, source_target_pairs={{0,4},{4,0},{8,12},{12,8},{16,20},{20,16},{24,28},{28,24},{1,5},{5... | collective-permute-start | bytes 786440 | tf_op jit(solution)/shard_map/ppermute | solution.py:441
  18.5 0.8 %shard_map.76 = (bf16[128,512]{1,0:T(8,128)(2,1)S(1)}, bf16[128,512]{1,0:T(8,128)(2,1)S(1)}) custom-call(bf16[128,2048]{1,0:T(8,128)(2,1)S(1)} %collective-permute-done.4.rows.refs_2_, bf16[2048,512]{1,0:T(8,128)(2,1)S(1)} %get-tuple-element.46.wk, bf16[2048,512]{1,0:T(8,128)(2,1)S(1)} %get-tuple-element.47.wv), custom_call_target="tpu_custom_call" | custom-call | flops 5368709 | bytes 5242 | tf_op jit(solution)/shard_map/pallas_call | solution.py:187
  19.2 0.9 %shard_map.77 = (bf16[128,512]{1,0:T(8,128)(2,1)S(1)}, bf16[128,512]{1,0:T(8,128)(2,1)S(1)}, bf16[2,4,32,128]{3,2,1,0:T(8,128)(2,1)S(1)}) custom-call(bf16[128,2048]{1,0:T(8,128)(2,1)S(1)} %collective-permute-done.6.rows.refs_3_, bf16[2048,512]{1,0:T(8,128)(2,1)S(1)} %get-tuple-element.46.wk, bf16[2048,512]{1,0:T(8,128)(2,1)S(1)} %get-tuple-element.47.wv, ...), custom_call_target="tpu_custom_call" | custom-call | flops 5368709 | bytes 5242 | tf_op jit(solution)/shard_map/pallas_call | solution.py:130
  20.1 2.6 %collective-permute-start.7 = (bf16[2,4,32,128]{3,2,1,0:T(8,128)(2,1)S(1)}, bf16[2,4,32,128]{3,2,1,0:T(8,128)(2,1)S(1)}, u32[]{:S(2)}, u32[]{:S(2)}) collective-permute-start(bf16[2,4,32,128]{3,2,1,0:T(8,128)(2,1)S(1)} %get-tuple-element.64.refs_6_), channel_id=1, source_target_pairs={{0,16},{4,20},{8,24},{12,28},{16,0},{20,4},{24,8},{28,12},{1,17},{... | collective-permute-start | bytes 196616 | tf_op jit(solution)/shard_map/ppermute | solution.py:441
  22.8 0.5 collective-permute-start.8
  23.3 0.5 collective-permute-start.9
  23.8 2.7 %shard_map.78 = (bf16[256,512]{1,0:T(8,128)(2,1)S(1)}, bf16[256,512]{1,0:T(8,128)(2,1)S(1)}, bf16[512,2048]{1,0:T(8,128)(2,1)S(1)}, bf16[2,4,32,128]{3,2,1,0:T(8,128)(2,1)S(1)}) custom-call(bf16[128,2048]{1,0:T(8,128)(2,1)S(1)} %get-tuple-element.55.refs_0_, bf16[128,2048]{1,0:T(8,128)(2,1)S(1)} %collective-permute-done.rows.refs_1_, ...), custom_call_target="tpu_custom_call" | custom-call | flops 10737418 | bytes 41943 | tf_op jit(solution)/shard_map/pallas_call | solution.py:163
  26.5 1.1 %collective-permute-start.10 = (bf16[2,4,32,128]{3,2,1,0:T(8,128)(2,1)S(1)}, bf16[2,4,32,128]{3,2,1,0:T(8,128)(2,1)S(1)}, u32[]{:S(2)}, u32[]{:S(2)}) collective-permute-start(bf16[2,4,32,128]{3,2,1,0:T(8,128)(2,1)S(1)} %get-tuple-element.66), channel_id=1, source_target_pairs={{0,4},{4,0},{8,12},{12,8},{16,20},{20,16},{24,28},{28,24},{1,5},{5... | collective-permute-start | bytes 196616 | tf_op jit(solution)/shard_map/ppermute | solution.py:441
  27.6 1.7 %collective-permute-done.8 = bf16[2,4,32,128]{3,2,1,0:T(8,128)(2,1)S(1)} collective-permute-done((bf16[2,4,32,128]{3,2,1,0:T(8,128)(2,1)S(1)}, bf16[2,4,32,128]{3,2,1,0:T(8,128)(2,1)S(1)}, u32[]{:S(2)}, u32[]{:S(2)}) %collective-permute-start.8) | collective-permute-done | bytes 65568 | tf_op jit(solution)/shard_map/ppermute | solution.py:441
  29.5 1.3 %collective-permute-done.10 = bf16[2,4,32,128]{3,2,1,0:T(8,128)(2,1)S(1)} collective-permute-done((bf16[2,4,32,128]{3,2,1,0:T(8,128)(2,1)S(1)}, bf16[2,4,32,128]{3,2,1,0:T(8,128)(2,1)S(1)}, u32[]{:S(2)}, u32[]{:S(2)}) %collective-permute-start.10) | collective-permute-done | bytes 65568 | tf_op jit(solution)/shard_map/ppermute | solution.py:441
  30.9 1.1 %collective-permute-start.12 = (bf16[3,2,4,32,128]{4,3,2,1,0:T(8,128)(2,1)S(1)}, bf16[3,2,4,32,128]{4,3,2,1,0:T(8,128)(2,1)S(1)}, u32[]{:S(2)}, u32[]{:S(2)}) collective-permute-start(bf16[3,2,4,32,128]{4,3,2,1,0:T(8,128)(2,1)S(1)} %pad_maximum_fusion.1.refs_4_.refs_12_), channel_id=1, source_target_pairs={{0,4},{4,0},{8,12},{12,8},{16,20},{20,16},{24,28},{28,24},{1,5},{5... | collective-permute-start | bytes 589832 | tf_op jit(solution)/shard_map/ppermute | solution.py:441
  31.9 2.8 %shard_map.79 = (f32[4,128,256]{2,1,0:T(8,128)S(1)}, f32[4,8,256]{2,1,0:T(8,128)S(1)}) custom-call(bf16[512,128]{1,0:T(8,128)(2,1)S(1)} %get-tuple-element.53.asking, bf16[1024,128]{1,0:T(8,128)(2,1)S(1)} %get-tuple-element.54.asked_of, bf16[256,512]{1,0:T(8,128)(2,1)S(1)} %get-tuple-element.72.refs_0_, ...), custom_call_target="tpu_custom_call" | custom-call | flops 4026531 | bytes 5242 | tf_op jit(solution)/shard_map/pallas_call | solution.py:394
  34.7 1.9 %collective-permute-done.12.refs_6_.refs_14_ = bf16[3,2,4,32,128]{4,3,2,1,0:T(8,128)(2,1)S(1)} collective-permute-done((bf16[3,2,4,32,128]{4,3,2,1,0:T(8,128)(2,1)S(1)}, bf16[3,2,4,32,128]{4,3,2,1,0:T(8,128)(2,1)S(1)}, u32[]{:S(2)}, u32[]{:S(2)}) %collective-permute-start.12) | collective-permute-done | bytes 196640 | tf_op jit(solution)/shard_map/ppermute | solution.py:441
  36.6 0.7 %shard_map.80 = (bf16[128,512]{1,0:T(8,128)(2,1)S(1)}, bf16[128,512]{1,0:T(8,128)(2,1)S(1)}) custom-call(bf16[512,128]{1,0:T(8,128)(2,1)S(1)} %get-tuple-element.53.asking, bf16[1024,128]{1,0:T(8,128)(2,1)S(1)} %get-tuple-element.54.asked_of, bf16[256,512]{1,0:T(8,128)(2,1)S(1)} %get-tuple-element.72.refs_0_, f32[4,128,256]{2,1,0:T(8,128)S(1)} %get-tuple-element.78.refs_1_, ...), custom_call_target="tpu_custom_call" | custom-call | flops 1342177 | bytes 5242 | tf_op jit(solution)/shard_map/pallas_call | solution.py:394
  37.4 1.3 %collective-permute-done.13.rows_1 = bf16[128,512]{1,0:T(8,128)(2,1)S(1)} collective-permute-done((bf16[128,512]{1,0:T(8,128)(2,1)S(1)}, bf16[128,512]{1,0:T(8,128)(2,1)S(1)}, u32[]{:S(2)}, u32[]{:S(2)}) %collective-permute-start.13) | collective-permute-done | bytes 131104 | tf_op jit(solution)/shard_map/ppermute | solution.py:441
  38.8 0.7 %shard_map.81 = bf16[128,2048]{1,0:T(8,128)(2,1)S(1)} custom-call(bf16[128,512]{1,0:T(8,128)(2,1)S(1)} %get-tuple-element.81.rows_0, bf16[128,512]{1,0:T(8,128)(2,1)S(1)} %collective-permute-done.13.rows_1, bf16[512,2048]{1,0:T(8,128)(2,1)S(1)} %get-tuple-element.83.weight_0, bf16[512,2048]{1,0:T(8,128)(2,1)S(1)} %collective-permute-done.5.weight_1), custom_call_target="tpu_custom_call" | custom-call | flops 5368709 | bytes 10485 | tf_op jit(solution)/shard_map/pallas_call | solution.py:424
  39.5 1.6 %collective-permute-start.15 = (bf16[128,2048]{1,0:T(8,128)(2,1)S(1)}, bf16[128,2048]{1,0:T(8,128)(2,1)S(1)}, u32[]{:S(2)}, u32[]{:S(2)}) collective-permute-start(bf16[128,2048]{1,0:T(8,128)(2,1)S(1)} %shard_map.81), channel_id=1, source_target_pairs={{0,2},{1,3},{2,0},{3,1},{4,6},{5,7},{6,4},{7,5},{8,10},{9,11},{10,... | collective-permute-start | bytes 1572872 | tf_op jit(solution)/shard_map/ppermute | solution.py:441
  41.1 3.5 %shard_map.82 = (bf16[128,512]{1,0:T(8,128)(2,1)S(1)}, bf16[128,512]{1,0:T(8,128)(2,1)S(1)}) custom-call(bf16[512,128]{1,0:T(8,128)(2,1)S(1)} %get-tuple-element.53.asking, bf16[1024,128]{1,0:T(8,128)(2,1)S(1)} %get-tuple-element.54.asked_of, bf16[256,512]{1,0:T(8,128)(2,1)S(1)} %get-tuple-element.84.refs_0_, ...), custom_call_target="tpu_custom_call" | custom-call | flops 5368709 | bytes 5242 | tf_op jit(solution)/shard_map/pallas_call | solution.py:394
  44.7 1.3 %collective-permute-done.14.rows_1 = bf16[128,512]{1,0:T(8,128)(2,1)S(1)} collective-permute-done((bf16[128,512]{1,0:T(8,128)(2,1)S(1)}, bf16[128,512]{1,0:T(8,128)(2,1)S(1)}, u32[]{:S(2)}, u32[]{:S(2)}) %collective-permute-start.14) | collective-permute-done | bytes 131104 | tf_op jit(solution)/shard_map/ppermute | solution.py:441
  46.0 0.7 %shard_map.83 = f32[128,2048]{1,0:T(8,128)S(1)} custom-call(bf16[128,512]{1,0:T(8,128)(2,1)S(1)} %get-tuple-element.85.rows_0, bf16[128,512]{1,0:T(8,128)(2,1)S(1)} %collective-permute-done.14.rows_1, bf16[512,2048]{1,0:T(8,128)(2,1)S(1)} %get-tuple-element.83.weight_0, bf16[512,2048]{1,0:T(8,128)(2,1)S(1)} %collective-permute-done.5.weight_1), custom_call_target="tpu_custom_call" | custom-call | flops 5368709 | bytes 10485 | tf_op jit(solution)/shard_map/pallas_call | solution.py:424
  46.8 6.8 %collective-permute-done.15 = bf16[128,2048]{1,0:T(8,128)(2,1)S(1)} collective-permute-done((bf16[128,2048]{1,0:T(8,128)(2,1)S(1)}, bf16[128,2048]{1,0:T(8,128)(2,1)S(1)}, u32[]{:S(2)}, u32[]{:S(2)}) %collective-permute-start.15) | collective-permute-done | bytes 524320 | tf_op jit(solution)/shard_map/ppermute | solution.py:441
  53.5 0.9 %add_convert_fusion = bf16[128,2048]{1,0:T(8,128)(2,1)} fusion(f32[128,2048]{1,0:T(8,128)S(1)} %shard_map.83, bf16[128,2048]{1,0:T(8,128)(2,1)S(1)} %collective-permute-done.15), kind=kLoop, calls=%fused_computation | loop fusion | flops 786432 | bytes 2097152 | tf_op jit(solution)/shard_map/convert_element_type | solution.py:498
  (19 shorter events, 0.8 us)
Async XLA Ops:
  0.0 16.8 %collective-permute-start.5 = (bf16[512,2048]{1,0:T(8,128)(2,1)}, bf16[512,2048]{1,0:T(8,128)(2,1)S(1)}, u32[]{:S(2)}, u32[]{:S(2)}) collective-permute-start(bf16[512,2048]{1,0:T(8,128)(2,1)} %refs_5_.1), channel_id=1, source_target_pairs={{0,1},{1,0},{2,3},{3,2},{4,5},{5,4},{6,7},{7,6},{8,9},{9,8},{10,11... | collective-permute-start | bytes 6291464 | tf_op jit(solution)/shard_map/ppermute | solution.py:441
  0.5 6.2 %collective-permute-start = (bf16[128,2048]{1,0:T(8,128)(2,1)}, bf16[128,2048]{1,0:T(8,128)(2,1)S(1)}, u32[]{:S(2)}, u32[]{:S(2)}) collective-permute-start(bf16[128,2048]{1,0:T(8,128)(2,1)} %rows_hbm.1), channel_id=1, source_target_pairs={{0,1},{1,0},{2,3},{3,2},{4,5},{5,4},{6,7},{7,6},{8,9},{9,8},{10,11... | collective-permute-start | bytes 1572872 | tf_op jit(solution)/shard_map/ppermute | solution.py:441
  0.5 16.3 %collective-permute-start.4 = (bf16[128,2048]{1,0:T(8,128)(2,1)}, bf16[128,2048]{1,0:T(8,128)(2,1)S(1)}, u32[]{:S(2)}, u32[]{:S(2)}) collective-permute-start(bf16[128,2048]{1,0:T(8,128)(2,1)} %rows_hbm.1), channel_id=1, source_target_pairs={{0,2},{1,3},{2,0},{3,1},{4,6},{5,7},{6,4},{7,5},{8,10},{9,11},{10,... | collective-permute-start | bytes 1572872 | tf_op jit(solution)/shard_map/ppermute | solution.py:441
  3.5 3.2 %copy-start = (s32[4,128]{1,0:T(4,128)S(1)}, s32[4,128]{1,0:T(4,128)}, u32[]{:S(2)}) copy-start(s32[4,128]{1,0:T(4,128)} %pattern.3) | copy-start | bytes 6148
  6.6 5.1 %copy-start.1 = (s32[8]{0:T(128)S(1)}, s32[8]{0:T(128)}, u32[]{:S(2)}) copy-start(s32[8]{0:T(128)} %param.13) | copy-start | bytes 100
  7.5 7.7 %collective-permute-start.1 = (bf16[2,4,32,128]{3,2,1,0:T(8,128)(2,1)S(1)}, bf16[2,4,32,128]{3,2,1,0:T(8,128)(2,1)S(1)}, u32[]{:S(2)}, u32[]{:S(2)}) collective-permute-start(bf16[2,4,32,128]{3,2,1,0:T(8,128)(2,1)S(1)} %get-tuple-element.50), channel_id=1, source_target_pairs={{0,16},{4,20},{8,24},{12,28},{16,0},{20,4},{24,8},{28,12},{1,17},{... | collective-permute-start | bytes 196616 | tf_op jit(solution)/shard_map/ppermute | solution.py:441
  10.1 6.4 %collective-permute-start.2 = (bf16[2,4,32,128]{3,2,1,0:T(8,128)(2,1)S(1)}, bf16[2,4,32,128]{3,2,1,0:T(8,128)(2,1)S(1)}, u32[]{:S(2)}, u32[]{:S(2)}) collective-permute-start(bf16[2,4,32,128]{3,2,1,0:T(8,128)(2,1)S(1)} %get-tuple-element.50), channel_id=1, source_target_pairs={{0,24},{4,28},{8,16},{12,20},{16,8},{20,12},{24,0},{28,4},{1,25},{... | collective-permute-start | bytes 196616 | tf_op jit(solution)/shard_map/ppermute | solution.py:441
  11.5 5.3 %collective-permute-start.3 = (bf16[2,4,32,128]{3,2,1,0:T(8,128)(2,1)S(1)}, bf16[2,4,32,128]{3,2,1,0:T(8,128)(2,1)S(1)}, u32[]{:S(2)}, u32[]{:S(2)}) collective-permute-start(bf16[2,4,32,128]{3,2,1,0:T(8,128)(2,1)S(1)} %get-tuple-element.50), channel_id=1, source_target_pairs={{0,8},{4,12},{8,0},{12,4},{16,24},{20,28},{24,16},{28,20},{1,9},{5... | collective-permute-start | bytes 196616 | tf_op jit(solution)/shard_map/ppermute | solution.py:441
  16.8 2.4 %collective-permute-start.6 = (bf16[128,2048]{1,0:T(8,128)(2,1)S(1)}, bf16[128,2048]{1,0:T(8,128)(2,1)S(1)}, u32[]{:S(2)}, u32[]{:S(2)}) collective-permute-start(bf16[128,2048]{1,0:T(8,128)(2,1)S(1)} %collective-permute-done.4.rows.refs_2_), channel_id=1, source_target_pairs={{0,1},{1,0},{2,3},{3,2},{4,5},{5,4},{6,7},{7,6},{8,9},{9,8},{10,11... | collective-permute-start | bytes 1572872 | tf_op jit(solution)/shard_map/ppermute | solution.py:441
  16.9 10.7 %collective-permute-start.11 = (bf16[4,2,4,32,128]{4,3,2,1,0:T(8,128)(2,1)S(1)}, bf16[4,2,4,32,128]{4,3,2,1,0:T(8,128)(2,1)S(1)}, u32[]{:S(2)}, u32[]{:S(2)}) collective-permute-start(bf16[4,2,4,32,128]{4,3,2,1,0:T(8,128)(2,1)S(1)} %pad_maximum_fusion.refs_9_), channel_id=1, source_target_pairs={{0,4},{4,0},{8,12},{12,8},{16,20},{20,16},{24,28},{28,24},{1,5},{5... | collective-permute-start | bytes 786440 | tf_op jit(solution)/shard_map/ppermute | solution.py:441
  20.1 7.4 %collective-permute-start.7 = (bf16[2,4,32,128]{3,2,1,0:T(8,128)(2,1)S(1)}, bf16[2,4,32,128]{3,2,1,0:T(8,128)(2,1)S(1)}, u32[]{:S(2)}, u32[]{:S(2)}) collective-permute-start(bf16[2,4,32,128]{3,2,1,0:T(8,128)(2,1)S(1)} %get-tuple-element.64.refs_6_), channel_id=1, source_target_pairs={{0,16},{4,20},{8,24},{12,28},{16,0},{20,4},{24,8},{28,12},{1,17},{... | collective-permute-start | bytes 196616 | tf_op jit(solution)/shard_map/ppermute | solution.py:441
  22.8 6.5 %collective-permute-start.8 = (bf16[2,4,32,128]{3,2,1,0:T(8,128)(2,1)S(1)}, bf16[2,4,32,128]{3,2,1,0:T(8,128)(2,1)S(1)}, u32[]{:S(2)}, u32[]{:S(2)}) collective-permute-start(bf16[2,4,32,128]{3,2,1,0:T(8,128)(2,1)S(1)} %get-tuple-element.64.refs_6_), channel_id=1, source_target_pairs={{0,24},{4,28},{8,16},{12,20},{16,8},{20,12},{24,0},{28,4},{1,25},{... | collective-permute-start | bytes 196616 | tf_op jit(solution)/shard_map/ppermute | solution.py:441
  23.3 6.2 %collective-permute-start.9 = (bf16[2,4,32,128]{3,2,1,0:T(8,128)(2,1)S(1)}, bf16[2,4,32,128]{3,2,1,0:T(8,128)(2,1)S(1)}, u32[]{:S(2)}, u32[]{:S(2)}) collective-permute-start(bf16[2,4,32,128]{3,2,1,0:T(8,128)(2,1)S(1)} %get-tuple-element.64.refs_6_), channel_id=1, source_target_pairs={{0,8},{4,12},{8,0},{12,4},{16,24},{20,28},{24,16},{28,20},{1,9},{5... | collective-permute-start | bytes 196616 | tf_op jit(solution)/shard_map/ppermute | solution.py:441
  26.5 4.3 %collective-permute-start.10 = (bf16[2,4,32,128]{3,2,1,0:T(8,128)(2,1)S(1)}, bf16[2,4,32,128]{3,2,1,0:T(8,128)(2,1)S(1)}, u32[]{:S(2)}, u32[]{:S(2)}) collective-permute-start(bf16[2,4,32,128]{3,2,1,0:T(8,128)(2,1)S(1)} %get-tuple-element.66), channel_id=1, source_target_pairs={{0,4},{4,0},{8,12},{12,8},{16,20},{20,16},{24,28},{28,24},{1,5},{5... | collective-permute-start | bytes 196616 | tf_op jit(solution)/shard_map/ppermute | solution.py:441
  30.9 5.7 %collective-permute-start.12 = (bf16[3,2,4,32,128]{4,3,2,1,0:T(8,128)(2,1)S(1)}, bf16[3,2,4,32,128]{4,3,2,1,0:T(8,128)(2,1)S(1)}, u32[]{:S(2)}, u32[]{:S(2)}) collective-permute-start(bf16[3,2,4,32,128]{4,3,2,1,0:T(8,128)(2,1)S(1)} %pad_maximum_fusion.1.refs_4_.refs_12_), channel_id=1, source_target_pairs={{0,4},{4,0},{8,12},{12,8},{16,20},{20,16},{24,28},{28,24},{1,5},{5... | collective-permute-start | bytes 589832 | tf_op jit(solution)/shard_map/ppermute | solution.py:441
  37.3 1.4 %collective-permute-start.13 = (bf16[128,512]{1,0:T(8,128)(2,1)S(1)}, bf16[128,512]{1,0:T(8,128)(2,1)S(1)}, u32[]{:S(2)}, u32[]{:S(2)}) collective-permute-start(bf16[128,512]{1,0:T(8,128)(2,1)S(1)} %get-tuple-element.82), channel_id=1, source_target_pairs={{0,1},{1,0},{2,3},{3,2},{4,5},{5,4},{6,7},{7,6},{8,9},{9,8},{10,11... | collective-permute-start | bytes 393224 | tf_op jit(solution)/shard_map/ppermute | solution.py:441
  39.5 14.0 %collective-permute-start.15 = (bf16[128,2048]{1,0:T(8,128)(2,1)S(1)}, bf16[128,2048]{1,0:T(8,128)(2,1)S(1)}, u32[]{:S(2)}, u32[]{:S(2)}) collective-permute-start(bf16[128,2048]{1,0:T(8,128)(2,1)S(1)} %shard_map.81), channel_id=1, source_target_pairs={{0,2},{1,3},{2,0},{3,1},{4,6},{5,7},{6,4},{7,5},{8,10},{9,11},{10,... | collective-permute-start | bytes 1572872 | tf_op jit(solution)/shard_map/ppermute | solution.py:441
  44.6 1.4 %collective-permute-start.14 = (bf16[128,512]{1,0:T(8,128)(2,1)S(1)}, bf16[128,512]{1,0:T(8,128)(2,1)S(1)}, u32[]{:S(2)}, u32[]{:S(2)}) collective-permute-start(bf16[128,512]{1,0:T(8,128)(2,1)S(1)} %get-tuple-element.86), channel_id=1, source_target_pairs={{0,1},{1,0},{2,3},{3,2},{4,5},{5,4},{6,7},{7,6},{8,9},{9,8},{10,11... | collective-permute-start | bytes 393224 | tf_op jit(solution)/shard_map/ppermute | solution.py:441

commit v11 on v10

--- a/solution.py
+++ b/solution.py
@@ -137,42 +137,60 @@
     )(rows, wk, wv, keys_0, values_0, pattern)
 
 
-def query_kernel(*refs):
-    rows, (wq_hbm, w_hbm, kept), outs, (wq, sems) = refs[:4], refs[4:7], refs[7:11], refs[11:]
-    w = outs[2]
+def query_kernel(rows_0, rows_1, wq_hbm, kept, queries, wq, passed, sems):
     parts = halves_of(wq.shape[1])
     copies = [
         pltpu.make_async_copy(wq_hbm.at[:, part], wq.at[:, part], sems.at[index])
         for index, part in enumerate(parts)
     ]
-    copies.append(pltpu.make_async_copy(w_hbm, w, sems.at[len(parts)]))
     for copy in copies:
         copy.start()
+    passed[...] = kept[...]
+    rows = jnp.concatenate([rows_0[...], rows_1[...]], axis=0)
     for part, copy in zip(parts, copies):
         copy.wait()
-        for pair, out in ((rows[:2], outs[0]), (rows[2:], outs[1])):
-            both = jnp.concatenate([ref[...] for ref in pair], axis=0)
-            out[:, part] = dot(both, wq[:, part]).astype(BF16)
-    outs[3][...] = kept[...]
-    copies[-1].wait()
-
-
-def query(rows, w_query, w_out, kept):
-    count, depth = rows[0].shape
+        queries[:, part] = dot(rows, wq[:, part]).astype(BF16)
+
+
+def query(rows_0, rows_1, w_query, kept):
+    count, depth = rows_0.shape
     width = w_query.shape[1]
     return pl.pallas_call(
         query_kernel,
-        in_specs=[IN_VMEM] * 4 + [IN_HBM] * 2 + [IN_VMEM],
-        out_specs=[IN_VMEM] * 4,
-        out_shape=[shape((2 * count, width))] * 2
-        + [pltpu.VMEM(w_out.shape, BF16), shape(kept.shape)],
-        scratch_shapes=[
+        in_specs=[IN_VMEM] * 2 + [IN_HBM, IN_VMEM],
+        out_specs=[IN_VMEM] * 3,
+        out_shape=[
+            shape((2 * count, width)),
             pltpu.VMEM(w_query.shape, BF16),
-            pltpu.SemaphoreType.DMA((1 + len(halves_of(width)),)),
+            shape(kept.shape),
         ],
-        compiler_params=params(),
-        cost_estimate=cost(8 * count * depth * width, 4 * depth * width),
-    )(*rows, keep_in_hbm(w_query), keep_in_hbm(w_out), kept)
+        scratch_shapes=[pltpu.SemaphoreType.DMA((len(halves_of(width)),))],
+        compiler_params=params(),
+        cost_estimate=cost(4 * count * depth * width, 2 * depth * width),
+    )(rows_0, rows_1, keep_in_hbm(w_query), kept)
+
+
+def last_query_kernel(rows_0, rows_1, wq, w_hbm, queries, w, sem):
+    copy = pltpu.make_async_copy(w_hbm, w, sem)
+    copy.start()
+    rows = jnp.concatenate([rows_0[...], rows_1[...]], axis=0)
+    for part in halves_of(wq.shape[1]):
+        queries[:, part] = dot(rows, wq[:, part]).astype(BF16)
+    copy.wait()
+
+
+def last_query(rows_0, rows_1, wq, w_out):
+    count, depth = rows_0.shape
+    width = wq.shape[1]
+    return pl.pallas_call(
+        last_query_kernel,
+        in_specs=[IN_VMEM] * 3 + [IN_HBM],
+        out_specs=[IN_VMEM] * 2,
+        out_shape=[shape((2 * count, width)), pltpu.VMEM(w_out.shape, BF16)],
+        scratch_shapes=[pltpu.SemaphoreType.DMA],
+        compiler_params=params(),
+        cost_estimate=cost(4 * count * depth * width, 2 * depth * width),
+    )(rows_0, rows_1, wq, keep_in_hbm(w_out))
 
 
 def across_kernel(rows, wk, wv, keys, values):
@@ -297,7 +315,7 @@
     half_count = (asked_of.shape[0] - span) // BLOCKS_HALF
 
     heads = queries.shape[1] // HEAD_SIZE
-    group = heads if few and not near else 1
+    group = 1 if not few else min(2, heads) if near else heads
 
     def some_heads(turn, _):
         those = [turn * group + i for i in range(group)]
@@ -470,8 +488,7 @@
         beyond = after(beyond, half_a[1][0])
     keys_2, values_2 = keys_and_values(across, wk, wv)
     keys_3, values_3, kept_b = second(after(beyond, keys_2), wk, wv, keys_2, values_2, pattern)
-    rows = [mine, beside, across, beyond]
-    query_a, query_b, wo, kept_again = query(rows, w_query, w_out, kept_b)
+    query_b, wq, kept_again = query(across, beyond, w_query, kept_b)
     near = [keys_0, keys_1, keys_2, keys_3], [values_0, values_1, values_2, values_3]
     call = functools.partial(attend, masks, few)
     if few:
@@ -483,10 +500,13 @@
         column, other = second_round(along_z)
         half_b = 1, [kept_b[None], column, along_y[None], other]
         asked = after(query_b, column)
+        mine = after(mine, column)
         begun = call(2 * BLOCK, asked, [half_a], near=near, finish=False)
     else:
         half_b = 1, [lax.all_gather(kept_b, "seq", axis=0)]
         begun = call(2 * BLOCK, query_b, [half_a], near=near, finish=False)
+    query_a, wo = last_query(mine, beside, wq, w_out)
+    query_b = after(query_b, query_a)
     keep_b, send_b = call(2 * BLOCK, query_b, [half_b], begun=begun)
     other_b = swap(send_b, 1)
     leaving = mix(keep_b, other_b, wo, wo_beside, BF16)

time: 54.6 us -> 54.5 us (level)
  Pallas kernels: 17.5 us -> 16.8 us
  waiting for transfers between devices: 18.9 us -> 19.5 us
    pallas_call x3, Pallas kernels: 7.03 us -> 4.78 us  [attend(): pl.pallas_call(functools.partial(attend_kernel, first_row, near is not No...]
    pallas_call x1 -> x2, Pallas kernels: 2.67 us -> 4.24 us  [the longest x1 2.62 us: query(): pl.pallas_call(query_kernel, in_specs=[IN_VMEM] * 2 + [IN_HBM, IN_VMEM],...]
    ppermute x16, waiting for transfers between devices: 18.9 us -> 19.5 us  [swap(): return lax.ppermute(array, axis, [(i, i ^ bit) for i in range(count)])]
  transfers between devices with their start and end apart: 16 -> 16, of which waited for: 10 -> 10; matrix products, arithmetic and copies ran while one was open for 0% -> 0% of each run, Pallas kernels for 30% -> 28%
where the time goes in v11:
time: 54.5 us; the launch traced here: 54.4 us
  waiting for transfers between devices  19.5 us (36%)
  starting transfers between devices  16.8 us (31%)
  Pallas kernels  16.8 us (31%)
  other arithmetic  1.04 us (2%)
    ppermute x16, waiting for transfers between devices, swap(): return lax.ppermute(array, axis, [(i, i ^ bit) for i in range(count)])  19.5 us
    ppermute x16, starting transfers between devices, swap(): return lax.ppermute(array, axis, [(i, i ^ bit) for i in range(count)])  16.8 us
    pallas_call x3, Pallas kernels, attend(): pl.pallas_call(functools.partial(attend_kernel, first_row, near is not No...  4.78 us
    pallas_call x1, Pallas kernels, first(): pl.pallas_call(first_kernel, in_specs=[IN_HBM] * 3, out_specs=[IN_VMEM] *...  3.14 us
    pallas_call x1, Pallas kernels, query(): pl.pallas_call(query_kernel, in_specs=[IN_VMEM] * 2 + [IN_HBM, IN_VMEM],...  2.62 us
    pallas_call x2, Pallas kernels, second(): pl.pallas_call(second_kernel, in_specs=[IN_VMEM] * 6, out_specs=[IN_VMEM]...  1.81 us
    pallas_call x1, Pallas kernels, last_query(): pl.pallas_call(last_query_kernel, in_specs=[IN_VMEM] * 3 + [IN_HBM], out_...  1.62 us
    pallas_call x2, Pallas kernels, mix(): pl.pallas_call(mix_kernel, in_specs=[IN_VMEM] * 4, out_specs=IN_VMEM, out...  1.42 us
  transfers between devices with their start and end apart: 16, of which 10 were waited for; matrix products, arithmetic and copies ran while one was open for 0% of the time, Pallas kernels for 28%

profile of v11, /device:TPU:0, one launch (start us, length us, event | category | flops | bytes accessed | tf_op | source)
XLA Modules:
  0.0 54.4 jit_solution(14185461718550285497)
XLA Ops:
  0.0 0.5 collective-permute-start.5
  0.5 2.9 %collective-permute-start.4 = (bf16[128,2048]{1,0:T(8,128)(2,1)}, bf16[128,2048]{1,0:T(8,128)(2,1)S(1)}, u32[]{:S(2)}, u32[]{:S(2)}) collective-permute-start(bf16[128,2048]{1,0:T(8,128)(2,1)} %rows_hbm.1), channel_id=1, source_target_pairs={{0,2},{1,3},{2,0},{3,1},{4,6},{5,7},{6,4},{7,5},{8,10},{9,11},{10,... | collective-permute-start | bytes 1572872 | tf_op jit(solution)/shard_map/ppermute | solution.py:459
  3.5 3.1 %shard_map.73 = (bf16[128,2048]{1,0:T(8,128)(2,1)S(1)}, bf16[2048,512]{1,0:T(8,128)(2,1)S(1)}, bf16[2048,512]{1,0:T(8,128)(2,1)S(1)}, bf16[128,512]{1,0:T(8,128)(2,1)S(1)}, bf16[128,512]{1,0:T(8,128)(2,1)S(1)}) custom-call(bf16[128,2048]{1,0:T(8,128)(2,1)} %rows_hbm.1, bf16[2048,512]{1,0:T(8,128)(2,1)} %wk_hbm.1, bf16[2048,512]{1,0:T(8,128)(2,1)} %wv_hbm.1), custom_call_target="tpu_custom_call" | custom-call | flops 5368709 | bytes 41943 | tf_op jit(solution)/shard_map/pallas_call | solution.py:98
  6.6 0.9 %shard_map.74 = (bf16[128,512]{1,0:T(8,128)(2,1)S(1)}, bf16[128,512]{1,0:T(8,128)(2,1)S(1)}, bf16[2,4,32,128]{3,2,1,0:T(8,128)(2,1)S(1)}) custom-call(bf16[128,2048]{1,0:T(8,128)(2,1)S(1)} %collective-permute-done.rows.rows_1, bf16[2048,512]{1,0:T(8,128)(2,1)S(1)} %get-tuple-element.49.wk, bf16[2048,512]{1,0:T(8,128)(2,1)S(1)} %get-tuple-element.50.wv, ...), custom_call_target="tpu_custom_call" | custom-call | flops 5368709 | bytes 5242 | tf_op jit(solution)/shard_map/pallas_call | solution.py:130
  7.5 2.6 %collective-permute-start.1 = (bf16[2,4,32,128]{3,2,1,0:T(8,128)(2,1)S(1)}, bf16[2,4,32,128]{3,2,1,0:T(8,128)(2,1)S(1)}, u32[]{:S(2)}, u32[]{:S(2)}) collective-permute-start(bf16[2,4,32,128]{3,2,1,0:T(8,128)(2,1)S(1)} %get-tuple-element.53), channel_id=1, source_target_pairs={{0,16},{4,20},{8,24},{12,28},{16,0},{20,4},{24,8},{28,12},{1,17},{... | collective-permute-start | bytes 196616 | tf_op jit(solution)/shard_map/ppermute | solution.py:459
  10.1 1.3 %collective-permute-start.2 = (bf16[2,4,32,128]{3,2,1,0:T(8,128)(2,1)S(1)}, bf16[2,4,32,128]{3,2,1,0:T(8,128)(2,1)S(1)}, u32[]{:S(2)}, u32[]{:S(2)}) collective-permute-start(bf16[2,4,32,128]{3,2,1,0:T(8,128)(2,1)S(1)} %get-tuple-element.53), channel_id=1, source_target_pairs={{0,24},{4,28},{8,16},{12,20},{16,8},{20,12},{24,0},{28,4},{1,25},{... | collective-permute-start | bytes 196616 | tf_op jit(solution)/shard_map/ppermute | solution.py:459
  11.8 0.7 %shard_map.75 = (bf16[512,128]{1,0:T(8,128)(2,1)S(1)}, bf16[1024,128]{1,0:T(8,128)(2,1)S(1)}) custom-call(s32[10]{0:T(128)S(1)} %pad_add_fusion.place), custom_call_target="tpu_custom_call" | custom-call | flops 83886 | bytes 2621 | tf_op jit(solution)/shard_map/pallas_call | solution.py:256
  12.5 2.7 %collective-permute-done.1 = bf16[2,4,32,128]{3,2,1,0:T(8,128)(2,1)S(1)} collective-permute-done((bf16[2,4,32,128]{3,2,1,0:T(8,128)(2,1)S(1)}, bf16[2,4,32,128]{3,2,1,0:T(8,128)(2,1)S(1)}, u32[]{:S(2)}, u32[]{:S(2)}) %collective-permute-start.1) | collective-permute-done | bytes 65568 | tf_op jit(solution)/shard_map/ppermute | solution.py:459
  15.2 1.3 %collective-permute-done.2 = bf16[2,4,32,128]{3,2,1,0:T(8,128)(2,1)S(1)} collective-permute-done((bf16[2,4,32,128]{3,2,1,0:T(8,128)(2,1)S(1)}, bf16[2,4,32,128]{3,2,1,0:T(8,128)(2,1)S(1)}, u32[]{:S(2)}, u32[]{:S(2)}) %collective-permute-start.2) | collective-permute-done | bytes 65568 | tf_op jit(solution)/shard_map/ppermute | solution.py:459
  16.9 1.6 %collective-permute-start.11 = (bf16[4,2,4,32,128]{4,3,2,1,0:T(8,128)(2,1)S(1)}, bf16[4,2,4,32,128]{4,3,2,1,0:T(8,128)(2,1)S(1)}, u32[]{:S(2)}, u32[]{:S(2)}) collective-permute-start(bf16[4,2,4,32,128]{4,3,2,1,0:T(8,128)(2,1)S(1)} %pad_maximum_fusion.refs_9_), channel_id=1, source_target_pairs={{0,4},{4,0},{8,12},{12,8},{16,20},{20,16},{24,28},{28,24},{1,5},{5... | collective-permute-start | bytes 786440 | tf_op jit(solution)/shard_map/ppermute | solution.py:459
  18.5 0.8 %shard_map.76 = (bf16[128,512]{1,0:T(8,128)(2,1)S(1)}, bf16[128,512]{1,0:T(8,128)(2,1)S(1)}) custom-call(bf16[128,2048]{1,0:T(8,128)(2,1)S(1)} %collective-permute-done.4.rows.rows_0, bf16[2048,512]{1,0:T(8,128)(2,1)S(1)} %get-tuple-element.49.wk, bf16[2048,512]{1,0:T(8,128)(2,1)S(1)} %get-tuple-element.50.wv), custom_call_target="tpu_custom_call" | custom-call | flops 5368709 | bytes 5242 | tf_op jit(solution)/shard_map/pallas_call | solution.py:205
  19.2 0.9 %shard_map.77 = (bf16[128,512]{1,0:T(8,128)(2,1)S(1)}, bf16[128,512]{1,0:T(8,128)(2,1)S(1)}, bf16[2,4,32,128]{3,2,1,0:T(8,128)(2,1)S(1)}) custom-call(bf16[128,2048]{1,0:T(8,128)(2,1)S(1)} %collective-permute-done.6.rows.rows_1, bf16[2048,512]{1,0:T(8,128)(2,1)S(1)} %get-tuple-element.49.wk, bf16[2048,512]{1,0:T(8,128)(2,1)S(1)} %get-tuple-element.50.wv, ...), custom_call_target="tpu_custom_call" | custom-call | flops 5368709 | bytes 5242 | tf_op jit(solution)/shard_map/pallas_call | solution.py:130
  20.1 2.6 %collective-permute-start.7 = (bf16[2,4,32,128]{3,2,1,0:T(8,128)(2,1)S(1)}, bf16[2,4,32,128]{3,2,1,0:T(8,128)(2,1)S(1)}, u32[]{:S(2)}, u32[]{:S(2)}) collective-permute-start(bf16[2,4,32,128]{3,2,1,0:T(8,128)(2,1)S(1)} %get-tuple-element.67.kept), channel_id=1, source_target_pairs={{0,16},{4,20},{8,24},{12,28},{16,0},{20,4},{24,8},{28,12},{1,17},{... | collective-permute-start | bytes 196616 | tf_op jit(solution)/shard_map/ppermute | solution.py:459
  22.8 0.5 collective-permute-start.8
  23.3 0.5 collective-permute-start.9
  23.8 2.6 %shard_map.78 = (bf16[256,512]{1,0:T(8,128)(2,1)S(1)}, bf16[2048,512]{1,0:T(8,128)(2,1)S(1)}, bf16[2,4,32,128]{3,2,1,0:T(8,128)(2,1)S(1)}) custom-call(bf16[128,2048]{1,0:T(8,128)(2,1)S(1)} %collective-permute-done.4.rows.rows_0, bf16[128,2048]{1,0:T(8,128)(2,1)S(1)} %collective-permute-done.6.rows.rows_1, bf16[2048,512]{1,0:T(8,128)(2,1)} %wq_hbm.1, ...), custom_call_target="tpu_custom_call" | custom-call | flops 5368709 | bytes 20971 | tf_op jit(solution)/shard_map/pallas_call | solution.py:158
  26.4 1.1 %collective-permute-start.10 = (bf16[2,4,32,128]{3,2,1,0:T(8,128)(2,1)S(1)}, bf16[2,4,32,128]{3,2,1,0:T(8,128)(2,1)S(1)}, u32[]{:S(2)}, u32[]{:S(2)}) collective-permute-start(bf16[2,4,32,128]{3,2,1,0:T(8,128)(2,1)S(1)} %get-tuple-element.68), channel_id=1, source_target_pairs={{0,4},{4,0},{8,12},{12,8},{16,20},{20,16},{24,28},{28,24},{1,5},{5... | collective-permute-start | bytes 196616 | tf_op jit(solution)/shard_map/ppermute | solution.py:459
  27.5 1.7 %collective-permute-done.8 = bf16[2,4,32,128]{3,2,1,0:T(8,128)(2,1)S(1)} collective-permute-done((bf16[2,4,32,128]{3,2,1,0:T(8,128)(2,1)S(1)}, bf16[2,4,32,128]{3,2,1,0:T(8,128)(2,1)S(1)}, u32[]{:S(2)}, u32[]{:S(2)}) %collective-permute-start.8) | collective-permute-done | bytes 65568 | tf_op jit(solution)/shard_map/ppermute | solution.py:459
  29.5 1.3 %collective-permute-done.10 = bf16[2,4,32,128]{3,2,1,0:T(8,128)(2,1)S(1)} collective-permute-done((bf16[2,4,32,128]{3,2,1,0:T(8,128)(2,1)S(1)}, bf16[2,4,32,128]{3,2,1,0:T(8,128)(2,1)S(1)}, u32[]{:S(2)}, u32[]{:S(2)}) %collective-permute-start.10) | collective-permute-done | bytes 65568 | tf_op jit(solution)/shard_map/ppermute | solution.py:459
  30.8 1.1 %collective-permute-start.12 = (bf16[3,2,4,32,128]{4,3,2,1,0:T(8,128)(2,1)S(1)}, bf16[3,2,4,32,128]{4,3,2,1,0:T(8,128)(2,1)S(1)}, u32[]{:S(2)}, u32[]{:S(2)}) collective-permute-start(bf16[3,2,4,32,128]{4,3,2,1,0:T(8,128)(2,1)S(1)} %pad_maximum_fusion.1.refs_4_.refs_12_), channel_id=1, source_target_pairs={{0,4},{4,0},{8,12},{12,8},{16,20},{20,16},{24,28},{28,24},{1,5},{5... | collective-permute-start | bytes 589832 | tf_op jit(solution)/shard_map/ppermute | solution.py:459
  31.9 1.6 %shard_map.79 = (bf16[256,512]{1,0:T(8,128)(2,1)S(1)}, bf16[512,2048]{1,0:T(8,128)(2,1)S(1)}) custom-call(bf16[128,2048]{1,0:T(8,128)(2,1)S(1)} %get-tuple-element.73.rows_0, bf16[128,2048]{1,0:T(8,128)(2,1)S(1)} %collective-permute-done.rows.rows_1, bf16[2048,512]{1,0:T(8,128)(2,1)S(1)} %get-tuple-element.74.wq, bf16[512,2048]{1,0:T(8,128)(2,1)} %w_hbm.1), custom_call_target="tpu_custom_call" | custom-call | flops 5368709 | bytes 20971 | tf_op jit(solution)/shard_map/pallas_call | solution.py:185
  33.5 1.9 %shard_map.80 = (f32[4,128,256]{2,1,0:T(8,128)S(1)}, f32[4,8,256]{2,1,0:T(8,128)S(1)}) custom-call(bf16[512,128]{1,0:T(8,128)(2,1)S(1)} %get-tuple-element.56.asking, bf16[1024,128]{1,0:T(8,128)(2,1)S(1)} %get-tuple-element.57.asked_of, bf16[256,512]{1,0:T(8,128)(2,1)S(1)} %get-tuple-element.78.refs_0_, ...), custom_call_target="tpu_custom_call" | custom-call | flops 4026531 | bytes 5242 | tf_op jit(solution)/shard_map/pallas_call | solution.py:412
  35.4 1.1 %collective-permute-done.12.refs_6_.refs_14_ = bf16[3,2,4,32,128]{4,3,2,1,0:T(8,128)(2,1)S(1)} collective-permute-done((bf16[3,2,4,32,128]{4,3,2,1,0:T(8,128)(2,1)S(1)}, bf16[3,2,4,32,128]{4,3,2,1,0:T(8,128)(2,1)S(1)}, u32[]{:S(2)}, u32[]{:S(2)}) %collective-permute-start.12) | collective-permute-done | bytes 196640 | tf_op jit(solution)/shard_map/ppermute | solution.py:459
  36.5 0.8 %shard_map.81 = (bf16[128,512]{1,0:T(8,128)(2,1)S(1)}, bf16[128,512]{1,0:T(8,128)(2,1)S(1)}) custom-call(bf16[512,128]{1,0:T(8,128)(2,1)S(1)} %get-tuple-element.56.asking, bf16[1024,128]{1,0:T(8,128)(2,1)S(1)} %get-tuple-element.57.asked_of, bf16[256,512]{1,0:T(8,128)(2,1)S(1)} %get-tuple-element.78.refs_0_, f32[4,128,256]{2,1,0:T(8,128)S(1)} %get-tuple-element.84.refs_1_, ...), custom_call_target="tpu_custom_call" | custom-call | flops 1342177 | bytes 5242 | tf_op jit(solution)/shard_map/pallas_call | solution.py:412
  37.4 1.3 %collective-permute-done.13.rows_1 = bf16[128,512]{1,0:T(8,128)(2,1)S(1)} collective-permute-done((bf16[128,512]{1,0:T(8,128)(2,1)S(1)}, bf16[128,512]{1,0:T(8,128)(2,1)S(1)}, u32[]{:S(2)}, u32[]{:S(2)}) %collective-permute-start.13) | collective-permute-done | bytes 131104 | tf_op jit(solution)/shard_map/ppermute | solution.py:459
  38.7 0.7 %shard_map.82 = bf16[128,2048]{1,0:T(8,128)(2,1)S(1)} custom-call(bf16[128,512]{1,0:T(8,128)(2,1)S(1)} %get-tuple-element.87.rows_0, bf16[128,512]{1,0:T(8,128)(2,1)S(1)} %collective-permute-done.13.rows_1, bf16[512,2048]{1,0:T(8,128)(2,1)S(1)} %get-tuple-element.89.weight_0, bf16[512,2048]{1,0:T(8,128)(2,1)S(1)} %collective-permute-done.5.weight_1), custom_call_target="tpu_custom_call" | custom-call | flops 5368709 | bytes 10485 | tf_op jit(solution)/shard_map/pallas_call | solution.py:442
  39.4 1.6 %collective-permute-start.15 = (bf16[128,2048]{1,0:T(8,128)(2,1)S(1)}, bf16[128,2048]{1,0:T(8,128)(2,1)S(1)}, u32[]{:S(2)}, u32[]{:S(2)}) collective-permute-start(bf16[128,2048]{1,0:T(8,128)(2,1)S(1)} %shard_map.82), channel_id=1, source_target_pairs={{0,2},{1,3},{2,0},{3,1},{4,6},{5,7},{6,4},{7,5},{8,10},{9,11},{10,... | collective-permute-start | bytes 1572872 | tf_op jit(solution)/shard_map/ppermute | solution.py:459
  41.1 2.1 %shard_map.83 = (bf16[128,512]{1,0:T(8,128)(2,1)S(1)}, bf16[128,512]{1,0:T(8,128)(2,1)S(1)}) custom-call(bf16[512,128]{1,0:T(8,128)(2,1)S(1)} %get-tuple-element.56.asking, bf16[1024,128]{1,0:T(8,128)(2,1)S(1)} %get-tuple-element.57.asked_of, bf16[256,512]{1,0:T(8,128)(2,1)S(1)} %get-tuple-element.90.refs_0_, ...), custom_call_target="tpu_custom_call" | custom-call | flops 5368709 | bytes 5242 | tf_op jit(solution)/shard_map/pallas_call | solution.py:412
  43.3 1.3 %collective-permute-done.14.rows_1 = bf16[128,512]{1,0:T(8,128)(2,1)S(1)} collective-permute-done((bf16[128,512]{1,0:T(8,128)(2,1)S(1)}, bf16[128,512]{1,0:T(8,128)(2,1)S(1)}, u32[]{:S(2)}, u32[]{:S(2)}) %collective-permute-start.14) | collective-permute-done | bytes 131104 | tf_op jit(solution)/shard_map/ppermute | solution.py:459
  44.6 0.7 %shard_map.84 = f32[128,2048]{1,0:T(8,128)S(1)} custom-call(bf16[128,512]{1,0:T(8,128)(2,1)S(1)} %get-tuple-element.91.rows_0, bf16[128,512]{1,0:T(8,128)(2,1)S(1)} %collective-permute-done.14.rows_1, bf16[512,2048]{1,0:T(8,128)(2,1)S(1)} %get-tuple-element.89.weight_0, bf16[512,2048]{1,0:T(8,128)(2,1)S(1)} %collective-permute-done.5.weight_1), custom_call_target="tpu_custom_call" | custom-call | flops 5368709 | bytes 10485 | tf_op jit(solution)/shard_map/pallas_call | solution.py:442
  45.3 8.2 %collective-permute-done.15 = bf16[128,2048]{1,0:T(8,128)(2,1)S(1)} collective-permute-done((bf16[128,2048]{1,0:T(8,128)(2,1)S(1)}, bf16[128,2048]{1,0:T(8,128)(2,1)S(1)}, u32[]{:S(2)}, u32[]{:S(2)}) %collective-permute-start.15) | collective-permute-done | bytes 524320 | tf_op jit(solution)/shard_map/ppermute | solution.py:459
  53.5 0.9 %add_convert_fusion = bf16[128,2048]{1,0:T(8,128)(2,1)} fusion(f32[128,2048]{1,0:T(8,128)S(1)} %shard_map.84, bf16[128,2048]{1,0:T(8,128)(2,1)S(1)} %collective-permute-done.15), kind=kLoop, calls=%fused_computation | loop fusion | flops 786432 | bytes 2097152 | tf_op jit(solution)/shard_map/convert_element_type | solution.py:518
  (20 shorter events, 1.1 us)
Async XLA Ops:
  0.0 16.8 %collective-permute-start.5 = (bf16[512,2048]{1,0:T(8,128)(2,1)}, bf16[512,2048]{1,0:T(8,128)(2,1)S(1)}, u32[]{:S(2)}, u32[]{:S(2)}) collective-permute-start(bf16[512,2048]{1,0:T(8,128)(2,1)} %w_hbm.1), channel_id=1, source_target_pairs={{0,1},{1,0},{2,3},{3,2},{4,5},{5,4},{6,7},{7,6},{8,9},{9,8},{10,11... | collective-permute-start | bytes 6291464 | tf_op jit(solution)/shard_map/ppermute | solution.py:459
  0.5 6.2 %collective-permute-start = (bf16[128,2048]{1,0:T(8,128)(2,1)}, bf16[128,2048]{1,0:T(8,128)(2,1)S(1)}, u32[]{:S(2)}, u32[]{:S(2)}) collective-permute-start(bf16[128,2048]{1,0:T(8,128)(2,1)} %rows_hbm.1), channel_id=1, source_target_pairs={{0,1},{1,0},{2,3},{3,2},{4,5},{5,4},{6,7},{7,6},{8,9},{9,8},{10,11... | collective-permute-start | bytes 1572872 | tf_op jit(solution)/shard_map/ppermute | solution.py:459
  0.5 16.3 %collective-permute-start.4 = (bf16[128,2048]{1,0:T(8,128)(2,1)}, bf16[128,2048]{1,0:T(8,128)(2,1)S(1)}, u32[]{:S(2)}, u32[]{:S(2)}) collective-permute-start(bf16[128,2048]{1,0:T(8,128)(2,1)} %rows_hbm.1), channel_id=1, source_target_pairs={{0,2},{1,3},{2,0},{3,1},{4,6},{5,7},{6,4},{7,5},{8,10},{9,11},{10,... | collective-permute-start | bytes 1572872 | tf_op jit(solution)/shard_map/ppermute | solution.py:459
  3.5 3.2 %copy-start = (s32[4,128]{1,0:T(4,128)S(1)}, s32[4,128]{1,0:T(4,128)}, u32[]{:S(2)}) copy-start(s32[4,128]{1,0:T(4,128)} %pattern.3) | copy-start | bytes 6148
  6.6 5.1 %copy-start.1 = (s32[8]{0:T(128)S(1)}, s32[8]{0:T(128)}, u32[]{:S(2)}) copy-start(s32[8]{0:T(128)} %param.13) | copy-start | bytes 100
  7.5 7.7 %collective-permute-start.1 = (bf16[2,4,32,128]{3,2,1,0:T(8,128)(2,1)S(1)}, bf16[2,4,32,128]{3,2,1,0:T(8,128)(2,1)S(1)}, u32[]{:S(2)}, u32[]{:S(2)}) collective-permute-start(bf16[2,4,32,128]{3,2,1,0:T(8,128)(2,1)S(1)} %get-tuple-element.53), channel_id=1, source_target_pairs={{0,16},{4,20},{8,24},{12,28},{16,0},{20,4},{24,8},{28,12},{1,17},{... | collective-permute-start | bytes 196616 | tf_op jit(solution)/shard_map/ppermute | solution.py:459
  10.1 6.4 %collective-permute-start.2 = (bf16[2,4,32,128]{3,2,1,0:T(8,128)(2,1)S(1)}, bf16[2,4,32,128]{3,2,1,0:T(8,128)(2,1)S(1)}, u32[]{:S(2)}, u32[]{:S(2)}) collective-permute-start(bf16[2,4,32,128]{3,2,1,0:T(8,128)(2,1)S(1)} %get-tuple-element.53), channel_id=1, source_target_pairs={{0,24},{4,28},{8,16},{12,20},{16,8},{20,12},{24,0},{28,4},{1,25},{... | collective-permute-start | bytes 196616 | tf_op jit(solution)/shard_map/ppermute | solution.py:459
  11.5 5.3 %collective-permute-start.3 = (bf16[2,4,32,128]{3,2,1,0:T(8,128)(2,1)S(1)}, bf16[2,4,32,128]{3,2,1,0:T(8,128)(2,1)S(1)}, u32[]{:S(2)}, u32[]{:S(2)}) collective-permute-start(bf16[2,4,32,128]{3,2,1,0:T(8,128)(2,1)S(1)} %get-tuple-element.53), channel_id=1, source_target_pairs={{0,8},{4,12},{8,0},{12,4},{16,24},{20,28},{24,16},{28,20},{1,9},{5... | collective-permute-start | bytes 196616 | tf_op jit(solution)/shard_map/ppermute | solution.py:459
  16.8 2.4 %collective-permute-start.6 = (bf16[128,2048]{1,0:T(8,128)(2,1)S(1)}, bf16[128,2048]{1,0:T(8,128)(2,1)S(1)}, u32[]{:S(2)}, u32[]{:S(2)}) collective-permute-start(bf16[128,2048]{1,0:T(8,128)(2,1)S(1)} %collective-permute-done.4.rows.rows_0), channel_id=1, source_target_pairs={{0,1},{1,0},{2,3},{3,2},{4,5},{5,4},{6,7},{7,6},{8,9},{9,8},{10,11... | collective-permute-start | bytes 1572872 | tf_op jit(solution)/shard_map/ppermute | solution.py:459
  16.9 10.7 %collective-permute-start.11 = (bf16[4,2,4,32,128]{4,3,2,1,0:T(8,128)(2,1)S(1)}, bf16[4,2,4,32,128]{4,3,2,1,0:T(8,128)(2,1)S(1)}, u32[]{:S(2)}, u32[]{:S(2)}) collective-permute-start(bf16[4,2,4,32,128]{4,3,2,1,0:T(8,128)(2,1)S(1)} %pad_maximum_fusion.refs_9_), channel_id=1, source_target_pairs={{0,4},{4,0},{8,12},{12,8},{16,20},{20,16},{24,28},{28,24},{1,5},{5... | collective-permute-start | bytes 786440 | tf_op jit(solution)/shard_map/ppermute | solution.py:459
  20.1 7.4 %collective-permute-start.7 = (bf16[2,4,32,128]{3,2,1,0:T(8,128)(2,1)S(1)}, bf16[2,4,32,128]{3,2,1,0:T(8,128)(2,1)S(1)}, u32[]{:S(2)}, u32[]{:S(2)}) collective-permute-start(bf16[2,4,32,128]{3,2,1,0:T(8,128)(2,1)S(1)} %get-tuple-element.67.kept), channel_id=1, source_target_pairs={{0,16},{4,20},{8,24},{12,28},{16,0},{20,4},{24,8},{28,12},{1,17},{... | collective-permute-start | bytes 196616 | tf_op jit(solution)/shard_map/ppermute | solution.py:459
  22.8 6.5 %collective-permute-start.8 = (bf16[2,4,32,128]{3,2,1,0:T(8,128)(2,1)S(1)}, bf16[2,4,32,128]{3,2,1,0:T(8,128)(2,1)S(1)}, u32[]{:S(2)}, u32[]{:S(2)}) collective-permute-start(bf16[2,4,32,128]{3,2,1,0:T(8,128)(2,1)S(1)} %get-tuple-element.67.kept), channel_id=1, source_target_pairs={{0,24},{4,28},{8,16},{12,20},{16,8},{20,12},{24,0},{28,4},{1,25},{... | collective-permute-start | bytes 196616 | tf_op jit(solution)/shard_map/ppermute | solution.py:459
  23.3 6.2 %collective-permute-start.9 = (bf16[2,4,32,128]{3,2,1,0:T(8,128)(2,1)S(1)}, bf16[2,4,32,128]{3,2,1,0:T(8,128)(2,1)S(1)}, u32[]{:S(2)}, u32[]{:S(2)}) collective-permute-start(bf16[2,4,32,128]{3,2,1,0:T(8,128)(2,1)S(1)} %get-tuple-element.67.kept), channel_id=1, source_target_pairs={{0,8},{4,12},{8,0},{12,4},{16,24},{20,28},{24,16},{28,20},{1,9},{5... | collective-permute-start | bytes 196616 | tf_op jit(solution)/shard_map/ppermute | solution.py:459
  26.4 4.3 %collective-permute-start.10 = (bf16[2,4,32,128]{3,2,1,0:T(8,128)(2,1)S(1)}, bf16[2,4,32,128]{3,2,1,0:T(8,128)(2,1)S(1)}, u32[]{:S(2)}, u32[]{:S(2)}) collective-permute-start(bf16[2,4,32,128]{3,2,1,0:T(8,128)(2,1)S(1)} %get-tuple-element.68), channel_id=1, source_target_pairs={{0,4},{4,0},{8,12},{12,8},{16,20},{20,16},{24,28},{28,24},{1,5},{5... | collective-permute-start | bytes 196616 | tf_op jit(solution)/shard_map/ppermute | solution.py:459
  30.8 5.7 %collective-permute-start.12 = (bf16[3,2,4,32,128]{4,3,2,1,0:T(8,128)(2,1)S(1)}, bf16[3,2,4,32,128]{4,3,2,1,0:T(8,128)(2,1)S(1)}, u32[]{:S(2)}, u32[]{:S(2)}) collective-permute-start(bf16[3,2,4,32,128]{4,3,2,1,0:T(8,128)(2,1)S(1)} %pad_maximum_fusion.1.refs_4_.refs_12_), channel_id=1, source_target_pairs={{0,4},{4,0},{8,12},{12,8},{16,20},{20,16},{24,28},{28,24},{1,5},{5... | collective-permute-start | bytes 589832 | tf_op jit(solution)/shard_map/ppermute | solution.py:459
  37.3 1.4 %collective-permute-start.13 = (bf16[128,512]{1,0:T(8,128)(2,1)S(1)}, bf16[128,512]{1,0:T(8,128)(2,1)S(1)}, u32[]{:S(2)}, u32[]{:S(2)}) collective-permute-start(bf16[128,512]{1,0:T(8,128)(2,1)S(1)} %get-tuple-element.88), channel_id=1, source_target_pairs={{0,1},{1,0},{2,3},{3,2},{4,5},{5,4},{6,7},{7,6},{8,9},{9,8},{10,11... | collective-permute-start | bytes 393224 | tf_op jit(solution)/shard_map/ppermute | solution.py:459
  39.4 14.0 %collective-permute-start.15 = (bf16[128,2048]{1,0:T(8,128)(2,1)S(1)}, bf16[128,2048]{1,0:T(8,128)(2,1)S(1)}, u32[]{:S(2)}, u32[]{:S(2)}) collective-permute-start(bf16[128,2048]{1,0:T(8,128)(2,1)S(1)} %shard_map.82), channel_id=1, source_target_pairs={{0,2},{1,3},{2,0},{3,1},{4,6},{5,7},{6,4},{7,5},{8,10},{9,11},{10,... | collective-permute-start | bytes 1572872 | tf_op jit(solution)/shard_map/ppermute | solution.py:459
  43.2 1.4 %collective-permute-start.14 = (bf16[128,512]{1,0:T(8,128)(2,1)S(1)}, bf16[128,512]{1,0:T(8,128)(2,1)S(1)}, u32[]{:S(2)}, u32[]{:S(2)}) collective-permute-start(bf16[128,512]{1,0:T(8,128)(2,1)S(1)} %get-tuple-element.92), channel_id=1, source_target_pairs={{0,1},{1,0},{2,3},{3,2},{4,5},{5,4},{6,7},{7,6},{8,9},{9,8},{10,11... | collective-permute-start | bytes 393224 | tf_op jit(solution)/shard_map/ppermute | solution.py:459

commit v12 on v11

--- a/solution.py
+++ b/solution.py
@@ -14,6 +14,7 @@
 BLOCKS_HALF = 2
 FAR_ROWS = BLOCKS_HALF * DILATED_KEPT
 GROUP = 8
+STREAMS = 8
 HIDDEN = -1e30
 SCALE = math.log2(math.e) / math.sqrt(HEAD_SIZE)
 BF16 = jnp.bfloat16
@@ -51,6 +52,17 @@
 
 def keep_in_hbm(array):
     return pltpu.with_memory_space_constraint(array, pltpu.HBM)
+
+
+def start_copies(source, target, sems, base):
+    rows = source.shape[0] // STREAMS
+    copies = []
+    for index in range(STREAMS):
+        where = slice(index * rows, (index + 1) * rows)
+        copy = pltpu.make_async_copy(source.at[where, :], target.at[where, :], sems.at[base + index])
+        copy.start()
+        copies.append(copy)
+    return copies
 
 
 def halves_of(width):
@@ -75,21 +87,16 @@
 
 
 def first_kernel(rows_hbm, wk_hbm, wv_hbm, rows, wk, wv, keys, values, sems):
-    parts = halves_of(wk.shape[1])
     whole = pltpu.make_async_copy(rows_hbm, rows, sems.at[0])
     whole.start()
-    copies = []
-    for index, part in enumerate(parts):
-        for side, (source, target) in enumerate(((wk_hbm, wk), (wv_hbm, wv))):
-            copy = pltpu.make_async_copy(
-                source.at[:, part], target.at[:, part], sems.at[1 + 2 * index + side]
-            )
-            copy.start()
-            copies.append((copy, target, part, (keys, values)[side]))
+    key_copies = start_copies(wk_hbm, wk, sems, 1)
+    value_copies = start_copies(wv_hbm, wv, sems, 1 + STREAMS)
     whole.wait()
-    for copy, weight, part, out in copies:
-        copy.wait()
-        out[:, part] = dot(rows[...], weight[:, part]).astype(BF16)
+    for copies, weight, out in ((key_copies, wk, keys), (value_copies, wv, values)):
+        for copy in copies:
+            copy.wait()
+        for part in halves_of(wk.shape[1]):
+            out[:, part] = dot(rows[...], weight[:, part]).astype(BF16)
 
 
 def first(rows, w_key, w_value):
@@ -106,7 +113,7 @@
             shape((count, width)),
             shape((count, width)),
         ],
-        scratch_shapes=[pltpu.SemaphoreType.DMA((1 + 2 * len(halves_of(width)),))],
+        scratch_shapes=[pltpu.SemaphoreType.DMA((1 + 2 * STREAMS,))],
         compiler_params=params(),
         cost_estimate=cost(4 * count * depth * width, 4 * depth * width),
     )(keep_in_hbm(rows), keep_in_hbm(w_key), keep_in_hbm(w_value))
@@ -138,17 +145,12 @@
 
 
 def query_kernel(rows_0, rows_1, wq_hbm, kept, queries, wq, passed, sems):
-    parts = halves_of(wq.shape[1])
-    copies = [
-        pltpu.make_async_copy(wq_hbm.at[:, part], wq.at[:, part], sems.at[index])
-        for index, part in enumerate(parts)
-    ]
-    for copy in copies:
-        copy.start()
+    copies = start_copies(wq_hbm, wq, sems, 0)
     passed[...] = kept[...]
     rows = jnp.concatenate([rows_0[...], rows_1[...]], axis=0)
-    for part, copy in zip(parts, copies):
+    for copy in copies:
         copy.wait()
+    for part in halves_of(wq.shape[1]):
         queries[:, part] = dot(rows, wq[:, part]).astype(BF16)
 
 
@@ -164,19 +166,19 @@
             pltpu.VMEM(w_query.shape, BF16),
             shape(kept.shape),
         ],
-        scratch_shapes=[pltpu.SemaphoreType.DMA((len(halves_of(width)),))],
+        scratch_shapes=[pltpu.SemaphoreType.DMA((STREAMS,))],
         compiler_params=params(),
         cost_estimate=cost(4 * count * depth * width, 2 * depth * width),
     )(rows_0, rows_1, keep_in_hbm(w_query), kept)
 
 
-def last_query_kernel(rows_0, rows_1, wq, w_hbm, queries, w, sem):
-    copy = pltpu.make_async_copy(w_hbm, w, sem)
-    copy.start()
+def last_query_kernel(rows_0, rows_1, wq, w_hbm, queries, w, sems):
+    copies = start_copies(w_hbm, w, sems, 0)
     rows = jnp.concatenate([rows_0[...], rows_1[...]], axis=0)
     for part in halves_of(wq.shape[1]):
         queries[:, part] = dot(rows, wq[:, part]).astype(BF16)
-    copy.wait()
+    for copy in copies:
+        copy.wait()
 
 
 def last_query(rows_0, rows_1, wq, w_out):
@@ -187,7 +189,7 @@
         in_specs=[IN_VMEM] * 3 + [IN_HBM],
         out_specs=[IN_VMEM] * 2,
         out_shape=[shape((2 * count, width)), pltpu.VMEM(w_out.shape, BF16)],
-        scratch_shapes=[pltpu.SemaphoreType.DMA],
+        scratch_shapes=[pltpu.SemaphoreType.DMA((STREAMS,))],
         compiler_params=params(),
         cost_estimate=cost(4 * count * depth * width, 2 * depth * width),
     )(rows_0, rows_1, wq, keep_in_hbm(w_out))

time: 54.5 us -> 54.3 us (level)
  transfers between devices with their start and end apart: 16 -> 16, of which waited for: 10 -> 11; matrix products, arithmetic and copies ran while one was open for 0% -> 0% of each run, Pallas kernels for 28% -> 28%
where the time goes in v12:
time: 54.3 us; the launch traced here: 54.1 us
  waiting for transfers between devices  19.3 us (36%)
  starting transfers between devices  17.1 us (31%)
  Pallas kernels  16.5 us (30%)
  other arithmetic  1.04 us (2%)
    ppermute x16, waiting for transfers between devices, swap(): return lax.ppermute(array, axis, [(i, i ^ bit) for i in range(count)])  19.3 us
    ppermute x16, starting transfers between devices, swap(): return lax.ppermute(array, axis, [(i, i ^ bit) for i in range(count)])  17.1 us
    pallas_call x3, Pallas kernels, attend(): pl.pallas_call(functools.partial(attend_kernel, first_row, near is not No...  4.78 us
    pallas_call x1, Pallas kernels, first(): pl.pallas_call(first_kernel, in_specs=[IN_HBM] * 3, out_specs=[IN_VMEM] *...  2.92 us
    pallas_call x1, Pallas kernels, query(): pl.pallas_call(query_kernel, in_specs=[IN_VMEM] * 2 + [IN_HBM, IN_VMEM],...  2.29 us
    pallas_call x2, Pallas kernels, second(): pl.pallas_call(second_kernel, in_specs=[IN_VMEM] * 6, out_specs=[IN_VMEM]...  1.81 us
    pallas_call x1, Pallas kernels, last_query(): pl.pallas_call(last_query_kernel, in_specs=[IN_VMEM] * 3 + [IN_HBM], out_...  1.79 us
    pallas_call x2, Pallas kernels, mix(): pl.pallas_call(mix_kernel, in_specs=[IN_VMEM] * 4, out_specs=IN_VMEM, out...  1.45 us
  transfers between devices with their start and end apart: 16, of which 11 were waited for; matrix products, arithmetic and copies ran while one was open for 0% of the time, Pallas kernels for 28%

profile of v12, /device:TPU:0, one launch (start us, length us, event | category | flops | bytes accessed | tf_op | source)
XLA Modules:
  0.0 54.1 jit_solution(6996377317726101567)
XLA Ops:
  0.5 2.9 %collective-permute-start.4 = (bf16[128,2048]{1,0:T(8,128)(2,1)}, bf16[128,2048]{1,0:T(8,128)(2,1)S(1)}, u32[]{:S(2)}, u32[]{:S(2)}) collective-permute-start(bf16[128,2048]{1,0:T(8,128)(2,1)} %rows_hbm.1), channel_id=1, source_target_pairs={{0,2},{1,3},{2,0},{3,1},{4,6},{5,7},{6,4},{7,5},{8,10},{9,11},{10,... | collective-permute-start | bytes 1572872 | tf_op jit(solution)/shard_map/ppermute | solution.py:461
  3.5 2.9 %shard_map.73 = (bf16[128,2048]{1,0:T(8,128)(2,1)S(1)}, bf16[2048,512]{1,0:T(8,128)(2,1)S(1)}, bf16[2048,512]{1,0:T(8,128)(2,1)S(1)}, bf16[128,512]{1,0:T(8,128)(2,1)S(1)}, bf16[128,512]{1,0:T(8,128)(2,1)S(1)}) custom-call(bf16[128,2048]{1,0:T(8,128)(2,1)} %rows_hbm.1, bf16[2048,512]{1,0:T(8,128)(2,1)} %wk_hbm.1, bf16[2048,512]{1,0:T(8,128)(2,1)} %wv_hbm.1), custom_call_target="tpu_custom_call" | custom-call | flops 5368709 | bytes 41943 | tf_op jit(solution)/shard_map/pallas_call | solution.py:105
  6.4 0.9 %shard_map.74 = (bf16[128,512]{1,0:T(8,128)(2,1)S(1)}, bf16[128,512]{1,0:T(8,128)(2,1)S(1)}, bf16[2,4,32,128]{3,2,1,0:T(8,128)(2,1)S(1)}) custom-call(bf16[128,2048]{1,0:T(8,128)(2,1)S(1)} %collective-permute-done.rows.rows_1, bf16[2048,512]{1,0:T(8,128)(2,1)S(1)} %get-tuple-element.49.wk, bf16[2048,512]{1,0:T(8,128)(2,1)S(1)} %get-tuple-element.50.wv, ...), custom_call_target="tpu_custom_call" | custom-call | flops 5368709 | bytes 5242 | tf_op jit(solution)/shard_map/pallas_call | solution.py:137
  7.3 2.8 %collective-permute-start.1 = (bf16[2,4,32,128]{3,2,1,0:T(8,128)(2,1)S(1)}, bf16[2,4,32,128]{3,2,1,0:T(8,128)(2,1)S(1)}, u32[]{:S(2)}, u32[]{:S(2)}) collective-permute-start(bf16[2,4,32,128]{3,2,1,0:T(8,128)(2,1)S(1)} %get-tuple-element.53), channel_id=1, source_target_pairs={{0,16},{4,20},{8,24},{12,28},{16,0},{20,4},{24,8},{28,12},{1,17},{... | collective-permute-start | bytes 196616 | tf_op jit(solution)/shard_map/ppermute | solution.py:461
  10.1 1.3 %collective-permute-start.2 = (bf16[2,4,32,128]{3,2,1,0:T(8,128)(2,1)S(1)}, bf16[2,4,32,128]{3,2,1,0:T(8,128)(2,1)S(1)}, u32[]{:S(2)}, u32[]{:S(2)}) collective-permute-start(bf16[2,4,32,128]{3,2,1,0:T(8,128)(2,1)S(1)} %get-tuple-element.53), channel_id=1, source_target_pairs={{0,24},{4,28},{8,16},{12,20},{16,8},{20,12},{24,0},{28,4},{1,25},{... | collective-permute-start | bytes 196616 | tf_op jit(solution)/shard_map/ppermute | solution.py:461
  11.7 0.7 %shard_map.75 = (bf16[512,128]{1,0:T(8,128)(2,1)S(1)}, bf16[1024,128]{1,0:T(8,128)(2,1)S(1)}) custom-call(s32[10]{0:T(128)S(1)} %pad_add_fusion.place), custom_call_target="tpu_custom_call" | custom-call | flops 83886 | bytes 2621 | tf_op jit(solution)/shard_map/pallas_call | solution.py:258
  12.4 1.6 %collective-permute-done.1 = bf16[2,4,32,128]{3,2,1,0:T(8,128)(2,1)S(1)} collective-permute-done((bf16[2,4,32,128]{3,2,1,0:T(8,128)(2,1)S(1)}, bf16[2,4,32,128]{3,2,1,0:T(8,128)(2,1)S(1)}, u32[]{:S(2)}, u32[]{:S(2)}) %collective-permute-start.1) | collective-permute-done | bytes 65568 | tf_op jit(solution)/shard_map/ppermute | solution.py:461
  14.1 2.4 %collective-permute-done.2 = bf16[2,4,32,128]{3,2,1,0:T(8,128)(2,1)S(1)} collective-permute-done((bf16[2,4,32,128]{3,2,1,0:T(8,128)(2,1)S(1)}, bf16[2,4,32,128]{3,2,1,0:T(8,128)(2,1)S(1)}, u32[]{:S(2)}, u32[]{:S(2)}) %collective-permute-start.2) | collective-permute-done | bytes 65568 | tf_op jit(solution)/shard_map/ppermute | solution.py:461
  16.7 1.7 %collective-permute-start.11 = (bf16[4,2,4,32,128]{4,3,2,1,0:T(8,128)(2,1)S(1)}, bf16[4,2,4,32,128]{4,3,2,1,0:T(8,128)(2,1)S(1)}, u32[]{:S(2)}, u32[]{:S(2)}) collective-permute-start(bf16[4,2,4,32,128]{4,3,2,1,0:T(8,128)(2,1)S(1)} %pad_maximum_fusion.refs_9_), channel_id=1, source_target_pairs={{0,4},{4,0},{8,12},{12,8},{16,20},{20,16},{24,28},{28,24},{1,5},{5... | collective-permute-start | bytes 786440 | tf_op jit(solution)/shard_map/ppermute | solution.py:461
  18.4 0.8 %shard_map.76 = (bf16[128,512]{1,0:T(8,128)(2,1)S(1)}, bf16[128,512]{1,0:T(8,128)(2,1)S(1)}) custom-call(bf16[128,2048]{1,0:T(8,128)(2,1)S(1)} %collective-permute-done.4.rows.rows_0, bf16[2048,512]{1,0:T(8,128)(2,1)S(1)} %get-tuple-element.49.wk, bf16[2048,512]{1,0:T(8,128)(2,1)S(1)} %get-tuple-element.50.wv), custom_call_target="tpu_custom_call" | custom-call | flops 5368709 | bytes 5242 | tf_op jit(solution)/shard_map/pallas_call | solution.py:207
  19.2 0.9 %shard_map.77 = (bf16[128,512]{1,0:T(8,128)(2,1)S(1)}, bf16[128,512]{1,0:T(8,128)(2,1)S(1)}, bf16[2,4,32,128]{3,2,1,0:T(8,128)(2,1)S(1)}) custom-call(bf16[128,2048]{1,0:T(8,128)(2,1)S(1)} %collective-permute-done.6.rows.rows_1, bf16[2048,512]{1,0:T(8,128)(2,1)S(1)} %get-tuple-element.49.wk, bf16[2048,512]{1,0:T(8,128)(2,1)S(1)} %get-tuple-element.50.wv, ...), custom_call_target="tpu_custom_call" | custom-call | flops 5368709 | bytes 5242 | tf_op jit(solution)/shard_map/pallas_call | solution.py:137
  20.1 2.7 %collective-permute-start.7 = (bf16[2,4,32,128]{3,2,1,0:T(8,128)(2,1)S(1)}, bf16[2,4,32,128]{3,2,1,0:T(8,128)(2,1)S(1)}, u32[]{:S(2)}, u32[]{:S(2)}) collective-permute-start(bf16[2,4,32,128]{3,2,1,0:T(8,128)(2,1)S(1)} %get-tuple-element.67.kept), channel_id=1, source_target_pairs={{0,16},{4,20},{8,24},{12,28},{16,0},{20,4},{24,8},{28,12},{1,17},{... | collective-permute-start | bytes 196616 | tf_op jit(solution)/shard_map/ppermute | solution.py:461
  22.8 0.6 %collective-permute-start.8 = (bf16[2,4,32,128]{3,2,1,0:T(8,128)(2,1)S(1)}, bf16[2,4,32,128]{3,2,1,0:T(8,128)(2,1)S(1)}, u32[]{:S(2)}, u32[]{:S(2)}) collective-permute-start(bf16[2,4,32,128]{3,2,1,0:T(8,128)(2,1)S(1)} %get-tuple-element.67.kept), channel_id=1, source_target_pairs={{0,24},{4,28},{8,16},{12,20},{16,8},{20,12},{24,0},{28,4},{1,25},{... | collective-permute-start | bytes 196616 | tf_op jit(solution)/shard_map/ppermute | solution.py:461
  23.4 0.5 collective-permute-start.9
  23.9 2.3 %shard_map.78 = (bf16[256,512]{1,0:T(8,128)(2,1)S(1)}, bf16[2048,512]{1,0:T(8,128)(2,1)S(1)}, bf16[2,4,32,128]{3,2,1,0:T(8,128)(2,1)S(1)}) custom-call(bf16[128,2048]{1,0:T(8,128)(2,1)S(1)} %collective-permute-done.4.rows.rows_0, bf16[128,2048]{1,0:T(8,128)(2,1)S(1)} %collective-permute-done.6.rows.rows_1, bf16[2048,512]{1,0:T(8,128)(2,1)} %wq_hbm.1, ...), custom_call_target="tpu_custom_call" | custom-call | flops 5368709 | bytes 20971 | tf_op jit(solution)/shard_map/pallas_call | solution.py:160
  26.2 1.1 %collective-permute-start.10 = (bf16[2,4,32,128]{3,2,1,0:T(8,128)(2,1)S(1)}, bf16[2,4,32,128]{3,2,1,0:T(8,128)(2,1)S(1)}, u32[]{:S(2)}, u32[]{:S(2)}) collective-permute-start(bf16[2,4,32,128]{3,2,1,0:T(8,128)(2,1)S(1)} %get-tuple-element.68), channel_id=1, source_target_pairs={{0,4},{4,0},{8,12},{12,8},{16,20},{20,16},{24,28},{28,24},{1,5},{5... | collective-permute-start | bytes 196616 | tf_op jit(solution)/shard_map/ppermute | solution.py:461
  27.2 0.8 %collective-permute-done.7 = bf16[2,4,32,128]{3,2,1,0:T(8,128)(2,1)S(1)} collective-permute-done((bf16[2,4,32,128]{3,2,1,0:T(8,128)(2,1)S(1)}, bf16[2,4,32,128]{3,2,1,0:T(8,128)(2,1)S(1)}, u32[]{:S(2)}, u32[]{:S(2)}) %collective-permute-start.7) | collective-permute-done | bytes 65568 | tf_op jit(solution)/shard_map/ppermute | solution.py:461
  28.0 1.3 %collective-permute-done.8 = bf16[2,4,32,128]{3,2,1,0:T(8,128)(2,1)S(1)} collective-permute-done((bf16[2,4,32,128]{3,2,1,0:T(8,128)(2,1)S(1)}, bf16[2,4,32,128]{3,2,1,0:T(8,128)(2,1)S(1)}, u32[]{:S(2)}, u32[]{:S(2)}) %collective-permute-start.8) | collective-permute-done | bytes 65568 | tf_op jit(solution)/shard_map/ppermute | solution.py:461
  29.5 1.0 %collective-permute-done.10 = bf16[2,4,32,128]{3,2,1,0:T(8,128)(2,1)S(1)} collective-permute-done((bf16[2,4,32,128]{3,2,1,0:T(8,128)(2,1)S(1)}, bf16[2,4,32,128]{3,2,1,0:T(8,128)(2,1)S(1)}, u32[]{:S(2)}, u32[]{:S(2)}) %collective-permute-start.10) | collective-permute-done | bytes 65568 | tf_op jit(solution)/shard_map/ppermute | solution.py:461
  30.5 1.1 %collective-permute-start.12 = (bf16[3,2,4,32,128]{4,3,2,1,0:T(8,128)(2,1)S(1)}, bf16[3,2,4,32,128]{4,3,2,1,0:T(8,128)(2,1)S(1)}, u32[]{:S(2)}, u32[]{:S(2)}) collective-permute-start(bf16[3,2,4,32,128]{4,3,2,1,0:T(8,128)(2,1)S(1)} %pad_maximum_fusion.1.refs_4_.refs_12_), channel_id=1, source_target_pairs={{0,4},{4,0},{8,12},{12,8},{16,20},{20,16},{24,28},{28,24},{1,5},{5... | collective-permute-start | bytes 589832 | tf_op jit(solution)/shard_map/ppermute | solution.py:461
  31.6 1.8 %shard_map.79 = (bf16[256,512]{1,0:T(8,128)(2,1)S(1)}, bf16[512,2048]{1,0:T(8,128)(2,1)S(1)}) custom-call(bf16[128,2048]{1,0:T(8,128)(2,1)S(1)} %get-tuple-element.73.rows_0, bf16[128,2048]{1,0:T(8,128)(2,1)S(1)} %collective-permute-done.rows.rows_1, bf16[2048,512]{1,0:T(8,128)(2,1)S(1)} %get-tuple-element.74.wq, bf16[512,2048]{1,0:T(8,128)(2,1)} %w_hbm.1), custom_call_target="tpu_custom_call" | custom-call | flops 5368709 | bytes 20971 | tf_op jit(solution)/shard_map/pallas_call | solution.py:187
  33.4 1.9 %shard_map.80 = (f32[4,128,256]{2,1,0:T(8,128)S(1)}, f32[4,8,256]{2,1,0:T(8,128)S(1)}) custom-call(bf16[512,128]{1,0:T(8,128)(2,1)S(1)} %get-tuple-element.56.asking, bf16[1024,128]{1,0:T(8,128)(2,1)S(1)} %get-tuple-element.57.asked_of, bf16[256,512]{1,0:T(8,128)(2,1)S(1)} %get-tuple-element.78.refs_0_, ...), custom_call_target="tpu_custom_call" | custom-call | flops 4026531 | bytes 5242 | tf_op jit(solution)/shard_map/pallas_call | solution.py:414
  35.3 1.0 %collective-permute-done.12.refs_6_.refs_14_ = bf16[3,2,4,32,128]{4,3,2,1,0:T(8,128)(2,1)S(1)} collective-permute-done((bf16[3,2,4,32,128]{4,3,2,1,0:T(8,128)(2,1)S(1)}, bf16[3,2,4,32,128]{4,3,2,1,0:T(8,128)(2,1)S(1)}, u32[]{:S(2)}, u32[]{:S(2)}) %collective-permute-start.12) | collective-permute-done | bytes 196640 | tf_op jit(solution)/shard_map/ppermute | solution.py:461
  36.3 0.8 %shard_map.81 = (bf16[128,512]{1,0:T(8,128)(2,1)S(1)}, bf16[128,512]{1,0:T(8,128)(2,1)S(1)}) custom-call(bf16[512,128]{1,0:T(8,128)(2,1)S(1)} %get-tuple-element.56.asking, bf16[1024,128]{1,0:T(8,128)(2,1)S(1)} %get-tuple-element.57.asked_of, bf16[256,512]{1,0:T(8,128)(2,1)S(1)} %get-tuple-element.78.refs_0_, f32[4,128,256]{2,1,0:T(8,128)S(1)} %get-tuple-element.84.refs_1_, ...), custom_call_target="tpu_custom_call" | custom-call | flops 1342177 | bytes 5242 | tf_op jit(solution)/shard_map/pallas_call | solution.py:414
  37.1 1.3 %collective-permute-done.13.rows_1 = bf16[128,512]{1,0:T(8,128)(2,1)S(1)} collective-permute-done((bf16[128,512]{1,0:T(8,128)(2,1)S(1)}, bf16[128,512]{1,0:T(8,128)(2,1)S(1)}, u32[]{:S(2)}, u32[]{:S(2)}) %collective-permute-start.13) | collective-permute-done | bytes 131104 | tf_op jit(solution)/shard_map/ppermute | solution.py:461
  38.4 0.7 %shard_map.82 = bf16[128,2048]{1,0:T(8,128)(2,1)S(1)} custom-call(bf16[128,512]{1,0:T(8,128)(2,1)S(1)} %get-tuple-element.87.rows_0, bf16[128,512]{1,0:T(8,128)(2,1)S(1)} %collective-permute-done.13.rows_1, bf16[512,2048]{1,0:T(8,128)(2,1)S(1)} %get-tuple-element.89.weight_0, bf16[512,2048]{1,0:T(8,128)(2,1)S(1)} %collective-permute-done.5.weight_1), custom_call_target="tpu_custom_call" | custom-call | flops 5368709 | bytes 10485 | tf_op jit(solution)/shard_map/pallas_call | solution.py:444
  39.2 1.6 %collective-permute-start.15 = (bf16[128,2048]{1,0:T(8,128)(2,1)S(1)}, bf16[128,2048]{1,0:T(8,128)(2,1)S(1)}, u32[]{:S(2)}, u32[]{:S(2)}) collective-permute-start(bf16[128,2048]{1,0:T(8,128)(2,1)S(1)} %shard_map.82), channel_id=1, source_target_pairs={{0,2},{1,3},{2,0},{3,1},{4,6},{5,7},{6,4},{7,5},{8,10},{9,11},{10,... | collective-permute-start | bytes 1572872 | tf_op jit(solution)/shard_map/ppermute | solution.py:461
  40.7 2.1 %shard_map.83 = (bf16[128,512]{1,0:T(8,128)(2,1)S(1)}, bf16[128,512]{1,0:T(8,128)(2,1)S(1)}) custom-call(bf16[512,128]{1,0:T(8,128)(2,1)S(1)} %get-tuple-element.56.asking, bf16[1024,128]{1,0:T(8,128)(2,1)S(1)} %get-tuple-element.57.asked_of, bf16[256,512]{1,0:T(8,128)(2,1)S(1)} %get-tuple-element.90.refs_0_, ...), custom_call_target="tpu_custom_call" | custom-call | flops 5368709 | bytes 5242 | tf_op jit(solution)/shard_map/pallas_call | solution.py:414
  42.9 1.3 %collective-permute-done.14.rows_1 = bf16[128,512]{1,0:T(8,128)(2,1)S(1)} collective-permute-done((bf16[128,512]{1,0:T(8,128)(2,1)S(1)}, bf16[128,512]{1,0:T(8,128)(2,1)S(1)}, u32[]{:S(2)}, u32[]{:S(2)}) %collective-permute-start.14) | collective-permute-done | bytes 131104 | tf_op jit(solution)/shard_map/ppermute | solution.py:461
  44.3 0.7 %shard_map.84 = f32[128,2048]{1,0:T(8,128)S(1)} custom-call(bf16[128,512]{1,0:T(8,128)(2,1)S(1)} %get-tuple-element.91.rows_0, bf16[128,512]{1,0:T(8,128)(2,1)S(1)} %collective-permute-done.14.rows_1, bf16[512,2048]{1,0:T(8,128)(2,1)S(1)} %get-tuple-element.89.weight_0, bf16[512,2048]{1,0:T(8,128)(2,1)S(1)} %collective-permute-done.5.weight_1), custom_call_target="tpu_custom_call" | custom-call | flops 5368709 | bytes 10485 | tf_op jit(solution)/shard_map/pallas_call | solution.py:444
  45.0 8.2 %collective-permute-done.15 = bf16[128,2048]{1,0:T(8,128)(2,1)S(1)} collective-permute-done((bf16[128,2048]{1,0:T(8,128)(2,1)S(1)}, bf16[128,2048]{1,0:T(8,128)(2,1)S(1)}, u32[]{:S(2)}, u32[]{:S(2)}) %collective-permute-start.15) | collective-permute-done | bytes 524320 | tf_op jit(solution)/shard_map/ppermute | solution.py:461
  53.2 0.9 %add_convert_fusion = bf16[128,2048]{1,0:T(8,128)(2,1)} fusion(f32[128,2048]{1,0:T(8,128)S(1)} %shard_map.84, bf16[128,2048]{1,0:T(8,128)(2,1)S(1)} %collective-permute-done.15), kind=kLoop, calls=%fused_computation | loop fusion | flops 786432 | bytes 2097152 | tf_op jit(solution)/shard_map/convert_element_type | solution.py:520
  (20 shorter events, 1.4 us)
Async XLA Ops:
  0.0 16.7 %collective-permute-start.5 = (bf16[512,2048]{1,0:T(8,128)(2,1)}, bf16[512,2048]{1,0:T(8,128)(2,1)S(1)}, u32[]{:S(2)}, u32[]{:S(2)}) collective-permute-start(bf16[512,2048]{1,0:T(8,128)(2,1)} %w_hbm.1), channel_id=1, source_target_pairs={{0,1},{1,0},{2,3},{3,2},{4,5},{5,4},{6,7},{7,6},{8,9},{9,8},{10,11... | collective-permute-start | bytes 6291464 | tf_op jit(solution)/shard_map/ppermute | solution.py:461
  0.5 5.9 %collective-permute-start = (bf16[128,2048]{1,0:T(8,128)(2,1)}, bf16[128,2048]{1,0:T(8,128)(2,1)S(1)}, u32[]{:S(2)}, u32[]{:S(2)}) collective-permute-start(bf16[128,2048]{1,0:T(8,128)(2,1)} %rows_hbm.1), channel_id=1, source_target_pairs={{0,1},{1,0},{2,3},{3,2},{4,5},{5,4},{6,7},{7,6},{8,9},{9,8},{10,11... | collective-permute-start | bytes 1572872 | tf_op jit(solution)/shard_map/ppermute | solution.py:461
  0.5 16.1 %collective-permute-start.4 = (bf16[128,2048]{1,0:T(8,128)(2,1)}, bf16[128,2048]{1,0:T(8,128)(2,1)S(1)}, u32[]{:S(2)}, u32[]{:S(2)}) collective-permute-start(bf16[128,2048]{1,0:T(8,128)(2,1)} %rows_hbm.1), channel_id=1, source_target_pairs={{0,2},{1,3},{2,0},{3,1},{4,6},{5,7},{6,4},{7,5},{8,10},{9,11},{10,... | collective-permute-start | bytes 1572872 | tf_op jit(solution)/shard_map/ppermute | solution.py:461
  3.5 2.9 %copy-start = (s32[4,128]{1,0:T(4,128)S(1)}, s32[4,128]{1,0:T(4,128)}, u32[]{:S(2)}) copy-start(s32[4,128]{1,0:T(4,128)} %pattern.3) | copy-start | bytes 6148
  6.4 5.3 %copy-start.1 = (s32[8]{0:T(128)S(1)}, s32[8]{0:T(128)}, u32[]{:S(2)}) copy-start(s32[8]{0:T(128)} %param.13) | copy-start | bytes 100
  7.3 6.8 %collective-permute-start.1 = (bf16[2,4,32,128]{3,2,1,0:T(8,128)(2,1)S(1)}, bf16[2,4,32,128]{3,2,1,0:T(8,128)(2,1)S(1)}, u32[]{:S(2)}, u32[]{:S(2)}) collective-permute-start(bf16[2,4,32,128]{3,2,1,0:T(8,128)(2,1)S(1)} %get-tuple-element.53), channel_id=1, source_target_pairs={{0,16},{4,20},{8,24},{12,28},{16,0},{20,4},{24,8},{28,12},{1,17},{... | collective-permute-start | bytes 196616 | tf_op jit(solution)/shard_map/ppermute | solution.py:461
  10.1 6.4 %collective-permute-start.2 = (bf16[2,4,32,128]{3,2,1,0:T(8,128)(2,1)S(1)}, bf16[2,4,32,128]{3,2,1,0:T(8,128)(2,1)S(1)}, u32[]{:S(2)}, u32[]{:S(2)}) collective-permute-start(bf16[2,4,32,128]{3,2,1,0:T(8,128)(2,1)S(1)} %get-tuple-element.53), channel_id=1, source_target_pairs={{0,24},{4,28},{8,16},{12,20},{16,8},{20,12},{24,0},{28,4},{1,25},{... | collective-permute-start | bytes 196616 | tf_op jit(solution)/shard_map/ppermute | solution.py:461
  11.4 5.2 %collective-permute-start.3 = (bf16[2,4,32,128]{3,2,1,0:T(8,128)(2,1)S(1)}, bf16[2,4,32,128]{3,2,1,0:T(8,128)(2,1)S(1)}, u32[]{:S(2)}, u32[]{:S(2)}) collective-permute-start(bf16[2,4,32,128]{3,2,1,0:T(8,128)(2,1)S(1)} %get-tuple-element.53), channel_id=1, source_target_pairs={{0,8},{4,12},{8,0},{12,4},{16,24},{20,28},{24,16},{28,20},{1,9},{5... | collective-permute-start | bytes 196616 | tf_op jit(solution)/shard_map/ppermute | solution.py:461
  16.7 2.6 %collective-permute-start.6 = (bf16[128,2048]{1,0:T(8,128)(2,1)S(1)}, bf16[128,2048]{1,0:T(8,128)(2,1)S(1)}, u32[]{:S(2)}, u32[]{:S(2)}) collective-permute-start(bf16[128,2048]{1,0:T(8,128)(2,1)S(1)} %collective-permute-done.4.rows.rows_0), channel_id=1, source_target_pairs={{0,1},{1,0},{2,3},{3,2},{4,5},{5,4},{6,7},{7,6},{8,9},{9,8},{10,11... | collective-permute-start | bytes 1572872 | tf_op jit(solution)/shard_map/ppermute | solution.py:461
  16.7 10.5 %collective-permute-start.11 = (bf16[4,2,4,32,128]{4,3,2,1,0:T(8,128)(2,1)S(1)}, bf16[4,2,4,32,128]{4,3,2,1,0:T(8,128)(2,1)S(1)}, u32[]{:S(2)}, u32[]{:S(2)}) collective-permute-start(bf16[4,2,4,32,128]{4,3,2,1,0:T(8,128)(2,1)S(1)} %pad_maximum_fusion.refs_9_), channel_id=1, source_target_pairs={{0,4},{4,0},{8,12},{12,8},{16,20},{20,16},{24,28},{28,24},{1,5},{5... | collective-permute-start | bytes 786440 | tf_op jit(solution)/shard_map/ppermute | solution.py:461
  20.1 7.9 %collective-permute-start.7 = (bf16[2,4,32,128]{3,2,1,0:T(8,128)(2,1)S(1)}, bf16[2,4,32,128]{3,2,1,0:T(8,128)(2,1)S(1)}, u32[]{:S(2)}, u32[]{:S(2)}) collective-permute-start(bf16[2,4,32,128]{3,2,1,0:T(8,128)(2,1)S(1)} %get-tuple-element.67.kept), channel_id=1, source_target_pairs={{0,16},{4,20},{8,24},{12,28},{16,0},{20,4},{24,8},{28,12},{1,17},{... | collective-permute-start | bytes 196616 | tf_op jit(solution)/shard_map/ppermute | solution.py:461
  22.8 6.5 %collective-permute-start.8 = (bf16[2,4,32,128]{3,2,1,0:T(8,128)(2,1)S(1)}, bf16[2,4,32,128]{3,2,1,0:T(8,128)(2,1)S(1)}, u32[]{:S(2)}, u32[]{:S(2)}) collective-permute-start(bf16[2,4,32,128]{3,2,1,0:T(8,128)(2,1)S(1)} %get-tuple-element.67.kept), channel_id=1, source_target_pairs={{0,24},{4,28},{8,16},{12,20},{16,8},{20,12},{24,0},{28,4},{1,25},{... | collective-permute-start | bytes 196616 | tf_op jit(solution)/shard_map/ppermute | solution.py:461
  23.4 6.1 %collective-permute-start.9 = (bf16[2,4,32,128]{3,2,1,0:T(8,128)(2,1)S(1)}, bf16[2,4,32,128]{3,2,1,0:T(8,128)(2,1)S(1)}, u32[]{:S(2)}, u32[]{:S(2)}) collective-permute-start(bf16[2,4,32,128]{3,2,1,0:T(8,128)(2,1)S(1)} %get-tuple-element.67.kept), channel_id=1, source_target_pairs={{0,8},{4,12},{8,0},{12,4},{16,24},{20,28},{24,16},{28,20},{1,9},{5... | collective-permute-start | bytes 196616 | tf_op jit(solution)/shard_map/ppermute | solution.py:461
  26.2 4.3 %collective-permute-start.10 = (bf16[2,4,32,128]{3,2,1,0:T(8,128)(2,1)S(1)}, bf16[2,4,32,128]{3,2,1,0:T(8,128)(2,1)S(1)}, u32[]{:S(2)}, u32[]{:S(2)}) collective-permute-start(bf16[2,4,32,128]{3,2,1,0:T(8,128)(2,1)S(1)} %get-tuple-element.68), channel_id=1, source_target_pairs={{0,4},{4,0},{8,12},{12,8},{16,20},{20,16},{24,28},{28,24},{1,5},{5... | collective-permute-start | bytes 196616 | tf_op jit(solution)/shard_map/ppermute | solution.py:461
  30.5 5.7 %collective-permute-start.12 = (bf16[3,2,4,32,128]{4,3,2,1,0:T(8,128)(2,1)S(1)}, bf16[3,2,4,32,128]{4,3,2,1,0:T(8,128)(2,1)S(1)}, u32[]{:S(2)}, u32[]{:S(2)}) collective-permute-start(bf16[3,2,4,32,128]{4,3,2,1,0:T(8,128)(2,1)S(1)} %pad_maximum_fusion.1.refs_4_.refs_12_), channel_id=1, source_target_pairs={{0,4},{4,0},{8,12},{12,8},{16,20},{20,16},{24,28},{28,24},{1,5},{5... | collective-permute-start | bytes 589832 | tf_op jit(solution)/shard_map/ppermute | solution.py:461
  37.0 1.4 %collective-permute-start.13 = (bf16[128,512]{1,0:T(8,128)(2,1)S(1)}, bf16[128,512]{1,0:T(8,128)(2,1)S(1)}, u32[]{:S(2)}, u32[]{:S(2)}) collective-permute-start(bf16[128,512]{1,0:T(8,128)(2,1)S(1)} %get-tuple-element.88), channel_id=1, source_target_pairs={{0,1},{1,0},{2,3},{3,2},{4,5},{5,4},{6,7},{7,6},{8,9},{9,8},{10,11... | collective-permute-start | bytes 393224 | tf_op jit(solution)/shard_map/ppermute | solution.py:461
  39.2 14.0 %collective-permute-start.15 = (bf16[128,2048]{1,0:T(8,128)(2,1)S(1)}, bf16[128,2048]{1,0:T(8,128)(2,1)S(1)}, u32[]{:S(2)}, u32[]{:S(2)}) collective-permute-start(bf16[128,2048]{1,0:T(8,128)(2,1)S(1)} %shard_map.82), channel_id=1, source_target_pairs={{0,2},{1,3},{2,0},{3,1},{4,6},{5,7},{6,4},{7,5},{8,10},{9,11},{10,... | collective-permute-start | bytes 1572872 | tf_op jit(solution)/shard_map/ppermute | solution.py:461
  42.8 1.4 %collective-permute-start.14 = (bf16[128,512]{1,0:T(8,128)(2,1)S(1)}, bf16[128,512]{1,0:T(8,128)(2,1)S(1)}, u32[]{:S(2)}, u32[]{:S(2)}) collective-permute-start(bf16[128,512]{1,0:T(8,128)(2,1)S(1)} %get-tuple-element.92), channel_id=1, source_target_pairs={{0,1},{1,0},{2,3},{3,2},{4,5},{5,4},{6,7},{7,6},{8,9},{9,8},{10,11... | collective-permute-start | bytes 393224 | tf_op jit(solution)/shard_map/ppermute | solution.py:461

commit v13 on v12

--- a/solution.py
+++ b/solution.py
@@ -144,55 +144,50 @@
     )(rows, wk, wv, keys_0, values_0, pattern)
 
 
-def query_kernel(rows_0, rows_1, wq_hbm, kept, queries, wq, passed, sems):
+def query_kernel(*refs):
+    rows, (wq_hbm, w_hbm), outs, (wq, sems) = refs[:4], refs[4:6], refs[6:9], refs[9:]
     copies = start_copies(wq_hbm, wq, sems, 0)
-    passed[...] = kept[...]
-    rows = jnp.concatenate([rows_0[...], rows_1[...]], axis=0)
+    more = start_copies(w_hbm, outs[2], sems, STREAMS)
     for copy in copies:
         copy.wait()
-    for part in halves_of(wq.shape[1]):
-        queries[:, part] = dot(rows, wq[:, part]).astype(BF16)
-
-
-def query(rows_0, rows_1, w_query, kept):
-    count, depth = rows_0.shape
+    for pair, out in ((rows[2:], outs[1]), (rows[:2], outs[0])):
+        both = jnp.concatenate([ref[...] for ref in pair], axis=0)
+        for part in halves_of(wq.shape[1]):
+            out[:, part] = dot(both, wq[:, part]).astype(BF16)
+    for copy in more:
+        copy.wait()
+
+
+def query(rows, w_query, w_out):
+    count, depth = rows[0].shape
     width = w_query.shape[1]
     return pl.pallas_call(
         query_kernel,
-        in_specs=[IN_VMEM] * 2 + [IN_HBM, IN_VMEM],
+        in_specs=[IN_VMEM] * 4 + [IN_HBM] * 2,
         out_specs=[IN_VMEM] * 3,
-        out_shape=[
-            shape((2 * count, width)),
+        out_shape=[shape((2 * count, width))] * 2 + [pltpu.VMEM(w_out.shape, BF16)],
+        scratch_shapes=[
             pltpu.VMEM(w_query.shape, BF16),
-            shape(kept.shape),
+            pltpu.SemaphoreType.DMA((2 * STREAMS,)),
         ],
-        scratch_shapes=[pltpu.SemaphoreType.DMA((STREAMS,))],
-        compiler_params=params(),
-        cost_estimate=cost(4 * count * depth * width, 2 * depth * width),
-    )(rows_0, rows_1, keep_in_hbm(w_query), kept)
-
-
-def last_query_kernel(rows_0, rows_1, wq, w_hbm, queries, w, sems):
-    copies = start_copies(w_hbm, w, sems, 0)
-    rows = jnp.concatenate([rows_0[...], rows_1[...]], axis=0)
-    for part in halves_of(wq.shape[1]):
-        queries[:, part] = dot(rows, wq[:, part]).astype(BF16)
-    for copy in copies:
-        copy.wait()
-
-
-def last_query(rows_0, rows_1, wq, w_out):
-    count, depth = rows_0.shape
-    width = wq.shape[1]
-    return pl.pallas_call(
-        last_query_kernel,
-        in_specs=[IN_VMEM] * 3 + [IN_HBM],
-        out_specs=[IN_VMEM] * 2,
-        out_shape=[shape((2 * count, width)), pltpu.VMEM(w_out.shape, BF16)],
-        scratch_shapes=[pltpu.SemaphoreType.DMA((STREAMS,))],
-        compiler_params=params(),
-        cost_estimate=cost(4 * count * depth * width, 2 * depth * width),
-    )(rows_0, rows_1, wq, keep_in_hbm(w_out))
+        compiler_params=params(),
+        cost_estimate=cost(8 * count * depth * width, 4 * depth * width),
+    )(*rows, keep_in_hbm(w_query), keep_in_hbm(w_out))
+
+
+def again_kernel(source, out):
+    out[...] = source[...]
+
+
+def again(kept):
+    return pl.pallas_call(
+        again_kernel,
+        in_specs=[IN_VMEM],
+        out_specs=IN_VMEM,
+        out_shape=shape(kept.shape),
+        compiler_params=params(),
+        cost_estimate=cost(0, 4 * kept.size),
+    )(kept)
 
 
 def across_kernel(rows, wk, wv, keys, values):
@@ -490,25 +485,21 @@
         beyond = after(beyond, half_a[1][0])
     keys_2, values_2 = keys_and_values(across, wk, wv)
     keys_3, values_3, kept_b = second(after(beyond, keys_2), wk, wv, keys_2, values_2, pattern)
-    query_b, wq, kept_again = query(across, beyond, w_query, kept_b)
     near = [keys_0, keys_1, keys_2, keys_3], [values_0, values_1, values_2, values_3]
     call = functools.partial(attend, masks, few)
     if few:
         along_z = first_round(kept_b)
-        along_y = swap(kept_again, Y_BIT, "seq")
-        *along_z, along_y, query_b, half_a[1][1] = lax.optimization_barrier(
-            (*along_z, along_y, query_b, half_a[1][1])
+        along_y = swap(again(kept_b), Y_BIT, "seq")
+        *along_z, along_y, half_a[1][1] = lax.optimization_barrier(
+            (*along_z, along_y, half_a[1][1])
         )
         column, other = second_round(along_z)
         half_b = 1, [kept_b[None], column, along_y[None], other]
-        asked = after(query_b, column)
         mine = after(mine, column)
-        begun = call(2 * BLOCK, asked, [half_a], near=near, finish=False)
     else:
         half_b = 1, [lax.all_gather(kept_b, "seq", axis=0)]
-        begun = call(2 * BLOCK, query_b, [half_a], near=near, finish=False)
-    query_a, wo = last_query(mine, beside, wq, w_out)
-    query_b = after(query_b, query_a)
+    query_a, query_b, wo = query([mine, beside, across, beyond], w_query, w_out)
+    begun = call(2 * BLOCK, query_b, [half_a], near=near, finish=False)
     keep_b, send_b = call(2 * BLOCK, query_b, [half_b], begun=begun)
     other_b = swap(send_b, 1)
     leaving = mix(keep_b, other_b, wo, wo_beside, BF16)

time: 54.3 us -> 53.5 us (0.985)
  Pallas kernels: 16.5 us -> 15.3 us
  waiting for transfers between devices: 19.3 us -> 19.9 us
    pallas_call x2, Pallas kernels: 4.07 us -> 2.91 us  [the longest x1 2.9 us: query(): pl.pallas_call(query_kernel, in_specs=[IN_VMEM] * 4 + [IN_HBM] * 2, out_s...]
    ppermute x16, waiting for transfers between devices: 19.3 us -> 19.9 us  [swap(): return lax.ppermute(array, axis, [(i, i ^ bit) for i in range(count)])]
  transfers between devices with their start and end apart: 16 -> 16, of which waited for: 11 -> 11; matrix products, arithmetic and copies ran while one was open for 0% -> 0% of each run, Pallas kernels for 28% -> 26%
where the time goes in v13:
time: 53.5 us; the launch traced here: 53.4 us
  waiting for transfers between devices  19.9 us (37%)
  starting transfers between devices  17 us (32%)
  Pallas kernels  15.3 us (29%)
  other arithmetic  1.04 us (2%)
    ppermute x16, waiting for transfers between devices, swap(): return lax.ppermute(array, axis, [(i, i ^ bit) for i in range(count)])  19.9 us
    ppermute x16, starting transfers between devices, swap(): return lax.ppermute(array, axis, [(i, i ^ bit) for i in range(count)])  17 us
    pallas_call x3, Pallas kernels, attend(): pl.pallas_call(functools.partial(attend_kernel, first_row, near is not No...  4.78 us
    pallas_call x1, Pallas kernels, first(): pl.pallas_call(first_kernel, in_specs=[IN_HBM] * 3, out_specs=[IN_VMEM] *...  2.92 us
    pallas_call x1, Pallas kernels, query(): pl.pallas_call(query_kernel, in_specs=[IN_VMEM] * 4 + [IN_HBM] * 2, out_s...  2.9 us
    pallas_call x2, Pallas kernels, second(): pl.pallas_call(second_kernel, in_specs=[IN_VMEM] * 6, out_specs=[IN_VMEM]...  1.81 us
    pallas_call x2, Pallas kernels, mix(): pl.pallas_call(mix_kernel, in_specs=[IN_VMEM] * 4, out_specs=IN_VMEM, out...  1.43 us
  transfers between devices with their start and end apart: 16, of which 11 were waited for; matrix products, arithmetic and copies ran while one was open for 0% of the time, Pallas kernels for 26%

profile of v13, /device:TPU:0, one launch (start us, length us, event | category | flops | bytes accessed | tf_op | source)
XLA Modules:
  0.0 53.4 jit_solution(1600503855891491586)
XLA Ops:
  0.0 0.5 collective-permute-start.5
  0.5 2.9 %collective-permute-start.4 = (bf16[128,2048]{1,0:T(8,128)(2,1)}, bf16[128,2048]{1,0:T(8,128)(2,1)S(1)}, u32[]{:S(2)}, u32[]{:S(2)}) collective-permute-start(bf16[128,2048]{1,0:T(8,128)(2,1)} %rows_hbm.1), channel_id=1, source_target_pairs={{0,2},{1,3},{2,0},{3,1},{4,6},{5,7},{6,4},{7,5},{8,10},{9,11},{10,... | collective-permute-start | bytes 1572872 | tf_op jit(solution)/shard_map/ppermute | solution.py:456
  3.5 2.9 %shard_map.73 = (bf16[128,2048]{1,0:T(8,128)(2,1)S(1)}, bf16[2048,512]{1,0:T(8,128)(2,1)S(1)}, bf16[2048,512]{1,0:T(8,128)(2,1)S(1)}, bf16[128,512]{1,0:T(8,128)(2,1)S(1)}, bf16[128,512]{1,0:T(8,128)(2,1)S(1)}) custom-call(bf16[128,2048]{1,0:T(8,128)(2,1)} %rows_hbm.1, bf16[2048,512]{1,0:T(8,128)(2,1)} %wk_hbm.1, bf16[2048,512]{1,0:T(8,128)(2,1)} %wv_hbm.1), custom_call_target="tpu_custom_call" | custom-call | flops 5368709 | bytes 41943 | tf_op jit(solution)/shard_map/pallas_call | solution.py:105
  6.4 0.9 %shard_map.74 = (bf16[128,512]{1,0:T(8,128)(2,1)S(1)}, bf16[128,512]{1,0:T(8,128)(2,1)S(1)}, bf16[2,4,32,128]{3,2,1,0:T(8,128)(2,1)S(1)}) custom-call(bf16[128,2048]{1,0:T(8,128)(2,1)S(1)} %collective-permute-done.rows.refs_1_, bf16[2048,512]{1,0:T(8,128)(2,1)S(1)} %get-tuple-element.44.wk, bf16[2048,512]{1,0:T(8,128)(2,1)S(1)} %get-tuple-element.45.wv, ...), custom_call_target="tpu_custom_call" | custom-call | flops 5368709 | bytes 5242 | tf_op jit(solution)/shard_map/pallas_call | solution.py:137
  7.3 2.8 %collective-permute-start.1 = (bf16[2,4,32,128]{3,2,1,0:T(8,128)(2,1)S(1)}, bf16[2,4,32,128]{3,2,1,0:T(8,128)(2,1)S(1)}, u32[]{:S(2)}, u32[]{:S(2)}) collective-permute-start(bf16[2,4,32,128]{3,2,1,0:T(8,128)(2,1)S(1)} %get-tuple-element.48), channel_id=1, source_target_pairs={{0,16},{4,20},{8,24},{12,28},{16,0},{20,4},{24,8},{28,12},{1,17},{... | collective-permute-start | bytes 196616 | tf_op jit(solution)/shard_map/ppermute | solution.py:456
  10.1 1.3 %collective-permute-start.2 = (bf16[2,4,32,128]{3,2,1,0:T(8,128)(2,1)S(1)}, bf16[2,4,32,128]{3,2,1,0:T(8,128)(2,1)S(1)}, u32[]{:S(2)}, u32[]{:S(2)}) collective-permute-start(bf16[2,4,32,128]{3,2,1,0:T(8,128)(2,1)S(1)} %get-tuple-element.48), channel_id=1, source_target_pairs={{0,24},{4,28},{8,16},{12,20},{16,8},{20,12},{24,0},{28,4},{1,25},{... | collective-permute-start | bytes 196616 | tf_op jit(solution)/shard_map/ppermute | solution.py:456
  11.7 0.7 %shard_map.75 = (bf16[512,128]{1,0:T(8,128)(2,1)S(1)}, bf16[1024,128]{1,0:T(8,128)(2,1)S(1)}) custom-call(s32[10]{0:T(128)S(1)} %pad_add_fusion.place), custom_call_target="tpu_custom_call" | custom-call | flops 83886 | bytes 2621 | tf_op jit(solution)/shard_map/pallas_call | solution.py:253
  12.4 1.6 %collective-permute-done.1 = bf16[2,4,32,128]{3,2,1,0:T(8,128)(2,1)S(1)} collective-permute-done((bf16[2,4,32,128]{3,2,1,0:T(8,128)(2,1)S(1)}, bf16[2,4,32,128]{3,2,1,0:T(8,128)(2,1)S(1)}, u32[]{:S(2)}, u32[]{:S(2)}) %collective-permute-start.1) | collective-permute-done | bytes 65568 | tf_op jit(solution)/shard_map/ppermute | solution.py:456
  14.1 2.4 %collective-permute-done.2 = bf16[2,4,32,128]{3,2,1,0:T(8,128)(2,1)S(1)} collective-permute-done((bf16[2,4,32,128]{3,2,1,0:T(8,128)(2,1)S(1)}, bf16[2,4,32,128]{3,2,1,0:T(8,128)(2,1)S(1)}, u32[]{:S(2)}, u32[]{:S(2)}) %collective-permute-start.2) | collective-permute-done | bytes 65568 | tf_op jit(solution)/shard_map/ppermute | solution.py:456
  16.7 1.7 %collective-permute-start.11 = (bf16[4,2,4,32,128]{4,3,2,1,0:T(8,128)(2,1)S(1)}, bf16[4,2,4,32,128]{4,3,2,1,0:T(8,128)(2,1)S(1)}, u32[]{:S(2)}, u32[]{:S(2)}) collective-permute-start(bf16[4,2,4,32,128]{4,3,2,1,0:T(8,128)(2,1)S(1)} %pad_maximum_fusion.refs_9_), channel_id=1, source_target_pairs={{0,4},{4,0},{8,12},{12,8},{16,20},{20,16},{24,28},{28,24},{1,5},{5... | collective-permute-start | bytes 786440 | tf_op jit(solution)/shard_map/ppermute | solution.py:456
  18.4 0.8 %shard_map.76 = (bf16[128,512]{1,0:T(8,128)(2,1)S(1)}, bf16[128,512]{1,0:T(8,128)(2,1)S(1)}) custom-call(bf16[128,2048]{1,0:T(8,128)(2,1)S(1)} %collective-permute-done.4.rows.refs_2_, bf16[2048,512]{1,0:T(8,128)(2,1)S(1)} %get-tuple-element.44.wk, bf16[2048,512]{1,0:T(8,128)(2,1)S(1)} %get-tuple-element.45.wv), custom_call_target="tpu_custom_call" | custom-call | flops 5368709 | bytes 5242 | tf_op jit(solution)/shard_map/pallas_call | solution.py:202
  19.2 0.9 %shard_map.77 = (bf16[128,512]{1,0:T(8,128)(2,1)S(1)}, bf16[128,512]{1,0:T(8,128)(2,1)S(1)}, bf16[2,4,32,128]{3,2,1,0:T(8,128)(2,1)S(1)}) custom-call(bf16[128,2048]{1,0:T(8,128)(2,1)S(1)} %collective-permute-done.6.rows.refs_3_, bf16[2048,512]{1,0:T(8,128)(2,1)S(1)} %get-tuple-element.44.wk, bf16[2048,512]{1,0:T(8,128)(2,1)S(1)} %get-tuple-element.45.wv, ...), custom_call_target="tpu_custom_call" | custom-call | flops 5368709 | bytes 5242 | tf_op jit(solution)/shard_map/pallas_call | solution.py:137
  20.1 2.7 %collective-permute-start.7 = (bf16[2,4,32,128]{3,2,1,0:T(8,128)(2,1)S(1)}, bf16[2,4,32,128]{3,2,1,0:T(8,128)(2,1)S(1)}, u32[]{:S(2)}, u32[]{:S(2)}) collective-permute-start(bf16[2,4,32,128]{3,2,1,0:T(8,128)(2,1)S(1)} %get-tuple-element.62.source), channel_id=1, source_target_pairs={{0,16},{4,20},{8,24},{12,28},{16,0},{20,4},{24,8},{28,12},{1,17},{... | collective-permute-start | bytes 196616 | tf_op jit(solution)/shard_map/ppermute | solution.py:456
  22.8 0.6 %collective-permute-start.8 = (bf16[2,4,32,128]{3,2,1,0:T(8,128)(2,1)S(1)}, bf16[2,4,32,128]{3,2,1,0:T(8,128)(2,1)S(1)}, u32[]{:S(2)}, u32[]{:S(2)}) collective-permute-start(bf16[2,4,32,128]{3,2,1,0:T(8,128)(2,1)S(1)} %get-tuple-element.62.source), channel_id=1, source_target_pairs={{0,24},{4,28},{8,16},{12,20},{16,8},{20,12},{24,0},{28,4},{1,25},{... | collective-permute-start | bytes 196616 | tf_op jit(solution)/shard_map/ppermute | solution.py:456
  23.4 0.5 collective-permute-start.9
  23.9 1.0 %collective-permute-start.10 = (bf16[2,4,32,128]{3,2,1,0:T(8,128)(2,1)S(1)}, bf16[2,4,32,128]{3,2,1,0:T(8,128)(2,1)S(1)}, u32[]{:S(2)}, u32[]{:S(2)}) collective-permute-start(bf16[2,4,32,128]{3,2,1,0:T(8,128)(2,1)S(1)} %shard_map.78), channel_id=1, source_target_pairs={{0,4},{4,0},{8,12},{12,8},{16,20},{20,16},{24,28},{28,24},{1,5},{5... | collective-permute-start | bytes 196616 | tf_op jit(solution)/shard_map/ppermute | solution.py:456
  24.9 0.6 %collective-permute-done.11.refs_10_ = bf16[4,2,4,32,128]{4,3,2,1,0:T(8,128)(2,1)S(1)} collective-permute-done((bf16[4,2,4,32,128]{4,3,2,1,0:T(8,128)(2,1)S(1)}, bf16[4,2,4,32,128]{4,3,2,1,0:T(8,128)(2,1)S(1)}, u32[]{:S(2)}, u32[]{:S(2)}) %collective-permute-start.11) | collective-permute-done | bytes 262176 | tf_op jit(solution)/shard_map/ppermute | solution.py:456
  25.5 2.5 %collective-permute-done.7 = bf16[2,4,32,128]{3,2,1,0:T(8,128)(2,1)S(1)} collective-permute-done((bf16[2,4,32,128]{3,2,1,0:T(8,128)(2,1)S(1)}, bf16[2,4,32,128]{3,2,1,0:T(8,128)(2,1)S(1)}, u32[]{:S(2)}, u32[]{:S(2)}) %collective-permute-start.7) | collective-permute-done | bytes 65568 | tf_op jit(solution)/shard_map/ppermute | solution.py:456
  28.0 1.3 %collective-permute-done.8 = bf16[2,4,32,128]{3,2,1,0:T(8,128)(2,1)S(1)} collective-permute-done((bf16[2,4,32,128]{3,2,1,0:T(8,128)(2,1)S(1)}, bf16[2,4,32,128]{3,2,1,0:T(8,128)(2,1)S(1)}, u32[]{:S(2)}, u32[]{:S(2)}) %collective-permute-start.8) | collective-permute-done | bytes 65568 | tf_op jit(solution)/shard_map/ppermute | solution.py:456
  29.5 1.0 %collective-permute-start.12 = (bf16[3,2,4,32,128]{4,3,2,1,0:T(8,128)(2,1)S(1)}, bf16[3,2,4,32,128]{4,3,2,1,0:T(8,128)(2,1)S(1)}, u32[]{:S(2)}, u32[]{:S(2)}) collective-permute-start(bf16[3,2,4,32,128]{4,3,2,1,0:T(8,128)(2,1)S(1)} %pad_maximum_fusion.1.refs_4_.refs_12_), channel_id=1, source_target_pairs={{0,4},{4,0},{8,12},{12,8},{16,20},{20,16},{24,28},{28,24},{1,5},{5... | collective-permute-start | bytes 589832 | tf_op jit(solution)/shard_map/ppermute | solution.py:456
  30.5 2.9 %shard_map.79 = (bf16[256,512]{1,0:T(8,128)(2,1)S(1)}, bf16[256,512]{1,0:T(8,128)(2,1)S(1)}, bf16[512,2048]{1,0:T(8,128)(2,1)S(1)}) custom-call(bf16[128,2048]{1,0:T(8,128)(2,1)S(1)} %get-tuple-element.66.refs_0_, bf16[128,2048]{1,0:T(8,128)(2,1)S(1)} %collective-permute-done.rows.refs_1_, bf16[128,2048]{1,0:T(8,128)(2,1)S(1)} %collective-permute-done.4.rows.refs_2_, ...), custom_call_target="tpu_custom_call" | custom-call | flops 10737418 | bytes 41943 | tf_op jit(solution)/shard_map/pallas_call | solution.py:164
  33.4 1.9 %shard_map.80 = (f32[4,128,256]{2,1,0:T(8,128)S(1)}, f32[4,8,256]{2,1,0:T(8,128)S(1)}) custom-call(bf16[512,128]{1,0:T(8,128)(2,1)S(1)} %get-tuple-element.51.asking, bf16[1024,128]{1,0:T(8,128)(2,1)S(1)} %get-tuple-element.52.asked_of, bf16[256,512]{1,0:T(8,128)(2,1)S(1)} %get-tuple-element.68.refs_0_, ...), custom_call_target="tpu_custom_call" | custom-call | flops 4026531 | bytes 5242 | tf_op jit(solution)/shard_map/pallas_call | solution.py:409
  35.3 0.3 collective-permute-done.12.refs_6_.refs_14_
  35.6 0.8 %shard_map.81 = (bf16[128,512]{1,0:T(8,128)(2,1)S(1)}, bf16[128,512]{1,0:T(8,128)(2,1)S(1)}) custom-call(bf16[512,128]{1,0:T(8,128)(2,1)S(1)} %get-tuple-element.51.asking, bf16[1024,128]{1,0:T(8,128)(2,1)S(1)} %get-tuple-element.52.asked_of, bf16[256,512]{1,0:T(8,128)(2,1)S(1)} %get-tuple-element.68.refs_0_, f32[4,128,256]{2,1,0:T(8,128)S(1)} %get-tuple-element.74.refs_1_, ...), custom_call_target="tpu_custom_call" | custom-call | flops 1342177 | bytes 5242 | tf_op jit(solution)/shard_map/pallas_call | solution.py:409
  36.4 1.3 %collective-permute-done.13.rows_1 = bf16[128,512]{1,0:T(8,128)(2,1)S(1)} collective-permute-done((bf16[128,512]{1,0:T(8,128)(2,1)S(1)}, bf16[128,512]{1,0:T(8,128)(2,1)S(1)}, u32[]{:S(2)}, u32[]{:S(2)}) %collective-permute-start.13) | collective-permute-done | bytes 131104 | tf_op jit(solution)/shard_map/ppermute | solution.py:456
  37.7 0.7 %shard_map.82 = bf16[128,2048]{1,0:T(8,128)(2,1)S(1)} custom-call(bf16[128,512]{1,0:T(8,128)(2,1)S(1)} %get-tuple-element.77.rows_0, bf16[128,512]{1,0:T(8,128)(2,1)S(1)} %collective-permute-done.13.rows_1, bf16[512,2048]{1,0:T(8,128)(2,1)S(1)} %get-tuple-element.79.weight_0, bf16[512,2048]{1,0:T(8,128)(2,1)S(1)} %collective-permute-done.5.weight_1), custom_call_target="tpu_custom_call" | custom-call | flops 5368709 | bytes 10485 | tf_op jit(solution)/shard_map/pallas_call | solution.py:439
  38.5 1.6 %collective-permute-start.15 = (bf16[128,2048]{1,0:T(8,128)(2,1)S(1)}, bf16[128,2048]{1,0:T(8,128)(2,1)S(1)}, u32[]{:S(2)}, u32[]{:S(2)}) collective-permute-start(bf16[128,2048]{1,0:T(8,128)(2,1)S(1)} %shard_map.82), channel_id=1, source_target_pairs={{0,2},{1,3},{2,0},{3,1},{4,6},{5,7},{6,4},{7,5},{8,10},{9,11},{10,... | collective-permute-start | bytes 1572872 | tf_op jit(solution)/shard_map/ppermute | solution.py:456
  40.0 2.1 %shard_map.83 = (bf16[128,512]{1,0:T(8,128)(2,1)S(1)}, bf16[128,512]{1,0:T(8,128)(2,1)S(1)}) custom-call(bf16[512,128]{1,0:T(8,128)(2,1)S(1)} %get-tuple-element.51.asking, bf16[1024,128]{1,0:T(8,128)(2,1)S(1)} %get-tuple-element.52.asked_of, bf16[256,512]{1,0:T(8,128)(2,1)S(1)} %get-tuple-element.80.refs_0_, ...), custom_call_target="tpu_custom_call" | custom-call | flops 5368709 | bytes 5242 | tf_op jit(solution)/shard_map/pallas_call | solution.py:409
  42.2 1.3 %collective-permute-done.14.rows_1 = bf16[128,512]{1,0:T(8,128)(2,1)S(1)} collective-permute-done((bf16[128,512]{1,0:T(8,128)(2,1)S(1)}, bf16[128,512]{1,0:T(8,128)(2,1)S(1)}, u32[]{:S(2)}, u32[]{:S(2)}) %collective-permute-start.14) | collective-permute-done | bytes 131104 | tf_op jit(solution)/shard_map/ppermute | solution.py:456
  43.6 0.7 %shard_map.84 = f32[128,2048]{1,0:T(8,128)S(1)} custom-call(bf16[128,512]{1,0:T(8,128)(2,1)S(1)} %get-tuple-element.81.rows_0, bf16[128,512]{1,0:T(8,128)(2,1)S(1)} %collective-permute-done.14.rows_1, bf16[512,2048]{1,0:T(8,128)(2,1)S(1)} %get-tuple-element.79.weight_0, bf16[512,2048]{1,0:T(8,128)(2,1)S(1)} %collective-permute-done.5.weight_1), custom_call_target="tpu_custom_call" | custom-call | flops 5368709 | bytes 10485 | tf_op jit(solution)/shard_map/pallas_call | solution.py:439
  44.3 8.2 %collective-permute-done.15 = bf16[128,2048]{1,0:T(8,128)(2,1)S(1)} collective-permute-done((bf16[128,2048]{1,0:T(8,128)(2,1)S(1)}, bf16[128,2048]{1,0:T(8,128)(2,1)S(1)}, u32[]{:S(2)}, u32[]{:S(2)}) %collective-permute-start.15) | collective-permute-done | bytes 524320 | tf_op jit(solution)/shard_map/ppermute | solution.py:456
  52.5 0.9 %add_convert_fusion = bf16[128,2048]{1,0:T(8,128)(2,1)} fusion(f32[128,2048]{1,0:T(8,128)S(1)} %shard_map.84, bf16[128,2048]{1,0:T(8,128)(2,1)S(1)} %collective-permute-done.15), kind=kLoop, calls=%fused_computation | loop fusion | flops 786432 | bytes 2097152 | tf_op jit(solution)/shard_map/convert_element_type | solution.py:511
  (20 shorter events, 1.0 us)
Async XLA Ops:
  0.0 16.7 %collective-permute-start.5 = (bf16[512,2048]{1,0:T(8,128)(2,1)}, bf16[512,2048]{1,0:T(8,128)(2,1)S(1)}, u32[]{:S(2)}, u32[]{:S(2)}) collective-permute-start(bf16[512,2048]{1,0:T(8,128)(2,1)} %refs_5_.1), channel_id=1, source_target_pairs={{0,1},{1,0},{2,3},{3,2},{4,5},{5,4},{6,7},{7,6},{8,9},{9,8},{10,11... | collective-permute-start | bytes 6291464 | tf_op jit(solution)/shard_map/ppermute | solution.py:456
  0.5 5.9 %collective-permute-start = (bf16[128,2048]{1,0:T(8,128)(2,1)}, bf16[128,2048]{1,0:T(8,128)(2,1)S(1)}, u32[]{:S(2)}, u32[]{:S(2)}) collective-permute-start(bf16[128,2048]{1,0:T(8,128)(2,1)} %rows_hbm.1), channel_id=1, source_target_pairs={{0,1},{1,0},{2,3},{3,2},{4,5},{5,4},{6,7},{7,6},{8,9},{9,8},{10,11... | collective-permute-start | bytes 1572872 | tf_op jit(solution)/shard_map/ppermute | solution.py:456
  0.5 16.1 %collective-permute-start.4 = (bf16[128,2048]{1,0:T(8,128)(2,1)}, bf16[128,2048]{1,0:T(8,128)(2,1)S(1)}, u32[]{:S(2)}, u32[]{:S(2)}) collective-permute-start(bf16[128,2048]{1,0:T(8,128)(2,1)} %rows_hbm.1), channel_id=1, source_target_pairs={{0,2},{1,3},{2,0},{3,1},{4,6},{5,7},{6,4},{7,5},{8,10},{9,11},{10,... | collective-permute-start | bytes 1572872 | tf_op jit(solution)/shard_map/ppermute | solution.py:456
  3.5 2.9 %copy-start = (s32[4,128]{1,0:T(4,128)S(1)}, s32[4,128]{1,0:T(4,128)}, u32[]{:S(2)}) copy-start(s32[4,128]{1,0:T(4,128)} %pattern.3) | copy-start | bytes 6148
  6.4 5.3 %copy-start.1 = (s32[8]{0:T(128)S(1)}, s32[8]{0:T(128)}, u32[]{:S(2)}) copy-start(s32[8]{0:T(128)} %param.13) | copy-start | bytes 100
  7.3 6.8 %collective-permute-start.1 = (bf16[2,4,32,128]{3,2,1,0:T(8,128)(2,1)S(1)}, bf16[2,4,32,128]{3,2,1,0:T(8,128)(2,1)S(1)}, u32[]{:S(2)}, u32[]{:S(2)}) collective-permute-start(bf16[2,4,32,128]{3,2,1,0:T(8,128)(2,1)S(1)} %get-tuple-element.48), channel_id=1, source_target_pairs={{0,16},{4,20},{8,24},{12,28},{16,0},{20,4},{24,8},{28,12},{1,17},{... | collective-permute-start | bytes 196616 | tf_op jit(solution)/shard_map/ppermute | solution.py:456
  10.1 6.4 %collective-permute-start.2 = (bf16[2,4,32,128]{3,2,1,0:T(8,128)(2,1)S(1)}, bf16[2,4,32,128]{3,2,1,0:T(8,128)(2,1)S(1)}, u32[]{:S(2)}, u32[]{:S(2)}) collective-permute-start(bf16[2,4,32,128]{3,2,1,0:T(8,128)(2,1)S(1)} %get-tuple-element.48), channel_id=1, source_target_pairs={{0,24},{4,28},{8,16},{12,20},{16,8},{20,12},{24,0},{28,4},{1,25},{... | collective-permute-start | bytes 196616 | tf_op jit(solution)/shard_map/ppermute | solution.py:456
  11.4 5.2 %collective-permute-start.3 = (bf16[2,4,32,128]{3,2,1,0:T(8,128)(2,1)S(1)}, bf16[2,4,32,128]{3,2,1,0:T(8,128)(2,1)S(1)}, u32[]{:S(2)}, u32[]{:S(2)}) collective-permute-start(bf16[2,4,32,128]{3,2,1,0:T(8,128)(2,1)S(1)} %get-tuple-element.48), channel_id=1, source_target_pairs={{0,8},{4,12},{8,0},{12,4},{16,24},{20,28},{24,16},{28,20},{1,9},{5... | collective-permute-start | bytes 196616 | tf_op jit(solution)/shard_map/ppermute | solution.py:456
  16.7 2.6 %collective-permute-start.6 = (bf16[128,2048]{1,0:T(8,128)(2,1)S(1)}, bf16[128,2048]{1,0:T(8,128)(2,1)S(1)}, u32[]{:S(2)}, u32[]{:S(2)}) collective-permute-start(bf16[128,2048]{1,0:T(8,128)(2,1)S(1)} %collective-permute-done.4.rows.refs_2_), channel_id=1, source_target_pairs={{0,1},{1,0},{2,3},{3,2},{4,5},{5,4},{6,7},{7,6},{8,9},{9,8},{10,11... | collective-permute-start | bytes 1572872 | tf_op jit(solution)/shard_map/ppermute | solution.py:456
  16.7 8.8 %collective-permute-start.11 = (bf16[4,2,4,32,128]{4,3,2,1,0:T(8,128)(2,1)S(1)}, bf16[4,2,4,32,128]{4,3,2,1,0:T(8,128)(2,1)S(1)}, u32[]{:S(2)}, u32[]{:S(2)}) collective-permute-start(bf16[4,2,4,32,128]{4,3,2,1,0:T(8,128)(2,1)S(1)} %pad_maximum_fusion.refs_9_), channel_id=1, source_target_pairs={{0,4},{4,0},{8,12},{12,8},{16,20},{20,16},{24,28},{28,24},{1,5},{5... | collective-permute-start | bytes 786440 | tf_op jit(solution)/shard_map/ppermute | solution.py:456
  20.1 7.9 %collective-permute-start.7 = (bf16[2,4,32,128]{3,2,1,0:T(8,128)(2,1)S(1)}, bf16[2,4,32,128]{3,2,1,0:T(8,128)(2,1)S(1)}, u32[]{:S(2)}, u32[]{:S(2)}) collective-permute-start(bf16[2,4,32,128]{3,2,1,0:T(8,128)(2,1)S(1)} %get-tuple-element.62.source), channel_id=1, source_target_pairs={{0,16},{4,20},{8,24},{12,28},{16,0},{20,4},{24,8},{28,12},{1,17},{... | collective-permute-start | bytes 196616 | tf_op jit(solution)/shard_map/ppermute | solution.py:456
  22.8 6.5 %collective-permute-start.8 = (bf16[2,4,32,128]{3,2,1,0:T(8,128)(2,1)S(1)}, bf16[2,4,32,128]{3,2,1,0:T(8,128)(2,1)S(1)}, u32[]{:S(2)}, u32[]{:S(2)}) collective-permute-start(bf16[2,4,32,128]{3,2,1,0:T(8,128)(2,1)S(1)} %get-tuple-element.62.source), channel_id=1, source_target_pairs={{0,24},{4,28},{8,16},{12,20},{16,8},{20,12},{24,0},{28,4},{1,25},{... | collective-permute-start | bytes 196616 | tf_op jit(solution)/shard_map/ppermute | solution.py:456
  23.4 6.1 %collective-permute-start.9 = (bf16[2,4,32,128]{3,2,1,0:T(8,128)(2,1)S(1)}, bf16[2,4,32,128]{3,2,1,0:T(8,128)(2,1)S(1)}, u32[]{:S(2)}, u32[]{:S(2)}) collective-permute-start(bf16[2,4,32,128]{3,2,1,0:T(8,128)(2,1)S(1)} %get-tuple-element.62.source), channel_id=1, source_target_pairs={{0,8},{4,12},{8,0},{12,4},{16,24},{20,28},{24,16},{28,20},{1,9},{5... | collective-permute-start | bytes 196616 | tf_op jit(solution)/shard_map/ppermute | solution.py:456
  23.9 5.6 %collective-permute-start.10 = (bf16[2,4,32,128]{3,2,1,0:T(8,128)(2,1)S(1)}, bf16[2,4,32,128]{3,2,1,0:T(8,128)(2,1)S(1)}, u32[]{:S(2)}, u32[]{:S(2)}) collective-permute-start(bf16[2,4,32,128]{3,2,1,0:T(8,128)(2,1)S(1)} %shard_map.78), channel_id=1, source_target_pairs={{0,4},{4,0},{8,12},{12,8},{16,20},{20,16},{24,28},{28,24},{1,5},{5... | collective-permute-start | bytes 196616 | tf_op jit(solution)/shard_map/ppermute | solution.py:456
  29.5 6.1 %collective-permute-start.12 = (bf16[3,2,4,32,128]{4,3,2,1,0:T(8,128)(2,1)S(1)}, bf16[3,2,4,32,128]{4,3,2,1,0:T(8,128)(2,1)S(1)}, u32[]{:S(2)}, u32[]{:S(2)}) collective-permute-start(bf16[3,2,4,32,128]{4,3,2,1,0:T(8,128)(2,1)S(1)} %pad_maximum_fusion.1.refs_4_.refs_12_), channel_id=1, source_target_pairs={{0,4},{4,0},{8,12},{12,8},{16,20},{20,16},{24,28},{28,24},{1,5},{5... | collective-permute-start | bytes 589832 | tf_op jit(solution)/shard_map/ppermute | solution.py:456
  36.3 1.4 %collective-permute-start.13 = (bf16[128,512]{1,0:T(8,128)(2,1)S(1)}, bf16[128,512]{1,0:T(8,128)(2,1)S(1)}, u32[]{:S(2)}, u32[]{:S(2)}) collective-permute-start(bf16[128,512]{1,0:T(8,128)(2,1)S(1)} %get-tuple-element.78), channel_id=1, source_target_pairs={{0,1},{1,0},{2,3},{3,2},{4,5},{5,4},{6,7},{7,6},{8,9},{9,8},{10,11... | collective-permute-start | bytes 393224 | tf_op jit(solution)/shard_map/ppermute | solution.py:456
  38.5 14.0 %collective-permute-start.15 = (bf16[128,2048]{1,0:T(8,128)(2,1)S(1)}, bf16[128,2048]{1,0:T(8,128)(2,1)S(1)}, u32[]{:S(2)}, u32[]{:S(2)}) collective-permute-start(bf16[128,2048]{1,0:T(8,128)(2,1)S(1)} %shard_map.82), channel_id=1, source_target_pairs={{0,2},{1,3},{2,0},{3,1},{4,6},{5,7},{6,4},{7,5},{8,10},{9,11},{10,... | collective-permute-start | bytes 1572872 | tf_op jit(solution)/shard_map/ppermute | solution.py:456
  42.2 1.4 %collective-permute-start.14 = (bf16[128,512]{1,0:T(8,128)(2,1)S(1)}, bf16[128,512]{1,0:T(8,128)(2,1)S(1)}, u32[]{:S(2)}, u32[]{:S(2)}) collective-permute-start(bf16[128,512]{1,0:T(8,128)(2,1)S(1)} %get-tuple-element.82), channel_id=1, source_target_pairs={{0,1},{1,0},{2,3},{3,2},{4,5},{5,4},{6,7},{7,6},{8,9},{9,8},{10,11... | collective-permute-start | bytes 393224 | tf_op jit(solution)/shard_map/ppermute | solution.py:456

commit v14 on v13

--- a/solution.py
+++ b/solution.py
@@ -485,21 +485,23 @@
         beyond = after(beyond, half_a[1][0])
     keys_2, values_2 = keys_and_values(across, wk, wv)
     keys_3, values_3, kept_b = second(after(beyond, keys_2), wk, wv, keys_2, values_2, pattern)
+    sent_later = again(kept_b)
+    query_a, query_b, wo = query([after(mine, sent_later), beside, across, beyond], w_query, w_out)
     near = [keys_0, keys_1, keys_2, keys_3], [values_0, values_1, values_2, values_3]
     call = functools.partial(attend, masks, few)
     if few:
         along_z = first_round(kept_b)
-        along_y = swap(again(kept_b), Y_BIT, "seq")
-        *along_z, along_y, half_a[1][1] = lax.optimization_barrier(
-            (*along_z, along_y, half_a[1][1])
+        along_y = swap(sent_later, Y_BIT, "seq")
+        *along_z, along_y, query_b, half_a[1][1] = lax.optimization_barrier(
+            (*along_z, along_y, query_b, half_a[1][1])
         )
         column, other = second_round(along_z)
         half_b = 1, [kept_b[None], column, along_y[None], other]
-        mine = after(mine, column)
+        asked = after(query_b, column)
     else:
         half_b = 1, [lax.all_gather(kept_b, "seq", axis=0)]
-    query_a, query_b, wo = query([mine, beside, across, beyond], w_query, w_out)
-    begun = call(2 * BLOCK, query_b, [half_a], near=near, finish=False)
+        asked = query_b
+    begun = call(2 * BLOCK, asked, [half_a], near=near, finish=False)
     keep_b, send_b = call(2 * BLOCK, query_b, [half_b], begun=begun)
     other_b = swap(send_b, 1)
     leaving = mix(keep_b, other_b, wo, wo_beside, BF16)

time: 53.5 us -> 53.6 us (level)
  transfers between devices with their start and end apart: 16 -> 16, of which waited for: 11 -> 10; matrix products, arithmetic and copies ran while one was open for 0% -> 0% of each run, Pallas kernels for 26% -> 26%
where the time goes in v14:
time: 53.6 us; the launch traced here: 53.5 us
  waiting for transfers between devices  19.9 us (37%)
  starting transfers between devices  17 us (32%)
  Pallas kernels  15.3 us (29%)
  other arithmetic  1.04 us (2%)
    ppermute x16, waiting for transfers between devices, swap(): return lax.ppermute(array, axis, [(i, i ^ bit) for i in range(count)])  19.9 us
    ppermute x16, starting transfers between devices, swap(): return lax.ppermute(array, axis, [(i, i ^ bit) for i in range(count)])  17 us
    pallas_call x3, Pallas kernels, attend(): pl.pallas_call(functools.partial(attend_kernel, first_row, near is not No...  4.77 us
    pallas_call x1, Pallas kernels, first(): pl.pallas_call(first_kernel, in_specs=[IN_HBM] * 3, out_specs=[IN_VMEM] *...  2.92 us
    pallas_call x1, Pallas kernels, query(): pl.pallas_call(query_kernel, in_specs=[IN_VMEM] * 4 + [IN_HBM] * 2, out_s...  2.9 us
    pallas_call x2, Pallas kernels, second(): pl.pallas_call(second_kernel, in_specs=[IN_VMEM] * 6, out_specs=[IN_VMEM]...  1.81 us
    pallas_call x2, Pallas kernels, mix(): pl.pallas_call(mix_kernel, in_specs=[IN_VMEM] * 4, out_specs=IN_VMEM, out...  1.43 us
  transfers between devices with their start and end apart: 16, of which 10 were waited for; matrix products, arithmetic and copies ran while one was open for 0% of the time, Pallas kernels for 26%

profile of v14, /device:TPU:0, one launch (start us, length us, event | category | flops | bytes accessed | tf_op | source)
XLA Modules:
  0.0 53.5 jit_solution(11261032663951255157)
XLA Ops:
  0.0 0.5 collective-permute-start.5
  0.5 2.9 %collective-permute-start.4 = (bf16[128,2048]{1,0:T(8,128)(2,1)}, bf16[128,2048]{1,0:T(8,128)(2,1)S(1)}, u32[]{:S(2)}, u32[]{:S(2)}) collective-permute-start(bf16[128,2048]{1,0:T(8,128)(2,1)} %rows_hbm.1), channel_id=1, source_target_pairs={{0,2},{1,3},{2,0},{3,1},{4,6},{5,7},{6,4},{7,5},{8,10},{9,11},{10,... | collective-permute-start | bytes 1572872 | tf_op jit(solution)/shard_map/ppermute | solution.py:456
  3.5 2.9 %shard_map.73 = (bf16[128,2048]{1,0:T(8,128)(2,1)S(1)}, bf16[2048,512]{1,0:T(8,128)(2,1)S(1)}, bf16[2048,512]{1,0:T(8,128)(2,1)S(1)}, bf16[128,512]{1,0:T(8,128)(2,1)S(1)}, bf16[128,512]{1,0:T(8,128)(2,1)S(1)}) custom-call(bf16[128,2048]{1,0:T(8,128)(2,1)} %rows_hbm.1, bf16[2048,512]{1,0:T(8,128)(2,1)} %wk_hbm.1, bf16[2048,512]{1,0:T(8,128)(2,1)} %wv_hbm.1), custom_call_target="tpu_custom_call" | custom-call | flops 5368709 | bytes 41943 | tf_op jit(solution)/shard_map/pallas_call | solution.py:105
  6.4 0.9 %shard_map.74 = (bf16[128,512]{1,0:T(8,128)(2,1)S(1)}, bf16[128,512]{1,0:T(8,128)(2,1)S(1)}, bf16[2,4,32,128]{3,2,1,0:T(8,128)(2,1)S(1)}) custom-call(bf16[128,2048]{1,0:T(8,128)(2,1)S(1)} %collective-permute-done.rows.refs_1_, bf16[2048,512]{1,0:T(8,128)(2,1)S(1)} %get-tuple-element.46.wk, bf16[2048,512]{1,0:T(8,128)(2,1)S(1)} %get-tuple-element.47.wv, ...), custom_call_target="tpu_custom_call" | custom-call | flops 5368709 | bytes 5242 | tf_op jit(solution)/shard_map/pallas_call | solution.py:137
  7.3 2.8 %collective-permute-start.1 = (bf16[2,4,32,128]{3,2,1,0:T(8,128)(2,1)S(1)}, bf16[2,4,32,128]{3,2,1,0:T(8,128)(2,1)S(1)}, u32[]{:S(2)}, u32[]{:S(2)}) collective-permute-start(bf16[2,4,32,128]{3,2,1,0:T(8,128)(2,1)S(1)} %get-tuple-element.50), channel_id=1, source_target_pairs={{0,16},{4,20},{8,24},{12,28},{16,0},{20,4},{24,8},{28,12},{1,17},{... | collective-permute-start | bytes 196616 | tf_op jit(solution)/shard_map/ppermute | solution.py:456
  10.1 1.3 %collective-permute-start.2 = (bf16[2,4,32,128]{3,2,1,0:T(8,128)(2,1)S(1)}, bf16[2,4,32,128]{3,2,1,0:T(8,128)(2,1)S(1)}, u32[]{:S(2)}, u32[]{:S(2)}) collective-permute-start(bf16[2,4,32,128]{3,2,1,0:T(8,128)(2,1)S(1)} %get-tuple-element.50), channel_id=1, source_target_pairs={{0,24},{4,28},{8,16},{12,20},{16,8},{20,12},{24,0},{28,4},{1,25},{... | collective-permute-start | bytes 196616 | tf_op jit(solution)/shard_map/ppermute | solution.py:456
  11.4 0.2 collective-permute-start.3
  11.7 0.7 %shard_map.75 = (bf16[512,128]{1,0:T(8,128)(2,1)S(1)}, bf16[1024,128]{1,0:T(8,128)(2,1)S(1)}) custom-call(s32[10]{0:T(128)S(1)} %pad_add_fusion.place), custom_call_target="tpu_custom_call" | custom-call | flops 83886 | bytes 2621 | tf_op jit(solution)/shard_map/pallas_call | solution.py:253
  12.4 1.6 %collective-permute-done.1 = bf16[2,4,32,128]{3,2,1,0:T(8,128)(2,1)S(1)} collective-permute-done((bf16[2,4,32,128]{3,2,1,0:T(8,128)(2,1)S(1)}, bf16[2,4,32,128]{3,2,1,0:T(8,128)(2,1)S(1)}, u32[]{:S(2)}, u32[]{:S(2)}) %collective-permute-start.1) | collective-permute-done | bytes 65568 | tf_op jit(solution)/shard_map/ppermute | solution.py:456
  14.1 2.4 %collective-permute-done.2 = bf16[2,4,32,128]{3,2,1,0:T(8,128)(2,1)S(1)} collective-permute-done((bf16[2,4,32,128]{3,2,1,0:T(8,128)(2,1)S(1)}, bf16[2,4,32,128]{3,2,1,0:T(8,128)(2,1)S(1)}, u32[]{:S(2)}, u32[]{:S(2)}) %collective-permute-start.2) | collective-permute-done | bytes 65568 | tf_op jit(solution)/shard_map/ppermute | solution.py:456
  16.7 1.7 %collective-permute-start.11 = (bf16[4,2,4,32,128]{4,3,2,1,0:T(8,128)(2,1)S(1)}, bf16[4,2,4,32,128]{4,3,2,1,0:T(8,128)(2,1)S(1)}, u32[]{:S(2)}, u32[]{:S(2)}) collective-permute-start(bf16[4,2,4,32,128]{4,3,2,1,0:T(8,128)(2,1)S(1)} %pad_maximum_fusion.refs_9_), channel_id=1, source_target_pairs={{0,4},{4,0},{8,12},{12,8},{16,20},{20,16},{24,28},{28,24},{1,5},{5... | collective-permute-start | bytes 786440 | tf_op jit(solution)/shard_map/ppermute | solution.py:456
  18.4 0.8 %shard_map.76 = (bf16[128,512]{1,0:T(8,128)(2,1)S(1)}, bf16[128,512]{1,0:T(8,128)(2,1)S(1)}) custom-call(bf16[128,2048]{1,0:T(8,128)(2,1)S(1)} %collective-permute-done.4.rows.refs_2_, bf16[2048,512]{1,0:T(8,128)(2,1)S(1)} %get-tuple-element.46.wk, bf16[2048,512]{1,0:T(8,128)(2,1)S(1)} %get-tuple-element.47.wv), custom_call_target="tpu_custom_call" | custom-call | flops 5368709 | bytes 5242 | tf_op jit(solution)/shard_map/pallas_call | solution.py:202
  19.2 0.9 %shard_map.77 = (bf16[128,512]{1,0:T(8,128)(2,1)S(1)}, bf16[128,512]{1,0:T(8,128)(2,1)S(1)}, bf16[2,4,32,128]{3,2,1,0:T(8,128)(2,1)S(1)}) custom-call(bf16[128,2048]{1,0:T(8,128)(2,1)S(1)} %collective-permute-done.6.rows.refs_3_, bf16[2048,512]{1,0:T(8,128)(2,1)S(1)} %get-tuple-element.46.wk, bf16[2048,512]{1,0:T(8,128)(2,1)S(1)} %get-tuple-element.47.wv, ...), custom_call_target="tpu_custom_call" | custom-call | flops 5368709 | bytes 5242 | tf_op jit(solution)/shard_map/pallas_call | solution.py:137
  20.1 2.7 %collective-permute-start.7 = (bf16[2,4,32,128]{3,2,1,0:T(8,128)(2,1)S(1)}, bf16[2,4,32,128]{3,2,1,0:T(8,128)(2,1)S(1)}, u32[]{:S(2)}, u32[]{:S(2)}) collective-permute-start(bf16[2,4,32,128]{3,2,1,0:T(8,128)(2,1)S(1)} %get-tuple-element.64.source), channel_id=1, source_target_pairs={{0,16},{4,20},{8,24},{12,28},{16,0},{20,4},{24,8},{28,12},{1,17},{... | collective-permute-start | bytes 196616 | tf_op jit(solution)/shard_map/ppermute | solution.py:456
  22.9 0.6 %collective-permute-start.8 = (bf16[2,4,32,128]{3,2,1,0:T(8,128)(2,1)S(1)}, bf16[2,4,32,128]{3,2,1,0:T(8,128)(2,1)S(1)}, u32[]{:S(2)}, u32[]{:S(2)}) collective-permute-start(bf16[2,4,32,128]{3,2,1,0:T(8,128)(2,1)S(1)} %get-tuple-element.64.source), channel_id=1, source_target_pairs={{0,24},{4,28},{8,16},{12,20},{16,8},{20,12},{24,0},{28,4},{1,25},{... | collective-permute-start | bytes 196616 | tf_op jit(solution)/shard_map/ppermute | solution.py:456
  23.4 0.5 collective-permute-start.9
  23.9 1.0 %collective-permute-start.10 = (bf16[2,4,32,128]{3,2,1,0:T(8,128)(2,1)S(1)}, bf16[2,4,32,128]{3,2,1,0:T(8,128)(2,1)S(1)}, u32[]{:S(2)}, u32[]{:S(2)}) collective-permute-start(bf16[2,4,32,128]{3,2,1,0:T(8,128)(2,1)S(1)} %shard_map.78), channel_id=1, source_target_pairs={{0,4},{4,0},{8,12},{12,8},{16,20},{20,16},{24,28},{28,24},{1,5},{5... | collective-permute-start | bytes 196616 | tf_op jit(solution)/shard_map/ppermute | solution.py:456
  24.9 2.9 %shard_map.79 = (bf16[256,512]{1,0:T(8,128)(2,1)S(1)}, bf16[256,512]{1,0:T(8,128)(2,1)S(1)}, bf16[512,2048]{1,0:T(8,128)(2,1)S(1)}) custom-call(bf16[128,2048]{1,0:T(8,128)(2,1)S(1)} %get-tuple-element.65.refs_0_, bf16[128,2048]{1,0:T(8,128)(2,1)S(1)} %collective-permute-done.rows.refs_1_, bf16[128,2048]{1,0:T(8,128)(2,1)S(1)} %collective-permute-done.4.rows.refs_2_, ...), custom_call_target="tpu_custom_call" | custom-call | flops 10737418 | bytes 41943 | tf_op jit(solution)/shard_map/pallas_call | solution.py:164
  28.1 1.3 %collective-permute-done.8 = bf16[2,4,32,128]{3,2,1,0:T(8,128)(2,1)S(1)} collective-permute-done((bf16[2,4,32,128]{3,2,1,0:T(8,128)(2,1)S(1)}, bf16[2,4,32,128]{3,2,1,0:T(8,128)(2,1)S(1)}, u32[]{:S(2)}, u32[]{:S(2)}) %collective-permute-start.8) | collective-permute-done | bytes 65568 | tf_op jit(solution)/shard_map/ppermute | solution.py:456
  29.3 0.2 collective-permute-done.9
  29.6 1.0 %collective-permute-start.12 = (bf16[3,2,4,32,128]{4,3,2,1,0:T(8,128)(2,1)S(1)}, bf16[3,2,4,32,128]{4,3,2,1,0:T(8,128)(2,1)S(1)}, u32[]{:S(2)}, u32[]{:S(2)}) collective-permute-start(bf16[3,2,4,32,128]{4,3,2,1,0:T(8,128)(2,1)S(1)} %pad_maximum_fusion.1.refs_4_.refs_12_), channel_id=1, source_target_pairs={{0,4},{4,0},{8,12},{12,8},{16,20},{20,16},{24,28},{28,24},{1,5},{5... | collective-permute-start | bytes 589832 | tf_op jit(solution)/shard_map/ppermute | solution.py:456
  30.6 1.9 %shard_map.80 = (f32[4,128,256]{2,1,0:T(8,128)S(1)}, f32[4,8,256]{2,1,0:T(8,128)S(1)}) custom-call(bf16[512,128]{1,0:T(8,128)(2,1)S(1)} %get-tuple-element.53.asking, bf16[1024,128]{1,0:T(8,128)(2,1)S(1)} %get-tuple-element.54.asked_of, bf16[256,512]{1,0:T(8,128)(2,1)S(1)} %get-tuple-element.72.refs_0_, ...), custom_call_target="tpu_custom_call" | custom-call | flops 4026531 | bytes 5242 | tf_op jit(solution)/shard_map/pallas_call | solution.py:409
  32.5 3.1 %collective-permute-done.12.refs_6_.refs_14_ = bf16[3,2,4,32,128]{4,3,2,1,0:T(8,128)(2,1)S(1)} collective-permute-done((bf16[3,2,4,32,128]{4,3,2,1,0:T(8,128)(2,1)S(1)}, bf16[3,2,4,32,128]{4,3,2,1,0:T(8,128)(2,1)S(1)}, u32[]{:S(2)}, u32[]{:S(2)}) %collective-permute-start.12) | collective-permute-done | bytes 196640 | tf_op jit(solution)/shard_map/ppermute | solution.py:456
  35.6 0.8 %shard_map.81 = (bf16[128,512]{1,0:T(8,128)(2,1)S(1)}, bf16[128,512]{1,0:T(8,128)(2,1)S(1)}) custom-call(bf16[512,128]{1,0:T(8,128)(2,1)S(1)} %get-tuple-element.53.asking, bf16[1024,128]{1,0:T(8,128)(2,1)S(1)} %get-tuple-element.54.asked_of, bf16[256,512]{1,0:T(8,128)(2,1)S(1)} %get-tuple-element.72.refs_0_, f32[4,128,256]{2,1,0:T(8,128)S(1)} %get-tuple-element.78.refs_1_, ...), custom_call_target="tpu_custom_call" | custom-call | flops 1342177 | bytes 5242 | tf_op jit(solution)/shard_map/pallas_call | solution.py:409
  36.5 1.3 %collective-permute-done.13.rows_1 = bf16[128,512]{1,0:T(8,128)(2,1)S(1)} collective-permute-done((bf16[128,512]{1,0:T(8,128)(2,1)S(1)}, bf16[128,512]{1,0:T(8,128)(2,1)S(1)}, u32[]{:S(2)}, u32[]{:S(2)}) %collective-permute-start.13) | collective-permute-done | bytes 131104 | tf_op jit(solution)/shard_map/ppermute | solution.py:456
  37.8 0.7 %shard_map.82 = bf16[128,2048]{1,0:T(8,128)(2,1)S(1)} custom-call(bf16[128,512]{1,0:T(8,128)(2,1)S(1)} %get-tuple-element.81.rows_0, bf16[128,512]{1,0:T(8,128)(2,1)S(1)} %collective-permute-done.13.rows_1, bf16[512,2048]{1,0:T(8,128)(2,1)S(1)} %get-tuple-element.83.weight_0, bf16[512,2048]{1,0:T(8,128)(2,1)S(1)} %collective-permute-done.5.weight_1), custom_call_target="tpu_custom_call" | custom-call | flops 5368709 | bytes 10485 | tf_op jit(solution)/shard_map/pallas_call | solution.py:439
  38.5 1.6 %collective-permute-start.15 = (bf16[128,2048]{1,0:T(8,128)(2,1)S(1)}, bf16[128,2048]{1,0:T(8,128)(2,1)S(1)}, u32[]{:S(2)}, u32[]{:S(2)}) collective-permute-start(bf16[128,2048]{1,0:T(8,128)(2,1)S(1)} %shard_map.82), channel_id=1, source_target_pairs={{0,2},{1,3},{2,0},{3,1},{4,6},{5,7},{6,4},{7,5},{8,10},{9,11},{10,... | collective-permute-start | bytes 1572872 | tf_op jit(solution)/shard_map/ppermute | solution.py:456
  40.1 2.1 %shard_map.83 = (bf16[128,512]{1,0:T(8,128)(2,1)S(1)}, bf16[128,512]{1,0:T(8,128)(2,1)S(1)}) custom-call(bf16[512,128]{1,0:T(8,128)(2,1)S(1)} %get-tuple-element.53.asking, bf16[1024,128]{1,0:T(8,128)(2,1)S(1)} %get-tuple-element.54.asked_of, bf16[256,512]{1,0:T(8,128)(2,1)S(1)} %get-tuple-element.84.refs_0_, ...), custom_call_target="tpu_custom_call" | custom-call | flops 5368709 | bytes 5242 | tf_op jit(solution)/shard_map/pallas_call | solution.py:409
  42.3 1.3 %collective-permute-done.14.rows_1 = bf16[128,512]{1,0:T(8,128)(2,1)S(1)} collective-permute-done((bf16[128,512]{1,0:T(8,128)(2,1)S(1)}, bf16[128,512]{1,0:T(8,128)(2,1)S(1)}, u32[]{:S(2)}, u32[]{:S(2)}) %collective-permute-start.14) | collective-permute-done | bytes 131104 | tf_op jit(solution)/shard_map/ppermute | solution.py:456
  43.6 0.7 %shard_map.84 = f32[128,2048]{1,0:T(8,128)S(1)} custom-call(bf16[128,512]{1,0:T(8,128)(2,1)S(1)} %get-tuple-element.85.rows_0, bf16[128,512]{1,0:T(8,128)(2,1)S(1)} %collective-permute-done.14.rows_1, bf16[512,2048]{1,0:T(8,128)(2,1)S(1)} %get-tuple-element.83.weight_0, bf16[512,2048]{1,0:T(8,128)(2,1)S(1)} %collective-permute-done.5.weight_1), custom_call_target="tpu_custom_call" | custom-call | flops 5368709 | bytes 10485 | tf_op jit(solution)/shard_map/pallas_call | solution.py:439
  44.3 8.2 %collective-permute-done.15 = bf16[128,2048]{1,0:T(8,128)(2,1)S(1)} collective-permute-done((bf16[128,2048]{1,0:T(8,128)(2,1)S(1)}, bf16[128,2048]{1,0:T(8,128)(2,1)S(1)}, u32[]{:S(2)}, u32[]{:S(2)}) %collective-permute-start.15) | collective-permute-done | bytes 524320 | tf_op jit(solution)/shard_map/ppermute | solution.py:456
  52.6 0.9 %add_convert_fusion = bf16[128,2048]{1,0:T(8,128)(2,1)} fusion(f32[128,2048]{1,0:T(8,128)S(1)} %shard_map.84, bf16[128,2048]{1,0:T(8,128)(2,1)S(1)} %collective-permute-done.15), kind=kLoop, calls=%fused_computation | loop fusion | flops 786432 | bytes 2097152 | tf_op jit(solution)/shard_map/convert_element_type | solution.py:513
  (20 shorter events, 0.7 us)
Async XLA Ops:
  0.0 16.7 %collective-permute-start.5 = (bf16[512,2048]{1,0:T(8,128)(2,1)}, bf16[512,2048]{1,0:T(8,128)(2,1)S(1)}, u32[]{:S(2)}, u32[]{:S(2)}) collective-permute-start(bf16[512,2048]{1,0:T(8,128)(2,1)} %refs_5_.1), channel_id=1, source_target_pairs={{0,1},{1,0},{2,3},{3,2},{4,5},{5,4},{6,7},{7,6},{8,9},{9,8},{10,11... | collective-permute-start | bytes 6291464 | tf_op jit(solution)/shard_map/ppermute | solution.py:456
  0.5 5.9 %collective-permute-start = (bf16[128,2048]{1,0:T(8,128)(2,1)}, bf16[128,2048]{1,0:T(8,128)(2,1)S(1)}, u32[]{:S(2)}, u32[]{:S(2)}) collective-permute-start(bf16[128,2048]{1,0:T(8,128)(2,1)} %rows_hbm.1), channel_id=1, source_target_pairs={{0,1},{1,0},{2,3},{3,2},{4,5},{5,4},{6,7},{7,6},{8,9},{9,8},{10,11... | collective-permute-start | bytes 1572872 | tf_op jit(solution)/shard_map/ppermute | solution.py:456
  0.5 16.1 %collective-permute-start.4 = (bf16[128,2048]{1,0:T(8,128)(2,1)}, bf16[128,2048]{1,0:T(8,128)(2,1)S(1)}, u32[]{:S(2)}, u32[]{:S(2)}) collective-permute-start(bf16[128,2048]{1,0:T(8,128)(2,1)} %rows_hbm.1), channel_id=1, source_target_pairs={{0,2},{1,3},{2,0},{3,1},{4,6},{5,7},{6,4},{7,5},{8,10},{9,11},{10,... | collective-permute-start | bytes 1572872 | tf_op jit(solution)/shard_map/ppermute | solution.py:456
  3.5 2.9 %copy-start = (s32[4,128]{1,0:T(4,128)S(1)}, s32[4,128]{1,0:T(4,128)}, u32[]{:S(2)}) copy-start(s32[4,128]{1,0:T(4,128)} %pattern.3) | copy-start | bytes 6148
  6.4 5.3 %copy-start.1 = (s32[8]{0:T(128)S(1)}, s32[8]{0:T(128)}, u32[]{:S(2)}) copy-start(s32[8]{0:T(128)} %param.13) | copy-start | bytes 100
  7.3 6.8 %collective-permute-start.1 = (bf16[2,4,32,128]{3,2,1,0:T(8,128)(2,1)S(1)}, bf16[2,4,32,128]{3,2,1,0:T(8,128)(2,1)S(1)}, u32[]{:S(2)}, u32[]{:S(2)}) collective-permute-start(bf16[2,4,32,128]{3,2,1,0:T(8,128)(2,1)S(1)} %get-tuple-element.50), channel_id=1, source_target_pairs={{0,16},{4,20},{8,24},{12,28},{16,0},{20,4},{24,8},{28,12},{1,17},{... | collective-permute-start | bytes 196616 | tf_op jit(solution)/shard_map/ppermute | solution.py:456
  10.1 6.4 %collective-permute-start.2 = (bf16[2,4,32,128]{3,2,1,0:T(8,128)(2,1)S(1)}, bf16[2,4,32,128]{3,2,1,0:T(8,128)(2,1)S(1)}, u32[]{:S(2)}, u32[]{:S(2)}) collective-permute-start(bf16[2,4,32,128]{3,2,1,0:T(8,128)(2,1)S(1)} %get-tuple-element.50), channel_id=1, source_target_pairs={{0,24},{4,28},{8,16},{12,20},{16,8},{20,12},{24,0},{28,4},{1,25},{... | collective-permute-start | bytes 196616 | tf_op jit(solution)/shard_map/ppermute | solution.py:456
  11.4 5.2 %collective-permute-start.3 = (bf16[2,4,32,128]{3,2,1,0:T(8,128)(2,1)S(1)}, bf16[2,4,32,128]{3,2,1,0:T(8,128)(2,1)S(1)}, u32[]{:S(2)}, u32[]{:S(2)}) collective-permute-start(bf16[2,4,32,128]{3,2,1,0:T(8,128)(2,1)S(1)} %get-tuple-element.50), channel_id=1, source_target_pairs={{0,8},{4,12},{8,0},{12,4},{16,24},{20,28},{24,16},{28,20},{1,9},{5... | collective-permute-start | bytes 196616 | tf_op jit(solution)/shard_map/ppermute | solution.py:456
  16.7 2.6 %collective-permute-start.6 = (bf16[128,2048]{1,0:T(8,128)(2,1)S(1)}, bf16[128,2048]{1,0:T(8,128)(2,1)S(1)}, u32[]{:S(2)}, u32[]{:S(2)}) collective-permute-start(bf16[128,2048]{1,0:T(8,128)(2,1)S(1)} %collective-permute-done.4.rows.refs_2_), channel_id=1, source_target_pairs={{0,1},{1,0},{2,3},{3,2},{4,5},{5,4},{6,7},{7,6},{8,9},{9,8},{10,11... | collective-permute-start | bytes 1572872 | tf_op jit(solution)/shard_map/ppermute | solution.py:456
  16.7 11.2 %collective-permute-start.11 = (bf16[4,2,4,32,128]{4,3,2,1,0:T(8,128)(2,1)S(1)}, bf16[4,2,4,32,128]{4,3,2,1,0:T(8,128)(2,1)S(1)}, u32[]{:S(2)}, u32[]{:S(2)}) collective-permute-start(bf16[4,2,4,32,128]{4,3,2,1,0:T(8,128)(2,1)S(1)} %pad_maximum_fusion.refs_9_), channel_id=1, source_target_pairs={{0,4},{4,0},{8,12},{12,8},{16,20},{20,16},{24,28},{28,24},{1,5},{5... | collective-permute-start | bytes 786440 | tf_op jit(solution)/shard_map/ppermute | solution.py:456
  20.1 7.9 %collective-permute-start.7 = (bf16[2,4,32,128]{3,2,1,0:T(8,128)(2,1)S(1)}, bf16[2,4,32,128]{3,2,1,0:T(8,128)(2,1)S(1)}, u32[]{:S(2)}, u32[]{:S(2)}) collective-permute-start(bf16[2,4,32,128]{3,2,1,0:T(8,128)(2,1)S(1)} %get-tuple-element.64.source), channel_id=1, source_target_pairs={{0,16},{4,20},{8,24},{12,28},{16,0},{20,4},{24,8},{28,12},{1,17},{... | collective-permute-start | bytes 196616 | tf_op jit(solution)/shard_map/ppermute | solution.py:456
  22.9 6.5 %collective-permute-start.8 = (bf16[2,4,32,128]{3,2,1,0:T(8,128)(2,1)S(1)}, bf16[2,4,32,128]{3,2,1,0:T(8,128)(2,1)S(1)}, u32[]{:S(2)}, u32[]{:S(2)}) collective-permute-start(bf16[2,4,32,128]{3,2,1,0:T(8,128)(2,1)S(1)} %get-tuple-element.64.source), channel_id=1, source_target_pairs={{0,24},{4,28},{8,16},{12,20},{16,8},{20,12},{24,0},{28,4},{1,25},{... | collective-permute-start | bytes 196616 | tf_op jit(solution)/shard_map/ppermute | solution.py:456
  23.4 6.1 %collective-permute-start.9 = (bf16[2,4,32,128]{3,2,1,0:T(8,128)(2,1)S(1)}, bf16[2,4,32,128]{3,2,1,0:T(8,128)(2,1)S(1)}, u32[]{:S(2)}, u32[]{:S(2)}) collective-permute-start(bf16[2,4,32,128]{3,2,1,0:T(8,128)(2,1)S(1)} %get-tuple-element.64.source), channel_id=1, source_target_pairs={{0,8},{4,12},{8,0},{12,4},{16,24},{20,28},{24,16},{28,20},{1,9},{5... | collective-permute-start | bytes 196616 | tf_op jit(solution)/shard_map/ppermute | solution.py:456
  23.9 5.6 %collective-permute-start.10 = (bf16[2,4,32,128]{3,2,1,0:T(8,128)(2,1)S(1)}, bf16[2,4,32,128]{3,2,1,0:T(8,128)(2,1)S(1)}, u32[]{:S(2)}, u32[]{:S(2)}) collective-permute-start(bf16[2,4,32,128]{3,2,1,0:T(8,128)(2,1)S(1)} %shard_map.78), channel_id=1, source_target_pairs={{0,4},{4,0},{8,12},{12,8},{16,20},{20,16},{24,28},{28,24},{1,5},{5... | collective-permute-start | bytes 196616 | tf_op jit(solution)/shard_map/ppermute | solution.py:456
  29.6 6.0 %collective-permute-start.12 = (bf16[3,2,4,32,128]{4,3,2,1,0:T(8,128)(2,1)S(1)}, bf16[3,2,4,32,128]{4,3,2,1,0:T(8,128)(2,1)S(1)}, u32[]{:S(2)}, u32[]{:S(2)}) collective-permute-start(bf16[3,2,4,32,128]{4,3,2,1,0:T(8,128)(2,1)S(1)} %pad_maximum_fusion.1.refs_4_.refs_12_), channel_id=1, source_target_pairs={{0,4},{4,0},{8,12},{12,8},{16,20},{20,16},{24,28},{28,24},{1,5},{5... | collective-permute-start | bytes 589832 | tf_op jit(solution)/shard_map/ppermute | solution.py:456
  36.4 1.4 %collective-permute-start.13 = (bf16[128,512]{1,0:T(8,128)(2,1)S(1)}, bf16[128,512]{1,0:T(8,128)(2,1)S(1)}, u32[]{:S(2)}, u32[]{:S(2)}) collective-permute-start(bf16[128,512]{1,0:T(8,128)(2,1)S(1)} %get-tuple-element.82), channel_id=1, source_target_pairs={{0,1},{1,0},{2,3},{3,2},{4,5},{5,4},{6,7},{7,6},{8,9},{9,8},{10,11... | collective-permute-start | bytes 393224 | tf_op jit(solution)/shard_map/ppermute | solution.py:456
  38.5 14.0 %collective-permute-start.15 = (bf16[128,2048]{1,0:T(8,128)(2,1)S(1)}, bf16[128,2048]{1,0:T(8,128)(2,1)S(1)}, u32[]{:S(2)}, u32[]{:S(2)}) collective-permute-start(bf16[128,2048]{1,0:T(8,128)(2,1)S(1)} %shard_map.82), channel_id=1, source_target_pairs={{0,2},{1,3},{2,0},{3,1},{4,6},{5,7},{6,4},{7,5},{8,10},{9,11},{10,... | collective-permute-start | bytes 1572872 | tf_op jit(solution)/shard_map/ppermute | solution.py:456
  42.2 1.4 %collective-permute-start.14 = (bf16[128,512]{1,0:T(8,128)(2,1)S(1)}, bf16[128,512]{1,0:T(8,128)(2,1)S(1)}, u32[]{:S(2)}, u32[]{:S(2)}) collective-permute-start(bf16[128,512]{1,0:T(8,128)(2,1)S(1)} %get-tuple-element.86), channel_id=1, source_target_pairs={{0,1},{1,0},{2,3},{3,2},{4,5},{5,4},{6,7},{7,6},{8,9},{9,8},{10,11... | collective-permute-start | bytes 393224 | tf_op jit(solution)/shard_map/ppermute | solution.py:456

commit v15 on v13

--- a/solution.py
+++ b/solution.py
@@ -15,6 +15,7 @@
 FAR_ROWS = BLOCKS_HALF * DILATED_KEPT
 GROUP = 8
 STREAMS = 8
+PARTS = 4
 HIDDEN = -1e30
 SCALE = math.log2(math.e) / math.sqrt(HEAD_SIZE)
 BF16 = jnp.bfloat16
@@ -425,25 +426,54 @@
     )(*operands)
 
 
-def mix_kernel(rows_0, rows_1, weight_0, weight_1, out):
+def mix_kernel(more, rows, weight, *refs):
+    out = refs[-1]
     tile = min(512, out.shape[1])
     for index in range(out.shape[1] // tile):
         part = slice(index * tile, (index + 1) * tile)
-        total = dot(rows_0[...], weight_0[:, part]) + dot(rows_1[...], weight_1[:, part])
+        total = dot(rows[...], weight[:, part])
+        if more:
+            total = total + refs[0][:, part]
         out[:, part] = total.astype(out.dtype)
 
 
-def mix(rows_0, rows_1, weight_0, weight_1, dtype):
-    rows, depth = rows_0.shape
-    width = weight_0.shape[1]
-    return pl.pallas_call(
-        mix_kernel,
-        in_specs=[IN_VMEM] * 4,
+def mix(rows, weight, dtype, begun=None):
+    count, depth = rows.shape
+    width = weight.shape[1]
+    operands = [rows, weight] + ([begun] if begun is not None else [])
+    return pl.pallas_call(
+        functools.partial(mix_kernel, begun is not None),
+        in_specs=[IN_VMEM] * len(operands),
         out_specs=IN_VMEM,
-        out_shape=shape((rows, width), dtype),
-        compiler_params=params(),
-        cost_estimate=cost(4 * rows * depth * width, 4 * rows * width),
-    )(rows_0, rows_1, weight_0, weight_1)
+        out_shape=shape((count, width), dtype),
+        compiler_params=params(),
+        cost_estimate=cost(2 * count * depth * width, 4 * count * width),
+    )(*operands)
+
+
+def add_kernel(own, arriving, out, held, sems):
+    rows = held.shape[0] // PARTS
+    copies = []
+    for index in range(PARTS):
+        where = slice(index * rows, (index + 1) * rows)
+        held[where, :] = (own[where, :] + arriving[where, :].astype(F32)).astype(BF16)
+        copy = pltpu.make_async_copy(held.at[where, :], out.at[where, :], sems.at[index])
+        copy.start()
+        copies.append(copy)
+    for copy in copies:
+        copy.wait()
+
+
+def add(own, arriving):
+    return pl.pallas_call(
+        add_kernel,
+        in_specs=[IN_VMEM] * 2,
+        out_specs=IN_HBM,
+        out_shape=shape(arriving.shape),
+        scratch_shapes=[pltpu.VMEM(arriving.shape, BF16), pltpu.SemaphoreType.DMA((PARTS,))],
+        compiler_params=params(),
+        cost_estimate=cost(own.size, 8 * own.size),
+    )(own, arriving)
 
 
 def shards(seqs, subs, normed, w_query, w_key, w_value, w_out, pattern, slide_lengths):
@@ -502,13 +532,13 @@
     begun = call(2 * BLOCK, query_b, [half_a], near=near, finish=False)
     keep_b, send_b = call(2 * BLOCK, query_b, [half_b], begun=begun)
     other_b = swap(send_b, 1)
-    leaving = mix(keep_b, other_b, wo, wo_beside, BF16)
+    leaving = mix(other_b, wo_beside, BF16, mix(keep_b, wo, F32))
     arriving = swap(leaving, 2)
     query_a = after(query_a, leaving)
     keep_a, send_a = call(0, query_a, [half_a, half_b], near=near)
     other_a = swap(send_a, 1)
-    own = mix(keep_a, other_a, wo, wo_beside, F32)
-    return (own + arriving.astype(F32)).astype(BF16)
+    own = mix(other_a, wo_beside, F32, mix(keep_a, wo, F32))
+    return add(own, arriving)
 
 
 def solution(mesh):

time: 53.5 us -> 53.2 us (level)
  Pallas kernels: 15.3 us -> 16.5 us
  other arithmetic: 1.04 us -> 0.14 us
  waiting for transfers between devices: 19.9 us -> 19.2 us
    pallas_call x2 -> x5, Pallas kernels: 1.43 us -> 2.64 us  [the longest x4 1.8 us: mix(): pl.pallas_call(functools.partial(mix_kernel, begun is not None), in_specs...]
    convert_element_type x1 -> x0, other arithmetic: 0.9 us -> none  [shards(): return (own + arriving.astype(F32)).astype(BF16)]
    ppermute x16, waiting for transfers between devices: 19.9 us -> 19.2 us  [swap(): return lax.ppermute(array, axis, [(i, i ^ bit) for i in range(count)])]
  transfers between devices with their start and end apart: 16 -> 16, of which waited for: 11 -> 11; matrix products, arithmetic and copies ran while one was open for 0% -> 0% of each run, Pallas kernels for 26% -> 27%
where the time goes in v15:
time: 53.2 us; the launch traced here: 53 us
  waiting for transfers between devices  19.2 us (36%)
  starting transfers between devices  17 us (32%)
  Pallas kernels  16.5 us (31%)
    ppermute x16, waiting for transfers between devices, swap(): return lax.ppermute(array, axis, [(i, i ^ bit) for i in range(count)])  19.2 us
    ppermute x16, starting transfers between devices, swap(): return lax.ppermute(array, axis, [(i, i ^ bit) for i in range(count)])  17 us
    pallas_call x3, Pallas kernels, attend(): pl.pallas_call(functools.partial(attend_kernel, first_row, near is not No...  4.77 us
    pallas_call x1, Pallas kernels, first(): pl.pallas_call(first_kernel, in_specs=[IN_HBM] * 3, out_specs=[IN_VMEM] *...  2.92 us
    pallas_call x1, Pallas kernels, query(): pl.pallas_call(query_kernel, in_specs=[IN_VMEM] * 4 + [IN_HBM] * 2, out_s...  2.9 us
    pallas_call x2, Pallas kernels, second(): pl.pallas_call(second_kernel, in_specs=[IN_VMEM] * 6, out_specs=[IN_VMEM]...  1.81 us
    pallas_call x4, Pallas kernels, mix(): pl.pallas_call(functools.partial(mix_kernel, begun is not None), in_specs...  1.8 us
  transfers between devices with their start and end apart: 16, of which 11 were waited for; matrix products, arithmetic and copies ran while one was open for 0% of the time, Pallas kernels for 27%

profile of v15, /device:TPU:0, one launch (start us, length us, event | category | flops | bytes accessed | tf_op | source)
XLA Modules:
  0.0 53.0 jit_solution(13939709167431690877)
XLA Ops:
  0.0 0.5 collective-permute-start.5
  0.5 2.9 %collective-permute-start.4 = (bf16[128,2048]{1,0:T(8,128)(2,1)}, bf16[128,2048]{1,0:T(8,128)(2,1)S(1)}, u32[]{:S(2)}, u32[]{:S(2)}) collective-permute-start(bf16[128,2048]{1,0:T(8,128)(2,1)} %rows_hbm.1), channel_id=1, source_target_pairs={{0,2},{1,3},{2,0},{3,1},{4,6},{5,7},{6,4},{7,5},{8,10},{9,11},{10,... | collective-permute-start | bytes 1572872 | tf_op jit(solution)/shard_map/ppermute | solution.py:486
  3.5 2.9 %shard_map.73 = (bf16[128,2048]{1,0:T(8,128)(2,1)S(1)}, bf16[2048,512]{1,0:T(8,128)(2,1)S(1)}, bf16[2048,512]{1,0:T(8,128)(2,1)S(1)}, bf16[128,512]{1,0:T(8,128)(2,1)S(1)}, bf16[128,512]{1,0:T(8,128)(2,1)S(1)}) custom-call(bf16[128,2048]{1,0:T(8,128)(2,1)} %rows_hbm.1, bf16[2048,512]{1,0:T(8,128)(2,1)} %wk_hbm.1, bf16[2048,512]{1,0:T(8,128)(2,1)} %wv_hbm.1), custom_call_target="tpu_custom_call" | custom-call | flops 5368709 | bytes 41943 | tf_op jit(solution)/shard_map/pallas_call | solution.py:106
  6.4 0.9 %shard_map.74 = (bf16[128,512]{1,0:T(8,128)(2,1)S(1)}, bf16[128,512]{1,0:T(8,128)(2,1)S(1)}, bf16[2,4,32,128]{3,2,1,0:T(8,128)(2,1)S(1)}) custom-call(bf16[128,2048]{1,0:T(8,128)(2,1)S(1)} %collective-permute-done.rows.refs_1_, bf16[2048,512]{1,0:T(8,128)(2,1)S(1)} %get-tuple-element.44.wk, bf16[2048,512]{1,0:T(8,128)(2,1)S(1)} %get-tuple-element.45.wv, ...), custom_call_target="tpu_custom_call" | custom-call | flops 5368709 | bytes 5242 | tf_op jit(solution)/shard_map/pallas_call | solution.py:138
  7.3 2.8 %collective-permute-start.1 = (bf16[2,4,32,128]{3,2,1,0:T(8,128)(2,1)S(1)}, bf16[2,4,32,128]{3,2,1,0:T(8,128)(2,1)S(1)}, u32[]{:S(2)}, u32[]{:S(2)}) collective-permute-start(bf16[2,4,32,128]{3,2,1,0:T(8,128)(2,1)S(1)} %get-tuple-element.48), channel_id=1, source_target_pairs={{0,16},{4,20},{8,24},{12,28},{16,0},{20,4},{24,8},{28,12},{1,17},{... | collective-permute-start | bytes 196616 | tf_op jit(solution)/shard_map/ppermute | solution.py:486
  10.1 1.3 %collective-permute-start.2 = (bf16[2,4,32,128]{3,2,1,0:T(8,128)(2,1)S(1)}, bf16[2,4,32,128]{3,2,1,0:T(8,128)(2,1)S(1)}, u32[]{:S(2)}, u32[]{:S(2)}) collective-permute-start(bf16[2,4,32,128]{3,2,1,0:T(8,128)(2,1)S(1)} %get-tuple-element.48), channel_id=1, source_target_pairs={{0,24},{4,28},{8,16},{12,20},{16,8},{20,12},{24,0},{28,4},{1,25},{... | collective-permute-start | bytes 196616 | tf_op jit(solution)/shard_map/ppermute | solution.py:486
  11.7 0.7 %shard_map.75 = (bf16[512,128]{1,0:T(8,128)(2,1)S(1)}, bf16[1024,128]{1,0:T(8,128)(2,1)S(1)}) custom-call(s32[10]{0:T(128)S(1)} %pad_add_fusion.place), custom_call_target="tpu_custom_call" | custom-call | flops 83886 | bytes 2621 | tf_op jit(solution)/shard_map/pallas_call | solution.py:254
  12.4 1.6 %collective-permute-done.1 = bf16[2,4,32,128]{3,2,1,0:T(8,128)(2,1)S(1)} collective-permute-done((bf16[2,4,32,128]{3,2,1,0:T(8,128)(2,1)S(1)}, bf16[2,4,32,128]{3,2,1,0:T(8,128)(2,1)S(1)}, u32[]{:S(2)}, u32[]{:S(2)}) %collective-permute-start.1) | collective-permute-done | bytes 65568 | tf_op jit(solution)/shard_map/ppermute | solution.py:486
  14.1 2.4 %collective-permute-done.2 = bf16[2,4,32,128]{3,2,1,0:T(8,128)(2,1)S(1)} collective-permute-done((bf16[2,4,32,128]{3,2,1,0:T(8,128)(2,1)S(1)}, bf16[2,4,32,128]{3,2,1,0:T(8,128)(2,1)S(1)}, u32[]{:S(2)}, u32[]{:S(2)}) %collective-permute-start.2) | collective-permute-done | bytes 65568 | tf_op jit(solution)/shard_map/ppermute | solution.py:486
  16.7 1.7 %collective-permute-start.11 = (bf16[4,2,4,32,128]{4,3,2,1,0:T(8,128)(2,1)S(1)}, bf16[4,2,4,32,128]{4,3,2,1,0:T(8,128)(2,1)S(1)}, u32[]{:S(2)}, u32[]{:S(2)}) collective-permute-start(bf16[4,2,4,32,128]{4,3,2,1,0:T(8,128)(2,1)S(1)} %pad_maximum_fusion.refs_9_), channel_id=1, source_target_pairs={{0,4},{4,0},{8,12},{12,8},{16,20},{20,16},{24,28},{28,24},{1,5},{5... | collective-permute-start | bytes 786440 | tf_op jit(solution)/shard_map/ppermute | solution.py:486
  18.4 0.8 %shard_map.76 = (bf16[128,512]{1,0:T(8,128)(2,1)S(1)}, bf16[128,512]{1,0:T(8,128)(2,1)S(1)}) custom-call(bf16[128,2048]{1,0:T(8,128)(2,1)S(1)} %collective-permute-done.4.rows.refs_2_, bf16[2048,512]{1,0:T(8,128)(2,1)S(1)} %get-tuple-element.44.wk, bf16[2048,512]{1,0:T(8,128)(2,1)S(1)} %get-tuple-element.45.wv), custom_call_target="tpu_custom_call" | custom-call | flops 5368709 | bytes 5242 | tf_op jit(solution)/shard_map/pallas_call | solution.py:203
  19.2 0.9 %shard_map.77 = (bf16[128,512]{1,0:T(8,128)(2,1)S(1)}, bf16[128,512]{1,0:T(8,128)(2,1)S(1)}, bf16[2,4,32,128]{3,2,1,0:T(8,128)(2,1)S(1)}) custom-call(bf16[128,2048]{1,0:T(8,128)(2,1)S(1)} %collective-permute-done.6.rows.refs_3_, bf16[2048,512]{1,0:T(8,128)(2,1)S(1)} %get-tuple-element.44.wk, bf16[2048,512]{1,0:T(8,128)(2,1)S(1)} %get-tuple-element.45.wv, ...), custom_call_target="tpu_custom_call" | custom-call | flops 5368709 | bytes 5242 | tf_op jit(solution)/shard_map/pallas_call | solution.py:138
  20.1 2.7 %collective-permute-start.7 = (bf16[2,4,32,128]{3,2,1,0:T(8,128)(2,1)S(1)}, bf16[2,4,32,128]{3,2,1,0:T(8,128)(2,1)S(1)}, u32[]{:S(2)}, u32[]{:S(2)}) collective-permute-start(bf16[2,4,32,128]{3,2,1,0:T(8,128)(2,1)S(1)} %get-tuple-element.62.source), channel_id=1, source_target_pairs={{0,16},{4,20},{8,24},{12,28},{16,0},{20,4},{24,8},{28,12},{1,17},{... | collective-permute-start | bytes 196616 | tf_op jit(solution)/shard_map/ppermute | solution.py:486
  22.8 0.6 %collective-permute-start.8 = (bf16[2,4,32,128]{3,2,1,0:T(8,128)(2,1)S(1)}, bf16[2,4,32,128]{3,2,1,0:T(8,128)(2,1)S(1)}, u32[]{:S(2)}, u32[]{:S(2)}) collective-permute-start(bf16[2,4,32,128]{3,2,1,0:T(8,128)(2,1)S(1)} %get-tuple-element.62.source), channel_id=1, source_target_pairs={{0,24},{4,28},{8,16},{12,20},{16,8},{20,12},{24,0},{28,4},{1,25},{... | collective-permute-start | bytes 196616 | tf_op jit(solution)/shard_map/ppermute | solution.py:486
  23.4 0.5 collective-permute-start.9
  23.9 1.0 %collective-permute-start.10 = (bf16[2,4,32,128]{3,2,1,0:T(8,128)(2,1)S(1)}, bf16[2,4,32,128]{3,2,1,0:T(8,128)(2,1)S(1)}, u32[]{:S(2)}, u32[]{:S(2)}) collective-permute-start(bf16[2,4,32,128]{3,2,1,0:T(8,128)(2,1)S(1)} %shard_map.78), channel_id=1, source_target_pairs={{0,4},{4,0},{8,12},{12,8},{16,20},{20,16},{24,28},{28,24},{1,5},{5... | collective-permute-start | bytes 196616 | tf_op jit(solution)/shard_map/ppermute | solution.py:486
  24.9 0.6 %collective-permute-done.11.refs_10_ = bf16[4,2,4,32,128]{4,3,2,1,0:T(8,128)(2,1)S(1)} collective-permute-done((bf16[4,2,4,32,128]{4,3,2,1,0:T(8,128)(2,1)S(1)}, bf16[4,2,4,32,128]{4,3,2,1,0:T(8,128)(2,1)S(1)}, u32[]{:S(2)}, u32[]{:S(2)}) %collective-permute-start.11) | collective-permute-done | bytes 262176 | tf_op jit(solution)/shard_map/ppermute | solution.py:486
  25.5 2.5 %collective-permute-done.7 = bf16[2,4,32,128]{3,2,1,0:T(8,128)(2,1)S(1)} collective-permute-done((bf16[2,4,32,128]{3,2,1,0:T(8,128)(2,1)S(1)}, bf16[2,4,32,128]{3,2,1,0:T(8,128)(2,1)S(1)}, u32[]{:S(2)}, u32[]{:S(2)}) %collective-permute-start.7) | collective-permute-done | bytes 65568 | tf_op jit(solution)/shard_map/ppermute | solution.py:486
  28.0 1.3 %collective-permute-done.8 = bf16[2,4,32,128]{3,2,1,0:T(8,128)(2,1)S(1)} collective-permute-done((bf16[2,4,32,128]{3,2,1,0:T(8,128)(2,1)S(1)}, bf16[2,4,32,128]{3,2,1,0:T(8,128)(2,1)S(1)}, u32[]{:S(2)}, u32[]{:S(2)}) %collective-permute-start.8) | collective-permute-done | bytes 65568 | tf_op jit(solution)/shard_map/ppermute | solution.py:486
  29.5 1.0 %collective-permute-start.12 = (bf16[3,2,4,32,128]{4,3,2,1,0:T(8,128)(2,1)S(1)}, bf16[3,2,4,32,128]{4,3,2,1,0:T(8,128)(2,1)S(1)}, u32[]{:S(2)}, u32[]{:S(2)}) collective-permute-start(bf16[3,2,4,32,128]{4,3,2,1,0:T(8,128)(2,1)S(1)} %pad_maximum_fusion.1.refs_4_.refs_12_), channel_id=1, source_target_pairs={{0,4},{4,0},{8,12},{12,8},{16,20},{20,16},{24,28},{28,24},{1,5},{5... | collective-permute-start | bytes 589832 | tf_op jit(solution)/shard_map/ppermute | solution.py:486
  30.5 2.9 %shard_map.79 = (bf16[256,512]{1,0:T(8,128)(2,1)S(1)}, bf16[256,512]{1,0:T(8,128)(2,1)S(1)}, bf16[512,2048]{1,0:T(8,128)(2,1)S(1)}) custom-call(bf16[128,2048]{1,0:T(8,128)(2,1)S(1)} %get-tuple-element.66.refs_0_, bf16[128,2048]{1,0:T(8,128)(2,1)S(1)} %collective-permute-done.rows.refs_1_, bf16[128,2048]{1,0:T(8,128)(2,1)S(1)} %collective-permute-done.4.rows.refs_2_, ...), custom_call_target="tpu_custom_call" | custom-call | flops 10737418 | bytes 41943 | tf_op jit(solution)/shard_map/pallas_call | solution.py:165
  33.4 1.9 %shard_map.80 = (f32[4,128,256]{2,1,0:T(8,128)S(1)}, f32[4,8,256]{2,1,0:T(8,128)S(1)}) custom-call(bf16[512,128]{1,0:T(8,128)(2,1)S(1)} %get-tuple-element.51.asking, bf16[1024,128]{1,0:T(8,128)(2,1)S(1)} %get-tuple-element.52.asked_of, bf16[256,512]{1,0:T(8,128)(2,1)S(1)} %get-tuple-element.68.refs_0_, ...), custom_call_target="tpu_custom_call" | custom-call | flops 4026531 | bytes 5242 | tf_op jit(solution)/shard_map/pallas_call | solution.py:410
  35.5 0.8 %shard_map.81 = (bf16[128,512]{1,0:T(8,128)(2,1)S(1)}, bf16[128,512]{1,0:T(8,128)(2,1)S(1)}) custom-call(bf16[512,128]{1,0:T(8,128)(2,1)S(1)} %get-tuple-element.51.asking, bf16[1024,128]{1,0:T(8,128)(2,1)S(1)} %get-tuple-element.52.asked_of, bf16[256,512]{1,0:T(8,128)(2,1)S(1)} %get-tuple-element.68.refs_0_, f32[4,128,256]{2,1,0:T(8,128)S(1)} %get-tuple-element.74.refs_1_, ...), custom_call_target="tpu_custom_call" | custom-call | flops 1342177 | bytes 5242 | tf_op jit(solution)/shard_map/pallas_call | solution.py:410
  36.4 0.4 shard_map.82.refs_0_
  36.8 0.9 %collective-permute-done.13.rows = bf16[128,512]{1,0:T(8,128)(2,1)S(1)} collective-permute-done((bf16[128,512]{1,0:T(8,128)(2,1)S(1)}, bf16[128,512]{1,0:T(8,128)(2,1)S(1)}, u32[]{:S(2)}, u32[]{:S(2)}) %collective-permute-start.13) | collective-permute-done | bytes 131104 | tf_op jit(solution)/shard_map/ppermute | solution.py:486
  37.7 0.5 shard_map.83
  38.2 1.6 %collective-permute-start.15 = (bf16[128,2048]{1,0:T(8,128)(2,1)S(1)}, bf16[128,2048]{1,0:T(8,128)(2,1)S(1)}, u32[]{:S(2)}, u32[]{:S(2)}) collective-permute-start(bf16[128,2048]{1,0:T(8,128)(2,1)S(1)} %shard_map.83), channel_id=1, source_target_pairs={{0,2},{1,3},{2,0},{3,1},{4,6},{5,7},{6,4},{7,5},{8,10},{9,11},{10,... | collective-permute-start | bytes 1572872 | tf_op jit(solution)/shard_map/ppermute | solution.py:486
  39.8 2.1 %shard_map.84 = (bf16[128,512]{1,0:T(8,128)(2,1)S(1)}, bf16[128,512]{1,0:T(8,128)(2,1)S(1)}) custom-call(bf16[512,128]{1,0:T(8,128)(2,1)S(1)} %get-tuple-element.51.asking, bf16[1024,128]{1,0:T(8,128)(2,1)S(1)} %get-tuple-element.52.asked_of, bf16[256,512]{1,0:T(8,128)(2,1)S(1)} %get-tuple-element.80.refs_0_, ...), custom_call_target="tpu_custom_call" | custom-call | flops 5368709 | bytes 5242 | tf_op jit(solution)/shard_map/pallas_call | solution.py:410
  42.4 0.9 %collective-permute-done.14.rows = bf16[128,512]{1,0:T(8,128)(2,1)S(1)} collective-permute-done((bf16[128,512]{1,0:T(8,128)(2,1)S(1)}, bf16[128,512]{1,0:T(8,128)(2,1)S(1)}, u32[]{:S(2)}, u32[]{:S(2)}) %collective-permute-start.14) | collective-permute-done | bytes 131104 | tf_op jit(solution)/shard_map/ppermute | solution.py:486
  43.3 0.4 shard_map.86.own
  43.8 8.4 %collective-permute-done.15.arriving = bf16[128,2048]{1,0:T(8,128)(2,1)S(1)} collective-permute-done((bf16[128,2048]{1,0:T(8,128)(2,1)S(1)}, bf16[128,2048]{1,0:T(8,128)(2,1)S(1)}, u32[]{:S(2)}, u32[]{:S(2)}) %collective-permute-start.15) | collective-permute-done | bytes 524320 | tf_op jit(solution)/shard_map/ppermute | solution.py:486
  52.2 0.8 %shard_map.87 = bf16[128,2048]{1,0:T(8,128)(2,1)} custom-call(f32[128,2048]{1,0:T(8,128)S(1)} %shard_map.86.own, bf16[128,2048]{1,0:T(8,128)(2,1)S(1)} %collective-permute-done.15.arriving), custom_call_target="tpu_custom_call" | custom-call | flops 2621 | bytes 20971 | tf_op jit(solution)/shard_map/pallas_call | solution.py:468
  (22 shorter events, 1.6 us)
Async XLA Ops:
  0.0 16.7 %collective-permute-start.5 = (bf16[512,2048]{1,0:T(8,128)(2,1)}, bf16[512,2048]{1,0:T(8,128)(2,1)S(1)}, u32[]{:S(2)}, u32[]{:S(2)}) collective-permute-start(bf16[512,2048]{1,0:T(8,128)(2,1)} %refs_5_.1), channel_id=1, source_target_pairs={{0,1},{1,0},{2,3},{3,2},{4,5},{5,4},{6,7},{7,6},{8,9},{9,8},{10,11... | collective-permute-start | bytes 6291464 | tf_op jit(solution)/shard_map/ppermute | solution.py:486
  0.5 5.9 %collective-permute-start = (bf16[128,2048]{1,0:T(8,128)(2,1)}, bf16[128,2048]{1,0:T(8,128)(2,1)S(1)}, u32[]{:S(2)}, u32[]{:S(2)}) collective-permute-start(bf16[128,2048]{1,0:T(8,128)(2,1)} %rows_hbm.1), channel_id=1, source_target_pairs={{0,1},{1,0},{2,3},{3,2},{4,5},{5,4},{6,7},{7,6},{8,9},{9,8},{10,11... | collective-permute-start | bytes 1572872 | tf_op jit(solution)/shard_map/ppermute | solution.py:486
  0.5 16.1 %collective-permute-start.4 = (bf16[128,2048]{1,0:T(8,128)(2,1)}, bf16[128,2048]{1,0:T(8,128)(2,1)S(1)}, u32[]{:S(2)}, u32[]{:S(2)}) collective-permute-start(bf16[128,2048]{1,0:T(8,128)(2,1)} %rows_hbm.1), channel_id=1, source_target_pairs={{0,2},{1,3},{2,0},{3,1},{4,6},{5,7},{6,4},{7,5},{8,10},{9,11},{10,... | collective-permute-start | bytes 1572872 | tf_op jit(solution)/shard_map/ppermute | solution.py:486
  3.5 2.9 %copy-start = (s32[4,128]{1,0:T(4,128)S(1)}, s32[4,128]{1,0:T(4,128)}, u32[]{:S(2)}) copy-start(s32[4,128]{1,0:T(4,128)} %pattern.3) | copy-start | bytes 6148
  6.4 5.3 %copy-start.1 = (s32[8]{0:T(128)S(1)}, s32[8]{0:T(128)}, u32[]{:S(2)}) copy-start(s32[8]{0:T(128)} %param.13) | copy-start | bytes 100
  7.3 6.8 %collective-permute-start.1 = (bf16[2,4,32,128]{3,2,1,0:T(8,128)(2,1)S(1)}, bf16[2,4,32,128]{3,2,1,0:T(8,128)(2,1)S(1)}, u32[]{:S(2)}, u32[]{:S(2)}) collective-permute-start(bf16[2,4,32,128]{3,2,1,0:T(8,128)(2,1)S(1)} %get-tuple-element.48), channel_id=1, source_target_pairs={{0,16},{4,20},{8,24},{12,28},{16,0},{20,4},{24,8},{28,12},{1,17},{... | collective-permute-start | bytes 196616 | tf_op jit(solution)/shard_map/ppermute | solution.py:486
  10.1 6.4 %collective-permute-start.2 = (bf16[2,4,32,128]{3,2,1,0:T(8,128)(2,1)S(1)}, bf16[2,4,32,128]{3,2,1,0:T(8,128)(2,1)S(1)}, u32[]{:S(2)}, u32[]{:S(2)}) collective-permute-start(bf16[2,4,32,128]{3,2,1,0:T(8,128)(2,1)S(1)} %get-tuple-element.48), channel_id=1, source_target_pairs={{0,24},{4,28},{8,16},{12,20},{16,8},{20,12},{24,0},{28,4},{1,25},{... | collective-permute-start | bytes 196616 | tf_op jit(solution)/shard_map/ppermute | solution.py:486
  11.4 5.2 %collective-permute-start.3 = (bf16[2,4,32,128]{3,2,1,0:T(8,128)(2,1)S(1)}, bf16[2,4,32,128]{3,2,1,0:T(8,128)(2,1)S(1)}, u32[]{:S(2)}, u32[]{:S(2)}) collective-permute-start(bf16[2,4,32,128]{3,2,1,0:T(8,128)(2,1)S(1)} %get-tuple-element.48), channel_id=1, source_target_pairs={{0,8},{4,12},{8,0},{12,4},{16,24},{20,28},{24,16},{28,20},{1,9},{5... | collective-permute-start | bytes 196616 | tf_op jit(solution)/shard_map/ppermute | solution.py:486
  16.7 2.6 %collective-permute-start.6 = (bf16[128,2048]{1,0:T(8,128)(2,1)S(1)}, bf16[128,2048]{1,0:T(8,128)(2,1)S(1)}, u32[]{:S(2)}, u32[]{:S(2)}) collective-permute-start(bf16[128,2048]{1,0:T(8,128)(2,1)S(1)} %collective-permute-done.4.rows.refs_2_), channel_id=1, source_target_pairs={{0,1},{1,0},{2,3},{3,2},{4,5},{5,4},{6,7},{7,6},{8,9},{9,8},{10,11... | collective-permute-start | bytes 1572872 | tf_op jit(solution)/shard_map/ppermute | solution.py:486
  16.7 8.8 %collective-permute-start.11 = (bf16[4,2,4,32,128]{4,3,2,1,0:T(8,128)(2,1)S(1)}, bf16[4,2,4,32,128]{4,3,2,1,0:T(8,128)(2,1)S(1)}, u32[]{:S(2)}, u32[]{:S(2)}) collective-permute-start(bf16[4,2,4,32,128]{4,3,2,1,0:T(8,128)(2,1)S(1)} %pad_maximum_fusion.refs_9_), channel_id=1, source_target_pairs={{0,4},{4,0},{8,12},{12,8},{16,20},{20,16},{24,28},{28,24},{1,5},{5... | collective-permute-start | bytes 786440 | tf_op jit(solution)/shard_map/ppermute | solution.py:486
  20.1 7.9 %collective-permute-start.7 = (bf16[2,4,32,128]{3,2,1,0:T(8,128)(2,1)S(1)}, bf16[2,4,32,128]{3,2,1,0:T(8,128)(2,1)S(1)}, u32[]{:S(2)}, u32[]{:S(2)}) collective-permute-start(bf16[2,4,32,128]{3,2,1,0:T(8,128)(2,1)S(1)} %get-tuple-element.62.source), channel_id=1, source_target_pairs={{0,16},{4,20},{8,24},{12,28},{16,0},{20,4},{24,8},{28,12},{1,17},{... | collective-permute-start | bytes 196616 | tf_op jit(solution)/shard_map/ppermute | solution.py:486
  22.8 6.5 %collective-permute-start.8 = (bf16[2,4,32,128]{3,2,1,0:T(8,128)(2,1)S(1)}, bf16[2,4,32,128]{3,2,1,0:T(8,128)(2,1)S(1)}, u32[]{:S(2)}, u32[]{:S(2)}) collective-permute-start(bf16[2,4,32,128]{3,2,1,0:T(8,128)(2,1)S(1)} %get-tuple-element.62.source), channel_id=1, source_target_pairs={{0,24},{4,28},{8,16},{12,20},{16,8},{20,12},{24,0},{28,4},{1,25},{... | collective-permute-start | bytes 196616 | tf_op jit(solution)/shard_map/ppermute | solution.py:486
  23.4 6.1 %collective-permute-start.9 = (bf16[2,4,32,128]{3,2,1,0:T(8,128)(2,1)S(1)}, bf16[2,4,32,128]{3,2,1,0:T(8,128)(2,1)S(1)}, u32[]{:S(2)}, u32[]{:S(2)}) collective-permute-start(bf16[2,4,32,128]{3,2,1,0:T(8,128)(2,1)S(1)} %get-tuple-element.62.source), channel_id=1, source_target_pairs={{0,8},{4,12},{8,0},{12,4},{16,24},{20,28},{24,16},{28,20},{1,9},{5... | collective-permute-start | bytes 196616 | tf_op jit(solution)/shard_map/ppermute | solution.py:486
  23.9 5.6 %collective-permute-start.10 = (bf16[2,4,32,128]{3,2,1,0:T(8,128)(2,1)S(1)}, bf16[2,4,32,128]{3,2,1,0:T(8,128)(2,1)S(1)}, u32[]{:S(2)}, u32[]{:S(2)}) collective-permute-start(bf16[2,4,32,128]{3,2,1,0:T(8,128)(2,1)S(1)} %shard_map.78), channel_id=1, source_target_pairs={{0,4},{4,0},{8,12},{12,8},{16,20},{20,16},{24,28},{28,24},{1,5},{5... | collective-permute-start | bytes 196616 | tf_op jit(solution)/shard_map/ppermute | solution.py:486
  29.5 6.0 %collective-permute-start.12 = (bf16[3,2,4,32,128]{4,3,2,1,0:T(8,128)(2,1)S(1)}, bf16[3,2,4,32,128]{4,3,2,1,0:T(8,128)(2,1)S(1)}, u32[]{:S(2)}, u32[]{:S(2)}) collective-permute-start(bf16[3,2,4,32,128]{4,3,2,1,0:T(8,128)(2,1)S(1)} %pad_maximum_fusion.1.refs_4_.refs_12_), channel_id=1, source_target_pairs={{0,4},{4,0},{8,12},{12,8},{16,20},{20,16},{24,28},{28,24},{1,5},{5... | collective-permute-start | bytes 589832 | tf_op jit(solution)/shard_map/ppermute | solution.py:486
  36.3 1.4 %collective-permute-start.13 = (bf16[128,512]{1,0:T(8,128)(2,1)S(1)}, bf16[128,512]{1,0:T(8,128)(2,1)S(1)}, u32[]{:S(2)}, u32[]{:S(2)}) collective-permute-start(bf16[128,512]{1,0:T(8,128)(2,1)S(1)} %get-tuple-element.77), channel_id=1, source_target_pairs={{0,1},{1,0},{2,3},{3,2},{4,5},{5,4},{6,7},{7,6},{8,9},{9,8},{10,11... | collective-permute-start | bytes 393224 | tf_op jit(solution)/shard_map/ppermute | solution.py:486
  38.2 14.0 %collective-permute-start.15 = (bf16[128,2048]{1,0:T(8,128)(2,1)S(1)}, bf16[128,2048]{1,0:T(8,128)(2,1)S(1)}, u32[]{:S(2)}, u32[]{:S(2)}) collective-permute-start(bf16[128,2048]{1,0:T(8,128)(2,1)S(1)} %shard_map.83), channel_id=1, source_target_pairs={{0,2},{1,3},{2,0},{3,1},{4,6},{5,7},{6,4},{7,5},{8,10},{9,11},{10,... | collective-permute-start | bytes 1572872 | tf_op jit(solution)/shard_map/ppermute | solution.py:486
  41.9 1.4 %collective-permute-start.14 = (bf16[128,512]{1,0:T(8,128)(2,1)S(1)}, bf16[128,512]{1,0:T(8,128)(2,1)S(1)}, u32[]{:S(2)}, u32[]{:S(2)}) collective-permute-start(bf16[128,512]{1,0:T(8,128)(2,1)S(1)} %get-tuple-element.81), channel_id=1, source_target_pairs={{0,1},{1,0},{2,3},{3,2},{4,5},{5,4},{6,7},{7,6},{8,9},{9,8},{10,11... | collective-permute-start | bytes 393224 | tf_op jit(solution)/shard_map/ppermute | solution.py:486

commit v16 on v15

--- a/solution.py
+++ b/solution.py
@@ -515,21 +515,25 @@
         beyond = after(beyond, half_a[1][0])
     keys_2, values_2 = keys_and_values(across, wk, wv)
     keys_3, values_3, kept_b = second(after(beyond, keys_2), wk, wv, keys_2, values_2, pattern)
+    sent_later = again(kept_b)
+    query_a, query_b, wo = query([after(mine, sent_later), beside, across, beyond], w_query, w_out)
     near = [keys_0, keys_1, keys_2, keys_3], [values_0, values_1, values_2, values_3]
     call = functools.partial(attend, masks, few)
     if few:
         along_z = first_round(kept_b)
-        along_y = swap(again(kept_b), Y_BIT, "seq")
-        *along_z, along_y, half_a[1][1] = lax.optimization_barrier(
-            (*along_z, along_y, half_a[1][1])
+        along_y = swap(sent_later, Y_BIT, "seq")
+        diagonal = swap(sent_later, Z_BITS[-1] | Y_BIT, "seq")
+        *along_z, along_y, diagonal, query_b, half_a[1][1] = lax.optimization_barrier(
+            (*along_z, along_y, diagonal, query_b, half_a[1][1])
         )
-        column, other = second_round(along_z)
-        half_b = 1, [kept_b[None], column, along_y[None], other]
-        mine = after(mine, column)
+        column, other = second_round(along_z[:-1])
+        nearest = along_z[-1][None]
+        half_b = 1, [kept_b[None], column, nearest, along_y[None], other, diagonal[None]]
+        asked = after(query_b, column)
     else:
         half_b = 1, [lax.all_gather(kept_b, "seq", axis=0)]
-    query_a, query_b, wo = query([mine, beside, across, beyond], w_query, w_out)
-    begun = call(2 * BLOCK, query_b, [half_a], near=near, finish=False)
+        asked = query_b
+    begun = call(2 * BLOCK, asked, [half_a], near=near, finish=False)
     keep_b, send_b = call(2 * BLOCK, query_b, [half_b], begun=begun)
     other_b = swap(send_b, 1)
     leaving = mix(other_b, wo_beside, BF16, mix(keep_b, wo, F32))

time: 53.2 us -> 54.1 us (1.017)
  starting transfers between devices: 17 us -> 19.1 us
  waiting for transfers between devices: 19.2 us -> 18 us
    ppermute x16 -> x17, starting transfers between devices: 17 us -> 19.1 us  [swap(): return lax.ppermute(array, axis, [(i, i ^ bit) for i in range(count)])]
    ppermute x16 -> x17, waiting for transfers between devices: 19.2 us -> 18 us  [swap(): return lax.ppermute(array, axis, [(i, i ^ bit) for i in range(count)])]
  transfers between devices with their start and end apart: 16 -> 17, of which waited for: 11 -> 9; matrix products, arithmetic and copies ran while one was open for 0% -> 0% of each run, Pallas kernels for 27% -> 27%
where the time goes in v16:
time: 54.1 us; the launch traced here: 54 us
  starting transfers between devices  19.1 us (35%)
  waiting for transfers between devices  18 us (33%)
  Pallas kernels  16.5 us (30%)
    ppermute x17, starting transfers between devices, swap(): return lax.ppermute(array, axis, [(i, i ^ bit) for i in range(count)])  19.1 us
    ppermute x17, waiting for transfers between devices, swap(): return lax.ppermute(array, axis, [(i, i ^ bit) for i in range(count)])  18 us
    pallas_call x3, Pallas kernels, attend(): pl.pallas_call(functools.partial(attend_kernel, first_row, near is not No...  4.78 us
    pallas_call x1, Pallas kernels, first(): pl.pallas_call(first_kernel, in_specs=[IN_HBM] * 3, out_specs=[IN_VMEM] *...  2.92 us
    pallas_call x1, Pallas kernels, query(): pl.pallas_call(query_kernel, in_specs=[IN_VMEM] * 4 + [IN_HBM] * 2, out_s...  2.9 us
    pallas_call x2, Pallas kernels, second(): pl.pallas_call(second_kernel, in_specs=[IN_VMEM] * 6, out_specs=[IN_VMEM]...  1.81 us
    pallas_call x4, Pallas kernels, mix(): pl.pallas_call(functools.partial(mix_kernel, begun is not None), in_specs...  1.8 us
  transfers between devices with their start and end apart: 17, of which 9 were waited for; matrix products, arithmetic and copies ran while one was open for 0% of the time, Pallas kernels for 27%

profile of v16, /device:TPU:0, one launch (start us, length us, event | category | flops | bytes accessed | tf_op | source)
XLA Modules:
  0.0 54.0 jit_solution(4855607627791833575)
XLA Ops:
  0.0 0.5 collective-permute-start.5
  0.5 2.9 %collective-permute-start.4 = (bf16[128,2048]{1,0:T(8,128)(2,1)}, bf16[128,2048]{1,0:T(8,128)(2,1)S(1)}, u32[]{:S(2)}, u32[]{:S(2)}) collective-permute-start(bf16[128,2048]{1,0:T(8,128)(2,1)} %rows_hbm.1), channel_id=1, source_target_pairs={{0,2},{1,3},{2,0},{3,1},{4,6},{5,7},{6,4},{7,5},{8,10},{9,11},{10,... | collective-permute-start | bytes 1572872 | tf_op jit(solution)/shard_map/ppermute | solution.py:486
  3.5 2.9 %shard_map.73 = (bf16[128,2048]{1,0:T(8,128)(2,1)S(1)}, bf16[2048,512]{1,0:T(8,128)(2,1)S(1)}, bf16[2048,512]{1,0:T(8,128)(2,1)S(1)}, bf16[128,512]{1,0:T(8,128)(2,1)S(1)}, bf16[128,512]{1,0:T(8,128)(2,1)S(1)}) custom-call(bf16[128,2048]{1,0:T(8,128)(2,1)} %rows_hbm.1, bf16[2048,512]{1,0:T(8,128)(2,1)} %wk_hbm.1, bf16[2048,512]{1,0:T(8,128)(2,1)} %wv_hbm.1), custom_call_target="tpu_custom_call" | custom-call | flops 5368709 | bytes 41943 | tf_op jit(solution)/shard_map/pallas_call | solution.py:106
  6.4 0.9 %shard_map.74 = (bf16[128,512]{1,0:T(8,128)(2,1)S(1)}, bf16[128,512]{1,0:T(8,128)(2,1)S(1)}, bf16[2,4,32,128]{3,2,1,0:T(8,128)(2,1)S(1)}) custom-call(bf16[128,2048]{1,0:T(8,128)(2,1)S(1)} %collective-permute-done.rows.refs_1_, bf16[2048,512]{1,0:T(8,128)(2,1)S(1)} %get-tuple-element.47.wk, bf16[2048,512]{1,0:T(8,128)(2,1)S(1)} %get-tuple-element.48.wv, ...), custom_call_target="tpu_custom_call" | custom-call | flops 5368709 | bytes 5242 | tf_op jit(solution)/shard_map/pallas_call | solution.py:138
  7.3 2.8 %collective-permute-start.1 = (bf16[2,4,32,128]{3,2,1,0:T(8,128)(2,1)S(1)}, bf16[2,4,32,128]{3,2,1,0:T(8,128)(2,1)S(1)}, u32[]{:S(2)}, u32[]{:S(2)}) collective-permute-start(bf16[2,4,32,128]{3,2,1,0:T(8,128)(2,1)S(1)} %get-tuple-element.51), channel_id=1, source_target_pairs={{0,16},{4,20},{8,24},{12,28},{16,0},{20,4},{24,8},{28,12},{1,17},{... | collective-permute-start | bytes 196616 | tf_op jit(solution)/shard_map/ppermute | solution.py:486
  10.1 1.3 %collective-permute-start.2 = (bf16[2,4,32,128]{3,2,1,0:T(8,128)(2,1)S(1)}, bf16[2,4,32,128]{3,2,1,0:T(8,128)(2,1)S(1)}, u32[]{:S(2)}, u32[]{:S(2)}) collective-permute-start(bf16[2,4,32,128]{3,2,1,0:T(8,128)(2,1)S(1)} %get-tuple-element.51), channel_id=1, source_target_pairs={{0,24},{4,28},{8,16},{12,20},{16,8},{20,12},{24,0},{28,4},{1,25},{... | collective-permute-start | bytes 196616 | tf_op jit(solution)/shard_map/ppermute | solution.py:486
  11.7 0.7 %shard_map.75 = (bf16[512,128]{1,0:T(8,128)(2,1)S(1)}, bf16[1024,128]{1,0:T(8,128)(2,1)S(1)}) custom-call(s32[10]{0:T(128)S(1)} %pad_add_fusion.place), custom_call_target="tpu_custom_call" | custom-call | flops 83886 | bytes 2621 | tf_op jit(solution)/shard_map/pallas_call | solution.py:254
  12.4 1.6 %collective-permute-done.1 = bf16[2,4,32,128]{3,2,1,0:T(8,128)(2,1)S(1)} collective-permute-done((bf16[2,4,32,128]{3,2,1,0:T(8,128)(2,1)S(1)}, bf16[2,4,32,128]{3,2,1,0:T(8,128)(2,1)S(1)}, u32[]{:S(2)}, u32[]{:S(2)}) %collective-permute-start.1) | collective-permute-done | bytes 65568 | tf_op jit(solution)/shard_map/ppermute | solution.py:486
  14.1 2.4 %collective-permute-done.2 = bf16[2,4,32,128]{3,2,1,0:T(8,128)(2,1)S(1)} collective-permute-done((bf16[2,4,32,128]{3,2,1,0:T(8,128)(2,1)S(1)}, bf16[2,4,32,128]{3,2,1,0:T(8,128)(2,1)S(1)}, u32[]{:S(2)}, u32[]{:S(2)}) %collective-permute-start.2) | collective-permute-done | bytes 65568 | tf_op jit(solution)/shard_map/ppermute | solution.py:486
  16.7 1.7 %collective-permute-start.12 = (bf16[4,2,4,32,128]{4,3,2,1,0:T(8,128)(2,1)S(1)}, bf16[4,2,4,32,128]{4,3,2,1,0:T(8,128)(2,1)S(1)}, u32[]{:S(2)}, u32[]{:S(2)}) collective-permute-start(bf16[4,2,4,32,128]{4,3,2,1,0:T(8,128)(2,1)S(1)} %pad_maximum_fusion.refs_9_), channel_id=1, source_target_pairs={{0,4},{4,0},{8,12},{12,8},{16,20},{20,16},{24,28},{28,24},{1,5},{5... | collective-permute-start | bytes 786440 | tf_op jit(solution)/shard_map/ppermute | solution.py:486
  18.4 0.8 %shard_map.76 = (bf16[128,512]{1,0:T(8,128)(2,1)S(1)}, bf16[128,512]{1,0:T(8,128)(2,1)S(1)}) custom-call(bf16[128,2048]{1,0:T(8,128)(2,1)S(1)} %collective-permute-done.4.rows.refs_2_, bf16[2048,512]{1,0:T(8,128)(2,1)S(1)} %get-tuple-element.47.wk, bf16[2048,512]{1,0:T(8,128)(2,1)S(1)} %get-tuple-element.48.wv), custom_call_target="tpu_custom_call" | custom-call | flops 5368709 | bytes 5242 | tf_op jit(solution)/shard_map/pallas_call | solution.py:203
  19.2 0.9 %shard_map.77 = (bf16[128,512]{1,0:T(8,128)(2,1)S(1)}, bf16[128,512]{1,0:T(8,128)(2,1)S(1)}, bf16[2,4,32,128]{3,2,1,0:T(8,128)(2,1)S(1)}) custom-call(bf16[128,2048]{1,0:T(8,128)(2,1)S(1)} %collective-permute-done.6.rows.refs_3_, bf16[2048,512]{1,0:T(8,128)(2,1)S(1)} %get-tuple-element.47.wk, bf16[2048,512]{1,0:T(8,128)(2,1)S(1)} %get-tuple-element.48.wv, ...), custom_call_target="tpu_custom_call" | custom-call | flops 5368709 | bytes 5242 | tf_op jit(solution)/shard_map/pallas_call | solution.py:138
  20.1 2.7 %collective-permute-start.7 = (bf16[2,4,32,128]{3,2,1,0:T(8,128)(2,1)S(1)}, bf16[2,4,32,128]{3,2,1,0:T(8,128)(2,1)S(1)}, u32[]{:S(2)}, u32[]{:S(2)}) collective-permute-start(bf16[2,4,32,128]{3,2,1,0:T(8,128)(2,1)S(1)} %get-tuple-element.65.source), channel_id=1, source_target_pairs={{0,16},{4,20},{8,24},{12,28},{16,0},{20,4},{24,8},{28,12},{1,17},{... | collective-permute-start | bytes 196616 | tf_op jit(solution)/shard_map/ppermute | solution.py:486
  22.9 0.6 %collective-permute-start.8 = (bf16[2,4,32,128]{3,2,1,0:T(8,128)(2,1)S(1)}, bf16[2,4,32,128]{3,2,1,0:T(8,128)(2,1)S(1)}, u32[]{:S(2)}, u32[]{:S(2)}) collective-permute-start(bf16[2,4,32,128]{3,2,1,0:T(8,128)(2,1)S(1)} %get-tuple-element.65.source), channel_id=1, source_target_pairs={{0,24},{4,28},{8,16},{12,20},{16,8},{20,12},{24,0},{28,4},{1,25},{... | collective-permute-start | bytes 196616 | tf_op jit(solution)/shard_map/ppermute | solution.py:486
  23.4 0.5 collective-permute-start.9
  23.9 1.0 %collective-permute-start.10 = (bf16[2,4,32,128]{3,2,1,0:T(8,128)(2,1)S(1)}, bf16[2,4,32,128]{3,2,1,0:T(8,128)(2,1)S(1)}, u32[]{:S(2)}, u32[]{:S(2)}) collective-permute-start(bf16[2,4,32,128]{3,2,1,0:T(8,128)(2,1)S(1)} %shard_map.78), channel_id=1, source_target_pairs={{0,4},{4,0},{8,12},{12,8},{16,20},{20,16},{24,28},{28,24},{1,5},{5... | collective-permute-start | bytes 196616 | tf_op jit(solution)/shard_map/ppermute | solution.py:486
  24.9 0.5 collective-permute-done.12.refs_10_
  25.5 1.9 %collective-permute-start.11 = (bf16[2,4,32,128]{3,2,1,0:T(8,128)(2,1)S(1)}, bf16[2,4,32,128]{3,2,1,0:T(8,128)(2,1)S(1)}, u32[]{:S(2)}, u32[]{:S(2)}) collective-permute-start(bf16[2,4,32,128]{3,2,1,0:T(8,128)(2,1)S(1)} %shard_map.78), channel_id=1, source_target_pairs={{0,12},{4,8},{8,4},{12,0},{16,28},{20,24},{24,20},{28,16},{1,13},{... | collective-permute-start | bytes 196616 | tf_op jit(solution)/shard_map/ppermute | solution.py:486
  27.4 2.9 %shard_map.79 = (bf16[256,512]{1,0:T(8,128)(2,1)S(1)}, bf16[256,512]{1,0:T(8,128)(2,1)S(1)}, bf16[512,2048]{1,0:T(8,128)(2,1)S(1)}) custom-call(bf16[128,2048]{1,0:T(8,128)(2,1)S(1)} %get-tuple-element.66.refs_0_, bf16[128,2048]{1,0:T(8,128)(2,1)S(1)} %collective-permute-done.rows.refs_1_, bf16[128,2048]{1,0:T(8,128)(2,1)S(1)} %collective-permute-done.4.rows.refs_2_, ...), custom_call_target="tpu_custom_call" | custom-call | flops 10737418 | bytes 41943 | tf_op jit(solution)/shard_map/pallas_call | solution.py:165
  30.3 1.0 %collective-permute-done.11 = bf16[2,4,32,128]{3,2,1,0:T(8,128)(2,1)S(1)} collective-permute-done((bf16[2,4,32,128]{3,2,1,0:T(8,128)(2,1)S(1)}, bf16[2,4,32,128]{3,2,1,0:T(8,128)(2,1)S(1)}, u32[]{:S(2)}, u32[]{:S(2)}) %collective-permute-start.11) | collective-permute-done | bytes 65568 | tf_op jit(solution)/shard_map/ppermute | solution.py:486
  31.3 1.2 %collective-permute-start.13 = (bf16[2,2,4,32,128]{4,3,2,1,0:T(8,128)(2,1)S(1)}, bf16[2,2,4,32,128]{4,3,2,1,0:T(8,128)(2,1)S(1)}, u32[]{:S(2)}, u32[]{:S(2)}) collective-permute-start(bf16[2,2,4,32,128]{4,3,2,1,0:T(8,128)(2,1)S(1)} %pad_maximum_fusion.1.refs_4_.refs_12_), channel_id=1, source_target_pairs={{0,4},{4,0},{8,12},{12,8},{16,20},{20,16},{24,28},{28,24},{1,5},{5... | collective-permute-start | bytes 393224 | tf_op jit(solution)/shard_map/ppermute | solution.py:486
  32.5 1.9 %shard_map.80 = (f32[4,128,256]{2,1,0:T(8,128)S(1)}, f32[4,8,256]{2,1,0:T(8,128)S(1)}) custom-call(bf16[512,128]{1,0:T(8,128)(2,1)S(1)} %get-tuple-element.54.asking, bf16[1024,128]{1,0:T(8,128)(2,1)S(1)} %get-tuple-element.55.asked_of, bf16[256,512]{1,0:T(8,128)(2,1)S(1)} %get-tuple-element.72.refs_0_, ...), custom_call_target="tpu_custom_call" | custom-call | flops 4026531 | bytes 5242 | tf_op jit(solution)/shard_map/pallas_call | solution.py:410
  34.4 2.0 %collective-permute-done.13.refs_7_.refs_15_ = bf16[2,2,4,32,128]{4,3,2,1,0:T(8,128)(2,1)S(1)} collective-permute-done((bf16[2,2,4,32,128]{4,3,2,1,0:T(8,128)(2,1)S(1)}, bf16[2,2,4,32,128]{4,3,2,1,0:T(8,128)(2,1)S(1)}, u32[]{:S(2)}, u32[]{:S(2)}) %collective-permute-start.13) | collective-permute-done | bytes 131104 | tf_op jit(solution)/shard_map/ppermute | solution.py:486
  36.4 0.8 %shard_map.81 = (bf16[128,512]{1,0:T(8,128)(2,1)S(1)}, bf16[128,512]{1,0:T(8,128)(2,1)S(1)}) custom-call(bf16[512,128]{1,0:T(8,128)(2,1)S(1)} %get-tuple-element.54.asking, bf16[1024,128]{1,0:T(8,128)(2,1)S(1)} %get-tuple-element.55.asked_of, bf16[256,512]{1,0:T(8,128)(2,1)S(1)} %get-tuple-element.72.refs_0_, f32[4,128,256]{2,1,0:T(8,128)S(1)} %get-tuple-element.78.refs_1_, ...), custom_call_target="tpu_custom_call" | custom-call | flops 1342177 | bytes 5242 | tf_op jit(solution)/shard_map/pallas_call | solution.py:410
  37.7 0.9 %collective-permute-done.14.rows = bf16[128,512]{1,0:T(8,128)(2,1)S(1)} collective-permute-done((bf16[128,512]{1,0:T(8,128)(2,1)S(1)}, bf16[128,512]{1,0:T(8,128)(2,1)S(1)}, u32[]{:S(2)}, u32[]{:S(2)}) %collective-permute-start.14) | collective-permute-done | bytes 131104 | tf_op jit(solution)/shard_map/ppermute | solution.py:486
  38.6 0.5 shard_map.83
  39.1 1.6 %collective-permute-start.16 = (bf16[128,2048]{1,0:T(8,128)(2,1)S(1)}, bf16[128,2048]{1,0:T(8,128)(2,1)S(1)}, u32[]{:S(2)}, u32[]{:S(2)}) collective-permute-start(bf16[128,2048]{1,0:T(8,128)(2,1)S(1)} %shard_map.83), channel_id=1, source_target_pairs={{0,2},{1,3},{2,0},{3,1},{4,6},{5,7},{6,4},{7,5},{8,10},{9,11},{10,... | collective-permute-start | bytes 1572872 | tf_op jit(solution)/shard_map/ppermute | solution.py:486
  40.7 2.1 %shard_map.84 = (bf16[128,512]{1,0:T(8,128)(2,1)S(1)}, bf16[128,512]{1,0:T(8,128)(2,1)S(1)}) custom-call(bf16[512,128]{1,0:T(8,128)(2,1)S(1)} %get-tuple-element.54.asking, bf16[1024,128]{1,0:T(8,128)(2,1)S(1)} %get-tuple-element.55.asked_of, bf16[256,512]{1,0:T(8,128)(2,1)S(1)} %get-tuple-element.86.refs_0_, ...), custom_call_target="tpu_custom_call" | custom-call | flops 5368709 | bytes 5242 | tf_op jit(solution)/shard_map/pallas_call | solution.py:410
  43.3 0.9 %collective-permute-done.15.rows = bf16[128,512]{1,0:T(8,128)(2,1)S(1)} collective-permute-done((bf16[128,512]{1,0:T(8,128)(2,1)S(1)}, bf16[128,512]{1,0:T(8,128)(2,1)S(1)}, u32[]{:S(2)}, u32[]{:S(2)}) %collective-permute-start.15) | collective-permute-done | bytes 131104 | tf_op jit(solution)/shard_map/ppermute | solution.py:486
  44.2 0.5 shard_map.86.own
  44.7 8.4 %collective-permute-done.16.arriving = bf16[128,2048]{1,0:T(8,128)(2,1)S(1)} collective-permute-done((bf16[128,2048]{1,0:T(8,128)(2,1)S(1)}, bf16[128,2048]{1,0:T(8,128)(2,1)S(1)}, u32[]{:S(2)}, u32[]{:S(2)}) %collective-permute-start.16) | collective-permute-done | bytes 524320 | tf_op jit(solution)/shard_map/ppermute | solution.py:486
  53.1 0.8 %shard_map.87 = bf16[128,2048]{1,0:T(8,128)(2,1)} custom-call(f32[128,2048]{1,0:T(8,128)S(1)} %shard_map.86.own, bf16[128,2048]{1,0:T(8,128)(2,1)S(1)} %collective-permute-done.16.arriving), custom_call_target="tpu_custom_call" | custom-call | flops 2621 | bytes 20971 | tf_op jit(solution)/shard_map/pallas_call | solution.py:468
  (24 shorter events, 1.6 us)
Async XLA Ops:
  0.0 16.7 %collective-permute-start.5 = (bf16[512,2048]{1,0:T(8,128)(2,1)}, bf16[512,2048]{1,0:T(8,128)(2,1)S(1)}, u32[]{:S(2)}, u32[]{:S(2)}) collective-permute-start(bf16[512,2048]{1,0:T(8,128)(2,1)} %refs_5_.1), channel_id=1, source_target_pairs={{0,1},{1,0},{2,3},{3,2},{4,5},{5,4},{6,7},{7,6},{8,9},{9,8},{10,11... | collective-permute-start | bytes 6291464 | tf_op jit(solution)/shard_map/ppermute | solution.py:486
  0.5 5.9 %collective-permute-start = (bf16[128,2048]{1,0:T(8,128)(2,1)}, bf16[128,2048]{1,0:T(8,128)(2,1)S(1)}, u32[]{:S(2)}, u32[]{:S(2)}) collective-permute-start(bf16[128,2048]{1,0:T(8,128)(2,1)} %rows_hbm.1), channel_id=1, source_target_pairs={{0,1},{1,0},{2,3},{3,2},{4,5},{5,4},{6,7},{7,6},{8,9},{9,8},{10,11... | collective-permute-start | bytes 1572872 | tf_op jit(solution)/shard_map/ppermute | solution.py:486
  0.5 16.1 %collective-permute-start.4 = (bf16[128,2048]{1,0:T(8,128)(2,1)}, bf16[128,2048]{1,0:T(8,128)(2,1)S(1)}, u32[]{:S(2)}, u32[]{:S(2)}) collective-permute-start(bf16[128,2048]{1,0:T(8,128)(2,1)} %rows_hbm.1), channel_id=1, source_target_pairs={{0,2},{1,3},{2,0},{3,1},{4,6},{5,7},{6,4},{7,5},{8,10},{9,11},{10,... | collective-permute-start | bytes 1572872 | tf_op jit(solution)/shard_map/ppermute | solution.py:486
  3.5 2.9 %copy-start = (s32[4,128]{1,0:T(4,128)S(1)}, s32[4,128]{1,0:T(4,128)}, u32[]{:S(2)}) copy-start(s32[4,128]{1,0:T(4,128)} %pattern.3) | copy-start | bytes 6148
  6.4 5.3 %copy-start.1 = (s32[8]{0:T(128)S(1)}, s32[8]{0:T(128)}, u32[]{:S(2)}) copy-start(s32[8]{0:T(128)} %param.13) | copy-start | bytes 100
  7.3 6.8 %collective-permute-start.1 = (bf16[2,4,32,128]{3,2,1,0:T(8,128)(2,1)S(1)}, bf16[2,4,32,128]{3,2,1,0:T(8,128)(2,1)S(1)}, u32[]{:S(2)}, u32[]{:S(2)}) collective-permute-start(bf16[2,4,32,128]{3,2,1,0:T(8,128)(2,1)S(1)} %get-tuple-element.51), channel_id=1, source_target_pairs={{0,16},{4,20},{8,24},{12,28},{16,0},{20,4},{24,8},{28,12},{1,17},{... | collective-permute-start | bytes 196616 | tf_op jit(solution)/shard_map/ppermute | solution.py:486
  10.1 6.4 %collective-permute-start.2 = (bf16[2,4,32,128]{3,2,1,0:T(8,128)(2,1)S(1)}, bf16[2,4,32,128]{3,2,1,0:T(8,128)(2,1)S(1)}, u32[]{:S(2)}, u32[]{:S(2)}) collective-permute-start(bf16[2,4,32,128]{3,2,1,0:T(8,128)(2,1)S(1)} %get-tuple-element.51), channel_id=1, source_target_pairs={{0,24},{4,28},{8,16},{12,20},{16,8},{20,12},{24,0},{28,4},{1,25},{... | collective-permute-start | bytes 196616 | tf_op jit(solution)/shard_map/ppermute | solution.py:486
  11.4 5.2 %collective-permute-start.3 = (bf16[2,4,32,128]{3,2,1,0:T(8,128)(2,1)S(1)}, bf16[2,4,32,128]{3,2,1,0:T(8,128)(2,1)S(1)}, u32[]{:S(2)}, u32[]{:S(2)}) collective-permute-start(bf16[2,4,32,128]{3,2,1,0:T(8,128)(2,1)S(1)} %get-tuple-element.51), channel_id=1, source_target_pairs={{0,8},{4,12},{8,0},{12,4},{16,24},{20,28},{24,16},{28,20},{1,9},{5... | collective-permute-start | bytes 196616 | tf_op jit(solution)/shard_map/ppermute | solution.py:486
  16.7 2.6 %collective-permute-start.6 = (bf16[128,2048]{1,0:T(8,128)(2,1)S(1)}, bf16[128,2048]{1,0:T(8,128)(2,1)S(1)}, u32[]{:S(2)}, u32[]{:S(2)}) collective-permute-start(bf16[128,2048]{1,0:T(8,128)(2,1)S(1)} %collective-permute-done.4.rows.refs_2_), channel_id=1, source_target_pairs={{0,1},{1,0},{2,3},{3,2},{4,5},{5,4},{6,7},{7,6},{8,9},{9,8},{10,11... | collective-permute-start | bytes 1572872 | tf_op jit(solution)/shard_map/ppermute | solution.py:486
  16.7 8.8 %collective-permute-start.12 = (bf16[4,2,4,32,128]{4,3,2,1,0:T(8,128)(2,1)S(1)}, bf16[4,2,4,32,128]{4,3,2,1,0:T(8,128)(2,1)S(1)}, u32[]{:S(2)}, u32[]{:S(2)}) collective-permute-start(bf16[4,2,4,32,128]{4,3,2,1,0:T(8,128)(2,1)S(1)} %pad_maximum_fusion.refs_9_), channel_id=1, source_target_pairs={{0,4},{4,0},{8,12},{12,8},{16,20},{20,16},{24,28},{28,24},{1,5},{5... | collective-permute-start | bytes 786440 | tf_op jit(solution)/shard_map/ppermute | solution.py:486
  20.1 10.1 %collective-permute-start.7 = (bf16[2,4,32,128]{3,2,1,0:T(8,128)(2,1)S(1)}, bf16[2,4,32,128]{3,2,1,0:T(8,128)(2,1)S(1)}, u32[]{:S(2)}, u32[]{:S(2)}) collective-permute-start(bf16[2,4,32,128]{3,2,1,0:T(8,128)(2,1)S(1)} %get-tuple-element.65.source), channel_id=1, source_target_pairs={{0,16},{4,20},{8,24},{12,28},{16,0},{20,4},{24,8},{28,12},{1,17},{... | collective-permute-start | bytes 196616 | tf_op jit(solution)/shard_map/ppermute | solution.py:486
  22.9 7.4 %collective-permute-start.8 = (bf16[2,4,32,128]{3,2,1,0:T(8,128)(2,1)S(1)}, bf16[2,4,32,128]{3,2,1,0:T(8,128)(2,1)S(1)}, u32[]{:S(2)}, u32[]{:S(2)}) collective-permute-start(bf16[2,4,32,128]{3,2,1,0:T(8,128)(2,1)S(1)} %get-tuple-element.65.source), channel_id=1, source_target_pairs={{0,24},{4,28},{8,16},{12,20},{16,8},{20,12},{24,0},{28,4},{1,25},{... | collective-permute-start | bytes 196616 | tf_op jit(solution)/shard_map/ppermute | solution.py:486
  23.4 6.8 %collective-permute-start.9 = (bf16[2,4,32,128]{3,2,1,0:T(8,128)(2,1)S(1)}, bf16[2,4,32,128]{3,2,1,0:T(8,128)(2,1)S(1)}, u32[]{:S(2)}, u32[]{:S(2)}) collective-permute-start(bf16[2,4,32,128]{3,2,1,0:T(8,128)(2,1)S(1)} %get-tuple-element.65.source), channel_id=1, source_target_pairs={{0,8},{4,12},{8,0},{12,4},{16,24},{20,28},{24,16},{28,20},{1,9},{5... | collective-permute-start | bytes 196616 | tf_op jit(solution)/shard_map/ppermute | solution.py:486
  23.9 6.4 %collective-permute-start.10 = (bf16[2,4,32,128]{3,2,1,0:T(8,128)(2,1)S(1)}, bf16[2,4,32,128]{3,2,1,0:T(8,128)(2,1)S(1)}, u32[]{:S(2)}, u32[]{:S(2)}) collective-permute-start(bf16[2,4,32,128]{3,2,1,0:T(8,128)(2,1)S(1)} %shard_map.78), channel_id=1, source_target_pairs={{0,4},{4,0},{8,12},{12,8},{16,20},{20,16},{24,28},{28,24},{1,5},{5... | collective-permute-start | bytes 196616 | tf_op jit(solution)/shard_map/ppermute | solution.py:486
  25.5 5.8 %collective-permute-start.11 = (bf16[2,4,32,128]{3,2,1,0:T(8,128)(2,1)S(1)}, bf16[2,4,32,128]{3,2,1,0:T(8,128)(2,1)S(1)}, u32[]{:S(2)}, u32[]{:S(2)}) collective-permute-start(bf16[2,4,32,128]{3,2,1,0:T(8,128)(2,1)S(1)} %shard_map.78), channel_id=1, source_target_pairs={{0,12},{4,8},{8,4},{12,0},{16,28},{20,24},{24,20},{28,16},{1,13},{... | collective-permute-start | bytes 196616 | tf_op jit(solution)/shard_map/ppermute | solution.py:486
  31.3 5.1 %collective-permute-start.13 = (bf16[2,2,4,32,128]{4,3,2,1,0:T(8,128)(2,1)S(1)}, bf16[2,2,4,32,128]{4,3,2,1,0:T(8,128)(2,1)S(1)}, u32[]{:S(2)}, u32[]{:S(2)}) collective-permute-start(bf16[2,2,4,32,128]{4,3,2,1,0:T(8,128)(2,1)S(1)} %pad_maximum_fusion.1.refs_4_.refs_12_), channel_id=1, source_target_pairs={{0,4},{4,0},{8,12},{12,8},{16,20},{20,16},{24,28},{28,24},{1,5},{5... | collective-permute-start | bytes 393224 | tf_op jit(solution)/shard_map/ppermute | solution.py:486
  37.2 1.4 %collective-permute-start.14 = (bf16[128,512]{1,0:T(8,128)(2,1)S(1)}, bf16[128,512]{1,0:T(8,128)(2,1)S(1)}, u32[]{:S(2)}, u32[]{:S(2)}) collective-permute-start(bf16[128,512]{1,0:T(8,128)(2,1)S(1)} %get-tuple-element.83), channel_id=1, source_target_pairs={{0,1},{1,0},{2,3},{3,2},{4,5},{5,4},{6,7},{7,6},{8,9},{9,8},{10,11... | collective-permute-start | bytes 393224 | tf_op jit(solution)/shard_map/ppermute | solution.py:486
  39.1 14.0 %collective-permute-start.16 = (bf16[128,2048]{1,0:T(8,128)(2,1)S(1)}, bf16[128,2048]{1,0:T(8,128)(2,1)S(1)}, u32[]{:S(2)}, u32[]{:S(2)}) collective-permute-start(bf16[128,2048]{1,0:T(8,128)(2,1)S(1)} %shard_map.83), channel_id=1, source_target_pairs={{0,2},{1,3},{2,0},{3,1},{4,6},{5,7},{6,4},{7,5},{8,10},{9,11},{10,... | collective-permute-start | bytes 1572872 | tf_op jit(solution)/shard_map/ppermute | solution.py:486
  42.8 1.4 %collective-permute-start.15 = (bf16[128,512]{1,0:T(8,128)(2,1)S(1)}, bf16[128,512]{1,0:T(8,128)(2,1)S(1)}, u32[]{:S(2)}, u32[]{:S(2)}) collective-permute-start(bf16[128,512]{1,0:T(8,128)(2,1)S(1)} %get-tuple-element.87), channel_id=1, source_target_pairs={{0,1},{1,0},{2,3},{3,2},{4,5},{5,4},{6,7},{7,6},{8,9},{9,8},{10,11... | collective-permute-start | bytes 393224 | tf_op jit(solution)/shard_map/ppermute | solution.py:486

commit v17 on v16

--- a/solution.py
+++ b/solution.py
@@ -313,7 +313,7 @@
     half_count = (asked_of.shape[0] - span) // BLOCKS_HALF
 
     heads = queries.shape[1] // HEAD_SIZE
-    group = 1 if not few else min(2, heads) if near else heads
+    group = 1 if not few else heads
 
     def some_heads(turn, _):
         those = [turn * group + i for i in range(group)]
@@ -516,24 +516,23 @@
     keys_2, values_2 = keys_and_values(across, wk, wv)
     keys_3, values_3, kept_b = second(after(beyond, keys_2), wk, wv, keys_2, values_2, pattern)
     sent_later = again(kept_b)
-    query_a, query_b, wo = query([after(mine, sent_later), beside, across, beyond], w_query, w_out)
     near = [keys_0, keys_1, keys_2, keys_3], [values_0, values_1, values_2, values_3]
     call = functools.partial(attend, masks, few)
     if few:
         along_z = first_round(kept_b)
         along_y = swap(sent_later, Y_BIT, "seq")
         diagonal = swap(sent_later, Z_BITS[-1] | Y_BIT, "seq")
-        *along_z, along_y, diagonal, query_b, half_a[1][1] = lax.optimization_barrier(
-            (*along_z, along_y, diagonal, query_b, half_a[1][1])
+        *along_z, along_y, diagonal, half_a[1][1] = lax.optimization_barrier(
+            (*along_z, along_y, diagonal, half_a[1][1])
         )
         column, other = second_round(along_z[:-1])
         nearest = along_z[-1][None]
         half_b = 1, [kept_b[None], column, nearest, along_y[None], other, diagonal[None]]
-        asked = after(query_b, column)
+        mine = after(mine, column)
     else:
         half_b = 1, [lax.all_gather(kept_b, "seq", axis=0)]
-        asked = query_b
-    begun = call(2 * BLOCK, asked, [half_a], near=near, finish=False)
+    query_a, query_b, wo = query([mine, beside, across, beyond], w_query, w_out)
+    begun = call(2 * BLOCK, query_b, [half_a], near=near, finish=False)
     keep_b, send_b = call(2 * BLOCK, query_b, [half_b], begun=begun)
     other_b = swap(send_b, 1)
     leaving = mix(other_b, wo_beside, BF16, mix(keep_b, wo, F32))

time: 54.1 us -> 54.5 us (level)
  waiting for transfers between devices: 18 us -> 19.3 us
  Pallas kernels: 16.5 us -> 15.7 us
    ppermute x17, waiting for transfers between devices: 18 us -> 19.3 us  [swap(): return lax.ppermute(array, axis, [(i, i ^ bit) for i in range(count)])]
    pallas_call x3, Pallas kernels: 4.78 us -> 3.93 us  [attend(): pl.pallas_call(functools.partial(attend_kernel, first_row, near is not No...]
  transfers between devices with their start and end apart: 17 -> 17, of which waited for: 9 -> 11; matrix products, arithmetic and copies ran while one was open for 0% -> 0% of each run, Pallas kernels for 27% -> 25%
where the time goes in v17:
time: 54.5 us; the launch traced here: 54.3 us
  waiting for transfers between devices  19.3 us (35%)
  starting transfers between devices  19 us (35%)
  Pallas kernels  15.7 us (29%)
    ppermute x17, waiting for transfers between devices, swap(): return lax.ppermute(array, axis, [(i, i ^ bit) for i in range(count)])  19.3 us
    ppermute x17, starting transfers between devices, swap(): return lax.ppermute(array, axis, [(i, i ^ bit) for i in range(count)])  19 us
    pallas_call x3, Pallas kernels, attend(): pl.pallas_call(functools.partial(attend_kernel, first_row, near is not No...  3.93 us
    pallas_call x1, Pallas kernels, first(): pl.pallas_call(first_kernel, in_specs=[IN_HBM] * 3, out_specs=[IN_VMEM] *...  2.92 us
    pallas_call x1, Pallas kernels, query(): pl.pallas_call(query_kernel, in_specs=[IN_VMEM] * 4 + [IN_HBM] * 2, out_s...  2.9 us
    pallas_call x2, Pallas kernels, second(): pl.pallas_call(second_kernel, in_specs=[IN_VMEM] * 6, out_specs=[IN_VMEM]...  1.81 us
    pallas_call x4, Pallas kernels, mix(): pl.pallas_call(functools.partial(mix_kernel, begun is not None), in_specs...  1.8 us
  transfers between devices with their start and end apart: 17, of which 11 were waited for; matrix products, arithmetic and copies ran while one was open for 0% of the time, Pallas kernels for 25%

profile of v17, /device:TPU:0, one launch (start us, length us, event | category | flops | bytes accessed | tf_op | source)
XLA Modules:
  0.0 54.3 jit_solution(4132886498640611073)
XLA Ops:
  0.5 2.9 %collective-permute-start.4 = (bf16[128,2048]{1,0:T(8,128)(2,1)}, bf16[128,2048]{1,0:T(8,128)(2,1)S(1)}, u32[]{:S(2)}, u32[]{:S(2)}) collective-permute-start(bf16[128,2048]{1,0:T(8,128)(2,1)} %rows_hbm.1), channel_id=1, source_target_pairs={{0,2},{1,3},{2,0},{3,1},{4,6},{5,7},{6,4},{7,5},{8,10},{9,11},{10,... | collective-permute-start | bytes 1572872 | tf_op jit(solution)/shard_map/ppermute | solution.py:486
  3.5 2.9 %shard_map.73 = (bf16[128,2048]{1,0:T(8,128)(2,1)S(1)}, bf16[2048,512]{1,0:T(8,128)(2,1)S(1)}, bf16[2048,512]{1,0:T(8,128)(2,1)S(1)}, bf16[128,512]{1,0:T(8,128)(2,1)S(1)}, bf16[128,512]{1,0:T(8,128)(2,1)S(1)}) custom-call(bf16[128,2048]{1,0:T(8,128)(2,1)} %rows_hbm.1, bf16[2048,512]{1,0:T(8,128)(2,1)} %wk_hbm.1, bf16[2048,512]{1,0:T(8,128)(2,1)} %wv_hbm.1), custom_call_target="tpu_custom_call" | custom-call | flops 5368709 | bytes 41943 | tf_op jit(solution)/shard_map/pallas_call | solution.py:106
  6.4 0.9 %shard_map.74 = (bf16[128,512]{1,0:T(8,128)(2,1)S(1)}, bf16[128,512]{1,0:T(8,128)(2,1)S(1)}, bf16[2,4,32,128]{3,2,1,0:T(8,128)(2,1)S(1)}) custom-call(bf16[128,2048]{1,0:T(8,128)(2,1)S(1)} %collective-permute-done.rows.refs_1_, bf16[2048,512]{1,0:T(8,128)(2,1)S(1)} %get-tuple-element.45.wk, bf16[2048,512]{1,0:T(8,128)(2,1)S(1)} %get-tuple-element.46.wv, ...), custom_call_target="tpu_custom_call" | custom-call | flops 5368709 | bytes 5242 | tf_op jit(solution)/shard_map/pallas_call | solution.py:138
  7.3 2.8 %collective-permute-start.1 = (bf16[2,4,32,128]{3,2,1,0:T(8,128)(2,1)S(1)}, bf16[2,4,32,128]{3,2,1,0:T(8,128)(2,1)S(1)}, u32[]{:S(2)}, u32[]{:S(2)}) collective-permute-start(bf16[2,4,32,128]{3,2,1,0:T(8,128)(2,1)S(1)} %get-tuple-element.49), channel_id=1, source_target_pairs={{0,16},{4,20},{8,24},{12,28},{16,0},{20,4},{24,8},{28,12},{1,17},{... | collective-permute-start | bytes 196616 | tf_op jit(solution)/shard_map/ppermute | solution.py:486
  10.1 1.3 %collective-permute-start.2 = (bf16[2,4,32,128]{3,2,1,0:T(8,128)(2,1)S(1)}, bf16[2,4,32,128]{3,2,1,0:T(8,128)(2,1)S(1)}, u32[]{:S(2)}, u32[]{:S(2)}) collective-permute-start(bf16[2,4,32,128]{3,2,1,0:T(8,128)(2,1)S(1)} %get-tuple-element.49), channel_id=1, source_target_pairs={{0,24},{4,28},{8,16},{12,20},{16,8},{20,12},{24,0},{28,4},{1,25},{... | collective-permute-start | bytes 196616 | tf_op jit(solution)/shard_map/ppermute | solution.py:486
  11.7 0.7 %shard_map.75 = (bf16[512,128]{1,0:T(8,128)(2,1)S(1)}, bf16[1024,128]{1,0:T(8,128)(2,1)S(1)}) custom-call(s32[10]{0:T(128)S(1)} %pad_add_fusion.place), custom_call_target="tpu_custom_call" | custom-call | flops 83886 | bytes 2621 | tf_op jit(solution)/shard_map/pallas_call | solution.py:254
  12.4 1.6 %collective-permute-done.1 = bf16[2,4,32,128]{3,2,1,0:T(8,128)(2,1)S(1)} collective-permute-done((bf16[2,4,32,128]{3,2,1,0:T(8,128)(2,1)S(1)}, bf16[2,4,32,128]{3,2,1,0:T(8,128)(2,1)S(1)}, u32[]{:S(2)}, u32[]{:S(2)}) %collective-permute-start.1) | collective-permute-done | bytes 65568 | tf_op jit(solution)/shard_map/ppermute | solution.py:486
  14.1 2.4 %collective-permute-done.2 = bf16[2,4,32,128]{3,2,1,0:T(8,128)(2,1)S(1)} collective-permute-done((bf16[2,4,32,128]{3,2,1,0:T(8,128)(2,1)S(1)}, bf16[2,4,32,128]{3,2,1,0:T(8,128)(2,1)S(1)}, u32[]{:S(2)}, u32[]{:S(2)}) %collective-permute-start.2) | collective-permute-done | bytes 65568 | tf_op jit(solution)/shard_map/ppermute | solution.py:486
  16.7 1.7 %collective-permute-start.12 = (bf16[4,2,4,32,128]{4,3,2,1,0:T(8,128)(2,1)S(1)}, bf16[4,2,4,32,128]{4,3,2,1,0:T(8,128)(2,1)S(1)}, u32[]{:S(2)}, u32[]{:S(2)}) collective-permute-start(bf16[4,2,4,32,128]{4,3,2,1,0:T(8,128)(2,1)S(1)} %pad_maximum_fusion.refs_9_), channel_id=1, source_target_pairs={{0,4},{4,0},{8,12},{12,8},{16,20},{20,16},{24,28},{28,24},{1,5},{5... | collective-permute-start | bytes 786440 | tf_op jit(solution)/shard_map/ppermute | solution.py:486
  18.4 0.8 %shard_map.76 = (bf16[128,512]{1,0:T(8,128)(2,1)S(1)}, bf16[128,512]{1,0:T(8,128)(2,1)S(1)}) custom-call(bf16[128,2048]{1,0:T(8,128)(2,1)S(1)} %collective-permute-done.4.rows.refs_2_, bf16[2048,512]{1,0:T(8,128)(2,1)S(1)} %get-tuple-element.45.wk, bf16[2048,512]{1,0:T(8,128)(2,1)S(1)} %get-tuple-element.46.wv), custom_call_target="tpu_custom_call" | custom-call | flops 5368709 | bytes 5242 | tf_op jit(solution)/shard_map/pallas_call | solution.py:203
  19.2 0.9 %shard_map.77 = (bf16[128,512]{1,0:T(8,128)(2,1)S(1)}, bf16[128,512]{1,0:T(8,128)(2,1)S(1)}, bf16[2,4,32,128]{3,2,1,0:T(8,128)(2,1)S(1)}) custom-call(bf16[128,2048]{1,0:T(8,128)(2,1)S(1)} %collective-permute-done.6.rows.refs_3_, bf16[2048,512]{1,0:T(8,128)(2,1)S(1)} %get-tuple-element.45.wk, bf16[2048,512]{1,0:T(8,128)(2,1)S(1)} %get-tuple-element.46.wv, ...), custom_call_target="tpu_custom_call" | custom-call | flops 5368709 | bytes 5242 | tf_op jit(solution)/shard_map/pallas_call | solution.py:138
  20.1 2.7 %collective-permute-start.7 = (bf16[2,4,32,128]{3,2,1,0:T(8,128)(2,1)S(1)}, bf16[2,4,32,128]{3,2,1,0:T(8,128)(2,1)S(1)}, u32[]{:S(2)}, u32[]{:S(2)}) collective-permute-start(bf16[2,4,32,128]{3,2,1,0:T(8,128)(2,1)S(1)} %get-tuple-element.63.source), channel_id=1, source_target_pairs={{0,16},{4,20},{8,24},{12,28},{16,0},{20,4},{24,8},{28,12},{1,17},{... | collective-permute-start | bytes 196616 | tf_op jit(solution)/shard_map/ppermute | solution.py:486
  22.8 0.6 %collective-permute-start.8 = (bf16[2,4,32,128]{3,2,1,0:T(8,128)(2,1)S(1)}, bf16[2,4,32,128]{3,2,1,0:T(8,128)(2,1)S(1)}, u32[]{:S(2)}, u32[]{:S(2)}) collective-permute-start(bf16[2,4,32,128]{3,2,1,0:T(8,128)(2,1)S(1)} %get-tuple-element.63.source), channel_id=1, source_target_pairs={{0,24},{4,28},{8,16},{12,20},{16,8},{20,12},{24,0},{28,4},{1,25},{... | collective-permute-start | bytes 196616 | tf_op jit(solution)/shard_map/ppermute | solution.py:486
  23.4 0.5 collective-permute-start.9
  23.9 1.0 %collective-permute-start.10 = (bf16[2,4,32,128]{3,2,1,0:T(8,128)(2,1)S(1)}, bf16[2,4,32,128]{3,2,1,0:T(8,128)(2,1)S(1)}, u32[]{:S(2)}, u32[]{:S(2)}) collective-permute-start(bf16[2,4,32,128]{3,2,1,0:T(8,128)(2,1)S(1)} %shard_map.78), channel_id=1, source_target_pairs={{0,4},{4,0},{8,12},{12,8},{16,20},{20,16},{24,28},{28,24},{1,5},{5... | collective-permute-start | bytes 196616 | tf_op jit(solution)/shard_map/ppermute | solution.py:486
  24.9 0.6 %collective-permute-done.12.refs_10_ = bf16[4,2,4,32,128]{4,3,2,1,0:T(8,128)(2,1)S(1)} collective-permute-done((bf16[4,2,4,32,128]{4,3,2,1,0:T(8,128)(2,1)S(1)}, bf16[4,2,4,32,128]{4,3,2,1,0:T(8,128)(2,1)S(1)}, u32[]{:S(2)}, u32[]{:S(2)}) %collective-permute-start.12) | collective-permute-done | bytes 262176 | tf_op jit(solution)/shard_map/ppermute | solution.py:486
  25.5 1.9 %collective-permute-start.11 = (bf16[2,4,32,128]{3,2,1,0:T(8,128)(2,1)S(1)}, bf16[2,4,32,128]{3,2,1,0:T(8,128)(2,1)S(1)}, u32[]{:S(2)}, u32[]{:S(2)}) collective-permute-start(bf16[2,4,32,128]{3,2,1,0:T(8,128)(2,1)S(1)} %shard_map.78), channel_id=1, source_target_pairs={{0,12},{4,8},{8,4},{12,0},{16,28},{20,24},{24,20},{28,16},{1,13},{... | collective-permute-start | bytes 196616 | tf_op jit(solution)/shard_map/ppermute | solution.py:486
  27.4 0.6 %collective-permute-done.7 = bf16[2,4,32,128]{3,2,1,0:T(8,128)(2,1)S(1)} collective-permute-done((bf16[2,4,32,128]{3,2,1,0:T(8,128)(2,1)S(1)}, bf16[2,4,32,128]{3,2,1,0:T(8,128)(2,1)S(1)}, u32[]{:S(2)}, u32[]{:S(2)}) %collective-permute-start.7) | collective-permute-done | bytes 65568 | tf_op jit(solution)/shard_map/ppermute | solution.py:486
  28.0 1.3 %collective-permute-done.8 = bf16[2,4,32,128]{3,2,1,0:T(8,128)(2,1)S(1)} collective-permute-done((bf16[2,4,32,128]{3,2,1,0:T(8,128)(2,1)S(1)}, bf16[2,4,32,128]{3,2,1,0:T(8,128)(2,1)S(1)}, u32[]{:S(2)}, u32[]{:S(2)}) %collective-permute-start.8) | collective-permute-done | bytes 65568 | tf_op jit(solution)/shard_map/ppermute | solution.py:486
  29.7 1.6 %collective-permute-done.11 = bf16[2,4,32,128]{3,2,1,0:T(8,128)(2,1)S(1)} collective-permute-done((bf16[2,4,32,128]{3,2,1,0:T(8,128)(2,1)S(1)}, bf16[2,4,32,128]{3,2,1,0:T(8,128)(2,1)S(1)}, u32[]{:S(2)}, u32[]{:S(2)}) %collective-permute-start.11) | collective-permute-done | bytes 65568 | tf_op jit(solution)/shard_map/ppermute | solution.py:486
  31.3 1.2 %collective-permute-start.13 = (bf16[2,2,4,32,128]{4,3,2,1,0:T(8,128)(2,1)S(1)}, bf16[2,2,4,32,128]{4,3,2,1,0:T(8,128)(2,1)S(1)}, u32[]{:S(2)}, u32[]{:S(2)}) collective-permute-start(bf16[2,2,4,32,128]{4,3,2,1,0:T(8,128)(2,1)S(1)} %pad_maximum_fusion.1.refs_4_.refs_12_), channel_id=1, source_target_pairs={{0,4},{4,0},{8,12},{12,8},{16,20},{20,16},{24,28},{28,24},{1,5},{5... | collective-permute-start | bytes 393224 | tf_op jit(solution)/shard_map/ppermute | solution.py:486
  32.4 2.9 %shard_map.79 = (bf16[256,512]{1,0:T(8,128)(2,1)S(1)}, bf16[256,512]{1,0:T(8,128)(2,1)S(1)}, bf16[512,2048]{1,0:T(8,128)(2,1)S(1)}) custom-call(bf16[128,2048]{1,0:T(8,128)(2,1)S(1)} %get-tuple-element.66.refs_0_, bf16[128,2048]{1,0:T(8,128)(2,1)S(1)} %collective-permute-done.rows.refs_1_, bf16[128,2048]{1,0:T(8,128)(2,1)S(1)} %collective-permute-done.4.rows.refs_2_, ...), custom_call_target="tpu_custom_call" | custom-call | flops 10737418 | bytes 41943 | tf_op jit(solution)/shard_map/pallas_call | solution.py:165
  35.3 1.5 %shard_map.80 = (f32[4,128,256]{2,1,0:T(8,128)S(1)}, f32[4,8,256]{2,1,0:T(8,128)S(1)}) custom-call(bf16[512,128]{1,0:T(8,128)(2,1)S(1)} %get-tuple-element.52.asking, bf16[1024,128]{1,0:T(8,128)(2,1)S(1)} %get-tuple-element.53.asked_of, bf16[256,512]{1,0:T(8,128)(2,1)S(1)} %get-tuple-element.68.refs_0_, ...), custom_call_target="tpu_custom_call" | custom-call | flops 4026531 | bytes 5242 | tf_op jit(solution)/shard_map/pallas_call | solution.py:410
  36.8 0.8 %shard_map.81 = (bf16[128,512]{1,0:T(8,128)(2,1)S(1)}, bf16[128,512]{1,0:T(8,128)(2,1)S(1)}) custom-call(bf16[512,128]{1,0:T(8,128)(2,1)S(1)} %get-tuple-element.52.asking, bf16[1024,128]{1,0:T(8,128)(2,1)S(1)} %get-tuple-element.53.asked_of, bf16[256,512]{1,0:T(8,128)(2,1)S(1)} %get-tuple-element.68.refs_0_, f32[4,128,256]{2,1,0:T(8,128)S(1)} %get-tuple-element.74.refs_1_, ...), custom_call_target="tpu_custom_call" | custom-call | flops 1342177 | bytes 5242 | tf_op jit(solution)/shard_map/pallas_call | solution.py:410
  38.1 0.9 %collective-permute-done.14.rows = bf16[128,512]{1,0:T(8,128)(2,1)S(1)} collective-permute-done((bf16[128,512]{1,0:T(8,128)(2,1)S(1)}, bf16[128,512]{1,0:T(8,128)(2,1)S(1)}, u32[]{:S(2)}, u32[]{:S(2)}) %collective-permute-start.14) | collective-permute-done | bytes 131104 | tf_op jit(solution)/shard_map/ppermute | solution.py:486
  39.0 0.5 shard_map.83
  39.5 1.6 %collective-permute-start.16 = (bf16[128,2048]{1,0:T(8,128)(2,1)S(1)}, bf16[128,2048]{1,0:T(8,128)(2,1)S(1)}, u32[]{:S(2)}, u32[]{:S(2)}) collective-permute-start(bf16[128,2048]{1,0:T(8,128)(2,1)S(1)} %shard_map.83), channel_id=1, source_target_pairs={{0,2},{1,3},{2,0},{3,1},{4,6},{5,7},{6,4},{7,5},{8,10},{9,11},{10,... | collective-permute-start | bytes 1572872 | tf_op jit(solution)/shard_map/ppermute | solution.py:486
  41.0 1.7 %shard_map.84 = (bf16[128,512]{1,0:T(8,128)(2,1)S(1)}, bf16[128,512]{1,0:T(8,128)(2,1)S(1)}) custom-call(bf16[512,128]{1,0:T(8,128)(2,1)S(1)} %get-tuple-element.52.asking, bf16[1024,128]{1,0:T(8,128)(2,1)S(1)} %get-tuple-element.53.asked_of, bf16[256,512]{1,0:T(8,128)(2,1)S(1)} %get-tuple-element.82.refs_0_, ...), custom_call_target="tpu_custom_call" | custom-call | flops 5368709 | bytes 5242 | tf_op jit(solution)/shard_map/pallas_call | solution.py:410
  43.3 0.9 %collective-permute-done.15.rows = bf16[128,512]{1,0:T(8,128)(2,1)S(1)} collective-permute-done((bf16[128,512]{1,0:T(8,128)(2,1)S(1)}, bf16[128,512]{1,0:T(8,128)(2,1)S(1)}, u32[]{:S(2)}, u32[]{:S(2)}) %collective-permute-start.15) | collective-permute-done | bytes 131104 | tf_op jit(solution)/shard_map/ppermute | solution.py:486
  44.2 0.5 shard_map.86.own
  44.6 8.9 %collective-permute-done.16.arriving = bf16[128,2048]{1,0:T(8,128)(2,1)S(1)} collective-permute-done((bf16[128,2048]{1,0:T(8,128)(2,1)S(1)}, bf16[128,2048]{1,0:T(8,128)(2,1)S(1)}, u32[]{:S(2)}, u32[]{:S(2)}) %collective-permute-start.16) | collective-permute-done | bytes 524320 | tf_op jit(solution)/shard_map/ppermute | solution.py:486
  53.5 0.8 %shard_map.87 = bf16[128,2048]{1,0:T(8,128)(2,1)} custom-call(f32[128,2048]{1,0:T(8,128)S(1)} %shard_map.86.own, bf16[128,2048]{1,0:T(8,128)(2,1)S(1)} %collective-permute-done.16.arriving), custom_call_target="tpu_custom_call" | custom-call | flops 2621 | bytes 20971 | tf_op jit(solution)/shard_map/pallas_call | solution.py:468
  (24 shorter events, 2.5 us)
Async XLA Ops:
  0.0 16.7 %collective-permute-start.5 = (bf16[512,2048]{1,0:T(8,128)(2,1)}, bf16[512,2048]{1,0:T(8,128)(2,1)S(1)}, u32[]{:S(2)}, u32[]{:S(2)}) collective-permute-start(bf16[512,2048]{1,0:T(8,128)(2,1)} %refs_5_.1), channel_id=1, source_target_pairs={{0,1},{1,0},{2,3},{3,2},{4,5},{5,4},{6,7},{7,6},{8,9},{9,8},{10,11... | collective-permute-start | bytes 6291464 | tf_op jit(solution)/shard_map/ppermute | solution.py:486
  0.5 5.9 %collective-permute-start = (bf16[128,2048]{1,0:T(8,128)(2,1)}, bf16[128,2048]{1,0:T(8,128)(2,1)S(1)}, u32[]{:S(2)}, u32[]{:S(2)}) collective-permute-start(bf16[128,2048]{1,0:T(8,128)(2,1)} %rows_hbm.1), channel_id=1, source_target_pairs={{0,1},{1,0},{2,3},{3,2},{4,5},{5,4},{6,7},{7,6},{8,9},{9,8},{10,11... | collective-permute-start | bytes 1572872 | tf_op jit(solution)/shard_map/ppermute | solution.py:486
  0.5 16.1 %collective-permute-start.4 = (bf16[128,2048]{1,0:T(8,128)(2,1)}, bf16[128,2048]{1,0:T(8,128)(2,1)S(1)}, u32[]{:S(2)}, u32[]{:S(2)}) collective-permute-start(bf16[128,2048]{1,0:T(8,128)(2,1)} %rows_hbm.1), channel_id=1, source_target_pairs={{0,2},{1,3},{2,0},{3,1},{4,6},{5,7},{6,4},{7,5},{8,10},{9,11},{10,... | collective-permute-start | bytes 1572872 | tf_op jit(solution)/shard_map/ppermute | solution.py:486
  3.5 2.9 %copy-start = (s32[4,128]{1,0:T(4,128)S(1)}, s32[4,128]{1,0:T(4,128)}, u32[]{:S(2)}) copy-start(s32[4,128]{1,0:T(4,128)} %pattern.3) | copy-start | bytes 6148
  6.4 5.3 %copy-start.1 = (s32[8]{0:T(128)S(1)}, s32[8]{0:T(128)}, u32[]{:S(2)}) copy-start(s32[8]{0:T(128)} %param.13) | copy-start | bytes 100
  7.3 6.8 %collective-permute-start.1 = (bf16[2,4,32,128]{3,2,1,0:T(8,128)(2,1)S(1)}, bf16[2,4,32,128]{3,2,1,0:T(8,128)(2,1)S(1)}, u32[]{:S(2)}, u32[]{:S(2)}) collective-permute-start(bf16[2,4,32,128]{3,2,1,0:T(8,128)(2,1)S(1)} %get-tuple-element.49), channel_id=1, source_target_pairs={{0,16},{4,20},{8,24},{12,28},{16,0},{20,4},{24,8},{28,12},{1,17},{... | collective-permute-start | bytes 196616 | tf_op jit(solution)/shard_map/ppermute | solution.py:486
  10.1 6.4 %collective-permute-start.2 = (bf16[2,4,32,128]{3,2,1,0:T(8,128)(2,1)S(1)}, bf16[2,4,32,128]{3,2,1,0:T(8,128)(2,1)S(1)}, u32[]{:S(2)}, u32[]{:S(2)}) collective-permute-start(bf16[2,4,32,128]{3,2,1,0:T(8,128)(2,1)S(1)} %get-tuple-element.49), channel_id=1, source_target_pairs={{0,24},{4,28},{8,16},{12,20},{16,8},{20,12},{24,0},{28,4},{1,25},{... | collective-permute-start | bytes 196616 | tf_op jit(solution)/shard_map/ppermute | solution.py:486
  11.4 5.2 %collective-permute-start.3 = (bf16[2,4,32,128]{3,2,1,0:T(8,128)(2,1)S(1)}, bf16[2,4,32,128]{3,2,1,0:T(8,128)(2,1)S(1)}, u32[]{:S(2)}, u32[]{:S(2)}) collective-permute-start(bf16[2,4,32,128]{3,2,1,0:T(8,128)(2,1)S(1)} %get-tuple-element.49), channel_id=1, source_target_pairs={{0,8},{4,12},{8,0},{12,4},{16,24},{20,28},{24,16},{28,20},{1,9},{5... | collective-permute-start | bytes 196616 | tf_op jit(solution)/shard_map/ppermute | solution.py:486
  16.7 2.6 %collective-permute-start.6 = (bf16[128,2048]{1,0:T(8,128)(2,1)S(1)}, bf16[128,2048]{1,0:T(8,128)(2,1)S(1)}, u32[]{:S(2)}, u32[]{:S(2)}) collective-permute-start(bf16[128,2048]{1,0:T(8,128)(2,1)S(1)} %collective-permute-done.4.rows.refs_2_), channel_id=1, source_target_pairs={{0,1},{1,0},{2,3},{3,2},{4,5},{5,4},{6,7},{7,6},{8,9},{9,8},{10,11... | collective-permute-start | bytes 1572872 | tf_op jit(solution)/shard_map/ppermute | solution.py:486
  16.7 8.8 %collective-permute-start.12 = (bf16[4,2,4,32,128]{4,3,2,1,0:T(8,128)(2,1)S(1)}, bf16[4,2,4,32,128]{4,3,2,1,0:T(8,128)(2,1)S(1)}, u32[]{:S(2)}, u32[]{:S(2)}) collective-permute-start(bf16[4,2,4,32,128]{4,3,2,1,0:T(8,128)(2,1)S(1)} %pad_maximum_fusion.refs_9_), channel_id=1, source_target_pairs={{0,4},{4,0},{8,12},{12,8},{16,20},{20,16},{24,28},{28,24},{1,5},{5... | collective-permute-start | bytes 786440 | tf_op jit(solution)/shard_map/ppermute | solution.py:486
  20.1 7.9 %collective-permute-start.7 = (bf16[2,4,32,128]{3,2,1,0:T(8,128)(2,1)S(1)}, bf16[2,4,32,128]{3,2,1,0:T(8,128)(2,1)S(1)}, u32[]{:S(2)}, u32[]{:S(2)}) collective-permute-start(bf16[2,4,32,128]{3,2,1,0:T(8,128)(2,1)S(1)} %get-tuple-element.63.source), channel_id=1, source_target_pairs={{0,16},{4,20},{8,24},{12,28},{16,0},{20,4},{24,8},{28,12},{1,17},{... | collective-permute-start | bytes 196616 | tf_op jit(solution)/shard_map/ppermute | solution.py:486
  22.8 6.5 %collective-permute-start.8 = (bf16[2,4,32,128]{3,2,1,0:T(8,128)(2,1)S(1)}, bf16[2,4,32,128]{3,2,1,0:T(8,128)(2,1)S(1)}, u32[]{:S(2)}, u32[]{:S(2)}) collective-permute-start(bf16[2,4,32,128]{3,2,1,0:T(8,128)(2,1)S(1)} %get-tuple-element.63.source), channel_id=1, source_target_pairs={{0,24},{4,28},{8,16},{12,20},{16,8},{20,12},{24,0},{28,4},{1,25},{... | collective-permute-start | bytes 196616 | tf_op jit(solution)/shard_map/ppermute | solution.py:486
  23.4 6.3 %collective-permute-start.9 = (bf16[2,4,32,128]{3,2,1,0:T(8,128)(2,1)S(1)}, bf16[2,4,32,128]{3,2,1,0:T(8,128)(2,1)S(1)}, u32[]{:S(2)}, u32[]{:S(2)}) collective-permute-start(bf16[2,4,32,128]{3,2,1,0:T(8,128)(2,1)S(1)} %get-tuple-element.63.source), channel_id=1, source_target_pairs={{0,8},{4,12},{8,0},{12,4},{16,24},{20,28},{24,16},{28,20},{1,9},{5... | collective-permute-start | bytes 196616 | tf_op jit(solution)/shard_map/ppermute | solution.py:486
  23.9 5.8 %collective-permute-start.10 = (bf16[2,4,32,128]{3,2,1,0:T(8,128)(2,1)S(1)}, bf16[2,4,32,128]{3,2,1,0:T(8,128)(2,1)S(1)}, u32[]{:S(2)}, u32[]{:S(2)}) collective-permute-start(bf16[2,4,32,128]{3,2,1,0:T(8,128)(2,1)S(1)} %shard_map.78), channel_id=1, source_target_pairs={{0,4},{4,0},{8,12},{12,8},{16,20},{20,16},{24,28},{28,24},{1,5},{5... | collective-permute-start | bytes 196616 | tf_op jit(solution)/shard_map/ppermute | solution.py:486
  25.5 5.8 %collective-permute-start.11 = (bf16[2,4,32,128]{3,2,1,0:T(8,128)(2,1)S(1)}, bf16[2,4,32,128]{3,2,1,0:T(8,128)(2,1)S(1)}, u32[]{:S(2)}, u32[]{:S(2)}) collective-permute-start(bf16[2,4,32,128]{3,2,1,0:T(8,128)(2,1)S(1)} %shard_map.78), channel_id=1, source_target_pairs={{0,12},{4,8},{8,4},{12,0},{16,28},{20,24},{24,20},{28,16},{1,13},{... | collective-permute-start | bytes 196616 | tf_op jit(solution)/shard_map/ppermute | solution.py:486
  31.3 5.5 %collective-permute-start.13 = (bf16[2,2,4,32,128]{4,3,2,1,0:T(8,128)(2,1)S(1)}, bf16[2,2,4,32,128]{4,3,2,1,0:T(8,128)(2,1)S(1)}, u32[]{:S(2)}, u32[]{:S(2)}) collective-permute-start(bf16[2,2,4,32,128]{4,3,2,1,0:T(8,128)(2,1)S(1)} %pad_maximum_fusion.1.refs_4_.refs_12_), channel_id=1, source_target_pairs={{0,4},{4,0},{8,12},{12,8},{16,20},{20,16},{24,28},{28,24},{1,5},{5... | collective-permute-start | bytes 393224 | tf_op jit(solution)/shard_map/ppermute | solution.py:486
  37.6 1.4 %collective-permute-start.14 = (bf16[128,512]{1,0:T(8,128)(2,1)S(1)}, bf16[128,512]{1,0:T(8,128)(2,1)S(1)}, u32[]{:S(2)}, u32[]{:S(2)}) collective-permute-start(bf16[128,512]{1,0:T(8,128)(2,1)S(1)} %get-tuple-element.79), channel_id=1, source_target_pairs={{0,1},{1,0},{2,3},{3,2},{4,5},{5,4},{6,7},{7,6},{8,9},{9,8},{10,11... | collective-permute-start | bytes 393224 | tf_op jit(solution)/shard_map/ppermute | solution.py:486
  39.5 14.0 %collective-permute-start.16 = (bf16[128,2048]{1,0:T(8,128)(2,1)S(1)}, bf16[128,2048]{1,0:T(8,128)(2,1)S(1)}, u32[]{:S(2)}, u32[]{:S(2)}) collective-permute-start(bf16[128,2048]{1,0:T(8,128)(2,1)S(1)} %shard_map.83), channel_id=1, source_target_pairs={{0,2},{1,3},{2,0},{3,1},{4,6},{5,7},{6,4},{7,5},{8,10},{9,11},{10,... | collective-permute-start | bytes 1572872 | tf_op jit(solution)/shard_map/ppermute | solution.py:486
  42.7 1.4 %collective-permute-start.15 = (bf16[128,512]{1,0:T(8,128)(2,1)S(1)}, bf16[128,512]{1,0:T(8,128)(2,1)S(1)}, u32[]{:S(2)}, u32[]{:S(2)}) collective-permute-start(bf16[128,512]{1,0:T(8,128)(2,1)S(1)} %get-tuple-element.83), channel_id=1, source_target_pairs={{0,1},{1,0},{2,3},{3,2},{4,5},{5,4},{6,7},{7,6},{8,9},{9,8},{10,11... | collective-permute-start | bytes 393224 | tf_op jit(solution)/shard_map/ppermute | solution.py:486
